TPU v7x, 32 devices: a whole 2x2x4 slice. The times are simulated.
32 devices in a mesh: wide: 8 (over z, y), narrow: 4 (over x, core).
Axes of the slice: x: 2, y: 2, z: 4, core: 2. Of those that a mesh axis runs over, the one named last changes fastest.
Arguments:
- noised: int32 [8, 1024], P('wide'), may hold values from 0 to 8191, as said below
- clean: int32 [8, 1024], P('wide'), may hold values from 0 to 8191
- timesteps: int32 [8, 1024], P('wide'), may hold values from 1 to 1000
- segments: int32 [8, 1024], P('wide'), may hold values from 0 to 7, never falling along the last dimension, each value on 1 to 512 neighbouring positions
- counted: int32 [8, 1024], P('wide'), may hold values from 0 to 1
- attn_in: float32 [2, 3, 768, 768], P(None, None, 'wide', 'narrow'), may hold values from -0.109375 to 0.109375
- attn_out: float32 [2, 768, 768], P(None, 'wide', 'narrow'), may hold values from -0.875 to 0.875
- ffn_in: float32 [2, 768, 3072], P(None, 'wide', 'narrow'), may hold values from -0.21875 to 0.21875
- ffn_out: float32 [2, 768, 3072], P(None, 'wide', 'narrow'), may hold values from -0.15625 to 0.15625
- tables: float32 [2, 768, 8192], P(None, 'wide', 'narrow')
- gains: float32 [5, 768], P(None, 'wide')
- attn_in_mean: float32 [2, 3, 768, 768], P(None, None, 'wide', 'narrow'), may hold values from -5.9604645e-07 to 5.9604645e-07
- attn_out_mean: float32 [2, 768, 768], P(None, 'wide', 'narrow'), may hold values from -5.9604645e-07 to 5.9604645e-07
- ffn_in_mean: float32 [2, 768, 3072], P(None, 'wide', 'narrow'), may hold values from -5.9604645e-07 to 5.9604645e-07
- ffn_out_mean: float32 [2, 768, 3072], P(None, 'wide', 'narrow'), may hold values from -5.9604645e-07 to 5.9604645e-07
- tables_mean: float32 [2, 768, 8192], P(None, 'wide', 'narrow'), may hold values from -5.9604645e-07 to 5.9604645e-07
- gains_mean: float32 [5, 768], P(None, 'wide'), may hold values from -2.3841858e-06 to 2.3841858e-06
- attn_in_square: float32 [2, 3, 768, 768], P(None, None, 'wide', 'narrow'), may hold values from 9.348406e-16 to 3.7393625e-15
- attn_out_square: float32 [2, 768, 768], P(None, 'wide', 'narrow'), may hold values from 9.348406e-16 to 3.7393625e-15
- ffn_in_square: float32 [2, 768, 3072], P(None, 'wide', 'narrow'), may hold values from 9.348406e-16 to 3.7393625e-15
- ffn_out_square: float32 [2, 768, 3072], P(None, 'wide', 'narrow'), may hold values from 9.348406e-16 to 3.7393625e-15
- tables_square: float32 [2, 768, 8192], P(None, 'wide', 'narrow')
- gains_square: float32 [5, 768], P(None, 'wide'), may hold values from 1.495745e-14 to 5.98298e-14
Outputs:
- loss_sum: float32 [], replicated
- token_total: float32 [], replicated
- grad_norm: float32 [], replicated
- attn_in_next: float32 [2, 3, 768, 768], P(None, None, 'wide', 'narrow')
- attn_in_mean_next: float32 [2, 3, 768, 768], P(None, None, 'wide', 'narrow')
- attn_in_square_next: float32 [2, 3, 768, 768], P(None, None, 'wide', 'narrow')
- attn_in_copy: bfloat16 [2, 3, 768, 768], P(None, None, 'wide', 'narrow')
- attn_out_next: float32 [2, 768, 768], P(None, 'wide', 'narrow')
- attn_out_mean_next: float32 [2, 768, 768], P(None, 'wide', 'narrow')
- attn_out_square_next: float32 [2, 768, 768], P(None, 'wide', 'narrow')
- attn_out_copy: bfloat16 [2, 768, 768], P(None, 'wide', 'narrow')
- ffn_in_next: float32 [2, 768, 3072], P(None, 'wide', 'narrow')
- ffn_in_mean_next: float32 [2, 768, 3072], P(None, 'wide', 'narrow')
- ffn_in_square_next: float32 [2, 768, 3072], P(None, 'wide', 'narrow')
- ffn_in_copy: bfloat16 [2, 768, 3072], P(None, 'wide', 'narrow')
- ffn_out_next: float32 [2, 768, 3072], P(None, 'wide', 'narrow')
- ffn_out_mean_next: float32 [2, 768, 3072], P(None, 'wide', 'narrow')
- ffn_out_square_next: float32 [2, 768, 3072], P(None, 'wide', 'narrow')
- ffn_out_copy: bfloat16 [2, 768, 3072], P(None, 'wide', 'narrow')
- tables_next: float32 [2, 768, 8192], P(None, 'wide', 'narrow')
- tables_mean_next: float32 [2, 768, 8192], P(None, 'wide', 'narrow')
- tables_square_next: float32 [2, 768, 8192], P(None, 'wide', 'narrow')
- tables_copy: bfloat16 [2, 768, 8192], P(None, 'wide', 'narrow')
- gains_next: float32 [5, 768], P(None, 'wide')
- gains_mean_next: float32 [5, 768], P(None, 'wide')
- gains_square_next: float32 [5, 768], P(None, 'wide')
- gains_copy: bfloat16 [5, 768], P(None, 'wide')
Inputs may be any that keep to these rules, and one draw needn't show every extreme that they name: noised tokens follow q(x_t | x_0) of the uniform plan: equal to clean with probability (1000 - t)/1000, else a uniform token.
All inputs are finite; a program needn't handle non-finite values.
Results may differ from a plain program's by a relative error of at most 0.004.
The roundings to bfloat16 on the way count: a program that leaves them out, or rounds other values in their place, can miss the bound.
Values may be sent and summed in bfloat16 or wider, within the bound.
A program may use at most 192 MiB of HBM per device.

v0:
```python
import math

import jax
import jax.numpy as jnp
from jax import lax
from jax.sharding import PartitionSpec as P

D = 768
HD = 64
V = 8192
STEPS = 1000
ADAM_STEP = 10


NORM_EPS = 1e-05
LEARN_RATE = 0.05
GAIN_RATE = 0.75
FIRST_DECAY = 0.9
SECOND_DECAY = 0.999
ADAM_EPS = 1e-08
WEIGHT_DECAY = 0.01
CLIP_NORM = 0.005


def add_heads(partial_value):
    return lax.psum(partial_value, "narrow")


def back_heads(partial_value):
    return lax.psum(partial_value, "narrow")


def rms_forward(value, gain):
    scale_row = lax.rsqrt(jnp.mean(value * value, axis=-1, keepdims=True) + NORM_EPS)
    return (value * scale_row * gain, scale_row)


def rms_backward(grad, value, scale_row, gain):
    unit = value * scale_row
    scaled = grad * gain
    back = scale_row * (scaled - unit * jnp.mean(scaled * unit, axis=-1, keepdims=True))
    return (back, jnp.sum(grad * unit, axis=0))


def time_features(timestep_row):
    half_width = D // 2
    rates = jnp.exp(-math.log(10000.0) * jnp.arange(half_width, dtype=jnp.float32) / half_width)
    angles = timestep_row.astype(jnp.float32)[:, None] * rates[None, :]
    return jnp.concatenate([jnp.sin(angles), jnp.cos(angles)], axis=1)


def masked_scores(queries, key_rows, segment):
    scores = jnp.einsum(
        "qhd,khd->hqk", queries, key_rows, preferred_element_type=jnp.float32
    ) * HD ** (-0.5)
    return jnp.where((segment[:, None] == segment[None, :])[None], scores, -1e30)


def attend(entry):
    queries, key_rows, values, segment = entry
    scores = masked_scores(queries, key_rows, segment)
    row_top = jnp.max(scores, axis=-1, keepdims=True)
    log_total = row_top + jnp.log(jnp.sum(jnp.exp(scores - row_top), axis=-1, keepdims=True))
    probs = jnp.exp(scores - log_total).astype(jnp.bfloat16)
    mixed = jnp.einsum("hqk,khd->qhd", probs, values, preferred_element_type=jnp.float32)
    return (mixed.astype(jnp.bfloat16), log_total)


def attend_back(entry):
    queries, key_rows, values, segment, log_total, grad_mixed = entry
    probs = jnp.exp(masked_scores(queries, key_rows, segment) - log_total)
    grad_probs = jnp.einsum("qhd,khd->hqk", grad_mixed, values, preferred_element_type=jnp.float32)
    grad_scores = (
        probs * (grad_probs - jnp.sum(probs * grad_probs, axis=-1, keepdims=True))
    ).astype(jnp.bfloat16)
    grad_query = jnp.einsum(
        "hqk,khd->qhd", grad_scores, key_rows, preferred_element_type=jnp.float32
    ) * HD ** (-0.5)
    grad_key = jnp.einsum(
        "hqk,qhd->khd", grad_scores, queries, preferred_element_type=jnp.float32
    ) * HD ** (-0.5)
    grad_value = jnp.einsum(
        "hqk,qhd->khd", probs.astype(jnp.bfloat16), grad_mixed, preferred_element_type=jnp.float32
    )
    return (grad_query, grad_key, grad_value)


def layer_forward(residual, segments, query_w, output_w, expand_w, reduce_w, gain_attn, gain_ffn):
    seq_count, seq_len = segments.shape
    normed, scale_one = rms_forward(residual, gain_attn)
    normed = normed.astype(jnp.bfloat16)
    projected = jnp.einsum(
        "sd,cde->cse", normed, query_w, preferred_element_type=jnp.float32
    ).astype(jnp.bfloat16)
    heads = projected.reshape(3, seq_count, seq_len, -1, HD)
    mixed, log_total = lax.map(attend, (heads[0], heads[1], heads[2], segments))
    mixed = mixed.reshape(seq_count * seq_len, -1)
    middle = residual + add_heads(
        jnp.einsum("se,de->sd", mixed, output_w, preferred_element_type=jnp.float32)
    )
    normed_two, scale_two = rms_forward(middle, gain_ffn)
    normed_two = normed_two.astype(jnp.bfloat16)
    before = jnp.dot(normed_two, expand_w, preferred_element_type=jnp.float32)
    after = jax.nn.gelu(before).astype(jnp.bfloat16)
    result = middle + add_heads(
        jnp.einsum("sf,df->sd", after, reduce_w, preferred_element_type=jnp.float32)
    )
    return (
        result,
        (
            residual,
            scale_one,
            normed,
            projected,
            log_total,
            mixed,
            middle,
            scale_two,
            normed_two,
            before,
            after,
        ),
    )


def layer_backward(
    grad, kept, segments, query_w, output_w, expand_w, reduce_w, gain_attn, gain_ffn
):
    (
        residual,
        scale_one,
        normed,
        projected,
        log_total,
        mixed,
        middle,
        scale_two,
        normed_two,
        before,
        after,
    ) = kept
    seq_count, seq_len = segments.shape
    grad_branch = grad.astype(jnp.bfloat16)
    grad_after = jnp.dot(grad_branch, reduce_w, preferred_element_type=jnp.float32)
    grad_reduce = jnp.einsum("sd,sf->df", grad_branch, after, preferred_element_type=jnp.float32)
    _, gelu_pull = jax.vjp(jax.nn.gelu, before)
    grad_before = gelu_pull(grad_after)[0].astype(jnp.bfloat16)
    grad_expand = jnp.einsum(
        "sd,sf->df", normed_two, grad_before, preferred_element_type=jnp.float32
    )
    grad_normed_two = back_heads(
        jnp.einsum("sf,df->sd", grad_before, expand_w, preferred_element_type=jnp.float32)
    )
    grad_middle, grad_gain_ffn = rms_backward(grad_normed_two, middle, scale_two, gain_ffn)
    grad_middle = grad_middle + grad
    grad_attn = grad_middle.astype(jnp.bfloat16)
    grad_mixed = jnp.dot(grad_attn, output_w, preferred_element_type=jnp.float32).astype(
        jnp.bfloat16
    )
    grad_output = jnp.einsum("sd,se->de", grad_attn, mixed, preferred_element_type=jnp.float32)
    heads = projected.reshape(3, seq_count, seq_len, -1, HD)
    grad_query, grad_key, grad_value = lax.map(
        attend_back,
        (
            heads[0],
            heads[1],
            heads[2],
            segments,
            log_total,
            grad_mixed.reshape(seq_count, seq_len, -1, HD),
        ),
    )
    grad_projected = (
        jnp.stack([grad_query, grad_key, grad_value])
        .reshape(3, seq_count * seq_len, -1)
        .astype(jnp.bfloat16)
    )
    grad_query_w = jnp.einsum(
        "sd,cse->cde", normed, grad_projected, preferred_element_type=jnp.float32
    )
    grad_normed = back_heads(
        jnp.einsum("cse,cde->sd", grad_projected, query_w, preferred_element_type=jnp.float32)
    )
    grad_input, grad_gain_attn = rms_backward(grad_normed, residual, scale_one, gain_attn)
    return (
        grad_input + grad_middle,
        (
            grad_query_w,
            grad_output,
            grad_expand,
            grad_reduce,
            jnp.stack([grad_gain_attn, grad_gain_ffn]),
        ),
    )


def adam(weight, grad, first, second, decay, rate):
    first_new = FIRST_DECAY * first + (1.0 - FIRST_DECAY) * grad
    second_new = SECOND_DECAY * second + (1.0 - SECOND_DECAY) * grad * grad
    first_hat = first_new / (1.0 - FIRST_DECAY**ADAM_STEP)
    second_hat = second_new / (1.0 - SECOND_DECAY**ADAM_STEP)
    weight_new = weight - rate * (first_hat / (jnp.sqrt(second_hat) + ADAM_EPS) + decay * weight)
    return (weight_new, first_new, second_new, weight_new.astype(jnp.bfloat16))


def per_device(
    noised,
    clean,
    timesteps,
    segments,
    counted,
    attn_in,
    attn_out,
    ffn_in,
    ffn_out,
    tables,
    gains,
    attn_in_mean,
    attn_out_mean,
    ffn_in_mean,
    ffn_out_mean,
    tables_mean,
    gains_mean,
    attn_in_square,
    attn_out_square,
    ffn_in_square,
    ffn_out_square,
    tables_square,
    gains_square,
):
    layers = attn_in.shape[0]
    mask = counted.reshape(-1).astype(jnp.float32)
    token_total = lax.psum(jnp.sum(mask), "wide")
    query_w, output_w, expand_w, reduce_w, table_w, gain_low = (
        lax.all_gather(attn_in.astype(jnp.bfloat16), "wide", axis=2, tiled=True),
        lax.all_gather(attn_out.astype(jnp.bfloat16), "wide", axis=1, tiled=True),
        lax.all_gather(ffn_in.astype(jnp.bfloat16), "wide", axis=1, tiled=True),
        lax.all_gather(ffn_out.astype(jnp.bfloat16), "wide", axis=1, tiled=True),
        lax.all_gather(tables.astype(jnp.bfloat16), "wide", axis=1, tiled=True),
        lax.all_gather(gains.astype(jnp.bfloat16), "wide", axis=1, tiled=True),
    )
    gain_w = gain_low.astype(jnp.float32)
    noised_flat = noised.reshape(-1)
    clean_flat = clean.reshape(-1)
    step_flat = timesteps.reshape(-1)
    vocab_local = table_w.shape[2]
    vocab_ids = lax.axis_index("narrow") * vocab_local + jnp.arange(vocab_local, dtype=jnp.int32)
    picks = (noised_flat[:, None] == vocab_ids[None, :]).astype(jnp.bfloat16)
    looked = add_heads(
        jnp.einsum("sv,dv->sd", picks, table_w[0], preferred_element_type=jnp.float32)
    )
    residual = math.sqrt(D) * looked + time_features(step_flat)
    kept_layers = []
    for layer_index in range(layers):
        residual, kept = layer_forward(
            residual,
            segments,
            query_w[layer_index],
            output_w[layer_index],
            expand_w[layer_index],
            reduce_w[layer_index],
            gain_w[2 * layer_index],
            gain_w[2 * layer_index + 1],
        )
        kept_layers.append(kept)
    final, scale_final = rms_forward(residual, gain_w[2 * layers])
    final_low = final.astype(jnp.bfloat16)
    logits = jnp.dot(final_low, table_w[1], preferred_element_type=jnp.float32)
    local_top = jnp.max(logits, axis=1)
    row_top = lax.pmax(local_top, "narrow")
    row_total = lax.psum(jnp.sum(jnp.exp(logits - row_top[:, None]), axis=1), "narrow")
    log_probs = logits - (row_top + jnp.log(row_total))[:, None]
    probs = jnp.exp(log_probs)
    clamped = jnp.maximum(step_flat, 2).astype(jnp.float32)[:, None]
    beta = 1.0 / (STEPS - clamped + 1.0)
    retain = (STEPS - clamped + 1.0) / STEPS
    spread = (clamped - 1.0) / (STEPS * V)
    at_noised = (vocab_ids[None, :] == noised_flat[:, None]).astype(jnp.float32)
    at_clean = (vocab_ids[None, :] == clean_flat[:, None]).astype(jnp.float32)
    forward_fac = beta / V + (1.0 - beta) * at_noised
    backward_fac = retain * at_clean + spread
    joint = forward_fac * backward_fac
    marginal = retain * probs + spread
    joint_total, cross, model_total, weighted, aligned, clean_logp = lax.psum(
        (
            jnp.sum(joint, axis=1),
            jnp.sum(joint * (jnp.log(backward_fac) - jnp.log(marginal)), axis=1),
            jnp.sum(forward_fac * marginal, axis=1),
            jnp.sum(probs * joint / marginal, axis=1),
            jnp.sum(forward_fac * probs, axis=1),
            jnp.sum(at_clean * log_probs, axis=1),
        ),
        "narrow",
    )
    divergence = cross / joint_total - jnp.log(joint_total) + jnp.log(model_total)
    first_step = step_flat == 1
    losses = jnp.where(first_step, -clean_logp, divergence)
    pull = retain * (
        -(joint / joint_total[:, None]) / marginal + forward_fac / model_total[:, None]
    )
    centre = retain[:, 0] * (-weighted / joint_total + aligned / model_total)
    grad_kl = probs * (pull - centre[:, None])
    grad_recon = probs - at_clean
    grad_logits = (
        (mask / token_total)[:, None] * jnp.where(first_step[:, None], grad_recon, grad_kl)
    ).astype(jnp.bfloat16)
    grad_table_out = jnp.einsum(
        "sd,sv->dv", final_low, grad_logits, preferred_element_type=jnp.float32
    )
    grad_final = back_heads(
        jnp.einsum("sv,dv->sd", grad_logits, table_w[1], preferred_element_type=jnp.float32)
    )
    grad_x, grad_gain_final = rms_backward(grad_final, residual, scale_final, gain_w[2 * layers])
    layer_grads = [None] * layers
    for layer_index in reversed(range(layers)):
        grad_x, produced = layer_backward(
            grad_x,
            kept_layers[layer_index],
            segments,
            query_w[layer_index],
            output_w[layer_index],
            expand_w[layer_index],
            reduce_w[layer_index],
            gain_w[2 * layer_index],
            gain_w[2 * layer_index + 1],
        )
        layer_grads[layer_index] = produced
    grad_look = (math.sqrt(D) * grad_x).astype(jnp.bfloat16)
    grad_table_in = jnp.einsum("sd,sv->dv", grad_look, picks, preferred_element_type=jnp.float32)
    stacked = [jnp.stack([entry[which] for entry in layer_grads]) for which in range(5)]
    gain_layers = stacked[4].reshape(2 * layers, -1)
    grad_tables_all = jnp.stack([grad_table_in, grad_table_out])
    grad_attn_in, grad_attn_out, grad_ffn_in, grad_ffn_out, grad_tables, grad_gains = (
        lax.psum_scatter(stacked[0], "wide", scatter_dimension=2, tiled=True),
        lax.psum_scatter(stacked[1], "wide", scatter_dimension=1, tiled=True),
        lax.psum_scatter(stacked[2], "wide", scatter_dimension=1, tiled=True),
        lax.psum_scatter(stacked[3], "wide", scatter_dimension=1, tiled=True),
        lax.psum_scatter(grad_tables_all, "wide", scatter_dimension=1, tiled=True),
        lax.psum_scatter(
            jnp.concatenate([gain_layers, grad_gain_final[None, :]], axis=0),
            "wide",
            scatter_dimension=1,
            tiled=True,
        ),
    )
    narrow_first = (lax.axis_index("narrow") == 0).astype(jnp.float32)
    squares = (
        jnp.sum(grad_attn_in * grad_attn_in)
        + jnp.sum(grad_attn_out * grad_attn_out)
        + jnp.sum(grad_ffn_in * grad_ffn_in)
        + jnp.sum(grad_ffn_out * grad_ffn_out)
        + jnp.sum(grad_tables * grad_tables)
        + narrow_first * jnp.sum(grad_gains * grad_gains)
    )
    squares, loss_sum = lax.psum(
        (squares, narrow_first * jnp.sum(mask * losses)), ("wide", "narrow")
    )
    grad_norm = jnp.sqrt(squares)
    factor = jnp.minimum(1.0, CLIP_NORM / (grad_norm + 1e-06))
    attn_in_next, attn_in_mean_next, attn_in_square_next, attn_in_copy = adam(
        attn_in, factor * grad_attn_in, attn_in_mean, attn_in_square, WEIGHT_DECAY, LEARN_RATE
    )
    attn_out_next, attn_out_mean_next, attn_out_square_next, attn_out_copy = adam(
        attn_out, factor * grad_attn_out, attn_out_mean, attn_out_square, WEIGHT_DECAY, LEARN_RATE
    )
    ffn_in_next, ffn_in_mean_next, ffn_in_square_next, ffn_in_copy = adam(
        ffn_in, factor * grad_ffn_in, ffn_in_mean, ffn_in_square, WEIGHT_DECAY, LEARN_RATE
    )
    ffn_out_next, ffn_out_mean_next, ffn_out_square_next, ffn_out_copy = adam(
        ffn_out, factor * grad_ffn_out, ffn_out_mean, ffn_out_square, WEIGHT_DECAY, LEARN_RATE
    )
    tables_next, tables_mean_next, tables_square_next, tables_copy = adam(
        tables, factor * grad_tables, tables_mean, tables_square, WEIGHT_DECAY, LEARN_RATE
    )
    gains_next, gains_mean_next, gains_square_next, gains_copy = adam(
        gains, factor * grad_gains, gains_mean, gains_square, 0.0, GAIN_RATE
    )
    return (
        loss_sum,
        token_total,
        grad_norm,
        attn_in_next,
        attn_in_mean_next,
        attn_in_square_next,
        attn_in_copy,
        attn_out_next,
        attn_out_mean_next,
        attn_out_square_next,
        attn_out_copy,
        ffn_in_next,
        ffn_in_mean_next,
        ffn_in_square_next,
        ffn_in_copy,
        ffn_out_next,
        ffn_out_mean_next,
        ffn_out_square_next,
        ffn_out_copy,
        tables_next,
        tables_mean_next,
        tables_square_next,
        tables_copy,
        gains_next,
        gains_mean_next,
        gains_square_next,
        gains_copy,
    )


def solution(mesh):
    placed = (
        P("wide", None),
        P("wide", None),
        P("wide", None),
        P("wide", None),
        P("wide", None),
        P(None, None, "wide", "narrow"),
        P(None, "wide", "narrow"),
        P(None, "wide", "narrow"),
        P(None, "wide", "narrow"),
        P(None, "wide", "narrow"),
        P(None, "wide"),
        P(None, None, "wide", "narrow"),
        P(None, "wide", "narrow"),
        P(None, "wide", "narrow"),
        P(None, "wide", "narrow"),
        P(None, "wide", "narrow"),
        P(None, "wide"),
        P(None, None, "wide", "narrow"),
        P(None, "wide", "narrow"),
        P(None, "wide", "narrow"),
        P(None, "wide", "narrow"),
        P(None, "wide", "narrow"),
        P(None, "wide"),
    )
    return jax.shard_map(
        per_device,
        mesh=mesh,
        in_specs=placed,
        out_specs=(
            P(),
            P(),
            P(),
            P(None, None, "wide", "narrow"),
            P(None, None, "wide", "narrow"),
            P(None, None, "wide", "narrow"),
            P(None, None, "wide", "narrow"),
            P(None, "wide", "narrow"),
            P(None, "wide", "narrow"),
            P(None, "wide", "narrow"),
            P(None, "wide", "narrow"),
            P(None, "wide", "narrow"),
            P(None, "wide", "narrow"),
            P(None, "wide", "narrow"),
            P(None, "wide", "narrow"),
            P(None, "wide", "narrow"),
            P(None, "wide", "narrow"),
            P(None, "wide", "narrow"),
            P(None, "wide", "narrow"),
            P(None, "wide", "narrow"),
            P(None, "wide", "narrow"),
            P(None, "wide", "narrow"),
            P(None, "wide", "narrow"),
            P(None, "wide"),
            P(None, "wide"),
            P(None, "wide"),
            P(None, "wide"),
        ),
        check_vma=False,
    )
```

profile of v0, /device:TPU:0, one launch (start us, length us, event | category | flops | bytes accessed | tf_op | source)
XLA Modules:
  0.0 1905.6 jit_solution(7629342030075855249)
XLA Ops:
  11.1 28.3 %all-gather = bf16[8,96,5]{1,2,0:T(8,128)(2,1)S(1)} all-gather(bf16[1,96,5]{1,2,0:T(8,128)(2,1)S(1)} %convert_bitcast_fusion.2), channel_id=1, replica_groups=mesh['wide'=8,'narrow'=4] {'wide'}, dimensions={0}, use_global_device_ids=true | all-gather | bytes 8640 | tf_op jit(solution)/shard_map/all_gather | solution.py:240
  40.2 36.4 %all_gather.21 = bf16[2,768,192]{2,1,0:T(8,128)(2,1)} all-gather(bf16[2,96,192]{2,1,0:T(8,128)(2,1)S(1)} %convert_element_type.196), channel_id=1, replica_groups=mesh['wide'=8,'narrow'=4] {'wide'}, dimensions={1}, use_global_device_ids=true | all-gather | bytes 663552 | tf_op jit(solution)/shard_map/all_gather | solution.py:236
  76.6 42.4 %all-gather.6.cloned.1.call-done = bf16[2,768,2048]{2,1,0:T(8,128)(2,1)} async-done(((bf16[2,96,2048]{2,1,0:T(8,128)(2,1)}), bf16[2,768,2048]{2,1,0:T(8,128)(2,1)}) %all-gather.6.cloned.1.call-update) | async-done | bytes 6291472 | tf_op jit(solution)/shard_map/all_gather | solution.py:239
  119.0 7.1 fusion.2
  128.4 7.1 multiply_sine_fusion
  135.5 38.1 %all-gather.8.cloned.1.call-done = bf16[2,3,768,192]{3,0,1,2:T(2,128)(2,1)} async-done(((bf16[2,3,96,192]{3,0,1,2:T(2,128)(2,1)}), bf16[2,3,768,192]{3,0,1,2:T(2,128)(2,1)}) %all-gather.8.cloned.1.call-update) | async-done | bytes 1769488 | tf_op jit(solution)/shard_map/all_gather | solution.py:235
  173.6 7.8 fusion.114
  183.5 59.5 %all-reduce.13.cloned.1.call-done = f32[1024,768]{1,0:T(8,128)} async-done(((f32[1024,768]{1,0:T(8,128)}), f32[1024,768]{1,0:T(8,128)}) %all-reduce.13.cloned.1.call-update) | async-done | bytes 3145744 | tf_op jit(solution)/shard_map/psum | solution.py:26
  256.7 4.6 convolution_convert_fusion.5
  268.7 64.5 %all-reduce.15.cloned.1.call-done = f32[1024,768]{1,0:T(8,128)} async-done(((f32[1024,768]{1,0:T(8,128)}), f32[1024,768]{1,0:T(8,128)}) %all-reduce.15.cloned.1.call-update) | async-done | bytes 3145744 | tf_op jit(solution)/shard_map/psum | solution.py:26
  337.1 50.9 %all-gather.10.cloned.1.call-done = bf16[2,768,768]{2,1,0:T(8,128)(2,1)} async-done(((bf16[2,96,768]{2,1,0:T(8,128)(2,1)}), bf16[2,768,768]{2,1,0:T(8,128)(2,1)}) %all-gather.10.cloned.1.call-update) | async-done | bytes 2359312 | tf_op jit(solution)/shard_map/all_gather | solution.py:237
  391.7 49.6 %all-gather.12.cloned.1.call-done = bf16[2,768,768]{2,1,0:T(8,128)(2,1)} async-done(((bf16[2,96,768]{2,1,0:T(8,128)(2,1)}), bf16[2,768,768]{2,1,0:T(8,128)(2,1)}) %all-gather.12.cloned.1.call-update) | async-done | bytes 2359312 | tf_op jit(solution)/shard_map/all_gather | solution.py:238
  441.3 4.9 fusion.66
  446.2 6.5 copy.172
  452.7 60.5 %all-reduce.17.cloned.1.call-done = f32[1024,768]{1,0:T(8,128)} async-done(((f32[1024,768]{1,0:T(8,128)}), f32[1024,768]{1,0:T(8,128)}) %all-reduce.17.cloned.1.call-update) | async-done | bytes 3145744 | tf_op jit(solution)/shard_map/psum | solution.py:26
  527.2 4.7 convolution_convert_fusion.4
  535.5 68.2 %all-reduce.19.cloned.1.call-done = f32[1024,768]{1,0:T(8,128)} async-done(((f32[1024,768]{1,0:T(8,128)}), f32[1024,768]{1,0:T(8,128)}) %all-reduce.19.cloned.1.call-update) | async-done | bytes 3145744 | tf_op jit(solution)/shard_map/psum | solution.py:26
  614.9 22.0 %psum.151 = f32[]{:T(128)} all-reduce(f32[]{:T(128)} %convert_reduce_fusion), channel_id=1, replica_groups=mesh['wide'=8,'narrow'=4] {'wide'}, use_global_device_ids=true, to_apply=%region_29.30 | all-reduce | flops 1 | bytes 8 | tf_op jit(solution)/shard_map/psum | solution.py:233
  639.3 43.0 %all-reduce.21.cloned.1.call-done = f32[1024,768]{1,0:T(8,128)} async-done(((f32[1024,768]{1,0:T(8,128)}), f32[1024,768]{1,0:T(8,128)}) %all-reduce.21.cloned.1.call-update) | async-done | bytes 3145744 | tf_op jit(solution)/shard_map/psum | solution.py:26
  685.6 9.5 fusion.117
  695.2 6.5 pmax.7
  701.6 5.2 exponential_reduce_fusion.2
  706.9 6.3 psum.145
  713.9 12.4 fusion.18
  726.3 12.2 all-reduce.1
  740.6 10.5 fusion.16
  753.1 6.9 fusion.42
  760.1 69.4 %all-reduce.23.cloned.1.call-done = f32[1024,768]{1,0:T(8,128)} async-done(((f32[1024,768]{1,0:T(8,128)}), f32[1024,768]{1,0:T(8,128)}) %all-reduce.23.cloned.1.call-update) | async-done | bytes 3145744 | tf_op jit(solution)/shard_map/psum | solution.py:30
  843.6 68.4 %all-reduce.25.cloned.1.call-done = f32[1024,768]{1,0:T(8,128)} async-done(((f32[1024,768]{1,0:T(8,128)}), f32[1024,768]{1,0:T(8,128)}) %all-reduce.25.cloned.1.call-update) | async-done | bytes 3145744 | tf_op jit(solution)/shard_map/psum | solution.py:30
  926.4 7.2 multiply_reduce_fusion.1
  933.6 7.0 multiply_convert_fusion.1
  948.3 68.2 %all-reduce.27.cloned.1.call-done = f32[1024,768]{1,0:T(8,128)} async-done(((f32[1024,768]{1,0:T(8,128)}), f32[1024,768]{1,0:T(8,128)}) %all-reduce.27.cloned.1.call-update) | async-done | bytes 3145744 | tf_op jit(solution)/shard_map/psum | solution.py:30
  1032.6 68.6 %all-reduce.29.cloned.1.call-done = f32[1024,768]{1,0:T(8,128)} async-done(((f32[1024,768]{1,0:T(8,128)}), f32[1024,768]{1,0:T(8,128)}) %all-reduce.29.cloned.1.call-update) | async-done | bytes 3145744 | tf_op jit(solution)/shard_map/psum | solution.py:30
  1105.7 4.6 multiply_add_fusion.1
  1117.0 7.2 multiply_reduce_fusion
  1124.2 7.0 multiply_convert_fusion
  1147.5 59.6 %all-reduce.31.cloned.1.call-done = f32[1024,768]{1,0:T(8,128)} async-done(((f32[1024,768]{1,0:T(8,128)}), f32[1024,768]{1,0:T(8,128)}) %all-reduce.31.cloned.1.call-update) | async-done | bytes 3145744 | tf_op jit(solution)/shard_map/psum | solution.py:30
  1224.8 4.7 copy.165
  1229.6 8.0 reshape.331
  1257.2 9.6 convolution_bitcast_fusion
  1266.9 6.9 fusion.25
  1273.8 11.3 pad_maximum_fusion
  1289.9 49.6 %reduce-scatter.21.cloned.1.call-done = f32[96,384]{1,0:T(8,128)} async-done(((f32[768,384]{1,0:T(8,128)}), f32[96,384]{1,0:T(8,128)}) %reduce-scatter.21.cloned.1.call-update) | async-done | bytes 147472
  1341.4 79.7 %reduce-scatter.19.cloned.1.call-done = f32[96,1152]{1,0:T(8,128)} async-done(((f32[768,1152]{1,0:T(8,128)}), f32[96,1152]{1,0:T(8,128)}) %reduce-scatter.19.cloned.1.call-update) | async-done | bytes 442384
  1425.0 94.4 %reduce-scatter.13.cloned.1.call-done = f32[2,96,768]{2,1,0:T(8,128)} async-done(((f32[2,768,768]{2,1,0:T(8,128)}), f32[2,96,768]{2,1,0:T(8,128)}) %reduce-scatter.13.cloned.1.call-update) | async-done | bytes 589840 | tf_op jit(solution)/shard_map/reduce_scatter | solution.py:336
  1521.9 96.3 %reduce-scatter.15.cloned.1.call-done = f32[2,96,768]{2,1,0:T(8,128)} async-done(((f32[2,768,768]{2,1,0:T(8,128)}), f32[2,96,768]{2,1,0:T(8,128)}) %reduce-scatter.15.cloned.1.call-update) | async-done | bytes 589840 | tf_op jit(solution)/shard_map/reduce_scatter | solution.py:337
  1620.6 208.0 %reduce-scatter.17.cloned.1.call-done = f32[2,96,2048]{2,1,0:T(8,128)} async-done(((f32[2,768,2048]{2,1,0:T(8,128)}), f32[2,96,2048]{2,1,0:T(8,128)}) %reduce-scatter.17.cloned.1.call-update) | async-done | bytes 1572880 | tf_op jit(solution)/shard_map/reduce_scatter | solution.py:338
  1833.1 39.6 %all-reduce = (f32[]{:T(128)}, f32[]{:T(128)}) all-reduce(f32[]{:T(128)S(6)} %mul.796, f32[]{:T(128)S(6)} %add.360), channel_id=1, replica_groups=mesh['wide'=8,'narrow'=4] {'wide','narrow'}, use_global_device_ids=true, to_apply=%region_27.28 | all-reduce | flops 2 | bytes 16 | tf_op jit(solution)/shard_map/psum | solution.py:355
  (465 shorter events, 231.6 us)
Async XLA Ops:
  7.2 32.3 %copy-start.60 = (f32[2,96,192]{2,1,0:T(8,128)S(1)}, f32[2,96,192]{2,1,0:T(8,128)}, u32[]{:S(2)}) copy-start(f32[2,96,192]{2,1,0:T(8,128)} %param.29) | copy-start | bytes 442372
  7.2 111.8 %copy-start.119 = (s32[1,1024]{1,0:T(1,128)S(1)}, s32[1,1024]{1,0:T(1,128)}, u32[]{:S(2)}) copy-start(s32[1,1024]{1,0:T(1,128)} %param.23) | copy-start | bytes 12292
  7.3 111.7 %all-gather.6.cloned.1.call-start = ((), (), s32[]{:S(2)}) async-start(), calls=%async_computation.6 | async-start | bytes 7077888 | tf_op jit(solution)/shard_map/all_gather | solution.py:239
  9.8 163.8 %all-gather.8.cloned.1.call-start = ((), (), s32[]{:S(2)}) async-start(), calls=%async_computation.8 | async-start | bytes 2654208 | tf_op jit(solution)/shard_map/all_gather | solution.py:235
  11.0 232.0 %all-reduce.13.cloned.1.call-start = ((), (), s32[]{:S(2)}) async-start(), calls=%async_computation.7 | async-start | bytes 6291456 | tf_op jit(solution)/shard_map/psum | solution.py:26
  39.6 86.5 %copy-start.104 = (s32[2048]{0:T(1024)}, s32[2048]{0:T(1024)S(1)}, u32[]{:S(2)}) copy-start(s32[2048]{0:T(1024)S(1)} %iota_add_fusion) | copy-start | bytes 24580
  40.2 206.1 %copy-start.88 = (f32[768]{0:T(1024)}, f32[768]{0:T(1024)S(1)}, u32[]{:S(2)}) copy-start(f32[768]{0:T(1024)S(1)} %get-tuple-element.257) | copy-start | bytes 9220
  40.2 347.8 %copy-start.90 = (f32[768]{0:T(1024)}, f32[768]{0:T(1024)S(1)}, u32[]{:S(2)}) copy-start(f32[768]{0:T(1024)S(1)} %get-tuple-element.256) | copy-start | bytes 9220
  40.2 475.5 %copy-start.85 = (f32[768]{0:T(1024)}, f32[768]{0:T(1024)S(1)}, u32[]{:S(2)}) copy-start(f32[768]{0:T(1024)S(1)} %get-tuple-element.255) | copy-start | bytes 9220
  126.1 207.0 %all-reduce.15.cloned.1.call-start = ((), (), s32[]{:S(2)}) async-start(), calls=%async_computation.9 | async-start | bytes 6291456 | tf_op jit(solution)/shard_map/psum | solution.py:26
  183.5 62.9 %copy-start.35 = (bf16[1,3,768,192]{2,3,1,0:T(8,128)(2,1)}, bf16[1,3,768,192]{2,3,1,0:T(8,128)(2,1)S(1)}, u32[]{:S(2)}) copy-start(bf16[1,3,768,192]{2,3,1,0:T(8,128)(2,1)S(1)} %copy.171) | copy-start | bytes 2654212
  264.4 68.7 %copy-start.10 = (f32[1024,768]{1,0:T(8,128)S(1)}, f32[1024,768]{1,0:T(8,128)}, u32[]{:S(2)}) copy-start(f32[1024,768]{1,0:T(8,128)} %copy-done.9) | copy-start | bytes 9437188
  264.4 123.5 %all-gather.10.cloned.1.call-start = ((), (), s32[]{:S(2)}) async-start(), calls=%async_computation.10 | async-start | bytes 2654208 | tf_op jit(solution)/shard_map/all_gather | solution.py:237
  266.5 174.8 %all-gather.12.cloned.1.call-start = ((), (), s32[]{:S(2)}) async-start(), calls=%async_computation.11 | async-start | bytes 2654208 | tf_op jit(solution)/shard_map/all_gather | solution.py:238
  268.4 244.9 %all-reduce.17.cloned.1.call-start = ((), (), s32[]{:S(2)}) async-start(), calls=%async_computation.12 | async-start | bytes 6291456 | tf_op jit(solution)/shard_map/psum | solution.py:26
  337.1 54.6 %copy-start.96 = (f32[1024]{0:T(1024)}, f32[1024]{0:T(1024)S(1)}, u32[]{:S(2)}) copy-start(f32[1024]{0:T(1024)S(1)} %add_rsqrt_fusion.3) | copy-start | bytes 12292
  391.7 54.5 %copy-start.132 = (f32[1024,768]{1,0:T(8,128)}, f32[1024,768]{1,0:T(8,128)S(1)}, u32[]{:S(2)}) copy-start(f32[1024,768]{1,0:T(8,128)S(1)} %fusion.64) | copy-start | bytes 9437188
  446.1 67.1 %copy-start.14 = (f32[1024,768]{1,0:T(8,128)S(1)}, f32[1024,768]{1,0:T(8,128)}, u32[]{:S(2)}) copy-start(f32[1024,768]{1,0:T(8,128)} %get-tuple-element.299) | copy-start | bytes 9437188
  446.2 157.5 %all-reduce.19.cloned.1.call-start = ((), (), s32[]{:S(2)}) async-start(), calls=%async_computation.13 | async-start | bytes 6291456 | tf_op jit(solution)/shard_map/psum | solution.py:26
  532.7 71.0 %copy-start.6 = (f32[1024,768]{1,0:T(8,128)S(1)}, f32[1024,768]{1,0:T(8,128)}, u32[]{:S(2)}) copy-start(f32[1024,768]{1,0:T(8,128)} %copy-done.5) | copy-start | bytes 9437188
  534.9 147.4 %all-reduce.21.cloned.1.call-start = ((), (), s32[]{:S(2)}) async-start(), calls=%async_computation.14 | async-start | bytes 6291456 | tf_op jit(solution)/shard_map/psum | solution.py:26
  613.6 23.9 %copy-start.103 = (s32[1,1024]{1,0:T(1,128)S(1)}, s32[1,1024]{1,0:T(1,128)}, u32[]{:S(2)}) copy-start(s32[1,1024]{1,0:T(1,128)} %param.25) | copy-start | bytes 12292
  613.6 215.8 %all-reduce.23.cloned.1.call-start = ((), (), s32[]{:S(2)}) async-start(), calls=%async_computation.15 | async-start | bytes 6291456 | tf_op jit(solution)/shard_map/psum | solution.py:30
  685.6 147.3 %copy-start.16 = (f32[1024,768]{1,0:T(8,128)}, f32[1024,768]{1,0:T(8,128)S(1)}, u32[]{:S(2)}) copy-start(f32[1024,768]{1,0:T(8,128)S(1)} %get-tuple-element.293) | copy-start | bytes 9437188
  713.9 12.4 copy-start.107
  760.1 152.0 %all-reduce.25.cloned.1.call-start = ((), (), s32[]{:S(2)}) async-start(), calls=%async_computation.16 | async-start | bytes 6291456 | tf_op jit(solution)/shard_map/psum | solution.py:30
  843.3 68.7 %copy-start.18 = (f32[1024,768]{1,0:T(8,128)S(1)}, f32[1024,768]{1,0:T(8,128)}, u32[]{:S(2)}) copy-start(f32[1024,768]{1,0:T(8,128)} %copy-done.17) | copy-start | bytes 9437188
  843.4 173.1 %all-reduce.27.cloned.1.call-start = ((), (), s32[]{:S(2)}) async-start(), calls=%async_computation.17 | async-start | bytes 6291456 | tf_op jit(solution)/shard_map/psum | solution.py:30
  926.4 17.5 copy-start.129
  947.8 68.7 %copy-start.79 = (f32[1024]{0:T(1024)S(1)}, f32[1024]{0:T(1024)}, u32[]{:S(2)}) copy-start(f32[1024]{0:T(1024)} %copy-done.78) | copy-start | bytes 12292
  947.8 68.7 %copy-start.86 = (f32[768]{0:T(1024)S(1)}, f32[768]{0:T(1024)}, u32[]{:S(2)}) copy-start(f32[768]{0:T(1024)} %copy-done.85) | copy-start | bytes 9220
  947.8 153.5 %all-reduce.29.cloned.1.call-start = ((), (), s32[]{:S(2)}) async-start(), calls=%async_computation.18 | async-start | bytes 6291456 | tf_op jit(solution)/shard_map/psum | solution.py:30
  1032.6 68.7 %copy-start.91 = (f32[768]{0:T(1024)S(1)}, f32[768]{0:T(1024)}, u32[]{:S(2)}) copy-start(f32[768]{0:T(1024)} %copy-done.90) | copy-start | bytes 9220
  1032.6 68.7 %copy-start.97 = (f32[1024]{0:T(1024)S(1)}, f32[1024]{0:T(1024)}, u32[]{:S(2)}) copy-start(f32[1024]{0:T(1024)} %copy-done.96) | copy-start | bytes 12292
  1032.6 174.5 %all-reduce.31.cloned.1.call-start = ((), (), s32[]{:S(2)}) async-start(), calls=%async_computation.21 | async-start | bytes 6291456 | tf_op jit(solution)/shard_map/psum | solution.py:30
  1117.0 17.5 copy-start.130
  1138.4 149.4 %reduce-scatter.23.cloned.1.call-start = ((), (), s32[]{:S(2)}) async-start(), calls=%async_computation.25 | async-start | bytes 442368
  1140.2 66.9 %copy-start.11 = (f32[1024,768]{1,0:T(8,128)S(1)}, f32[1024,768]{1,0:T(8,128)}, u32[]{:S(2)}) copy-start(f32[1024,768]{1,0:T(8,128)} %copy-done.9) | copy-start | bytes 9437188
  1140.2 66.9 %copy-start.84 = (f32[1024]{0:T(1024)S(1)}, f32[1024]{0:T(1024)}, u32[]{:S(2)}) copy-start(f32[1024]{0:T(1024)} %copy-done.83) | copy-start | bytes 12292
  1140.2 66.9 %copy-start.89 = (f32[768]{0:T(1024)S(1)}, f32[768]{0:T(1024)}, u32[]{:S(2)}) copy-start(f32[768]{0:T(1024)} %copy-done.88) | copy-start | bytes 9220
  1147.5 62.9 %copy-start.117 = (f32[1,768]{1,0:T(1,128)S(1)}, f32[1,768]{1,0:T(1,128)}, u32[]{:S(2)}) copy-start(f32[1,768]{1,0:T(1,128)} %stack.124) | copy-start | bytes 9220
  1147.5 62.9 %copy-start.118 = (f32[1,768]{1,0:T(1,128)S(1)}, f32[1,768]{1,0:T(1,128)}, u32[]{:S(2)}) copy-start(f32[1,768]{1,0:T(1,128)} %stack.123) | copy-start | bytes 9220
  1147.5 63.0 %copy-start.116 = (f32[1,768]{1,0:T(1,128)S(1)}, f32[1,768]{1,0:T(1,128)}, u32[]{:S(2)}) copy-start(f32[1,768]{1,0:T(1,128)} %broadcast_in_dim.132) | copy-start | bytes 9220
  1211.4 128.1 %reduce-scatter.21.cloned.1.call-start = ((), (), s32[]{:S(2)}) async-start(), calls=%async_computation.24 | async-start | bytes 1327104
  1220.7 200.4 %reduce-scatter.19.cloned.1.call-start = ((), (), s32[]{:S(2)}) async-start(), calls=%async_computation.23 | async-start | bytes 3981312
  1237.6 281.8 %reduce-scatter.13.cloned.1.call-start = ((), (), s32[]{:S(2)}) async-start(), calls=%async_computation.19 | async-start | bytes 5308416 | tf_op jit(solution)/shard_map/reduce_scatter | solution.py:336
  1246.8 371.4 %reduce-scatter.15.cloned.1.call-start = ((), (), s32[]{:S(2)}) async-start(), calls=%async_computation.20 | async-start | bytes 5308416 | tf_op jit(solution)/shard_map/reduce_scatter | solution.py:337
  1256.6 572.1 %reduce-scatter.17.cloned.1.call-start = ((), (), s32[]{:S(2)}) async-start(), calls=%async_computation.22 | async-start | bytes 14155776 | tf_op jit(solution)/shard_map/reduce_scatter | solution.py:338
  (118 other events, 495.8 us)
Sparse Core Ops, SparseCore 0:
  10.9 108.0 all-gather.5
  121.8 51.8 all-gather.7
  176.0 66.9 all-reduce.12
  264.6 68.5 all-reduce.14
  335.8 52.1 all-gather.9
  390.6 50.6 all-gather.11
  446.3 66.9 all-reduce.16
  535.1 68.5 all-reduce.18
  613.8 68.5 all-reduce.20
  760.2 69.2 all-reduce.22
  843.5 68.5 all-reduce.24
  947.9 68.5 all-reduce.26
  1032.7 68.5 all-reduce.28
  1138.5 68.5 all-reduce.30
  1211.6 61.5 reduce-scatter.22
  1276.4 63.1 reduce-scatter.20
  1343.0 78.0 reduce-scatter.18
  1424.6 94.7 reduce-scatter.12
  1523.1 95.0 reduce-scatter.14
  1621.6 207.0 reduce-scatter.16
where the time goes:
time: 1910 us
  waiting for transfers between devices  1340 us (70%)
  other arithmetic  157 us (8%)
  blocking collectives  151 us (8%)
  matrix products  146 us (8%)
  local copies, waits for them, and re-layouts  85.8 us (4%)
  between operations  22.8 us (1%)
    psum x5, waiting for transfers between devices, back_heads(): return lax.psum(partial_value, 'narrow')  334 us
    psum x5, waiting for transfers between devices, add_heads(): return lax.psum(partial_value, 'narrow')  296 us
    reduce_scatter x1, waiting for transfers between devices, per_device(): lax.psum_scatter(grad_tables_all, 'wide', scatter_dimension=1, tiled=True)  208 us
    unnamed x23, waiting for transfers between devices  130 us
    reduce_scatter x1, waiting for transfers between devices, per_device(): lax.psum_scatter(stacked[3], 'wide', scatter_dimension=1, tiled=True)  96.3 us
    reduce_scatter x1, waiting for transfers between devices, per_device(): lax.psum_scatter(stacked[2], 'wide', scatter_dimension=1, tiled=True)  94.4 us
    unnamed x319, local copies, waits for them, and re-layouts  74.6 us
    all_gather x1, waiting for transfers between devices, per_device(): lax.all_gather(ffn_in.astype(jnp.bfloat16), 'wide', axis=1, tiled=True)  50.9 us
  transfers between devices with their start and end apart: 20, of which 19 were waited for; matrix products, arithmetic and copies ran while one was open for 7% of the time, Pallas kernels for 0%

commit v1 on v0

--- a/solution.py
+++ b/solution.py
@@ -1,8 +1,11 @@
+import functools
 import math
 
 import jax
 import jax.numpy as jnp
 from jax import lax
+from jax.experimental import pallas as pl
+from jax.experimental.pallas import tpu as pltpu
 from jax.sharding import PartitionSpec as P
 
 D = 768
@@ -203,7 +206,7 @@
     return (weight_new, first_new, second_new, weight_new.astype(jnp.bfloat16))
 
 
-def per_device(
+def general_device(
     noised,
     clean,
     timesteps,
@@ -406,7 +409,854 @@
     )
 
 
+MESH = pl.DeviceIdType.MESH
+F32 = jnp.float32
+BF16 = jnp.bfloat16
+CHUNKS = 4
+VMEM_LIMIT = 56 * 1024 * 1024
+FORWARD_KIND = BF16
+BACKWARD_KIND = BF16
+
+
+def whole_vmem():
+    return pl.BlockSpec(memory_space=pltpu.VMEM)
+
+
+def dot_nn(a, b):
+    return lax.dot_general(a, b, (((1,), (0,)), ((), ())), preferred_element_type=F32)
+
+
+def dot_nt(a, b):
+    return lax.dot_general(a, b, (((1,), (1,)), ((), ())), preferred_element_type=F32)
+
+
+def remote(src, dst, send_sem, recv_sem, device):
+    return pltpu.make_async_remote_copy(
+        src_ref=src,
+        dst_ref=dst,
+        send_sem=send_sem,
+        recv_sem=recv_sem,
+        device_id=device,
+        device_id_type=MESH,
+    )
+
+
+def greet(devices):
+    barrier = pltpu.get_barrier_semaphore()
+    for device in devices:
+        pl.semaphore_signal(barrier, inc=1, device_id=device, device_id_type=MESH)
+    pl.semaphore_wait(barrier, len(devices))
+
+
+def group_places(seq_len):
+    me = lax.axis_index("narrow")
+    core = lax.rem(me, 2)
+    half = seq_len // 2
+    mine = pl.multiple_of(core * half, half)
+    other = pl.multiple_of((1 - core) * half, half)
+    return ({"narrow": me + 1 - 2 * core}, {"narrow": lax.rem(me + 2, 4)}, mine, other)
+
+
+class Exchange:
+    def __init__(self, refs, sems, base, sibling, partner):
+        self.near_out, self.near_in, self.far_out, self.far_in = refs
+        self.send, self.recv = sems
+        self.base, self.sibling, self.partner = base, sibling, partner
+
+    def near(self, j):
+        return remote(
+            self.near_out.at[j],
+            self.near_in.at[j],
+            self.send.at[self.base, j],
+            self.recv.at[self.base, j],
+            self.sibling,
+        )
+
+    def far(self, j):
+        return remote(
+            self.far_out.at[j],
+            self.far_in.at[j],
+            self.send.at[self.base + 1, j],
+            self.recv.at[self.base + 1, j],
+            self.partner,
+        )
+
+    def give(self, j, value):
+        self.near_out[j] = value
+        self.near(j).start()
+
+    def pass_on(self, j, value):
+        self.near(j).wait_recv()
+        self.far_out[j] = (value + self.near_in[j]).astype(self.far_out.dtype)
+        self.far(j).start()
+
+    def take(self, j):
+        self.far(j).wait_recv()
+        return self.far_out[j].astype(F32) + self.far_in[j].astype(F32)
+
+    def close(self):
+        for j in range(CHUNKS):
+            self.near(j).wait_send()
+            self.far(j).wait_send()
+
+    @staticmethod
+    def scratch(chunk, width, kind):
+        return [
+            pltpu.VMEM((CHUNKS, chunk, width), F32),
+            pltpu.VMEM((CHUNKS, chunk, width), F32),
+            pltpu.VMEM((CHUNKS, chunk, width), kind),
+            pltpu.VMEM((CHUNKS, chunk, width), kind),
+        ]
+
+
+class Share:
+    def __init__(self, ref, sems, base, sibling, mine, chunk):
+        self.ref, self.base, self.sibling, self.mine, self.chunk = ref, base, sibling, mine, chunk
+        self.send, self.recv = sems
+
+    def piece(self, j):
+        rows = self.ref.at[pl.ds(pl.multiple_of(self.mine + j * self.chunk, self.chunk), self.chunk)]
+        return remote(rows, rows, self.send.at[self.base, j], self.recv.at[self.base, j], self.sibling)
+
+    def put(self, j, value):
+        self.ref[pl.ds(pl.multiple_of(self.mine + j * self.chunk, self.chunk), self.chunk), :] = value
+        self.piece(j).start()
+
+    def arrived(self, j):
+        self.piece(j).wait_recv()
+
+    def close(self):
+        for j in range(CHUNKS):
+            self.piece(j).wait_send()
+
+
+def norm_of(value, gain):
+    scale = lax.rsqrt(jnp.mean(value * value, axis=-1, keepdims=True) + NORM_EPS)
+    return value * scale * gain
+
+
+def norm_back(grad, value, gain):
+    scale = lax.rsqrt(jnp.mean(value * value, axis=-1, keepdims=True) + NORM_EPS)
+    unit = value * scale
+    scaled = grad * gain
+    back = scale * (scaled - unit * jnp.mean(scaled * unit, axis=-1, keepdims=True))
+    return (back, jnp.sum(grad * unit, axis=0, keepdims=True))
+
+
+GELU_A = math.sqrt(2.0 / math.pi)
+GELU_B = 0.044715
+
+
+def gelu_of(x):
+    return 0.5 * x * (1.0 + jnp.tanh(GELU_A * (x + GELU_B * (x * x * x))))
+
+
+def gelu_slope(x):
+    square = x * x
+    t = jnp.tanh(GELU_A * (x + GELU_B * (x * square)))
+    return 0.5 * (1.0 + t) + 0.5 * x * (1.0 - t * t) * (GELU_A * (1.0 + 3.0 * GELU_B * square))
+
+
+def rows_at(start, j, chunk):
+    return pl.ds(pl.multiple_of(start + j * chunk, chunk), chunk)
+
+
+def embed_kernel(ids, extra, table, gain, resid, normed, near_out, near_in, far_out, far_in, send, recv):
+    seq_len, width = normed.shape
+    chunk = seq_len // 2 // CHUNKS
+    sibling, partner, mine, other = group_places(seq_len)
+    vocab = table.shape[1]
+    first = lax.axis_index("narrow") * vocab
+    greet([sibling, partner])
+    trade = Exchange((near_out, near_in, far_out, far_in), (send, recv), 0, sibling, partner)
+    share = Share(normed, (send, recv), 2, sibling, mine, chunk)
+
+    def partial(start, j):
+        here = ids[rows_at(start, j, chunk), :] - first
+        columns = lax.broadcasted_iota(jnp.int32, (chunk, vocab), 1)
+        picks = (here == columns).astype(F32).astype(BF16)
+        return dot_nt(picks, table[...])
+
+    trade.give(0, partial(other, 0))
+    for j in range(CHUNKS):
+        if j + 1 < CHUNKS:
+            trade.give(j + 1, partial(other, j + 1))
+        trade.pass_on(j, partial(mine, j))
+    for j in range(CHUNKS):
+        x = math.sqrt(width) * trade.take(j) + extra[rows_at(0, j, chunk), :]
+        resid[rows_at(0, j, chunk), :] = x
+        share.put(j, norm_of(x, gain[...]).astype(BF16))
+    for j in range(CHUNKS):
+        share.arrived(j)
+    trade.close()
+    share.close()
+
+
+def embed(ids, extra, table, gain, collective_id):
+    seq_len, width = ids.shape[0], table.shape[0]
+    chunk = seq_len // 2 // CHUNKS
+    return pl.pallas_call(
+        embed_kernel,
+        out_shape=(
+            jax.ShapeDtypeStruct((seq_len // 2, width), F32),
+            jax.ShapeDtypeStruct((seq_len, width), BF16),
+        ),
+        in_specs=[whole_vmem()] * 4,
+        out_specs=(whole_vmem(),) * 2,
+        scratch_shapes=Exchange.scratch(chunk, width, FORWARD_KIND)
+        + [pltpu.SemaphoreType.DMA((3, CHUNKS)), pltpu.SemaphoreType.DMA((3, CHUNKS))],
+        compiler_params=pltpu.CompilerParams(
+            collective_id=collective_id, has_side_effects=True, vmem_limit_bytes=VMEM_LIMIT
+        ),
+        name="embed",
+    )(ids, extra, table, gain)
+
+
+def ffn_kernel(
+    mixed, resid, w_out, w_in, w_red, gain, gain_next,
+    middle, normed, before, after, result, normed_next,
+    near_out, near_in, far_out, far_in, near_out2, near_in2, far_out2, far_in2, own2, send, recv,
+):
+    seq_len = normed.shape[0]
+    chunk = seq_len // 2 // CHUNKS
+    sibling, partner, mine, other = group_places(seq_len)
+    greet([sibling, partner])
+    sems = (send, recv)
+    first = Exchange((near_out, near_in, far_out, far_in), sems, 0, sibling, partner)
+    second = Exchange((near_out2, near_in2, far_out2, far_in2), sems, 2, sibling, partner)
+    share = Share(normed, sems, 4, sibling, mine, chunk)
+    share_next = Share(normed_next, sems, 5, sibling, mine, chunk)
+
+    def project(start, j):
+        return dot_nt(mixed[rows_at(start, j, chunk), :], w_out[...])
+
+    def feed(rows):
+        pre = dot_nn(normed[rows, :], w_in[...])
+        before[rows, :] = pre
+        act = gelu_of(pre).astype(BF16)
+        after[rows, :] = act
+        return dot_nt(act, w_red[...])
+
+    first.give(0, project(other, 0))
+    for j in range(CHUNKS):
+        if j + 1 < CHUNKS:
+            first.give(j + 1, project(other, j + 1))
+        first.pass_on(j, project(mine, j))
+    for j in range(CHUNKS):
+        rows = rows_at(0, j, chunk)
+        mid = resid[rows, :] + first.take(j)
+        middle[rows, :] = mid
+        share.put(j, norm_of(mid, gain[...]).astype(BF16))
+        own2[j] = feed(rows_at(mine, j, chunk))
+        share.arrived(j)
+        second.give(j, feed(rows_at(other, j, chunk)))
+        if j >= 1:
+            second.pass_on(j - 1, own2[j - 1])
+    second.pass_on(CHUNKS - 1, own2[CHUNKS - 1])
+    for j in range(CHUNKS):
+        rows = rows_at(0, j, chunk)
+        x = middle[rows, :] + second.take(j)
+        result[rows, :] = x
+        share_next.put(j, norm_of(x, gain_next[...]).astype(BF16))
+    for j in range(CHUNKS):
+        share_next.arrived(j)
+    for part in (first, second, share, share_next):
+        part.close()
+
+
+def ffn_forward(mixed, resid, w_out, w_in, w_red, gain, gain_next, collective_id):
+    seq_len, width, hidden = mixed.shape[0], w_in.shape[0], w_in.shape[1]
+    half, chunk = seq_len // 2, seq_len // 2 // CHUNKS
+    return pl.pallas_call(
+        ffn_kernel,
+        out_shape=(
+            jax.ShapeDtypeStruct((half, width), F32),
+            jax.ShapeDtypeStruct((seq_len, width), BF16),
+            jax.ShapeDtypeStruct((seq_len, hidden), F32),
+            jax.ShapeDtypeStruct((seq_len, hidden), BF16),
+            jax.ShapeDtypeStruct((half, width), F32),
+            jax.ShapeDtypeStruct((seq_len, width), BF16),
+        ),
+        in_specs=[whole_vmem()] * 7,
+        out_specs=(whole_vmem(),) * 6,
+        scratch_shapes=Exchange.scratch(chunk, width, FORWARD_KIND)
+        + Exchange.scratch(chunk, width, FORWARD_KIND)
+        + [
+            pltpu.VMEM((CHUNKS, chunk, width), F32),
+            pltpu.SemaphoreType.DMA((6, CHUNKS)),
+            pltpu.SemaphoreType.DMA((6, CHUNKS)),
+        ],
+        compiler_params=pltpu.CompilerParams(
+            collective_id=collective_id, has_side_effects=True, vmem_limit_bytes=VMEM_LIMIT
+        ),
+        name="ffn_forward",
+    )(mixed, resid, w_out, w_in, w_red, gain, gain_next)
+
+
+TILE = 256
+
+
+def weight_grad(left_t, right, out):
+    columns = right.shape[1]
+    tile = TILE if columns % TILE == 0 else columns
+
+    def step(i, _):
+        where = pl.ds(pl.multiple_of(i * tile, tile), tile)
+        out[:, where] = dot_nn(left_t[...], right[:, where]).astype(out.dtype)
+        return 0
+
+    if tile == columns:
+        out[...] = dot_nn(left_t[...], right[...]).astype(out.dtype)
+    else:
+        lax.fori_loop(0, columns // tile, step, 0)
+
+
+def ffn_back_kernel(
+    grad, branch, w_red, w_in, w_out, before, after, normed, middle, gain, mixed,
+    grad_middle, grad_attn, grad_mixed, d_red, d_in, d_out, d_gain,
+    grad_before, turned, near_out, near_in, far_out, far_in, send, recv,
+):
+    seq_len = normed.shape[0]
+    chunk = seq_len // 2 // CHUNKS
+    sibling, partner, mine, other = group_places(seq_len)
+    greet([sibling, partner])
+    sems = (send, recv)
+    trade = Exchange((near_out, near_in, far_out, far_in), sems, 0, sibling, partner)
+    share = Share(grad_attn, sems, 2, sibling, mine, chunk)
+
+    def partial(start, j):
+        rows = rows_at(start, j, chunk)
+        back = dot_nn(branch[rows, :], w_red[...])
+        low = (back * gelu_slope(before[rows, :])).astype(BF16)
+        grad_before[rows, :] = low
+        return dot_nt(low, w_in[...])
+
+    trade.give(0, partial(other, 0))
+    for j in range(CHUNKS):
+        if j + 1 < CHUNKS:
+            trade.give(j + 1, partial(other, j + 1))
+        trade.pass_on(j, partial(mine, j))
+    turned[...] = jnp.transpose(branch[...])
+    weight_grad(turned, after, d_red)
+    turned[...] = jnp.transpose(normed[...])
+    weight_grad(turned, grad_before, d_in)
+    gain_total = jnp.zeros(gain.shape, F32)
+    for j in range(CHUNKS):
+        rows = rows_at(0, j, chunk)
+        back, gain_part = norm_back(trade.take(j), middle[rows, :], gain[...])
+        gain_total = gain_total + gain_part
+        total = back + grad[rows, :]
+        grad_middle[rows, :] = total
+        share.put(j, total.astype(BF16))
+        here = rows_at(mine, j, chunk)
+        grad_mixed[here, :] = dot_nn(grad_attn[here, :], w_out[...]).astype(BF16)
+    for j in range(CHUNKS):
+        share.arrived(j)
+        here = rows_at(other, j, chunk)
+        grad_mixed[here, :] = dot_nn(grad_attn[here, :], w_out[...]).astype(BF16)
+    d_gain[...] = gain_total
+    turned[...] = jnp.transpose(grad_attn[...])
+    weight_grad(turned, mixed, d_out)
+    trade.close()
+    share.close()
+
+
+def ffn_backward(grad, branch, w_red, w_in, w_out, before, after, normed, middle, gain, mixed, collective_id):
+    seq_len, width = normed.shape
+    half, chunk = seq_len // 2, seq_len // 2 // CHUNKS
+    return pl.pallas_call(
+        ffn_back_kernel,
+        out_shape=(
+            jax.ShapeDtypeStruct((half, width), F32),
+            jax.ShapeDtypeStruct((seq_len, width), BF16),
+            jax.ShapeDtypeStruct(mixed.shape, BF16),
+            jax.ShapeDtypeStruct(w_red.shape, BF16),
+            jax.ShapeDtypeStruct(w_in.shape, BF16),
+            jax.ShapeDtypeStruct(w_out.shape, BF16),
+            jax.ShapeDtypeStruct(gain.shape, F32),
+        ),
+        in_specs=[whole_vmem()] * 11,
+        out_specs=(whole_vmem(),) * 7,
+        scratch_shapes=[
+            pltpu.VMEM(before.shape, BF16),
+            pltpu.VMEM((width, seq_len), BF16),
+        ]
+        + Exchange.scratch(chunk, width, BACKWARD_KIND)
+        + [pltpu.SemaphoreType.DMA((3, CHUNKS)), pltpu.SemaphoreType.DMA((3, CHUNKS))],
+        compiler_params=pltpu.CompilerParams(
+            collective_id=collective_id, has_side_effects=True, vmem_limit_bytes=VMEM_LIMIT
+        ),
+        name="ffn_backward",
+    )(grad, branch, w_red, w_in, w_out, before, after, normed, middle, gain, mixed)
+
+
+def norm_back_kernel(
+    scale, grads, weights, normed, value, gain, upstream,
+    grad_out, branch, d_weights, d_gain,
+    turned, near_out, near_in, far_out, far_in, send, recv,
+):
+    seq_len, width = normed.shape
+    chunk = seq_len // 2 // CHUNKS
+    sibling, partner, mine, other = group_places(seq_len)
+    greet([sibling, partner])
+    sems = (send, recv)
+    trade = Exchange((near_out, near_in, far_out, far_in), sems, 0, sibling, partner)
+    share = Share(branch, sems, 2, sibling, mine, chunk)
+
+    def partial(start, j):
+        rows = rows_at(start, j, chunk)
+        total = None
+        for which in range(grads.shape[0]):
+            part = dot_nt(grads[which, rows, :], weights[which])
+            total = part if total is None else total + part
+        return total
+
+    trade.give(0, partial(other, 0))
+    for j in range(CHUNKS):
+        if j + 1 < CHUNKS:
+            trade.give(j + 1, partial(other, j + 1))
+        trade.pass_on(j, partial(mine, j))
+    turned[...] = jnp.transpose(normed[...])
+    for which in range(grads.shape[0]):
+        weight_grad(turned, grads.at[which], d_weights.at[which])
+    gain_total = jnp.zeros(gain.shape, F32)
+    for j in range(CHUNKS):
+        rows = rows_at(0, j, chunk)
+        back, gain_part = norm_back(trade.take(j), value[rows, :], gain[...])
+        gain_total = gain_total + gain_part
+        if upstream is not None:
+            back = back + upstream[rows, :]
+        grad_out[rows, :] = back
+        share.put(j, (back if scale is None else scale * back).astype(BF16))
+    d_gain[...] = gain_total
+    for j in range(CHUNKS):
+        share.arrived(j)
+    trade.close()
+    share.close()
+
+
+def norm_backward(grads, weights, normed, value, gain, upstream, scale, collective_id):
+    seq_len, width = normed.shape
+    half, chunk = seq_len // 2, seq_len // 2 // CHUNKS
+    operands = [grads, weights, normed, value, gain] + ([] if upstream is None else [upstream])
+
+    def kernel(*refs):
+        given, rest = list(refs[: len(operands)]), refs[len(operands) :]
+        if upstream is None:
+            given.append(None)
+        norm_back_kernel(scale, *given, *rest)
+
+    return pl.pallas_call(
+        kernel,
+        out_shape=(
+            jax.ShapeDtypeStruct((half, width), F32),
+            jax.ShapeDtypeStruct((seq_len, width), BF16),
+            jax.ShapeDtypeStruct(weights.shape, BF16),
+            jax.ShapeDtypeStruct(gain.shape, F32),
+        ),
+        in_specs=[whole_vmem()] * len(operands),
+        out_specs=(whole_vmem(),) * 4,
+        scratch_shapes=[pltpu.VMEM((width, seq_len), BF16)]
+        + Exchange.scratch(chunk, width, BACKWARD_KIND)
+        + [pltpu.SemaphoreType.DMA((3, CHUNKS)), pltpu.SemaphoreType.DMA((3, CHUNKS))],
+        compiler_params=pltpu.CompilerParams(
+            collective_id=collective_id, has_side_effects=True, vmem_limit_bytes=VMEM_LIMIT
+        ),
+        name="norm_backward",
+    )(*operands)
+
+
+def wide_places(count):
+    me = lax.axis_index("wide")
+    fast = lax.rem(me, 2)
+    slow = me // 2
+    return (me, slow, fast, count // 2)
+
+
+def gather_kernel(arrays, lead, *refs):
+    shards, outs = refs[:arrays], refs[arrays : 2 * arrays]
+    lows = refs[2 * arrays : 3 * arrays]
+    local, slow_send, slow_recv, fast_send, fast_recv = refs[3 * arrays :]
+    count = outs[0].shape[lead[0]]
+    me, slow, fast, slows = wide_places(count)
+    beside = me + 1 - 2 * fast
+
+    def at(which, owner):
+        out = outs[which]
+        return out.at[(slice(None),) * lead[which] + (owner,)]
+
+    def along(step):
+        return 2 * lax.rem(slow + step, slows) + fast
+
+    def back(step):
+        return 2 * lax.rem(slow + slows - step, slows) + fast
+
+    def slow_copy(which, step):
+        return remote(
+            lows[which], at(which, me), slow_send.at[which, step - 1], slow_recv.at[which, step - 1],
+            {"wide": along(step)},
+        )
+
+    def fast_copy(which, step):
+        block = at(which, back(step))
+        return remote(
+            lows[which] if step == 0 else block, block, fast_send.at[which, step], fast_recv.at[which, step],
+            {"wide": beside},
+        )
+
+    greet([{"wide": along(step)} for step in range(1, slows)] + [{"wide": beside}])
+    for which in range(arrays):
+        lows[which][...] = shards[which][...].astype(lows[which].dtype)
+        for step in range(1, slows):
+            slow_copy(which, step).start()
+        fast_copy(which, 0).start()
+        pltpu.make_async_copy(lows[which], at(which, me), local.at[which]).start()
+    for which in range(arrays):
+        for step in range(1, slows):
+            slow_copy(which, step).wait_recv()
+            fast_copy(which, step).start()
+    for which in range(arrays):
+        for step in range(slows):
+            fast_copy(which, step).wait()
+            if step:
+                slow_copy(which, step).wait_send()
+        pltpu.make_async_copy(lows[which], at(which, me), local.at[which]).wait()
+
+
+def gather_wide(shards, leads, kinds, count, collective_id):
+    arrays = len(shards)
+    slows = count // 2
+    return pl.pallas_call(
+        functools.partial(gather_kernel, arrays, leads),
+        out_shape=tuple(
+            jax.ShapeDtypeStruct(s.shape[:lead] + (count,) + s.shape[lead:], kind)
+            for s, lead, kind in zip(shards, leads, kinds)
+        ),
+        in_specs=[whole_vmem()] * arrays,
+        out_specs=(pl.BlockSpec(memory_space=pl.ANY),) * arrays,
+        scratch_shapes=[pltpu.VMEM(s.shape, kind) for s, kind in zip(shards, kinds)]
+        + [
+            pltpu.SemaphoreType.DMA((arrays,)),
+            pltpu.SemaphoreType.DMA((arrays, slows - 1)),
+            pltpu.SemaphoreType.DMA((arrays, slows - 1)),
+            pltpu.SemaphoreType.DMA((arrays, slows)),
+            pltpu.SemaphoreType.DMA((arrays, slows)),
+        ],
+        compiler_params=pltpu.CompilerParams(
+            collective_id=collective_id, has_side_effects=True, vmem_limit_bytes=VMEM_LIMIT
+        ),
+        name="gather_weights",
+    )(*shards)
+
+
+def scatter_kernel(arrays, lead, *refs):
+    fulls, outs = refs[:arrays], refs[arrays : 2 * arrays]
+    fast_in = refs[2 * arrays : 3 * arrays]
+    sums = refs[3 * arrays : 4 * arrays]
+    slow_in = refs[4 * arrays : 5 * arrays]
+    paired, paired_in, fast_send, fast_recv, slow_send, slow_recv, near_send, near_recv = refs[5 * arrays :]
+    count = fulls[0].shape[lead[0]]
+    me, slow, fast, slows = wide_places(count)
+    beside = me + 1 - 2 * fast
+    place = lax.axis_index("narrow")
+    sibling = {"narrow": place + 1 - 2 * lax.rem(place, 2)}
+    sources = list(fulls[:-1]) + [paired]
+
+    def block(which, owner):
+        return sources[which].at[(slice(None),) * lead[which] + (owner,)]
+
+    def along(step):
+        return lax.rem(slow + step, slows)
+
+    def fast_copy(which, step):
+        owner = 2 * along(step) + 1 - fast
+        return remote(
+            block(which, owner), fast_in[which].at[step], fast_send.at[which, step], fast_recv.at[which, step],
+            {"wide": beside},
+        )
+
+    def slow_copy(which, step):
+        return remote(
+            sums[which].at[step - 1], slow_in[which].at[step - 1],
+            slow_send.at[which, step - 1], slow_recv.at[which, step - 1],
+            {"wide": 2 * along(step) + fast},
+        )
+
+    greet([{"wide": 2 * along(step) + fast} for step in range(1, slows)] + [{"wide": beside}, sibling])
+    near = remote(fulls[-1], paired_in, near_send, near_recv, sibling)
+    near.start()
+    for which in range(arrays):
+        if which == arrays - 1:
+            near.wait()
+            paired[...] = fulls[-1][...] + paired_in[...]
+        for step in list(range(1, slows)) + [0]:
+            fast_copy(which, step).start()
+    for which in range(arrays):
+        for step in range(1, slows):
+            fast_copy(which, step).wait_recv()
+            owner = 2 * along(step) + fast
+            total = block(which, owner)[...].astype(F32) + fast_in[which][step].astype(F32)
+            sums[which][step - 1] = total.astype(sums[which].dtype)
+            slow_copy(which, step).start()
+    for which in range(arrays):
+        fast_copy(which, 0).wait_recv()
+        total = block(which, me)[...].astype(F32) + fast_in[which][0].astype(F32)
+        for step in range(1, slows):
+            slow_copy(which, step).wait_recv()
+            total = total + slow_in[which][step - 1].astype(F32)
+        outs[which][...] = total
+    for which in range(arrays):
+        for step in range(slows):
+            fast_copy(which, step).wait_send()
+            if step:
+                slow_copy(which, step).wait_send()
+
+
+def scatter_wide(fulls, leads, collective_id):
+    arrays = len(fulls)
+    count = fulls[0].shape[leads[0]]
+    slows = count // 2
+    shapes = [f.shape[:lead] + f.shape[lead + 1 :] for f, lead in zip(fulls, leads)]
+    kinds = [f.dtype for f in fulls]
+    return pl.pallas_call(
+        functools.partial(scatter_kernel, arrays, leads),
+        out_shape=tuple(jax.ShapeDtypeStruct(shape, F32) for shape in shapes),
+        in_specs=[whole_vmem()] * arrays,
+        out_specs=(whole_vmem(),) * arrays,
+        scratch_shapes=[pltpu.VMEM((slows,) + shape, kind) for shape, kind in zip(shapes, kinds)]
+        + [pltpu.VMEM((slows - 1,) + shape, kind) for shape, kind in zip(shapes, kinds)]
+        + [pltpu.VMEM((slows - 1,) + shape, kind) for shape, kind in zip(shapes, kinds)]
+        + [pltpu.VMEM(fulls[-1].shape, F32)] * 2
+        + [
+            pltpu.SemaphoreType.DMA((arrays, slows)),
+            pltpu.SemaphoreType.DMA((arrays, slows)),
+            pltpu.SemaphoreType.DMA((arrays, slows - 1)),
+            pltpu.SemaphoreType.DMA((arrays, slows - 1)),
+            pltpu.SemaphoreType.DMA,
+            pltpu.SemaphoreType.DMA,
+        ],
+        compiler_params=pltpu.CompilerParams(
+            collective_id=collective_id, has_side_effects=True, vmem_limit_bytes=VMEM_LIMIT
+        ),
+        name="scatter_grads",
+    )(*fulls)
+
+
+def shares_tile(wide, narrow, noised, attn_in, attn_out, ffn_in):
+    rows, seq_len = noised.shape
+    return (
+        narrow == 4
+        and wide % 2 == 0
+        and rows == 1
+        and seq_len % (2 * CHUNKS * 128) == 0
+        and attn_out.shape[1] % 16 == 0
+        and ffn_in.shape[2] % 128 == 0
+    )
+
+
+def per_device(wide, narrow, *arrays):
+    noised, attn_in, attn_out, ffn_in = arrays[0], arrays[5], arrays[6], arrays[7]
+    if shares_tile(wide, narrow, noised, attn_in, attn_out, ffn_in):
+        return tiled_device(wide, *arrays)
+    return general_device(*arrays)
+
+
+def tiled_device(
+    wide,
+    noised,
+    clean,
+    timesteps,
+    segments,
+    counted,
+    attn_in,
+    attn_out,
+    ffn_in,
+    ffn_out,
+    tables,
+    gains,
+    attn_in_mean,
+    attn_out_mean,
+    ffn_in_mean,
+    ffn_out_mean,
+    tables_mean,
+    gains_mean,
+    attn_in_square,
+    attn_out_square,
+    ffn_in_square,
+    ffn_out_square,
+    tables_square,
+    gains_square,
+):
+    layers = attn_in.shape[0]
+    gain_rows, gain_cols = gains.shape
+    mask = counted.reshape(-1).astype(jnp.float32)
+    seq_len = mask.shape[0]
+    half = seq_len // 2
+    core = lax.rem(lax.axis_index("narrow"), 2)
+    small = jnp.pad(
+        jnp.concatenate(
+            [
+                lax.reduce_precision(gains, 8, 7),
+                jnp.full((1, gain_cols), jnp.sum(mask), jnp.float32),
+            ]
+        ),
+        ((0, -(gain_rows + 1) % 8), (0, -gain_cols % 128)),
+    )
+    shards, leads, kinds = [small, tables[0]], [0, 0], [F32, BF16]
+    for layer in range(layers):
+        shards += [attn_in[layer], attn_out[layer], ffn_in[layer], ffn_out[layer]]
+        leads += [1, 0, 0, 0]
+        kinds += [BF16] * 4
+    shards.append(tables[1])
+    leads.append(0)
+    kinds.append(BF16)
+    small_all, *weights = gather_wide(shards, leads, kinds, wide, 0)
+    token_total = jnp.sum(small_all[:, gain_rows, 0])
+    gain_w = small_all[:, :gain_rows, :gain_cols].transpose(1, 0, 2).reshape(gain_rows, 1, -1)
+    table_first = weights[0].reshape(-1, tables.shape[2])
+    table_last = weights[-1].reshape(-1, tables.shape[2])
+    query_w, output_w, expand_w, reduce_w = [], [], [], []
+    for layer in range(layers):
+        four = weights[1 + 4 * layer : 5 + 4 * layer]
+        query_w.append(four[0].reshape(four[0].shape[0], -1, four[0].shape[-1]))
+        output_w.append(four[1].reshape(-1, four[1].shape[-1]))
+        expand_w.append(four[2].reshape(-1, four[2].shape[-1]))
+        reduce_w.append(four[3].reshape(-1, four[3].shape[-1]))
+
+    noised_flat = noised.reshape(-1)
+    clean_flat = clean.reshape(-1)
+    step_flat = timesteps.reshape(-1)
+    vocab_local = tables.shape[2]
+    vocab_ids = lax.axis_index("narrow") * vocab_local + jnp.arange(vocab_local, dtype=jnp.int32)
+    extra = time_features(lax.dynamic_slice(step_flat, (core * half,), (half,)))
+    residual, normed = embed(noised_flat[:, None], extra, table_first, gain_w[0], 1)
+    segment = segments[0]
+    kept = []
+    for layer in range(layers):
+        projected = jnp.einsum(
+            "sd,cde->cse", normed, query_w[layer], preferred_element_type=jnp.float32
+        ).astype(jnp.bfloat16)
+        heads = projected.reshape(3, seq_len, -1, HD)
+        mixed, log_total = attend((heads[0], heads[1], heads[2], segment))
+        mixed = mixed.reshape(seq_len, -1)
+        middle, normed_two, before, after, result, normed_next = ffn_forward(
+            mixed, residual, output_w[layer], expand_w[layer], reduce_w[layer],
+            gain_w[2 * layer + 1], gain_w[2 * layer + 2], 2 + layer,
+        )
+        kept.append((residual, normed, heads, log_total, mixed, middle, normed_two, before, after))
+        residual, normed = result, normed_next
+
+    logits = jnp.dot(normed, table_last, preferred_element_type=jnp.float32)
+    local_top = jnp.max(logits, axis=1)
+    row_top = lax.pmax(local_top, "narrow")
+    row_total = lax.psum(jnp.sum(jnp.exp(logits - row_top[:, None]), axis=1), "narrow")
+    log_probs = logits - (row_top + jnp.log(row_total))[:, None]
+    probs = jnp.exp(log_probs)
+    clamped = jnp.maximum(step_flat, 2).astype(jnp.float32)[:, None]
+    beta = 1.0 / (STEPS - clamped + 1.0)
+    retain = (STEPS - clamped + 1.0) / STEPS
+    spread = (clamped - 1.0) / (STEPS * V)
+    at_noised = (vocab_ids[None, :] == noised_flat[:, None]).astype(jnp.float32)
+    at_clean = (vocab_ids[None, :] == clean_flat[:, None]).astype(jnp.float32)
+    forward_fac = beta / V + (1.0 - beta) * at_noised
+    backward_fac = retain * at_clean + spread
+    joint = forward_fac * backward_fac
+    marginal = retain * probs + spread
+    joint_total, cross, model_total, weighted, aligned, clean_logp = lax.psum(
+        (
+            jnp.sum(joint, axis=1),
+            jnp.sum(joint * (jnp.log(backward_fac) - jnp.log(marginal)), axis=1),
+            jnp.sum(forward_fac * marginal, axis=1),
+            jnp.sum(probs * joint / marginal, axis=1),
+            jnp.sum(forward_fac * probs, axis=1),
+            jnp.sum(at_clean * log_probs, axis=1),
+        ),
+        "narrow",
+    )
+    divergence = cross / joint_total - jnp.log(joint_total) + jnp.log(model_total)
+    first_step = step_flat == 1
+    losses = jnp.where(first_step, -clean_logp, divergence)
+    pull = retain * (
+        -(joint / joint_total[:, None]) / marginal + forward_fac / model_total[:, None]
+    )
+    centre = retain[:, 0] * (-weighted / joint_total + aligned / model_total)
+    grad_kl = probs * (pull - centre[:, None])
+    grad_recon = probs - at_clean
+    grad_logits = (
+        (mask / token_total)[:, None] * jnp.where(first_step[:, None], grad_recon, grad_kl)
+    ).astype(jnp.bfloat16)
+
+    grad, branch, d_last, gain_final = norm_backward(
+        grad_logits[None], table_last[None], normed, residual, gain_w[2 * layers], None, None, 2 + layers
+    )
+    next_id = 3 + layers
+    gain_grads = [None] * (2 * layers) + [gain_final]
+    grads = [None] * (4 * layers)
+    for layer in reversed(range(layers)):
+        residual, normed, heads, log_total, mixed, middle, normed_two, before, after = kept[layer]
+        grad_middle, grad_attn, grad_mixed, d_red, d_in, d_out, gain_two = ffn_backward(
+            grad, branch, reduce_w[layer], expand_w[layer], output_w[layer], before, after,
+            normed_two, middle, gain_w[2 * layer + 1], mixed, next_id,
+        )
+        pulled = attend_back(
+            (heads[0], heads[1], heads[2], segment, log_total, grad_mixed.reshape(seq_len, -1, HD))
+        )
+        grad_projected = jnp.stack(pulled).reshape(3, seq_len, -1).astype(jnp.bfloat16)
+        grad, branch, d_query, gain_one = norm_backward(
+            grad_projected, query_w[layer], normed, residual, gain_w[2 * layer], grad_middle,
+            math.sqrt(D) if layer == 0 else None, next_id + 1,
+        )
+        next_id += 2
+        gain_grads[2 * layer], gain_grads[2 * layer + 1] = gain_one, gain_two
+        grads[4 * layer : 4 * layer + 4] = [d_query, d_out, d_in, d_red]
+    picks = (noised_flat[:, None] == vocab_ids[None, :]).astype(jnp.bfloat16)
+    d_first = jnp.einsum("sd,sv->dv", branch, picks, preferred_element_type=jnp.float32)
+
+    def by_owner(value, lead):
+        shape = value.shape
+        return value.astype(jnp.bfloat16).reshape(shape[:lead] + (wide, shape[lead] // wide) + shape[lead + 1 :])
+
+    small_grad = jnp.pad(
+        jnp.concatenate(gain_grads).reshape(gain_rows, wide, gain_cols).transpose(1, 0, 2),
+        ((0, 0), (0, -gain_rows % 8), (0, -gain_cols % 128)),
+    )
+    fulls = [by_owner(value, lead) for value, lead in zip(grads, leads[2:])]
+    fulls += [by_owner(d_last[0], 0), by_owner(d_first, 0), small_grad]
+    own = scatter_wide(fulls, leads[2:] + [0, 0], next_id)
+    grad_attn_in, grad_attn_out, grad_ffn_in, grad_ffn_out = [
+        jnp.stack([own[4 * layer + which] for layer in range(layers)]) for which in range(4)
+    ]
+    grad_tables = jnp.stack([own[4 * layers + 1], own[4 * layers]])
+    grad_gains = own[-1][:gain_rows, :gain_cols]
+    narrow_first = (lax.axis_index("narrow") == 0).astype(jnp.float32)
+    squares = (
+        jnp.sum(grad_attn_in * grad_attn_in)
+        + jnp.sum(grad_attn_out * grad_attn_out)
+        + jnp.sum(grad_ffn_in * grad_ffn_in)
+        + jnp.sum(grad_ffn_out * grad_ffn_out)
+        + jnp.sum(grad_tables * grad_tables)
+        + narrow_first * jnp.sum(grad_gains * grad_gains)
+    )
+    squares, loss_sum = lax.psum(
+        (squares, narrow_first * jnp.sum(mask * losses)), ("wide", "narrow")
+    )
+    grad_norm = jnp.sqrt(squares)
+    factor = jnp.minimum(1.0, CLIP_NORM / (grad_norm + 1e-06))
+    results = [loss_sum, token_total, grad_norm]
+    for weight, gradient, first, second, decay, rate in (
+        (attn_in, grad_attn_in, attn_in_mean, attn_in_square, WEIGHT_DECAY, LEARN_RATE),
+        (attn_out, grad_attn_out, attn_out_mean, attn_out_square, WEIGHT_DECAY, LEARN_RATE),
+        (ffn_in, grad_ffn_in, ffn_in_mean, ffn_in_square, WEIGHT_DECAY, LEARN_RATE),
+        (ffn_out, grad_ffn_out, ffn_out_mean, ffn_out_square, WEIGHT_DECAY, LEARN_RATE),
+        (tables, grad_tables, tables_mean, tables_square, WEIGHT_DECAY, LEARN_RATE),
+        (gains, grad_gains, gains_mean, gains_square, 0.0, GAIN_RATE),
+    ):
+        results += adam(weight, factor * gradient, first, second, decay, rate)
+    return tuple(results)
+
+
 def solution(mesh):
+    wide, narrow = mesh.shape["wide"], mesh.shape["narrow"]
     placed = (
         P("wide", None),
         P("wide", None),
@@ -433,7 +1283,7 @@
         P(None, "wide"),
     )
     return jax.shard_map(
-        per_device,
+        functools.partial(per_device, wide, narrow),
         mesh=mesh,
         in_specs=placed,
         out_specs=(

time: 1910 us -> 924 us (0.48)
  waiting for transfers between devices: 1340 us -> 0 us
  Pallas kernels: 0 us -> 642 us
  blocking collectives: 151 us -> 63.7 us
  matrix products: 146 us -> 76.7 us
  other arithmetic: 157 us -> 95.7 us
  local copies, waits for them, and re-layouts: 85.8 us -> 27.2 us
    pallas_call x0 -> x10, Pallas kernels: none -> 642 us  [the longest x1 186 us: gather_wide(): pl.pallas_call(functools.partial(gather_kernel, arrays, leads), out_shape...]
    psum x10 -> x0, waiting for transfers between devices: 630 us -> none  [the longest x5 334 us: back_heads(): return lax.psum(partial_value, 'narrow')]
    reduce_scatter x3 -> x0, waiting for transfers between devices: 399 us -> none  [the longest x1 208 us: per_device(): lax.psum_scatter(grad_tables_all, 'wide', scatter_dimension=1, tiled=True)]
    all_gather x4 -> x0, waiting for transfers between devices: 181 us -> none  [the longest x1 50.9 us: per_device(): lax.all_gather(ffn_in.astype(jnp.bfloat16), 'wide', axis=1, tiled=True)]
    unnamed x23 -> x0, waiting for transfers between devices: 130 us -> none
    dot_general x27 -> x4, matrix products: 101 us -> 22.4 us  [the longest x1 8.99 us: tiled_device(): logits = jnp.dot(normed, table_last, preferred_element_type=jnp.float32)]
    unnamed x319 -> x62, local copies, waits for them, and re-layouts: 74.6 us -> 1.64 us
    all_gather x2 -> x0, blocking collectives: 64.7 us -> none  [the longest x1 36.4 us: per_device(): lax.all_gather(attn_out.astype(jnp.bfloat16), 'wide', axis=1, tiled=True)]
  transfers between devices with their start and end apart: 20 -> 0, of which waited for: 19 -> 0; matrix products, arithmetic and copies ran while one was open for 7% -> 0% of each run, Pallas kernels for 0% -> 0%
where the time goes in v1:
time: 924 us; the launch traced here: 914 us
  Pallas kernels  642 us (69%)
  other arithmetic  95.7 us (10%)
  matrix products  76.7 us (8%)
  blocking collectives  63.7 us (7%)
  local copies, waits for them, and re-layouts  27.2 us (3%)
    pallas_call x1, Pallas kernels, gather_wide(): pl.pallas_call(functools.partial(gather_kernel, arrays, leads), out_shape...  186 us
    pallas_call x1, Pallas kernels, scatter_wide(): pl.pallas_call(functools.partial(scatter_kernel, arrays, leads), out_shap...  176 us
    pallas_call x2, Pallas kernels, ffn_forward(): pl.pallas_call(ffn_kernel, out_shape=(jax.ShapeDtypeStruct((half, width),...  94.2 us
    pallas_call x3, Pallas kernels, norm_backward(): pl.pallas_call(kernel, out_shape=(jax.ShapeDtypeStruct((half, width), F32...  90.2 us
    pallas_call x2, Pallas kernels, ffn_backward(): pl.pallas_call(ffn_back_kernel, out_shape=(jax.ShapeDtypeStruct((half, wi...  65.7 us
    psum x1, blocking collectives, tiled_device(): lax.psum((squares, narrow_first * jnp.sum(mask * losses)), ('wide', 'narr...  39.8 us
    pallas_call x1, Pallas kernels, embed(): pl.pallas_call(embed_kernel, out_shape=(jax.ShapeDtypeStruct((seq_len //...  29.9 us

profile of v1, /device:TPU:0, one launch (start us, length us, event | category | flops | bytes accessed | tf_op | source)
XLA Modules:
  0.0 913.8 jit_solution(17307848205496641262)
XLA Ops:
  10.2 1.9 slice_bitcast_fusion.4
  12.1 2.4 broadcast_compare_fusion
  14.5 2.3 slice_bitcast_fusion.2
  16.8 2.8 multiply_sine_fusion
  22.1 186.5 %gather_weights.1 = (f32[8,8,128]{2,1,0:T(8,128)}, bf16[8,96,2048]{2,1,0:T(8,128)(2,1)}, bf16[3,8,96,192]{3,2,1,0:T(8,128)(2,1)}, bf16[8,96,192]{2,1,0:T(8,128)(...) custom-call(f32[8,128]{1,0:T(8,128)} %select_select_fusion.refs_0_, ...), custom_call_target="tpu_custom_call" | custom-call | tf_op jit(solution)/shard_map/gather_weights/pallas_call | solution.py:929
  214.0 29.9 %embed.1 = (f32[512,768]{1,0:T(8,128)}, bf16[1024,768]{1,0:T(8,128)(2,1)}) custom-call(s32[1024,1]{1,0:T(8,128)} %copy.72.ids, f32[512,768]{1,0:T(8,128)} %pad_maximum_fusion.extra, bf16[768,2048]{1,0:T(8,128)(2,1)} %bitcast.167, f32[1,768]{1,0:T(1,128)} %squeeze.86.gain.refs_4_), custom_call_target="tpu_custom_call" | custom-call | tf_op jit(solution)/shard_map/embed/pallas_call | solution.py:598
  243.9 3.3 fusion.39
  248.8 3.9 fusion
  252.6 4.4 exponential_reduce_fusion.1
  257.1 5.8 convolution_convert_fusion.3
  262.9 2.0 copy.75.mixed
  264.9 47.0 %ffn_forward.2 = (f32[512,768]{1,0:T(8,128)}, bf16[1024,768]{1,0:T(8,128)(2,1)}, f32[1024,768]{1,0:T(8,128)}, bf16[1024,768]{1,0:T(8,128)(2,1)}, f32[512,768]{1,0:T(8,128)}, /*index=5*/bf16[1024,768]{1,0:T(8,128)(2,1)}) custom-call(bf16[1024,192]{1,0:T(8,128)(2,1)} %copy.75.mixed, f32[512,768]{1,0:T(8,128)} %get-tuple-element.91.resid.refs_3_, ...), custom_call_target="tpu_custom_call" | custom-call | tf_op jit(solution)/shard_map/ffn_forward/pallas_call | solution.py:670
  312.0 3.3 fusion.36
  316.8 3.9 fusion.1
  320.7 4.4 exponential_reduce_fusion
  325.1 5.5 convolution_convert_fusion.2
  330.6 2.0 copy.78.mixed
  332.6 47.2 %ffn_forward.3 = (f32[512,768]{1,0:T(8,128)}, bf16[1024,768]{1,0:T(8,128)(2,1)}, f32[1024,768]{1,0:T(8,128)}, bf16[1024,768]{1,0:T(8,128)(2,1)}, f32[512,768]{1,0:T(8,128)}, /*index=5*/bf16[1024,768]{1,0:T(8,128)(2,1)}) custom-call(bf16[1024,192]{1,0:T(8,128)(2,1)} %copy.78.mixed, f32[512,768]{1,0:T(8,128)} %get-tuple-element.96.resid.refs_3_, ...), custom_call_target="tpu_custom_call" | custom-call | tf_op jit(solution)/shard_map/ffn_forward/pallas_call | solution.py:670
  379.8 9.0 fusion.73
  388.8 7.6 pmax.7
  396.5 4.6 exponential_reduce_fusion.2
  401.1 5.9 psum.63
  407.1 11.7 %fusion.14 = (f32[1024]{0:T(1024)S(1)}, f32[1024]{0:T(1024)S(1)}, f32[1024]{0:T(1024)S(1)}, f32[1024]{0:T(1024)S(1)}, f32[1024]{0:T(1024)S(1)}, /*index=5*/f32[1024]{0:T(1024)S(1)}) fusion(f32[1024,2048]{1,0:T(8,128)} %get-tuple-element.218, f32[1024]{0:T(1024)S(1)} %bitcast.227, f32[1024]{0:T(1024)S(1)} %bitcast.217, f32[1024]{0:T(1024)S(1)} %bitcast.229, ...), kind=kLoop, calls=%fused_computation.33 | loop fusion | flops 48228352 | bytes 8450048 | tf_op jit(solution)/shard_map/reduce_sum | solution.py:1170
  418.8 10.3 %all-reduce.4 = (f32[1024]{0:T(1024)S(1)}, f32[1024]{0:T(1024)S(1)}, f32[1024]{0:T(1024)S(1)}, f32[1024]{0:T(1024)S(1)}, f32[1024]{0:T(1024)S(1)}, /*index=5*/f32[1024]{0:T(1024)S(1)}) all-reduce(f32[1024]{0:T(1024)S(1)} %get-tuple-element.147, f32[1024]{0:T(1024)S(1)} %get-tuple-element.150, ...), channel_id=1, replica_groups=mesh['wide'=8,'narrow'=4] {'narrow'}, use_global_device_ids=true, to_apply=%region_16.17 | all-reduce | flops 6144 | bytes 49152 | tf_op jit(solution)/shard_map/psum | solution.py:1165
  430.9 12.0 %fusion.21.refs_0_ = bf16[1,1024,2048]{2,1,0:T(8,128)(2,1)} fusion(f32[1024]{0:T(1024)S(1)} %get-tuple-element.206, f32[1024]{0:T(1024)S(1)} %get-tuple-element.158, f32[1024]{0:T(1024)S(1)} %get-tuple-element.159, f32[1024]{0:T(1024)S(1)} %bitcast.228, f32[1024]{0:T(1024)S(1)} %bitcast.230, s32[1024]{0:T(1024)S(1)} %bitcast.223, f32[1024]{0:T(1024)S(1)} %bitcast.226, ...), kind=kLoop, calls=%fused_computation.41 | loop fusion | flops 48234496 | bytes 12637184 | tf_op jit(solution)/shard_map/broadcast_in_dim | solution.py:1190
  442.9 32.5 %norm_backward.3 = (f32[512,768]{1,0:T(8,128)}, bf16[1024,768]{1,0:T(8,128)(2,1)}, bf16[1,768,2048]{2,1,0:T(8,128)(2,1)}, f32[1,768]{1,0:T(1,128)}) custom-call(bf16[1,1024,2048]{2,1,0:T(8,128)(2,1)} %fusion.21.refs_0_, bf16[1,768,2048]{2,1,0:T(8,128)(2,1)} %bitcast.166, bf16[1024,768]{1,0:T(8,128)(2,1)} %get-tuple-element.100.refs_2_, ...), custom_call_target="tpu_custom_call" | custom-call | tf_op jit(solution)/shard_map/norm_backward/pallas_call | solution.py:849
  475.4 32.9 %ffn_backward.2 = (f32[512,768]{1,0:T(8,128)}, bf16[1024,768]{1,0:T(8,128)(2,1)}, bf16[1024,192]{1,0:T(8,128)(2,1)}, bf16[768,768]{1,0:T(8,128)(2,1)}, bf16[768,...) custom-call(f32[512,768]{1,0:T(8,128)} %get-tuple-element.103.grad, ...), custom_call_target="tpu_custom_call" | custom-call | tf_op jit(solution)/shard_map/ffn_backward/pallas_call | solution.py:767
  509.6 6.5 convolution_convert_fusion.1
  516.3 7.1 multiply_reduce_fusion.1
  523.5 7.4 multiply_convert_fusion.1
  530.8 2.8 fusion.43
  533.6 2.0 fusion.42
  539.5 28.9 %norm_backward.4 = (f32[512,768]{1,0:T(8,128)}, bf16[1024,768]{1,0:T(8,128)(2,1)}, bf16[3,768,192]{2,1,0:T(8,128)(2,1)}, f32[1,768]{1,0:T(1,128)}) custom-call(bf16[3,1024,192]{2,1,0:T(8,128)(2,1)} %pad_maximum_fusion.1.refs_0_, bf16[3,768,192]{2,1,0:T(8,128)(2,1)} %bitcast.205, bf16[1024,768]{1,0:T(8,128)(2,1)} %get-tuple-element.95.refs_2_, ...), custom_call_target="tpu_custom_call" | custom-call | tf_op jit(solution)/shard_map/norm_backward/pallas_call | solution.py:849
  568.3 32.8 %ffn_backward.3 = (f32[512,768]{1,0:T(8,128)}, bf16[1024,768]{1,0:T(8,128)(2,1)}, bf16[1024,192]{1,0:T(8,128)(2,1)}, bf16[768,768]{1,0:T(8,128)(2,1)}, bf16[768,...) custom-call(f32[512,768]{1,0:T(8,128)} %get-tuple-element.111.grad, ...), custom_call_target="tpu_custom_call" | custom-call | tf_op jit(solution)/shard_map/ffn_backward/pallas_call | solution.py:767
  602.4 6.5 convolution_convert_fusion
  609.1 7.1 multiply_reduce_fusion
  616.2 7.1 multiply_convert_fusion
  623.4 2.0 fusion.45
  628.6 28.8 %norm_backward.5 = (f32[512,768]{1,0:T(8,128)}, bf16[1024,768]{1,0:T(8,128)(2,1)}, bf16[3,768,192]{2,1,0:T(8,128)(2,1)}, f32[1,768]{1,0:T(1,128)}) custom-call(bf16[3,1024,192]{2,1,0:T(8,128)(2,1)} %pad_maximum_fusion.2.refs_0_, bf16[3,768,192]{2,1,0:T(8,128)(2,1)} %bitcast.203, bf16[1024,768]{1,0:T(8,128)(2,1)} %get-tuple-element.90.refs_2_, ...), custom_call_target="tpu_custom_call" | custom-call | tf_op jit(solution)/shard_map/norm_backward/pallas_call | solution.py:849
  658.9 6.8 fusion.22
  665.8 176.0 %scatter_grads.1 = (f32[3,96,192]{2,1,0:T(8,128)}, f32[96,192]{1,0:T(8,128)}, f32[96,768]{1,0:T(8,128)}, f32[96,768]{1,0:T(8,128)}, f32[3,96,192]{2,1,0:T(8,128)...) custom-call(bf16[3,8,96,192]{3,2,1,0:T(8,128)(2,1)} %bitcast.189, ...), custom_call_target="tpu_custom_call" | custom-call | tf_op jit(solution)/shard_map/scatter_grads/pallas_call | solution.py:1021
  843.7 2.4 multiply_reduce_fusion.4
  846.1 2.0 multiply_reduce_fusion.5
  856.5 39.8 %all-reduce.3 = (f32[]{:T(128)}, f32[]{:T(128)}) all-reduce(f32[]{:T(128)S(6)} %mul.402, f32[]{:T(128)S(6)} %add.223), channel_id=1, replica_groups=mesh['wide'=8,'narrow'=4] {'wide','narrow'}, use_global_device_ids=true, to_apply=%region_18.19 | all-reduce | flops 2 | bytes 16 | tf_op jit(solution)/shard_map/psum | solution.py:1240
  898.6 2.2 fusion.66
  900.8 3.2 fusion.62
  904.0 3.2 fusion.64
  908.9 3.3 fusion.60
  (111 shorter events, 42.9 us)
Async XLA Ops:
  0.7 20.2 %copy-start.3 = (f32[2,96,2048]{2,1,0:T(8,128)S(1)}, f32[2,96,2048]{2,1,0:T(8,128)}, u32[]{:S(2)}) copy-start(f32[2,96,2048]{2,1,0:T(8,128)} %param.32) | copy-start | bytes 4718596
  248.0 0.7 copy-start.5
  252.6 10.3 %copy-start = (f32[3,1024,1024]{1,2,0:T(8,128)}, f32[3,1024,1024]{1,2,0:T(8,128)S(1)}, u32[]{:S(2)}) copy-start(f32[3,1024,1024]{1,2,0:T(8,128)S(1)} %get-tuple-element.214) | copy-start | bytes 37748740
  316.1 0.7 copy-start.7
  316.1 4.6 copy-start.9
  320.7 9.9 %copy-start.1 = (f32[3,1024,1024]{1,2,0:T(8,128)}, f32[3,1024,1024]{1,2,0:T(8,128)S(1)}, u32[]{:S(2)}) copy-start(f32[3,1024,1024]{1,2,0:T(8,128)S(1)} %get-tuple-element.216) | copy-start | bytes 37748740
  388.8 18.2 %copy-start.22 = (s32[1,1024]{1,0:T(1,128)S(1)}, s32[1,1024]{1,0:T(1,128)}, u32[]{:S(2)}) copy-start(s32[1,1024]{1,0:T(1,128)} %param.23) | copy-start | bytes 12292
  388.8 18.2 %copy-start.24 = (s32[1,1024]{1,0:T(1,128)S(1)}, s32[1,1024]{1,0:T(1,128)}, u32[]{:S(2)}) copy-start(s32[1,1024]{1,0:T(1,128)} %param.24) | copy-start | bytes 12292
  475.4 34.2 %copy-start.2 = (pred[1024,1024]{0,1:T(8,128)(4,1)S(1)}, pred[1024,1024]{0,1:T(8,128)(4,1)}, u32[]{:S(2)}) copy-start(pred[1024,1024]{0,1:T(8,128)(4,1)} %broadcast_compare_fusion) | copy-start | bytes 3145732
  509.6 6.8 copy-start.15
  523.4 7.4 copy-start.10
  523.5 10.2 %copy-start.8 = (bf16[1,1024,192]{1,2,0:T(8,128)(2,1)S(1)}, bf16[1,1024,192]{1,2,0:T(8,128)(2,1)}, u32[]{:S(2)}) copy-start(bf16[1,1024,192]{1,2,0:T(8,128)(2,1)} %copy-done.7) | copy-start | bytes 1179652
  602.4 6.8 copy-start.14
  616.2 7.2 copy-start.6
  625.4 32.0 %copy-start.27 = (f32[1,768]{1,0:T(1,128)S(1)}, f32[1,768]{1,0:T(1,128)}, u32[]{:S(2)}) copy-start(f32[1,768]{1,0:T(1,128)} %get-tuple-element.133) | copy-start | bytes 9220
  625.4 32.0 %copy-start.28 = (f32[1,768]{1,0:T(1,128)S(1)}, f32[1,768]{1,0:T(1,128)}, u32[]{:S(2)}) copy-start(f32[1,768]{1,0:T(1,128)} %get-tuple-element.132) | copy-start | bytes 9220
  625.4 32.0 %copy-start.29 = (f32[1,768]{1,0:T(1,128)S(1)}, f32[1,768]{1,0:T(1,128)}, u32[]{:S(2)}) copy-start(f32[1,768]{1,0:T(1,128)} %get-tuple-element.131) | copy-start | bytes 9220
  625.5 32.0 %copy-start.30 = (f32[1,768]{1,0:T(1,128)S(1)}, f32[1,768]{1,0:T(1,128)}, u32[]{:S(2)}) copy-start(f32[1,768]{1,0:T(1,128)} %get-tuple-element.130) | copy-start | bytes 9220
  665.8 231.4 %copy-start.23 = (f32[5,96]{1,0:T(8,128)S(1)}, f32[5,96]{1,0:T(8,128)}, u32[]{:S(2)}) copy-start(f32[5,96]{1,0:T(8,128)} %param.33) | copy-start | bytes 5764
  665.8 231.4 %copy-start.25 = (f32[5,96]{1,0:T(8,128)S(1)}, f32[5,96]{1,0:T(8,128)}, u32[]{:S(2)}) copy-start(f32[5,96]{1,0:T(8,128)} %param.39) | copy-start | bytes 5764
  665.8 231.4 %copy-start.26 = (f32[5,96]{1,0:T(8,128)S(1)}, f32[5,96]{1,0:T(8,128)}, u32[]{:S(2)}) copy-start(f32[5,96]{1,0:T(8,128)} %param.45) | copy-start | bytes 5764
  841.8 65.4 %copy-start.18 = (f32[3,96,192]{2,1,0:T(8,128)S(1)}, f32[3,96,192]{2,1,0:T(8,128)}, u32[]{:S(2)}) copy-start(f32[3,96,192]{2,1,0:T(8,128)} %get-tuple-element.134) | copy-start | bytes 663556
  846.1 62.7 %copy-start.4 = (f32[2,96,2048]{2,1,0:T(8,128)S(1)}, f32[2,96,2048]{2,1,0:T(8,128)}, u32[]{:S(2)}) copy-start(f32[2,96,2048]{2,1,0:T(8,128)} %param.32) | copy-start | bytes 4718596
  846.1 62.7 %copy-start.11 = (f32[96,2048]{1,0:T(8,128)S(1)}, f32[96,2048]{1,0:T(8,128)}, u32[]{:S(2)}) copy-start(f32[96,2048]{1,0:T(8,128)} %get-tuple-element.143) | copy-start | bytes 2359300
  846.1 62.7 %copy-start.12 = (f32[96,2048]{1,0:T(8,128)S(1)}, f32[96,2048]{1,0:T(8,128)}, u32[]{:S(2)}) copy-start(f32[96,2048]{1,0:T(8,128)} %get-tuple-element.142) | copy-start | bytes 2359300
  897.1 10.1 %copy-start.13 = (f32[2,3,96,192]{3,2,1,0:T(8,128)S(1)}, f32[2,3,96,192]{3,2,1,0:T(8,128)}, u32[]{:S(2)}) copy-start(f32[2,3,96,192]{3,2,1,0:T(8,128)} %param.28) | copy-start | bytes 1327108
  897.1 10.1 %copy-start.19 = (f32[3,96,192]{2,1,0:T(8,128)S(1)}, f32[3,96,192]{2,1,0:T(8,128)}, u32[]{:S(2)}) copy-start(f32[3,96,192]{2,1,0:T(8,128)} %get-tuple-element.135) | copy-start | bytes 663556
  897.1 10.1 %copy-start.20 = (f32[2,3,96,192]{3,2,1,0:T(8,128)S(1)}, f32[2,3,96,192]{3,2,1,0:T(8,128)}, u32[]{:S(2)}) copy-start(f32[2,3,96,192]{3,2,1,0:T(8,128)} %param.34) | copy-start | bytes 1327108
  897.1 10.1 %copy-start.21 = (f32[2,3,96,192]{3,2,1,0:T(8,128)S(1)}, f32[2,3,96,192]{3,2,1,0:T(8,128)}, u32[]{:S(2)}) copy-start(f32[2,3,96,192]{3,2,1,0:T(8,128)} %param.40) | copy-start | bytes 1327108
  897.1 11.7 %copy-start.16 = (f32[2,96,2048]{2,1,0:T(8,128)S(1)}, f32[2,96,2048]{2,1,0:T(8,128)}, u32[]{:S(2)}) copy-start(f32[2,96,2048]{2,1,0:T(8,128)} %param.38) | copy-start | bytes 4718596
  897.2 11.7 %copy-start.17 = (f32[2,96,2048]{2,1,0:T(8,128)S(1)}, f32[2,96,2048]{2,1,0:T(8,128)}, u32[]{:S(2)}) copy-start(f32[2,96,2048]{2,1,0:T(8,128)} %param.44) | copy-start | bytes 4718596

commit v2 on v1

--- a/solution.py
+++ b/solution.py
@@ -1042,6 +1042,421 @@
     )(*fulls)
 
 
+def head_lanes(value, head, size):
+    lanes = lax.broadcasted_iota(jnp.int32, value.shape, 1)
+    inside = (lanes >= head * size) & (lanes < (head + 1) * size)
+    return jnp.where(inside, value, jnp.zeros_like(value))
+
+
+def attention_kernel(normed, weights, key_seg, query_seg, projected, mixed, bias, values_t):
+    seq_len = normed.shape[0]
+    width = mixed.shape[1]
+    block = bias.shape[1]
+    heads = width // HD
+
+    def project(i, _):
+        rows = rows_at(0, i, block)
+        for which in range(3):
+            projected[which, rows, :] = dot_nn(normed[rows, :], weights[which]).astype(BF16)
+        return 0
+
+    lax.fori_loop(0, seq_len // block, project, 0)
+    values_t[...] = jnp.transpose(projected[2])
+
+    def queries(i, _):
+        rows = rows_at(0, i, block)
+        bias[...] = jnp.where(key_seg[...] == query_seg[:, rows], 0.0, -1e30)
+        asked = projected[0, rows, :] * HD ** (-0.5)
+        parts = []
+        for head in range(heads):
+            scores = dot_nt(projected[1], head_lanes(asked, head, HD)) + bias[...]
+            powers = jnp.exp(scores - jnp.max(scores, axis=0, keepdims=True))
+            probs = (powers * (1.0 / jnp.sum(powers, axis=0, keepdims=True))).astype(BF16)
+            parts.append(dot_nn(values_t[head * HD : (head + 1) * HD, :], probs))
+        mixed[rows, :] = jnp.transpose(jnp.concatenate(parts, axis=0)).astype(BF16)
+        return 0
+
+    lax.fori_loop(0, seq_len // block, queries, 0)
+
+
+QUERY_BLOCK = 256
+
+
+def attention(normed, weights, key_seg, query_seg):
+    seq_len, width = normed.shape[0], weights.shape[2]
+    block = min(QUERY_BLOCK, seq_len)
+    return pl.pallas_call(
+        attention_kernel,
+        out_shape=(
+            jax.ShapeDtypeStruct((3, seq_len, width), BF16),
+            jax.ShapeDtypeStruct((seq_len, width), BF16),
+        ),
+        in_specs=[whole_vmem()] * 4,
+        out_specs=(whole_vmem(),) * 2,
+        scratch_shapes=[pltpu.VMEM((seq_len, block), F32), pltpu.VMEM((width, seq_len), BF16)],
+        compiler_params=pltpu.CompilerParams(vmem_limit_bytes=VMEM_LIMIT),
+        name="attention",
+    )(normed, weights, key_seg, query_seg)
+
+
+def attention_back_kernel(projected, grad_mixed, key_seg, query_seg, out, bias, keys_t, grad_keys, grad_values):
+    seq_len, width = grad_mixed.shape
+    block = bias.shape[1]
+    heads = width // HD
+    scale = HD ** (-0.5)
+    keys_t[...] = jnp.transpose(projected[1])
+    grad_keys[...] = jnp.zeros(grad_keys.shape, F32)
+    grad_values[...] = jnp.zeros(grad_values.shape, F32)
+
+    def queries(i, _):
+        rows = rows_at(0, i, block)
+        bias[...] = jnp.where(key_seg[...] == query_seg[:, rows], 0.0, -1e30)
+        asked = projected[0, rows, :] * scale
+        given = grad_mixed[rows, :]
+        parts = []
+        for head in range(heads):
+            query = head_lanes(asked, head, HD)
+            grad = head_lanes(given, head, HD)
+            scores = dot_nt(projected[1], query) + bias[...]
+            powers = jnp.exp(scores - jnp.max(scores, axis=0, keepdims=True))
+            probs = powers * (1.0 / jnp.sum(powers, axis=0, keepdims=True))
+            grad_probs = dot_nt(projected[2], grad)
+            centre = jnp.sum(probs * grad_probs, axis=0, keepdims=True)
+            grad_scores = (probs * (grad_probs - centre)).astype(BF16)
+            parts.append(dot_nn(keys_t[head * HD : (head + 1) * HD, :], grad_scores))
+            grad_keys[...] += dot_nn(grad_scores, query)
+            grad_values[...] += dot_nn(probs.astype(BF16), grad)
+        out[0, rows, :] = (jnp.transpose(jnp.concatenate(parts, axis=0)) * scale).astype(BF16)
+        return 0
+
+    lax.fori_loop(0, seq_len // block, queries, 0)
+    out[1] = grad_keys[...].astype(BF16)
+    out[2] = grad_values[...].astype(BF16)
+
+
+def attention_back(projected, grad_mixed, key_seg, query_seg):
+    seq_len, width = grad_mixed.shape
+    block = min(QUERY_BLOCK, seq_len)
+    return pl.pallas_call(
+        attention_back_kernel,
+        out_shape=jax.ShapeDtypeStruct(projected.shape, BF16),
+        in_specs=[whole_vmem()] * 4,
+        out_specs=whole_vmem(),
+        scratch_shapes=[
+            pltpu.VMEM((seq_len, block), F32),
+            pltpu.VMEM((width, seq_len), BF16),
+            pltpu.VMEM((seq_len, width), F32),
+            pltpu.VMEM((seq_len, width), F32),
+        ],
+        compiler_params=pltpu.CompilerParams(vmem_limit_bytes=VMEM_LIMIT),
+        name="attention_back",
+    )(projected, grad_mixed, key_seg, query_seg)
+
+
+LANES = 128
+
+
+def spread(row):
+    return jnp.transpose(jnp.broadcast_to(row, (LANES, LANES)))
+
+
+def to_rows(columns):
+    lanes = lax.broadcasted_iota(jnp.int32, (LANES, LANES), 1)
+    total = jnp.zeros((LANES, LANES), F32)
+    for k, column in enumerate(columns):
+        total = jnp.where(lanes == k, column, total)
+    return jnp.transpose(total)[:8, :]
+
+
+def loss_kernel(
+    normed, table, info, value, gain,
+    grad_out, branch, d_table, d_gain, losses,
+    logits, grads, places, turned, stat_out, stat_in, sum_out, sum_in,
+    near_out, near_in, far_out, far_in, send, recv, stat_send, stat_recv, sum_send, sum_recv,
+):
+    seq_len, width = normed.shape
+    chunk = seq_len // 2 // CHUNKS
+    vocab = table.shape[1]
+    tiles = vocab // LANES
+    blocks = seq_len // LANES
+    me = lax.axis_index("narrow")
+    sibling, partner, mine, other = group_places(seq_len)
+    peers = [{"narrow": lax.rem(me + k, 4)} for k in range(1, 4)]
+    greet(peers)
+    sems = (send, recv)
+    trade = Exchange((near_out, near_in, far_out, far_in), sems, 0, sibling, partner)
+    share = Share(branch, sems, 2, sibling, mine, chunk)
+    first = (me * vocab).astype(F32)
+    whole = 4.0 * vocab
+    lanes = lax.broadcasted_iota(jnp.int32, (LANES, LANES), 1).astype(F32)
+
+    def stat_copy(b, k):
+        return remote(stat_out.at[b], stat_in.at[k, b], stat_send.at[k, b], stat_recv.at[k, b], peers[k])
+
+    def sum_copy(b, k):
+        return remote(sum_out.at[b], sum_in.at[k, b], sum_send.at[k, b], sum_recv.at[k, b], peers[k])
+
+    def tile_at(t):
+        return pl.ds(pl.multiple_of(t * LANES, LANES), LANES)
+
+    def ask(b, _):
+        rows = rows_at(0, b, LANES)
+        logits[rows, :] = dot_nn(normed[rows, :], table[...])
+        here = info[:, rows]
+        at_noised = spread(here[0:1] - first)
+        at_clean = spread(here[1:2] - first)
+        places[b, 0] = at_noised
+        places[b, 1] = at_clean
+
+        def top_step(t, top):
+            return jnp.maximum(top, logits[rows, tile_at(t)])
+
+        top = lax.fori_loop(1, tiles, top_step, logits[rows, tile_at(0)], unroll=4)
+        top = jnp.max(top, axis=1, keepdims=True)
+        top_wide = jnp.broadcast_to(top, (LANES, LANES))
+
+        def sum_step(t, totals):
+            powers, noised, clean = totals
+            piece = logits[rows, tile_at(t)]
+            column = lanes + (t * LANES).astype(F32)
+            return (
+                powers + jnp.exp(piece - top_wide),
+                noised + jnp.where(column == at_noised, piece, 0.0),
+                clean + jnp.where(column == at_clean, piece, 0.0),
+            )
+
+        zero = jnp.zeros((LANES, LANES), F32)
+        totals = lax.fori_loop(0, tiles, sum_step, (zero, zero, zero))
+        stat_out[b] = to_rows([top] + [jnp.sum(total, axis=1, keepdims=True) for total in totals])
+        for k in range(3):
+            stat_copy(b, k).start()
+        return 0
+
+    lax.fori_loop(0, blocks, ask, 0)
+
+    def scalars(b):
+        here = info[:, rows_at(0, b, LANES)]
+        step = jnp.maximum(here[2:3], 2.0)
+        left = STEPS - step + 1.0
+        beta = 1.0 / left
+        keep = left / STEPS
+        rest = (step - 1.0) / (STEPS * whole)
+        own = stat_out[b]
+        others = [stat_in[k, b] for k in range(3)]
+        top = own[0:1]
+        for stat in others:
+            top = jnp.maximum(top, stat[0:1])
+        total = own[1:2] * jnp.exp(own[0:1] - top)
+        noised, clean = own[2:3], own[3:4]
+        for stat in others:
+            total = total + stat[1:2] * jnp.exp(stat[0:1] - top)
+            noised, clean = noised + stat[2:3], clean + stat[3:4]
+        return here, beta, keep, rest, top + jnp.log(total), noised, clean
+
+    def measure(b, _):
+        rows = rows_at(0, b, LANES)
+        for k in range(3):
+            stat_copy(b, k).wait_recv()
+        _, _, keep, rest, log_total, _, _ = scalars(b)
+        log_wide = spread(log_total)
+        ratio = spread(keep / rest)
+
+        def step(t, totals):
+            logs, shares = totals
+            probs = jnp.exp(logits[rows, tile_at(t)] - log_wide)
+            logits[rows, tile_at(t)] = probs
+            grown = 1.0 + probs * ratio
+            return (logs + jnp.log(grown), shares + probs / grown)
+
+        zero = jnp.zeros((LANES, LANES), F32)
+        totals = lax.fori_loop(0, tiles, step, (zero, zero))
+        sum_out[b] = to_rows([jnp.sum(total, axis=1, keepdims=True) for total in totals])
+        for k in range(3):
+            sum_copy(b, k).start()
+        return 0
+
+    lax.fori_loop(0, blocks, measure, 0)
+
+    def pull(b):
+        rows = rows_at(0, b, LANES)
+        for k in range(3):
+            sum_copy(b, k).wait_recv()
+        here, beta, keep, rest, log_total, noised, clean = scalars(b)
+        sums = sum_out[b] + sum_in[0, b] + sum_in[1, b] + sum_in[2, b]
+        log_sum, share_sum = sums[0:1], sums[1:2] / rest
+        same = here[0:1] == here[1:2]
+        first_step = here[2:3] == 1.0
+        base_a, more_a = beta / whole, 1.0 - beta
+        base_w = base_a * rest
+        joint = whole * base_w + more_a * rest + base_a * keep + jnp.where(same, more_a * keep, 0.0)
+        ratio = keep / rest
+        prob_n, prob_c = jnp.exp(noised - log_total), jnp.exp(clean - log_total)
+        grown_n, grown_c = 1.0 + prob_n * ratio, 1.0 + prob_c * ratio
+        marginal_n, marginal_c = rest * grown_n, rest * grown_c
+        log_n, log_c = jnp.log(grown_n), jnp.log(grown_c)
+        weight_n = jnp.where(same, 0.0, more_a * rest)
+        weight_c = jnp.where(same, more_a * rest + base_a * keep + more_a * keep, base_a * keep)
+        lift = jnp.log((keep + rest) / rest)
+        cross = -base_w * log_sum - weight_n * log_n - weight_c * log_c + (base_w + weight_c) * lift
+        model = base_a * (keep + whole * rest) + more_a * marginal_n
+        divergence = cross / joint - jnp.log(joint) + jnp.log(model)
+        loss = jnp.where(first_step, log_total - clean, divergence)
+        losses[:, rows] = here[4:5] * loss
+        weighted = base_w * share_sum + weight_n * prob_n / marginal_n + weight_c * prob_c / marginal_c
+        aligned = base_a + more_a * prob_n
+        centre = keep * (aligned / model - weighted / joint)
+        scale = here[3:4]
+        zero = jnp.zeros_like(scale)
+        even = scale * jnp.where(first_step, 1.0, keep * base_a / model - centre)
+        bent = scale * jnp.where(first_step, zero, -keep * base_w / joint / rest)
+        at_n = prob_n * keep * (more_a / model - weight_n / joint / marginal_n)
+        at_c = -prob_c * keep * (weight_c / joint / marginal_c)
+        extra_n = spread(scale * jnp.where(first_step, zero, at_n))
+        extra_c = spread(scale * jnp.where(first_step, -1.0, at_c))
+        even, bent, ratio = spread(even), spread(bent), spread(ratio)
+        at_noised, at_clean = places[b, 0], places[b, 1]
+
+        def step(t, _):
+            probs = logits[rows, tile_at(t)]
+            column = lanes + (t * LANES).astype(F32)
+            grad = probs * (even + bent / (1.0 + probs * ratio))
+            grad = grad + jnp.where(column == at_noised, extra_n, 0.0)
+            grad = grad + jnp.where(column == at_clean, extra_c, 0.0)
+            grads[rows, tile_at(t)] = grad.astype(BF16)
+            return 0
+
+        lax.fori_loop(0, tiles, step, 0)
+
+    def partial(start, j):
+        base = start // LANES + j * (chunk // LANES)
+        for b in range(chunk // LANES):
+            pull(base + b)
+        return dot_nt(grads[rows_at(start, j, chunk), :], table[...])
+
+    trade.give(0, partial(other, 0))
+    for j in range(CHUNKS):
+        if j + 1 < CHUNKS:
+            trade.give(j + 1, partial(other, j + 1))
+        trade.pass_on(j, partial(mine, j))
+    turned[...] = jnp.transpose(normed[...])
+    weight_grad(turned, grads, d_table)
+    gain_total = jnp.zeros(gain.shape, F32)
+    for j in range(CHUNKS):
+        rows = rows_at(0, j, chunk)
+        back, gain_part = norm_back(trade.take(j), value[rows, :], gain[...])
+        gain_total = gain_total + gain_part
+        grad_out[rows, :] = back
+        share.put(j, back.astype(BF16))
+    d_gain[...] = gain_total
+    for j in range(CHUNKS):
+        share.arrived(j)
+    trade.close()
+    share.close()
+
+    def finish(b, _):
+        for k in range(3):
+            stat_copy(b, k).wait_send()
+            sum_copy(b, k).wait_send()
+        return 0
+
+    lax.fori_loop(0, blocks, finish, 0)
+
+
+def loss_and_back(normed, table, info, value, gain, collective_id):
+    seq_len, width = normed.shape
+    vocab = table.shape[1]
+    half, chunk, blocks = seq_len // 2, seq_len // 2 // CHUNKS, seq_len // LANES
+    return pl.pallas_call(
+        loss_kernel,
+        out_shape=(
+            jax.ShapeDtypeStruct((half, width), F32),
+            jax.ShapeDtypeStruct((seq_len, width), BF16),
+            jax.ShapeDtypeStruct(table.shape, BF16),
+            jax.ShapeDtypeStruct(gain.shape, F32),
+            jax.ShapeDtypeStruct((1, seq_len), F32),
+        ),
+        in_specs=[whole_vmem()] * 5,
+        out_specs=(whole_vmem(),) * 5,
+        scratch_shapes=[
+            pltpu.VMEM((seq_len, vocab), F32),
+            pltpu.VMEM((seq_len, vocab), BF16),
+            pltpu.VMEM((blocks, 2, LANES, LANES), F32),
+            pltpu.VMEM((width, seq_len), BF16),
+            pltpu.VMEM((blocks, 8, LANES), F32),
+            pltpu.VMEM((3, blocks, 8, LANES), F32),
+            pltpu.VMEM((blocks, 8, LANES), F32),
+            pltpu.VMEM((3, blocks, 8, LANES), F32),
+        ]
+        + Exchange.scratch(chunk, width, BACKWARD_KIND)
+        + [pltpu.SemaphoreType.DMA((3, CHUNKS)), pltpu.SemaphoreType.DMA((3, CHUNKS))]
+        + [pltpu.SemaphoreType.DMA((3, blocks))] * 4,
+        compiler_params=pltpu.CompilerParams(
+            collective_id=collective_id, has_side_effects=True, vmem_limit_bytes=VMEM_LIMIT
+        ),
+        name="loss_and_back",
+    )(normed, table, info, value, gain)
+
+
+def scalars_kernel(given, out, near, along, across, send, recv):
+    count = 2 * along.shape[0]
+    me, slow, fast, slows = wide_places(count)
+    place = lax.axis_index("narrow")
+    beside = me + 1 - 2 * fast
+    group = near.shape[0]
+
+    def near_copy(step):
+        return remote(
+            near.at[place], near.at[place], send.at[0, step - 1], recv.at[0, step - 1],
+            {"narrow": lax.rem(place + step, group)},
+        )
+
+    def along_copy(step):
+        return remote(
+            along.at[slow], along.at[slow], send.at[1, step - 1], recv.at[1, step - 1],
+            {"wide": 2 * lax.rem(slow + step, slows) + fast},
+        )
+
+    greet(
+        [{"narrow": lax.rem(place + step, group)} for step in range(1, group)]
+        + [{"wide": 2 * lax.rem(slow + step, slows) + fast} for step in range(1, slows)]
+        + [{"wide": beside}]
+    )
+    near[place] = given[...]
+    for step in range(1, group):
+        near_copy(step).start()
+    for step in range(1, group):
+        near_copy(step).wait()
+    along[slow] = jnp.sum(near[...], axis=0)
+    for step in range(1, slows):
+        along_copy(step).start()
+    for step in range(1, slows):
+        along_copy(step).wait()
+    across[0] = jnp.sum(along[...], axis=0)
+    last = remote(across.at[0], across.at[1], send.at[2, 0], recv.at[2, 0], {"wide": beside})
+    last.start()
+    last.wait()
+    out[...] = across[0] + across[1]
+
+
+def sum_scalars(given, wide, narrow, collective_id):
+    steps = max(wide // 2, narrow) - 1
+    return pl.pallas_call(
+        scalars_kernel,
+        out_shape=jax.ShapeDtypeStruct(given.shape, F32),
+        in_specs=[whole_vmem()],
+        out_specs=whole_vmem(),
+        scratch_shapes=[
+            pltpu.VMEM((narrow,) + given.shape, F32),
+            pltpu.VMEM((wide // 2,) + given.shape, F32),
+            pltpu.VMEM((2,) + given.shape, F32),
+            pltpu.SemaphoreType.DMA((3, steps)),
+            pltpu.SemaphoreType.DMA((3, steps)),
+        ],
+        compiler_params=pltpu.CompilerParams(collective_id=collective_id, has_side_effects=True),
+        name="sum_scalars",
+    )(given)
+
+
 def shares_tile(wide, narrow, noised, attn_in, attn_out, ffn_in):
     rows, seq_len = noised.shape
     return (
@@ -1130,78 +1545,34 @@
     vocab_ids = lax.axis_index("narrow") * vocab_local + jnp.arange(vocab_local, dtype=jnp.int32)
     extra = time_features(lax.dynamic_slice(step_flat, (core * half,), (half,)))
     residual, normed = embed(noised_flat[:, None], extra, table_first, gain_w[0], 1)
-    segment = segments[0]
+    key_seg, query_seg = segments.reshape(-1, 1), segments.reshape(1, -1)
     kept = []
     for layer in range(layers):
-        projected = jnp.einsum(
-            "sd,cde->cse", normed, query_w[layer], preferred_element_type=jnp.float32
-        ).astype(jnp.bfloat16)
-        heads = projected.reshape(3, seq_len, -1, HD)
-        mixed, log_total = attend((heads[0], heads[1], heads[2], segment))
-        mixed = mixed.reshape(seq_len, -1)
+        projected, mixed = attention(normed, query_w[layer], key_seg, query_seg)
         middle, normed_two, before, after, result, normed_next = ffn_forward(
             mixed, residual, output_w[layer], expand_w[layer], reduce_w[layer],
             gain_w[2 * layer + 1], gain_w[2 * layer + 2], 2 + layer,
         )
-        kept.append((residual, normed, heads, log_total, mixed, middle, normed_two, before, after))
+        kept.append((residual, normed, projected, mixed, middle, normed_two, before, after))
         residual, normed = result, normed_next
 
-    logits = jnp.dot(normed, table_last, preferred_element_type=jnp.float32)
-    local_top = jnp.max(logits, axis=1)
-    row_top = lax.pmax(local_top, "narrow")
-    row_total = lax.psum(jnp.sum(jnp.exp(logits - row_top[:, None]), axis=1), "narrow")
-    log_probs = logits - (row_top + jnp.log(row_total))[:, None]
-    probs = jnp.exp(log_probs)
-    clamped = jnp.maximum(step_flat, 2).astype(jnp.float32)[:, None]
-    beta = 1.0 / (STEPS - clamped + 1.0)
-    retain = (STEPS - clamped + 1.0) / STEPS
-    spread = (clamped - 1.0) / (STEPS * V)
-    at_noised = (vocab_ids[None, :] == noised_flat[:, None]).astype(jnp.float32)
-    at_clean = (vocab_ids[None, :] == clean_flat[:, None]).astype(jnp.float32)
-    forward_fac = beta / V + (1.0 - beta) * at_noised
-    backward_fac = retain * at_clean + spread
-    joint = forward_fac * backward_fac
-    marginal = retain * probs + spread
-    joint_total, cross, model_total, weighted, aligned, clean_logp = lax.psum(
-        (
-            jnp.sum(joint, axis=1),
-            jnp.sum(joint * (jnp.log(backward_fac) - jnp.log(marginal)), axis=1),
-            jnp.sum(forward_fac * marginal, axis=1),
-            jnp.sum(probs * joint / marginal, axis=1),
-            jnp.sum(forward_fac * probs, axis=1),
-            jnp.sum(at_clean * log_probs, axis=1),
-        ),
-        "narrow",
-    )
-    divergence = cross / joint_total - jnp.log(joint_total) + jnp.log(model_total)
-    first_step = step_flat == 1
-    losses = jnp.where(first_step, -clean_logp, divergence)
-    pull = retain * (
-        -(joint / joint_total[:, None]) / marginal + forward_fac / model_total[:, None]
-    )
-    centre = retain[:, 0] * (-weighted / joint_total + aligned / model_total)
-    grad_kl = probs * (pull - centre[:, None])
-    grad_recon = probs - at_clean
-    grad_logits = (
-        (mask / token_total)[:, None] * jnp.where(first_step[:, None], grad_recon, grad_kl)
-    ).astype(jnp.bfloat16)
-
-    grad, branch, d_last, gain_final = norm_backward(
-        grad_logits[None], table_last[None], normed, residual, gain_w[2 * layers], None, None, 2 + layers
+    info = jnp.stack(
+        [noised_flat.astype(F32), clean_flat.astype(F32), step_flat.astype(F32), mask / token_total, mask]
+        + [jnp.zeros_like(mask)] * 3
+    )
+    grad, branch, d_last, gain_final, losses = loss_and_back(
+        normed, table_last, info, residual, gain_w[2 * layers], 2 + layers
     )
     next_id = 3 + layers
     gain_grads = [None] * (2 * layers) + [gain_final]
     grads = [None] * (4 * layers)
     for layer in reversed(range(layers)):
-        residual, normed, heads, log_total, mixed, middle, normed_two, before, after = kept[layer]
+        residual, normed, projected, mixed, middle, normed_two, before, after = kept[layer]
         grad_middle, grad_attn, grad_mixed, d_red, d_in, d_out, gain_two = ffn_backward(
             grad, branch, reduce_w[layer], expand_w[layer], output_w[layer], before, after,
             normed_two, middle, gain_w[2 * layer + 1], mixed, next_id,
         )
-        pulled = attend_back(
-            (heads[0], heads[1], heads[2], segment, log_total, grad_mixed.reshape(seq_len, -1, HD))
-        )
-        grad_projected = jnp.stack(pulled).reshape(3, seq_len, -1).astype(jnp.bfloat16)
+        grad_projected = attention_back(projected, grad_mixed, key_seg, query_seg)
         grad, branch, d_query, gain_one = norm_backward(
             grad_projected, query_w[layer], normed, residual, gain_w[2 * layer], grad_middle,
             math.sqrt(D) if layer == 0 else None, next_id + 1,
@@ -1221,7 +1592,7 @@
         ((0, 0), (0, -gain_rows % 8), (0, -gain_cols % 128)),
     )
     fulls = [by_owner(value, lead) for value, lead in zip(grads, leads[2:])]
-    fulls += [by_owner(d_last[0], 0), by_owner(d_first, 0), small_grad]
+    fulls += [by_owner(d_last, 0), by_owner(d_first, 0), small_grad]
     own = scatter_wide(fulls, leads[2:] + [0, 0], next_id)
     grad_attn_in, grad_attn_out, grad_ffn_in, grad_ffn_out = [
         jnp.stack([own[4 * layer + which] for layer in range(layers)]) for which in range(4)
@@ -1237,9 +1608,10 @@
         + jnp.sum(grad_tables * grad_tables)
         + narrow_first * jnp.sum(grad_gains * grad_gains)
     )
-    squares, loss_sum = lax.psum(
-        (squares, narrow_first * jnp.sum(mask * losses)), ("wide", "narrow")
-    )
+    lanes = lax.broadcasted_iota(jnp.int32, (8, 128), 1)
+    both = jnp.where(lanes == 0, squares, jnp.where(lanes == 1, narrow_first * jnp.sum(losses), 0.0))
+    both = sum_scalars(both, wide, 4, next_id + 1)
+    squares, loss_sum = both[0, 0], both[0, 1]
     grad_norm = jnp.sqrt(squares)
     factor = jnp.minimum(1.0, CLIP_NORM / (grad_norm + 1e-06))
     results = [loss_sum, token_total, grad_norm]

time: 924 us -> 818 us (0.89)
  Pallas kernels: 642 us -> 748 us
  matrix products: 76.7 us -> 6.91 us
  other arithmetic: 95.7 us -> 30.7 us
  blocking collectives: 63.7 us -> 0 us
  local copies, waits for them, and re-layouts: 27.2 us -> 15.8 us
    pallas_call x0 -> x6, Pallas kernels: none -> 137 us  [the longest x1 58.9 us: loss_and_back(): pl.pallas_call(loss_kernel, out_shape=(jax.ShapeDtypeStruct((half, width)...]
    dot_general x15 -> x0, matrix products: 69.8 us -> none  [the longest x2 14.2 us: attend_back(): jnp.einsum('qhd,khd->hqk', grad_mixed, values, preferred_element_type=jnp...]
    psum x3 -> x0, blocking collectives: 56 us -> none  [the longest x1 39.8 us: tiled_device(): lax.psum((squares, narrow_first * jnp.sum(mask * losses)), ('wide', 'narr...]
    pallas_call x3 -> x2, Pallas kernels: 90.2 us -> 57.9 us  [norm_backward(): pl.pallas_call(kernel, out_shape=(jax.ShapeDtypeStruct((half, width), F32...]
    reduce_sum x4 -> x1, other arithmetic: 25.1 us -> 1.3 us  [tiled_device(): jnp.sum(losses)]
    convert_element_type x2 -> x3, other arithmetic: 14.5 us -> 0.02 us  [the longest x1 0.01 us: tiled_device(): noised_flat.astype(F32)]
    broadcast_in_dim x1 -> x0, other arithmetic: 12 us -> none  [tiled_device(): grad_logits[None]]
where the time goes in v2:
time: 818 us; the launch traced here: 809 us
  Pallas kernels  748 us (91%)
  other arithmetic  30.7 us (4%)
  local copies, waits for them, and re-layouts  15.8 us (2%)
    pallas_call x1, Pallas kernels, gather_wide(): pl.pallas_call(functools.partial(gather_kernel, arrays, leads), out_shape...  186 us
    pallas_call x1, Pallas kernels, scatter_wide(): pl.pallas_call(functools.partial(scatter_kernel, arrays, leads), out_shap...  176 us
    pallas_call x2, Pallas kernels, ffn_forward(): pl.pallas_call(ffn_kernel, out_shape=(jax.ShapeDtypeStruct((half, width),...  94.2 us
    pallas_call x2, Pallas kernels, ffn_backward(): pl.pallas_call(ffn_back_kernel, out_shape=(jax.ShapeDtypeStruct((half, wi...  66 us
    pallas_call x1, Pallas kernels, loss_and_back(): pl.pallas_call(loss_kernel, out_shape=(jax.ShapeDtypeStruct((half, width)...  58.9 us
    pallas_call x2, Pallas kernels, norm_backward(): pl.pallas_call(kernel, out_shape=(jax.ShapeDtypeStruct((half, width), F32...  57.9 us
    pallas_call x2, Pallas kernels, attention_back(): pl.pallas_call(attention_back_kernel, out_shape=jax.ShapeDtypeStruct(proj...  37.1 us
    pallas_call x1, Pallas kernels, embed(): pl.pallas_call(embed_kernel, out_shape=(jax.ShapeDtypeStruct((seq_len //...  29.9 us

profile of v2, /device:TPU:0, one launch (start us, length us, event | category | flops | bytes accessed | tf_op | source)
XLA Modules:
  0.0 809.2 jit_solution(12126616661052401535)
XLA Ops:
  0.7 1.7 copy.50.ids
  2.4 0.7 dynamic-slice_convert_fusion
  3.1 2.8 multiply_sine_fusion
  5.9 1.3 pad_maximum_fusion.extra
  7.8 1.2 select_select_fusion.refs_0_
  9.1 1.3 slice_bitcast_fusion
  10.4 0.8 slice_bitcast_fusion.4
  11.2 0.7 slice_bitcast_fusion.8
  11.9 1.0 slice_bitcast_fusion.2
  12.9 186.5 %gather_weights.1 = (f32[8,8,128]{2,1,0:T(8,128)}, bf16[8,96,2048]{2,1,0:T(8,128)(2,1)}, bf16[3,8,96,192]{3,2,1,0:T(8,128)(2,1)}, bf16[8,96,192]{2,1,0:T(8,128)(...) custom-call(f32[8,128]{1,0:T(8,128)} %select_select_fusion.refs_0_, ...), custom_call_target="tpu_custom_call" | custom-call | tf_op jit(solution)/shard_map/gather_weights/pallas_call | solution.py:929
  199.4 0.8 slice_bitcast_fusion.10
  200.2 0.7 squeeze.65.gain.refs_4_
  200.9 29.9 %embed.1 = (f32[512,768]{1,0:T(8,128)}, bf16[1024,768]{1,0:T(8,128)(2,1)}) custom-call(s32[1024,1]{1,0:T(8,128)} %copy.50.ids, f32[512,768]{1,0:T(8,128)} %pad_maximum_fusion.extra, bf16[768,2048]{1,0:T(8,128)(2,1)} %bitcast.81, f32[1,768]{1,0:T(1,128)} %squeeze.65.gain.refs_4_), custom_call_target="tpu_custom_call" | custom-call | tf_op jit(solution)/shard_map/embed/pallas_call | solution.py:598
  230.8 1.0 copy.51.key_seg
  231.8 13.5 %attention.2 = (bf16[3,1024,192]{2,1,0:T(8,128)(2,1)}, bf16[1024,192]{1,0:T(8,128)(2,1)}) custom-call(bf16[1024,768]{1,0:T(8,128)(2,1)} %get-tuple-element.93.normed.refs_2_, bf16[3,768,192]{2,1,0:T(8,128)(2,1)} %bitcast.70, s32[1024,1]{1,0:T(8,128)} %copy.51.key_seg, s32[1,1024]{1,0:T(1,128)} %query_seg.7), custom_call_target="tpu_custom_call" | custom-call | tf_op jit(solution)/shard_map/attention/pallas_call | solution.py:1088
  245.4 0.7 squeeze.66.gain
  246.0 0.7 squeeze.67.gain_next.refs_4_
  246.7 47.2 %ffn_forward.2 = (f32[512,768]{1,0:T(8,128)}, bf16[1024,768]{1,0:T(8,128)(2,1)}, f32[1024,768]{1,0:T(8,128)}, bf16[1024,768]{1,0:T(8,128)(2,1)}, f32[512,768]{1,0:T(8,128)}, /*index=5*/bf16[1024,768]{1,0:T(8,128)(2,1)}) custom-call(bf16[1024,192]{1,0:T(8,128)(2,1)} %get-tuple-element.96.mixed, f32[512,768]{1,0:T(8,128)} %get-tuple-element.97.resid.refs_3_, ...), custom_call_target="tpu_custom_call" | custom-call | tf_op jit(solution)/shard_map/ffn_forward/pallas_call | solution.py:670
  293.9 13.9 %attention.3 = (bf16[3,1024,192]{2,1,0:T(8,128)(2,1)}, bf16[1024,192]{1,0:T(8,128)(2,1)}) custom-call(bf16[1024,768]{1,0:T(8,128)(2,1)} %get-tuple-element.101.normed.refs_2_, bf16[3,768,192]{2,1,0:T(8,128)(2,1)} %bitcast.72, s32[1024,1]{1,0:T(8,128)} %copy.51.key_seg, s32[1,1024]{1,0:T(1,128)} %query_seg.7), custom_call_target="tpu_custom_call" | custom-call | tf_op jit(solution)/shard_map/attention/pallas_call | solution.py:1088
  307.8 0.7 squeeze.68.gain
  308.5 0.7 squeeze.69.gain_next.gain
  309.2 47.0 %ffn_forward.3 = (f32[512,768]{1,0:T(8,128)}, bf16[1024,768]{1,0:T(8,128)(2,1)}, f32[1024,768]{1,0:T(8,128)}, bf16[1024,768]{1,0:T(8,128)(2,1)}, f32[512,768]{1,0:T(8,128)}, /*index=5*/bf16[1024,768]{1,0:T(8,128)(2,1)}) custom-call(bf16[1024,192]{1,0:T(8,128)(2,1)} %get-tuple-element.104.mixed, f32[512,768]{1,0:T(8,128)} %get-tuple-element.105.resid.refs_3_, ...), custom_call_target="tpu_custom_call" | custom-call | tf_op jit(solution)/shard_map/ffn_forward/pallas_call | solution.py:670
  356.2 1.4 slice_reduce_fusion.5
  357.6 0.7 broadcast_divide_fusion
  358.3 0.7 stack.57.info
  359.0 58.9 %loss_and_back.1 = (f32[512,768]{1,0:T(8,128)}, bf16[1024,768]{1,0:T(8,128)(2,1)}, bf16[768,2048]{1,0:T(8,128)(2,1)}, f32[1,768]{1,0:T(1,128)}, f32[1,1024]{1,0:T(1,128)}) custom-call(bf16[1024,768]{1,0:T(8,128)(2,1)} %get-tuple-element.109.normed, bf16[768,2048]{1,0:T(8,128)(2,1)} %bitcast.80, f32[8,1024]{1,0:T(8,128)} %stack.57.info, ...), custom_call_target="tpu_custom_call" | custom-call | tf_op jit(solution)/shard_map/loss_and_back/pallas_call | solution.py:1369
  417.9 1.3 reduce_sum.89
  419.8 32.9 %ffn_backward.2 = (f32[512,768]{1,0:T(8,128)}, bf16[1024,768]{1,0:T(8,128)(2,1)}, bf16[1024,192]{1,0:T(8,128)(2,1)}, bf16[768,768]{1,0:T(8,128)(2,1)}, bf16[768,...) custom-call(f32[512,768]{1,0:T(8,128)} %get-tuple-element.112.grad, ...), custom_call_target="tpu_custom_call" | custom-call | tf_op jit(solution)/shard_map/ffn_backward/pallas_call | solution.py:767
  452.7 18.7 %attention_back.2.refs_0_ = bf16[3,1024,192]{2,1,0:T(8,128)(2,1)} custom-call(bf16[3,1024,192]{2,1,0:T(8,128)(2,1)} %get-tuple-element.103.projected, bf16[1024,192]{1,0:T(8,128)(2,1)} %get-tuple-element.118.grad_mixed, s32[1024,1]{1,0:T(8,128)} %copy.51.key_seg, s32[1,1024]{1,0:T(1,128)} %query_seg.7), custom_call_target="tpu_custom_call" | custom-call | tf_op jit(solution)/shard_map/attention_back/pallas_call | solution.py:1140
  471.5 28.8 %norm_backward.2 = (f32[512,768]{1,0:T(8,128)}, bf16[1024,768]{1,0:T(8,128)(2,1)}, bf16[3,768,192]{2,1,0:T(8,128)(2,1)}, f32[1,768]{1,0:T(1,128)}) custom-call(bf16[3,1024,192]{2,1,0:T(8,128)(2,1)} %attention_back.2.refs_0_, bf16[3,768,192]{2,1,0:T(8,128)(2,1)} %bitcast.73, bf16[1024,768]{1,0:T(8,128)(2,1)} %get-tuple-element.101.normed.refs_2_, ...), custom_call_target="tpu_custom_call" | custom-call | tf_op jit(solution)/shard_map/norm_backward/pallas_call | solution.py:849
  500.3 33.1 %ffn_backward.3 = (f32[512,768]{1,0:T(8,128)}, bf16[1024,768]{1,0:T(8,128)(2,1)}, bf16[1024,192]{1,0:T(8,128)(2,1)}, bf16[768,768]{1,0:T(8,128)(2,1)}, bf16[768,...) custom-call(f32[512,768]{1,0:T(8,128)} %get-tuple-element.120.grad, ...), custom_call_target="tpu_custom_call" | custom-call | tf_op jit(solution)/shard_map/ffn_backward/pallas_call | solution.py:767
  533.4 18.3 %attention_back.3.refs_0_ = bf16[3,1024,192]{2,1,0:T(8,128)(2,1)} custom-call(bf16[3,1024,192]{2,1,0:T(8,128)(2,1)} %get-tuple-element.95.projected, bf16[1024,192]{1,0:T(8,128)(2,1)} %get-tuple-element.126.grad_mixed, s32[1024,1]{1,0:T(8,128)} %copy.51.key_seg, s32[1,1024]{1,0:T(1,128)} %query_seg.7), custom_call_target="tpu_custom_call" | custom-call | tf_op jit(solution)/shard_map/attention_back/pallas_call | solution.py:1140
  551.8 29.0 %norm_backward.3 = (f32[512,768]{1,0:T(8,128)}, bf16[1024,768]{1,0:T(8,128)(2,1)}, bf16[3,768,192]{2,1,0:T(8,128)(2,1)}, f32[1,768]{1,0:T(1,128)}) custom-call(bf16[3,1024,192]{2,1,0:T(8,128)(2,1)} %attention_back.3.refs_0_, bf16[3,768,192]{2,1,0:T(8,128)(2,1)} %bitcast.71, bf16[1024,768]{1,0:T(8,128)(2,1)} %get-tuple-element.93.normed.refs_2_, ...), custom_call_target="tpu_custom_call" | custom-call | tf_op jit(solution)/shard_map/norm_backward/pallas_call | solution.py:849
  580.9 6.9 fusion.4
  588.6 176.1 %scatter_grads.1 = (f32[3,96,192]{2,1,0:T(8,128)}, f32[96,192]{1,0:T(8,128)}, f32[96,768]{1,0:T(8,128)}, f32[96,768]{1,0:T(8,128)}, f32[3,96,192]{2,1,0:T(8,128)...) custom-call(bf16[3,8,96,192]{3,2,1,0:T(8,128)(2,1)} %bitcast.91, ...), custom_call_target="tpu_custom_call" | custom-call | tf_op jit(solution)/shard_map/scatter_grads/pallas_call | solution.py:1021
  764.7 1.9 multiply_reduce_fusion.3
  766.6 1.6 multiply_reduce_fusion.4
  769.5 1.8 multiply_reduce_fusion.2
  772.0 1.8 multiply_reduce_fusion.1
  774.5 1.0 multiply_reduce_fusion
  778.0 14.0 %sum_scalars.1 = f32[8,128]{1,0:T(8,128)} custom-call(f32[8,128]{1,0:T(8,128)} %broadcast_select_fusion.given), custom_call_target="tpu_custom_call" | custom-call | tf_op jit(solution)/shard_map/sum_scalars/pallas_call | solution.py:1443
  792.0 1.3 fusion.26
  794.2 3.2 fusion.24
  797.5 0.9 fusion.22
  798.9 1.6 fusion.20
  801.2 1.6 fusion.18
  803.2 0.6 copy-done.9
  803.9 3.3 fusion.16
  (97 shorter events, 5.0 us)
Async XLA Ops:
  5.9 1.3 copy-start.28
  5.9 1.3 copy-start.26
  5.9 3.1 copy-start
  9.1 1.3 copy-start.3
  9.1 2.2 copy-start.15
  10.3 1.5 copy-start.4
  10.3 1.5 copy-start.6
  200.9 29.9 %copy-start.25 = (s32[1,1024]{1,0:T(1,128)S(1)}, s32[1,1024]{1,0:T(1,128)}, u32[]{:S(2)}) copy-start(s32[1,1024]{1,0:T(1,128)} %query_seg.7) | copy-start | bytes 12292
  309.2 47.0 %copy-start.27 = (s32[1,1024]{1,0:T(1,128)S(1)}, s32[1,1024]{1,0:T(1,128)}, u32[]{:S(2)}) copy-start(s32[1,1024]{1,0:T(1,128)} %param.23) | copy-start | bytes 12292
  309.2 47.0 %copy-start.33 = (s32[1,1024]{1,0:T(1,128)S(1)}, s32[1,1024]{1,0:T(1,128)}, u32[]{:S(2)}) copy-start(s32[1,1024]{1,0:T(1,128)} %param.24) | copy-start | bytes 12292
  309.2 47.1 %copy-start.30 = (s32[1,1024]{1,0:T(1,128)S(1)}, s32[1,1024]{1,0:T(1,128)}, u32[]{:S(2)}) copy-start(s32[1,1024]{1,0:T(1,128)} %param.25) | copy-start | bytes 12292
  580.8 7.0 copy-start.34
  580.8 7.0 copy-start.35
  580.8 6.9 copy-start.36
  580.9 6.9 copy-start.37
  580.9 6.9 copy-start.38
  764.6 9.8 %copy-start.1 = (f32[96,2048]{1,0:T(8,128)S(1)}, f32[96,2048]{1,0:T(8,128)}, u32[]{:S(2)}) copy-start(f32[96,2048]{1,0:T(8,128)} %get-tuple-element.152) | copy-start | bytes 2359300
  764.6 9.8 %copy-start.2 = (f32[96,2048]{1,0:T(8,128)S(1)}, f32[96,2048]{1,0:T(8,128)}, u32[]{:S(2)}) copy-start(f32[96,2048]{1,0:T(8,128)} %get-tuple-element.151) | copy-start | bytes 2359300
  766.6 9.5 %copy-start.29 = (f32[8,128]{1,0:T(8,128)S(1)}, f32[8,128]{1,0:T(8,128)}, u32[]{:S(2)}) copy-start(f32[8,128]{1,0:T(8,128)} %get-tuple-element.153) | copy-start | bytes 12292
  766.6 27.5 %copy-start.14 = (f32[3,96,192]{2,1,0:T(8,128)S(1)}, f32[3,96,192]{2,1,0:T(8,128)}, u32[]{:S(2)}) copy-start(f32[3,96,192]{2,1,0:T(8,128)} %get-tuple-element.143) | copy-start | bytes 663556
  794.1 3.3 copy-start.16
  794.1 3.3 copy-start.21
  794.1 3.3 copy-start.22
  794.1 3.3 copy-start.23
  794.1 3.3 copy-start.24
  794.1 4.3 copy-start.17
  794.2 4.3 copy-start.18
  797.4 1.1 copy-start.5
  797.4 1.4 copy-start.12
  797.4 1.5 copy-start.13
  798.9 1.6 copy-start.7
  798.9 1.6 copy-start.10
  798.9 1.6 copy-start.11
  798.9 2.1 copy-start.19
  798.9 2.3 copy-start.20
  801.2 2.0 copy-start.8
  801.2 2.6 copy-start.9
  803.9 3.3 copy-start.31
  803.9 3.3 copy-start.32

commit v3 on v2

--- a/solution.py
+++ b/solution.py
@@ -530,6 +530,214 @@
             self.piece(j).wait_send()
 
 
+class Carry:
+    def __init__(self, loads):
+        self.loads = loads
+        self.pieces = [(load, piece) for load in loads for piece in range(load.pieces)]
+        self.relayed = 0
+
+    def peers(self):
+        ways = []
+        for load in self.loads:
+            ways += [way for way in load.ways if way not in ways]
+        me, slow, fast, slows = wide_places(self.loads[0].count) if self.loads else (0, 0, 0, 0)
+        found = []
+        if "slow" in ways:
+            found += [{"wide": 2 * lax.rem(slow + step, slows) + fast} for step in range(1, slows)]
+        if "fast" in ways:
+            found.append({"wide": me + 1 - 2 * fast})
+        return found
+
+    def start(self):
+        for load in self.loads:
+            load.start()
+
+    def relay(self, part):
+        until = int(part * len(self.pieces) + 0.5)
+        for load, piece in self.pieces[self.relayed : until]:
+            load.relay(piece)
+        self.relayed = max(self.relayed, until)
+
+    def finish(self):
+        self.relay(1.0)
+        for load in self.loads:
+            load.finish()
+
+
+class GatherLoad:
+    ways = ("slow", "fast")
+
+    def __init__(self, weights, index, lead, count, pieces=1):
+        self.index, self.lead, self.count, self.pieces = index, lead, count, pieces
+        shape, slows = weights.shape[1:], count // 2
+        self.rows = shape[-2] // pieces
+        self.operands, self.in_specs = [weights], [whole_vmem()]
+        self.outs = [jax.ShapeDtypeStruct(shape[:lead] + (count,) + shape[lead:], BF16)]
+        self.out_specs = [pl.BlockSpec(memory_space=pl.ANY)]
+        self.scratch = [pltpu.VMEM(shape, BF16), pltpu.SemaphoreType.DMA] + [
+            pltpu.SemaphoreType.DMA((pieces, slows))
+        ] * 4
+
+    def bind(self, given, out, scratch):
+        self.shard, self.out = given[0], out[0]
+        self.low, self.local, self.slow_send, self.slow_recv, self.fast_send, self.fast_recv = scratch
+        self.me, self.slow, self.fast, self.slows = wide_places(self.count)
+
+    def cut(self, ref, piece):
+        if self.pieces == 1:
+            return ref
+        return ref.at[(slice(None),) * (len(ref.shape) - 2) + (pl.ds(piece * self.rows, self.rows),)]
+
+    def at(self, owner):
+        return self.out.at[(slice(None),) * self.lead + (owner,)]
+
+    def slow_copy(self, piece, step):
+        return remote(
+            self.cut(self.low, piece), self.cut(self.at(self.me), piece),
+            self.slow_send.at[piece, step], self.slow_recv.at[piece, step],
+            {"wide": 2 * lax.rem(self.slow + step, self.slows) + self.fast},
+        )
+
+    def fast_copy(self, piece, step):
+        block = self.cut(self.at(2 * lax.rem(self.slow + self.slows - step, self.slows) + self.fast), piece)
+        return remote(
+            self.cut(self.low, piece) if step == 0 else block, block,
+            self.fast_send.at[piece, step], self.fast_recv.at[piece, step],
+            {"wide": self.me + 1 - 2 * self.fast},
+        )
+
+    def own_copy(self):
+        return pltpu.make_async_copy(self.low, self.at(self.me), self.local)
+
+    def start(self):
+        self.low[...] = self.shard[self.index].astype(BF16)
+        for piece in range(self.pieces):
+            for step in range(1, self.slows):
+                self.slow_copy(piece, step).start()
+            self.fast_copy(piece, 0).start()
+        self.own_copy().start()
+
+    def relay(self, piece):
+        for step in range(1, self.slows):
+            self.slow_copy(piece, step).wait_recv()
+            self.fast_copy(piece, step).start()
+
+    def finish(self):
+        for piece in range(self.pieces):
+            for step in range(self.slows):
+                self.fast_copy(piece, step).wait()
+                if step:
+                    self.slow_copy(piece, step).wait_send()
+        self.own_copy().wait()
+
+
+class PairLoad:
+    ways = ("fast",)
+    pieces = 0
+
+    def __init__(self, full, lead, count):
+        self.lead, self.count = lead, count
+        shape, slows = full.shape[:lead] + full.shape[lead + 1 :], count // 2
+        self.operands, self.in_specs = [full], [whole_vmem()]
+        self.outs, self.out_specs = [jax.ShapeDtypeStruct((slows,) + shape, BF16)], [whole_vmem()]
+        self.scratch = [pltpu.VMEM((slows,) + shape, BF16)] + [pltpu.SemaphoreType.DMA((slows,))] * 2
+
+    def bind(self, given, out, scratch):
+        self.full, self.out = given[0], out[0]
+        self.came, self.send, self.recv = scratch
+        self.me, self.slow, self.fast, self.slows = wide_places(self.count)
+
+    def block(self, step, fast):
+        owner = 2 * lax.rem(self.slow + step, self.slows) + fast
+        return self.full.at[(slice(None),) * self.lead + (owner,)]
+
+    def copy(self, step):
+        return remote(
+            self.block(step, 1 - self.fast), self.came.at[step], self.send.at[step], self.recv.at[step],
+            {"wide": self.me + 1 - 2 * self.fast},
+        )
+
+    def start(self):
+        for step in range(self.slows):
+            self.copy(step).start()
+
+    def finish(self):
+        for step in range(self.slows):
+            self.copy(step).wait()
+            total = self.block(step, self.fast)[...].astype(F32) + self.came[step].astype(F32)
+            self.out[step] = total.astype(BF16)
+
+
+class LineLoad:
+    ways = ("slow",)
+    pieces = 0
+
+    def __init__(self, sums, count):
+        self.count = count
+        slows = count // 2
+        self.operands, self.in_specs = [sums], [whole_vmem()]
+        self.outs, self.out_specs = [jax.ShapeDtypeStruct(sums.shape[1:], F32)], [whole_vmem()]
+        self.scratch = [pltpu.VMEM(sums.shape, BF16)] + [pltpu.SemaphoreType.DMA((slows,))] * 2
+
+    def bind(self, given, out, scratch):
+        self.sums, self.out = given[0], out[0]
+        self.came, self.send, self.recv = scratch
+        self.me, self.slow, self.fast, self.slows = wide_places(self.count)
+
+    def copy(self, step):
+        return remote(
+            self.sums.at[step], self.came.at[step], self.send.at[step], self.recv.at[step],
+            {"wide": 2 * lax.rem(self.slow + step, self.slows) + self.fast},
+        )
+
+    def start(self):
+        for step in range(1, self.slows):
+            self.copy(step).start()
+
+    def finish(self):
+        total = self.sums[0].astype(F32)
+        for step in range(1, self.slows):
+            self.copy(step).wait()
+            total = total + self.came[step].astype(F32)
+        self.out[...] = total
+
+
+def run(body, name, operands, outs, scratch, collective_id=None, loads=()):
+    counts = [len(operands)] + [len(load.operands) for load in loads]
+    counts += [len(outs)] + [len(load.outs) for load in loads]
+    counts += [len(scratch)] + [len(load.scratch) for load in loads]
+    parts = 1 + len(loads)
+
+    def kernel(*refs):
+        groups, place = [], 0
+        for count in counts:
+            groups.append(refs[place : place + count])
+            place += count
+        for k, load in enumerate(loads, 1):
+            load.bind(groups[k], groups[parts + k], groups[2 * parts + k])
+        main = groups[0] + groups[parts] + groups[2 * parts]
+        body(*main, carry=Carry(list(loads)))
+
+    results = pl.pallas_call(
+        kernel,
+        out_shape=tuple(outs) + tuple(out for load in loads for out in load.outs),
+        in_specs=[whole_vmem()] * len(operands) + [spec for load in loads for spec in load.in_specs],
+        out_specs=(whole_vmem(),) * len(outs) + tuple(spec for load in loads for spec in load.out_specs),
+        scratch_shapes=list(scratch) + [s for load in loads for s in load.scratch],
+        compiler_params=pltpu.CompilerParams(
+            collective_id=collective_id,
+            has_side_effects=collective_id is not None,
+            vmem_limit_bytes=VMEM_LIMIT,
+        ),
+        name=name,
+    )(*operands, *[operand for load in loads for operand in load.operands])
+    return results[: len(outs)], results[len(outs) :]
+
+
+def sems(kinds):
+    return [pltpu.SemaphoreType.DMA((kinds, CHUNKS)), pltpu.SemaphoreType.DMA((kinds, CHUNKS))]
+
+
 def norm_of(value, gain):
     scale = lax.rsqrt(jnp.mean(value * value, axis=-1, keepdims=True) + NORM_EPS)
     return value * scale * gain
@@ -615,12 +823,13 @@
 def ffn_kernel(
     mixed, resid, w_out, w_in, w_red, gain, gain_next,
     middle, normed, before, after, result, normed_next,
-    near_out, near_in, far_out, far_in, near_out2, near_in2, far_out2, far_in2, own2, send, recv,
+    near_out, near_in, far_out, far_in, near_out2, near_in2, far_out2, far_in2, own2, send, recv, carry,
 ):
     seq_len = normed.shape[0]
     chunk = seq_len // 2 // CHUNKS
     sibling, partner, mine, other = group_places(seq_len)
-    greet([sibling, partner])
+    greet([sibling, partner] + carry.peers())
+    carry.start()
     sems = (send, recv)
     first = Exchange((near_out, near_in, far_out, far_in), sems, 0, sibling, partner)
     second = Exchange((near_out2, near_in2, far_out2, far_in2), sems, 2, sibling, partner)
@@ -653,44 +862,43 @@
         if j >= 1:
             second.pass_on(j - 1, own2[j - 1])
     second.pass_on(CHUNKS - 1, own2[CHUNKS - 1])
+    carry.relay(0.5)
     for j in range(CHUNKS):
         rows = rows_at(0, j, chunk)
         x = middle[rows, :] + second.take(j)
         result[rows, :] = x
         share_next.put(j, norm_of(x, gain_next[...]).astype(BF16))
+        if j == CHUNKS - 2:
+            carry.relay(0.75)
     for j in range(CHUNKS):
         share_next.arrived(j)
     for part in (first, second, share, share_next):
         part.close()
-
-
-def ffn_forward(mixed, resid, w_out, w_in, w_red, gain, gain_next, collective_id):
+    carry.finish()
+
+
+def ffn_forward(mixed, resid, w_out, w_in, w_red, gain, gain_next, collective_id, loads):
     seq_len, width, hidden = mixed.shape[0], w_in.shape[0], w_in.shape[1]
     half, chunk = seq_len // 2, seq_len // 2 // CHUNKS
-    return pl.pallas_call(
+    return run(
         ffn_kernel,
-        out_shape=(
+        "ffn_forward",
+        [mixed, resid, w_out, w_in, w_red, gain, gain_next],
+        [
             jax.ShapeDtypeStruct((half, width), F32),
             jax.ShapeDtypeStruct((seq_len, width), BF16),
             jax.ShapeDtypeStruct((seq_len, hidden), F32),
             jax.ShapeDtypeStruct((seq_len, hidden), BF16),
             jax.ShapeDtypeStruct((half, width), F32),
             jax.ShapeDtypeStruct((seq_len, width), BF16),
-        ),
-        in_specs=[whole_vmem()] * 7,
-        out_specs=(whole_vmem(),) * 6,
-        scratch_shapes=Exchange.scratch(chunk, width, FORWARD_KIND)
+        ],
+        Exchange.scratch(chunk, width, FORWARD_KIND)
         + Exchange.scratch(chunk, width, FORWARD_KIND)
-        + [
-            pltpu.VMEM((CHUNKS, chunk, width), F32),
-            pltpu.SemaphoreType.DMA((6, CHUNKS)),
-            pltpu.SemaphoreType.DMA((6, CHUNKS)),
-        ],
-        compiler_params=pltpu.CompilerParams(
-            collective_id=collective_id, has_side_effects=True, vmem_limit_bytes=VMEM_LIMIT
-        ),
-        name="ffn_forward",
-    )(mixed, resid, w_out, w_in, w_red, gain, gain_next)
+        + [pltpu.VMEM((CHUNKS, chunk, width), F32)]
+        + sems(6),
+        collective_id,
+        loads,
+    )
 
 
 TILE = 256
@@ -714,12 +922,13 @@
 def ffn_back_kernel(
     grad, branch, w_red, w_in, w_out, before, after, normed, middle, gain, mixed,
     grad_middle, grad_attn, grad_mixed, d_red, d_in, d_out, d_gain,
-    grad_before, turned, near_out, near_in, far_out, far_in, send, recv,
+    grad_before, turned, near_out, near_in, far_out, far_in, send, recv, carry,
 ):
     seq_len = normed.shape[0]
     chunk = seq_len // 2 // CHUNKS
     sibling, partner, mine, other = group_places(seq_len)
-    greet([sibling, partner])
+    greet([sibling, partner] + carry.peers())
+    carry.start()
     sems = (send, recv)
     trade = Exchange((near_out, near_in, far_out, far_in), sems, 0, sibling, partner)
     share = Share(grad_attn, sems, 2, sibling, mine, chunk)
@@ -759,14 +968,17 @@
     weight_grad(turned, mixed, d_out)
     trade.close()
     share.close()
-
-
-def ffn_backward(grad, branch, w_red, w_in, w_out, before, after, normed, middle, gain, mixed, collective_id):
+    carry.finish()
+
+
+def ffn_backward(grad, branch, w_red, w_in, w_out, before, after, normed, middle, gain, mixed, collective_id, loads):
     seq_len, width = normed.shape
     half, chunk = seq_len // 2, seq_len // 2 // CHUNKS
-    return pl.pallas_call(
+    return run(
         ffn_back_kernel,
-        out_shape=(
+        "ffn_backward",
+        [grad, branch, w_red, w_in, w_out, before, after, normed, middle, gain, mixed],
+        [
             jax.ShapeDtypeStruct((half, width), F32),
             jax.ShapeDtypeStruct((seq_len, width), BF16),
             jax.ShapeDtypeStruct(mixed.shape, BF16),
@@ -774,31 +986,25 @@
             jax.ShapeDtypeStruct(w_in.shape, BF16),
             jax.ShapeDtypeStruct(w_out.shape, BF16),
             jax.ShapeDtypeStruct(gain.shape, F32),
-        ),
-        in_specs=[whole_vmem()] * 11,
-        out_specs=(whole_vmem(),) * 7,
-        scratch_shapes=[
-            pltpu.VMEM(before.shape, BF16),
-            pltpu.VMEM((width, seq_len), BF16),
-        ]
+        ],
+        [pltpu.VMEM(before.shape, BF16), pltpu.VMEM((width, seq_len), BF16)]
         + Exchange.scratch(chunk, width, BACKWARD_KIND)
-        + [pltpu.SemaphoreType.DMA((3, CHUNKS)), pltpu.SemaphoreType.DMA((3, CHUNKS))],
-        compiler_params=pltpu.CompilerParams(
-            collective_id=collective_id, has_side_effects=True, vmem_limit_bytes=VMEM_LIMIT
-        ),
-        name="ffn_backward",
-    )(grad, branch, w_red, w_in, w_out, before, after, normed, middle, gain, mixed)
+        + sems(3),
+        collective_id,
+        loads,
+    )
 
 
 def norm_back_kernel(
     scale, grads, weights, normed, value, gain, upstream,
     grad_out, branch, d_weights, d_gain,
-    turned, near_out, near_in, far_out, far_in, send, recv,
+    turned, near_out, near_in, far_out, far_in, send, recv, carry,
 ):
     seq_len, width = normed.shape
     chunk = seq_len // 2 // CHUNKS
     sibling, partner, mine, other = group_places(seq_len)
-    greet([sibling, partner])
+    greet([sibling, partner] + carry.peers())
+    carry.start()
     sems = (send, recv)
     trade = Exchange((near_out, near_in, far_out, far_in), sems, 0, sibling, partner)
     share = Share(branch, sems, 2, sibling, mine, chunk)
@@ -824,8 +1030,7 @@
         rows = rows_at(0, j, chunk)
         back, gain_part = norm_back(trade.take(j), value[rows, :], gain[...])
         gain_total = gain_total + gain_part
-        if upstream is not None:
-            back = back + upstream[rows, :]
+        back = back + upstream[rows, :]
         grad_out[rows, :] = back
         share.put(j, (back if scale is None else scale * back).astype(BF16))
     d_gain[...] = gain_total
@@ -833,37 +1038,26 @@
         share.arrived(j)
     trade.close()
     share.close()
-
-
-def norm_backward(grads, weights, normed, value, gain, upstream, scale, collective_id):
+    carry.finish()
+
+
+def norm_backward(grads, weights, normed, value, gain, upstream, scale, collective_id, loads):
     seq_len, width = normed.shape
     half, chunk = seq_len // 2, seq_len // 2 // CHUNKS
-    operands = [grads, weights, normed, value, gain] + ([] if upstream is None else [upstream])
-
-    def kernel(*refs):
-        given, rest = list(refs[: len(operands)]), refs[len(operands) :]
-        if upstream is None:
-            given.append(None)
-        norm_back_kernel(scale, *given, *rest)
-
-    return pl.pallas_call(
-        kernel,
-        out_shape=(
+    return run(
+        functools.partial(norm_back_kernel, scale),
+        "norm_backward",
+        [grads, weights, normed, value, gain, upstream],
+        [
             jax.ShapeDtypeStruct((half, width), F32),
             jax.ShapeDtypeStruct((seq_len, width), BF16),
             jax.ShapeDtypeStruct(weights.shape, BF16),
             jax.ShapeDtypeStruct(gain.shape, F32),
-        ),
-        in_specs=[whole_vmem()] * len(operands),
-        out_specs=(whole_vmem(),) * 4,
-        scratch_shapes=[pltpu.VMEM((width, seq_len), BF16)]
-        + Exchange.scratch(chunk, width, BACKWARD_KIND)
-        + [pltpu.SemaphoreType.DMA((3, CHUNKS)), pltpu.SemaphoreType.DMA((3, CHUNKS))],
-        compiler_params=pltpu.CompilerParams(
-            collective_id=collective_id, has_side_effects=True, vmem_limit_bytes=VMEM_LIMIT
-        ),
-        name="norm_backward",
-    )(*operands)
+        ],
+        [pltpu.VMEM((width, seq_len), BF16)] + Exchange.scratch(chunk, width, BACKWARD_KIND) + sems(3),
+        collective_id,
+        loads,
+    )
 
 
 def wide_places(count):
@@ -949,7 +1143,7 @@
     )(*shards)
 
 
-def scatter_kernel(arrays, lead, *refs):
+def scatter_kernel(arrays, lead, *refs, carry):
     fulls, outs = refs[:arrays], refs[arrays : 2 * arrays]
     fast_in = refs[2 * arrays : 3 * arrays]
     sums = refs[3 * arrays : 4 * arrays]
@@ -983,6 +1177,7 @@
         )
 
     greet([{"wide": 2 * along(step) + fast} for step in range(1, slows)] + [{"wide": beside}, sibling])
+    carry.start()
     near = remote(fulls[-1], paired_in, near_send, near_recv, sibling)
     near.start()
     for which in range(arrays):
@@ -1010,20 +1205,20 @@
             fast_copy(which, step).wait_send()
             if step:
                 slow_copy(which, step).wait_send()
-
-
-def scatter_wide(fulls, leads, collective_id):
+    carry.finish()
+
+
+def scatter_wide(fulls, leads, collective_id, loads):
     arrays = len(fulls)
-    count = fulls[0].shape[leads[0]]
-    slows = count // 2
+    slows = fulls[0].shape[leads[0]] // 2
     shapes = [f.shape[:lead] + f.shape[lead + 1 :] for f, lead in zip(fulls, leads)]
     kinds = [f.dtype for f in fulls]
-    return pl.pallas_call(
+    return run(
         functools.partial(scatter_kernel, arrays, leads),
-        out_shape=tuple(jax.ShapeDtypeStruct(shape, F32) for shape in shapes),
-        in_specs=[whole_vmem()] * arrays,
-        out_specs=(whole_vmem(),) * arrays,
-        scratch_shapes=[pltpu.VMEM((slows,) + shape, kind) for shape, kind in zip(shapes, kinds)]
+        "scatter_grads",
+        fulls,
+        [jax.ShapeDtypeStruct(shape, F32) for shape in shapes],
+        [pltpu.VMEM((slows,) + shape, kind) for shape, kind in zip(shapes, kinds)]
         + [pltpu.VMEM((slows - 1,) + shape, kind) for shape, kind in zip(shapes, kinds)]
         + [pltpu.VMEM((slows - 1,) + shape, kind) for shape, kind in zip(shapes, kinds)]
         + [pltpu.VMEM(fulls[-1].shape, F32)] * 2
@@ -1035,11 +1230,9 @@
             pltpu.SemaphoreType.DMA,
             pltpu.SemaphoreType.DMA,
         ],
-        compiler_params=pltpu.CompilerParams(
-            collective_id=collective_id, has_side_effects=True, vmem_limit_bytes=VMEM_LIMIT
-        ),
-        name="scatter_grads",
-    )(*fulls)
+        collective_id,
+        loads,
+    )
 
 
 def head_lanes(value, head, size):
@@ -1099,11 +1292,14 @@
     )(normed, weights, key_seg, query_seg)
 
 
-def attention_back_kernel(projected, grad_mixed, key_seg, query_seg, out, bias, keys_t, grad_keys, grad_values):
+def attention_back_kernel(projected, grad_mixed, key_seg, query_seg, out, bias, keys_t, grad_keys, grad_values, carry):
     seq_len, width = grad_mixed.shape
     block = bias.shape[1]
     heads = width // HD
     scale = HD ** (-0.5)
+    if carry.loads:
+        greet(carry.peers())
+    carry.start()
     keys_t[...] = jnp.transpose(projected[1])
     grad_keys[...] = jnp.zeros(grad_keys.shape, F32)
     grad_values[...] = jnp.zeros(grad_values.shape, F32)
@@ -1132,25 +1328,26 @@
     lax.fori_loop(0, seq_len // block, queries, 0)
     out[1] = grad_keys[...].astype(BF16)
     out[2] = grad_values[...].astype(BF16)
-
-
-def attention_back(projected, grad_mixed, key_seg, query_seg):
+    carry.finish()
+
+
+def attention_back(projected, grad_mixed, key_seg, query_seg, collective_id, loads):
     seq_len, width = grad_mixed.shape
     block = min(QUERY_BLOCK, seq_len)
-    return pl.pallas_call(
+    return run(
         attention_back_kernel,
-        out_shape=jax.ShapeDtypeStruct(projected.shape, BF16),
-        in_specs=[whole_vmem()] * 4,
-        out_specs=whole_vmem(),
-        scratch_shapes=[
+        "attention_back",
+        [projected, grad_mixed, key_seg, query_seg],
+        [jax.ShapeDtypeStruct(projected.shape, BF16)],
+        [
             pltpu.VMEM((seq_len, block), F32),
             pltpu.VMEM((width, seq_len), BF16),
             pltpu.VMEM((seq_len, width), F32),
             pltpu.VMEM((seq_len, width), F32),
         ],
-        compiler_params=pltpu.CompilerParams(vmem_limit_bytes=VMEM_LIMIT),
-        name="attention_back",
-    )(projected, grad_mixed, key_seg, query_seg)
+        collective_id if loads else None,
+        loads,
+    )
 
 
 LANES = 128
@@ -1517,26 +1714,17 @@
         ),
         ((0, -(gain_rows + 1) % 8), (0, -gain_cols % 128)),
     )
-    shards, leads, kinds = [small, tables[0]], [0, 0], [F32, BF16]
-    for layer in range(layers):
-        shards += [attn_in[layer], attn_out[layer], ffn_in[layer], ffn_out[layer]]
-        leads += [1, 0, 0, 0]
-        kinds += [BF16] * 4
-    shards.append(tables[1])
-    leads.append(0)
-    kinds.append(BF16)
-    small_all, *weights = gather_wide(shards, leads, kinds, wide, 0)
+    first_layer = [attn_in[0], attn_out[0], ffn_in[0], ffn_out[0]]
+    leads = (1, 0, 0, 0)
+    small_all, table_first, *weights = gather_wide(
+        [small, tables[0]] + first_layer, (0, 0) + leads, [F32] + [BF16] * 5, wide, 0
+    )
     token_total = jnp.sum(small_all[:, gain_rows, 0])
     gain_w = small_all[:, :gain_rows, :gain_cols].transpose(1, 0, 2).reshape(gain_rows, 1, -1)
-    table_first = weights[0].reshape(-1, tables.shape[2])
-    table_last = weights[-1].reshape(-1, tables.shape[2])
-    query_w, output_w, expand_w, reduce_w = [], [], [], []
-    for layer in range(layers):
-        four = weights[1 + 4 * layer : 5 + 4 * layer]
-        query_w.append(four[0].reshape(four[0].shape[0], -1, four[0].shape[-1]))
-        output_w.append(four[1].reshape(-1, four[1].shape[-1]))
-        expand_w.append(four[2].reshape(-1, four[2].shape[-1]))
-        reduce_w.append(four[3].reshape(-1, four[3].shape[-1]))
+    table_first = table_first.reshape(-1, tables.shape[2])
+
+    def joined(value, lead):
+        return value.reshape(value.shape[:lead] + (-1,) + value.shape[lead + 2 :])
 
     noised_flat = noised.reshape(-1)
     clean_flat = clean.reshape(-1)
@@ -1548,13 +1736,22 @@
     key_seg, query_seg = segments.reshape(-1, 1), segments.reshape(1, -1)
     kept = []
     for layer in range(layers):
-        projected, mixed = attention(normed, query_w[layer], key_seg, query_seg)
-        middle, normed_two, before, after, result, normed_next = ffn_forward(
-            mixed, residual, output_w[layer], expand_w[layer], reduce_w[layer],
-            gain_w[2 * layer + 1], gain_w[2 * layer + 2], 2 + layer,
+        query_w, output_w, expand_w, reduce_w = four = [joined(value, lead) for value, lead in zip(weights, leads)]
+        if layer + 1 < layers:
+            loads = [
+                GatherLoad(value, layer + 1, lead, wide)
+                for value, lead in zip((attn_in, attn_out, ffn_in, ffn_out), leads)
+            ]
+        else:
+            loads = [GatherLoad(tables, 1, 0, wide, 3)]
+        projected, mixed = attention(normed, query_w, key_seg, query_seg)
+        (middle, normed_two, before, after, result, normed_next), weights = ffn_forward(
+            mixed, residual, output_w, expand_w, reduce_w,
+            gain_w[2 * layer + 1], gain_w[2 * layer + 2], 2 + layer, loads,
         )
-        kept.append((residual, normed, projected, mixed, middle, normed_two, before, after))
+        kept.append((residual, normed, projected, mixed, middle, normed_two, before, after, four))
         residual, normed = result, normed_next
+    table_last = joined(weights[0], 0)
 
     info = jnp.stack(
         [noised_flat.astype(F32), clean_flat.astype(F32), step_flat.astype(F32), mask / token_total, mask]
@@ -1565,40 +1762,78 @@
     )
     next_id = 3 + layers
     gain_grads = [None] * (2 * layers) + [gain_final]
-    grads = [None] * (4 * layers)
+    own = {}
+
+    def by_owner(value, lead):
+        shape = value.shape
+        return value.reshape(shape[:lead] + (wide, shape[lead] // wide) + shape[lead + 1 :])
+
+    class Route:
+        waiting, halfway = [], []
+
+        def take(self, pairs, lines):
+            self.now = self.waiting[:pairs], self.halfway[:lines]
+            self.waiting, self.halfway = self.waiting[pairs:], self.halfway[lines:]
+            return [PairLoad(by_owner(value, lead), lead, wide) for _, value, lead in self.now[0]] + [
+                LineLoad(sums, wide) for _, sums in self.now[1]
+            ]
+
+        def back(self, results):
+            pairs, lines = self.now
+            self.halfway = self.halfway + [(key, sums) for (key, _, _), sums in zip(pairs, results)]
+            for (key, _), total in zip(lines, results[len(pairs) :]):
+                own[key] = total
+
+    route = Route()
+    route.waiting = [(("tables", 1), d_last, 0)]
     for layer in reversed(range(layers)):
-        residual, normed, projected, mixed, middle, normed_two, before, after = kept[layer]
-        grad_middle, grad_attn, grad_mixed, d_red, d_in, d_out, gain_two = ffn_backward(
-            grad, branch, reduce_w[layer], expand_w[layer], output_w[layer], before, after,
-            normed_two, middle, gain_w[2 * layer + 1], mixed, next_id,
+        residual, normed, projected, mixed, middle, normed_two, before, after, four = kept[layer]
+        query_w, output_w, expand_w, reduce_w = four
+        top = layer == layers - 1
+        loads = route.take(1, 3)
+        (grad_middle, grad_attn, grad_mixed, d_red, d_in, d_out, gain_two), carried = ffn_backward(
+            grad, branch, reduce_w, expand_w, output_w, before, after,
+            normed_two, middle, gain_w[2 * layer + 1], mixed, next_id, loads,
         )
-        grad_projected = attention_back(projected, grad_mixed, key_seg, query_seg)
-        grad, branch, d_query, gain_one = norm_backward(
-            grad_projected, query_w[layer], normed, residual, gain_w[2 * layer], grad_middle,
-            math.sqrt(D) if layer == 0 else None, next_id + 1,
+        route.back(carried)
+        route.waiting += [(("ffn_out", layer), d_red, 0), (("ffn_in", layer), d_in, 0)]
+        loads = route.take(1, 0 if top else 1)
+        (grad_projected,), carried = attention_back(projected, grad_mixed, key_seg, query_seg, next_id + 1, loads)
+        route.back(carried)
+        route.waiting += [(("attn_out", layer), d_out, 0)]
+        loads = route.take(3, 1)
+        (grad, branch, d_query, gain_one), carried = norm_backward(
+            grad_projected, query_w, normed, residual, gain_w[2 * layer], grad_middle,
+            math.sqrt(D) if layer == 0 else None, next_id + 2, loads,
         )
-        next_id += 2
+        route.back(carried)
+        route.waiting += [(("attn_in", layer), d_query, 1)]
+        next_id += 3
         gain_grads[2 * layer], gain_grads[2 * layer + 1] = gain_one, gain_two
-        grads[4 * layer : 4 * layer + 4] = [d_query, d_out, d_in, d_red]
     picks = (noised_flat[:, None] == vocab_ids[None, :]).astype(jnp.bfloat16)
     d_first = jnp.einsum("sd,sv->dv", branch, picks, preferred_element_type=jnp.float32)
-
-    def by_owner(value, lead):
-        shape = value.shape
-        return value.astype(jnp.bfloat16).reshape(shape[:lead] + (wide, shape[lead] // wide) + shape[lead + 1 :])
 
     small_grad = jnp.pad(
         jnp.concatenate(gain_grads).reshape(gain_rows, wide, gain_cols).transpose(1, 0, 2),
         ((0, 0), (0, -gain_rows % 8), (0, -gain_cols % 128)),
     )
-    fulls = [by_owner(value, lead) for value, lead in zip(grads, leads[2:])]
-    fulls += [by_owner(d_last, 0), by_owner(d_first, 0), small_grad]
-    own = scatter_wide(fulls, leads[2:] + [0, 0], next_id)
-    grad_attn_in, grad_attn_out, grad_ffn_in, grad_ffn_out = [
-        jnp.stack([own[4 * layer + which] for layer in range(layers)]) for which in range(4)
+    rest = route.waiting + [(("tables", 0), d_first.astype(BF16), 0)]
+    lines = route.halfway
+    (*sums, total_small), carried = scatter_wide(
+        [by_owner(value, lead) for _, value, lead in rest] + [small_grad],
+        [lead for _, _, lead in rest] + [0],
+        next_id,
+        [LineLoad(value, wide) for _, value in lines],
+    )
+    for (key, _, _), total in zip(rest, sums):
+        own[key] = total
+    for (key, _), total in zip(lines, carried):
+        own[key] = total
+    grad_attn_in, grad_attn_out, grad_ffn_in, grad_ffn_out, grad_tables = [
+        jnp.stack([own[name, index] for index in range(2)])
+        for name in ("attn_in", "attn_out", "ffn_in", "ffn_out", "tables")
     ]
-    grad_tables = jnp.stack([own[4 * layers + 1], own[4 * layers]])
-    grad_gains = own[-1][:gain_rows, :gain_cols]
+    grad_gains = total_small[:gain_rows, :gain_cols]
     narrow_first = (lax.axis_index("narrow") == 0).astype(jnp.float32)
     squares = (
         jnp.sum(grad_attn_in * grad_attn_in)

time: 818 us -> 709 us (0.87)
  Pallas kernels: 748 us -> 640 us
    pallas_call x1, Pallas kernels: 186 us -> 97.8 us  [gather_wide(): pl.pallas_call(functools.partial(gather_kernel, arrays, leads), out_shape...]
    pallas_call x9, Pallas kernels: 431 us -> 414 us  [run(): pl.pallas_call(kernel, out_shape=tuple(outs) + tuple((out for load in loa...]
where the time goes in v3:
time: 709 us; the launch traced here: 700 us
  Pallas kernels  640 us (90%)
  other arithmetic  29.2 us (4%)
  local copies, waits for them, and re-layouts  15.1 us (2%)
  between operations  7.94 us (1%)
    pallas_call x9, Pallas kernels, run(): pl.pallas_call(kernel, out_shape=tuple(outs) + tuple((out for load in loa...  414 us
    pallas_call x1, Pallas kernels, gather_wide(): pl.pallas_call(functools.partial(gather_kernel, arrays, leads), out_shape...  97.8 us
    pallas_call x1, Pallas kernels, loss_and_back(): pl.pallas_call(loss_kernel, out_shape=(jax.ShapeDtypeStruct((half, width)...  58.8 us
    pallas_call x1, Pallas kernels, embed(): pl.pallas_call(embed_kernel, out_shape=(jax.ShapeDtypeStruct((seq_len //...  30.1 us
    pallas_call x2, Pallas kernels, attention(): pl.pallas_call(attention_kernel, out_shape=(jax.ShapeDtypeStruct((3, seq_...  27.5 us

profile of v3, /device:TPU:0, one launch (start us, length us, event | category | flops | bytes accessed | tf_op | source)
XLA Modules:
  0.0 699.5 jit_solution(8063035335677809299)
XLA Ops:
  0.7 1.7 copy.50.ids
  2.4 0.7 dynamic-slice_convert_fusion
  3.1 2.8 multiply_sine_fusion
  5.9 1.3 pad_maximum_fusion.extra
  7.8 1.2 select_select_fusion.refs_0_
  9.1 0.9 slice_bitcast_fusion.refs_1_
  10.0 0.7 slice_bitcast_fusion.3.refs_2_
  10.8 0.6 slice_bitcast_fusion.4.refs_3_
  11.4 0.8 slice_bitcast_fusion.1
  12.3 97.8 %gather_weights.1 = (f32[8,8,128]{2,1,0:T(8,128)}, bf16[8,96,2048]{2,1,0:T(8,128)(2,1)}, bf16[3,8,96,192]{3,2,1,0:T(8,128)(2,1)}, bf16[8,96,192]{2,1,0:T(8,128)(...) custom-call(f32[8,128]{1,0:T(8,128)} %select_select_fusion.refs_0_, ...), custom_call_target="tpu_custom_call" | custom-call | tf_op jit(solution)/shard_map/gather_weights/pallas_call | solution.py:1123
  110.0 0.8 slice_bitcast_fusion.5
  110.9 0.7 squeeze.45.gain.refs_4_
  111.5 30.1 %embed.1 = (f32[512,768]{1,0:T(8,128)}, bf16[1024,768]{1,0:T(8,128)(2,1)}) custom-call(s32[1024,1]{1,0:T(8,128)} %copy.50.ids, f32[512,768]{1,0:T(8,128)} %pad_maximum_fusion.extra, bf16[768,2048]{1,0:T(8,128)(2,1)} %bitcast.71, f32[1,768]{1,0:T(1,128)} %squeeze.45.gain.refs_4_), custom_call_target="tpu_custom_call" | custom-call | tf_op jit(solution)/shard_map/embed/pallas_call | solution.py:806
  141.6 1.0 copy.51.key_seg.refs_2_
  142.6 13.5 %attention.2 = (bf16[3,1024,192]{2,1,0:T(8,128)(2,1)}, bf16[1024,192]{1,0:T(8,128)(2,1)}) custom-call(bf16[1024,768]{1,0:T(8,128)(2,1)} %get-tuple-element.103.normed.refs_2_, bf16[3,768,192]{2,1,0:T(8,128)(2,1)} %bitcast.62, s32[1024,1]{1,0:T(8,128)} %copy.51.key_seg.refs_2_, s32[1,1024]{1,0:T(1,128)} %refs_3_.3), custom_call_target="tpu_custom_call" | custom-call | tf_op jit(solution)/shard_map/attention/pallas_call | solution.py:1281
  156.2 0.7 squeeze.46.refs_5_.refs_9_
  156.8 0.7 squeeze.47.refs_6_.refs_4_
  157.5 74.5 %ffn_forward.2 = (f32[512,768]{1,0:T(8,128)}, bf16[1024,768]{1,0:T(8,128)(2,1)}, f32[1024,768]{1,0:T(8,128)}, bf16[1024,768]{1,0:T(8,128)(2,1)}, f32[512,768]{1,...) custom-call(bf16[1024,192]{1,0:T(8,128)(2,1)} %get-tuple-element.106, ...), custom_call_target="tpu_custom_call" | custom-call | tf_op jit(solution)/shard_map/ffn_forward/pallas_call | solution.py:721
  232.0 13.9 %attention.3 = (bf16[3,1024,192]{2,1,0:T(8,128)(2,1)}, bf16[1024,192]{1,0:T(8,128)(2,1)}) custom-call(bf16[1024,768]{1,0:T(8,128)(2,1)} %get-tuple-element.111.normed.refs_2_, bf16[3,768,192]{2,1,0:T(8,128)(2,1)} %bitcast.56, s32[1024,1]{1,0:T(8,128)} %copy.51.key_seg.refs_2_, s32[1,1024]{1,0:T(1,128)} %refs_3_.3), custom_call_target="tpu_custom_call" | custom-call | tf_op jit(solution)/shard_map/attention/pallas_call | solution.py:1281
  246.0 0.7 squeeze.48.refs_5_.refs_9_
  246.6 0.7 squeeze.49.refs_6_.gain
  247.3 63.6 %ffn_forward.3 = (f32[512,768]{1,0:T(8,128)}, bf16[1024,768]{1,0:T(8,128)(2,1)}, f32[1024,768]{1,0:T(8,128)}, bf16[1024,768]{1,0:T(8,128)(2,1)}, f32[512,768]{1,...) custom-call(bf16[1024,192]{1,0:T(8,128)(2,1)} %get-tuple-element.114.refs_0_.refs_10_, ...), custom_call_target="tpu_custom_call" | custom-call | tf_op jit(solution)/shard_map/ffn_forward/pallas_call | solution.py:721
  311.0 1.4 slice_reduce_fusion.5
  312.4 0.7 broadcast_divide_fusion
  313.1 0.7 stack.57.info
  313.7 58.8 %loss_and_back.1 = (f32[512,768]{1,0:T(8,128)}, bf16[1024,768]{1,0:T(8,128)(2,1)}, bf16[768,2048]{1,0:T(8,128)(2,1)}, f32[1,768]{1,0:T(1,128)}, f32[1,1024]{1,0:T(1,128)}) custom-call(bf16[1024,768]{1,0:T(8,128)(2,1)} %get-tuple-element.119.normed, bf16[768,2048]{1,0:T(8,128)(2,1)} %bitcast.69, f32[8,1024]{1,0:T(8,128)} %stack.57.info, ...), custom_call_target="tpu_custom_call" | custom-call | tf_op jit(solution)/shard_map/loss_and_back/pallas_call | solution.py:1566
  372.5 1.3 reduce_sum.89
  374.5 46.2 %ffn_backward.2 = (f32[512,768]{1,0:T(8,128)}, bf16[1024,768]{1,0:T(8,128)(2,1)}, bf16[1024,192]{1,0:T(8,128)(2,1)}, bf16[768,768]{1,0:T(8,128)(2,1)}, bf16[768,...) custom-call(f32[512,768]{1,0:T(8,128)} %get-tuple-element.122.refs_0_, ...), custom_call_target="tpu_custom_call" | custom-call | tf_op jit(solution)/shard_map/ffn_backward/pallas_call | solution.py:721
  420.7 21.0 %attention_back.2 = (bf16[3,1024,192]{2,1,0:T(8,128)(2,1)}, bf16[4,96,768]{2,1,0:T(8,128)(2,1)}) custom-call(bf16[3,1024,192]{2,1,0:T(8,128)(2,1)} %get-tuple-element.113.refs_0_, bf16[1024,192]{1,0:T(8,128)(2,1)} %get-tuple-element.129.refs_1_, s32[1024,1]{1,0:T(8,128)} %copy.51.key_seg.refs_2_, s32[1,1024]{1,0:T(1,128)} %refs_3_.3, ...), custom_call_target="tpu_custom_call" | custom-call | tf_op jit(solution)/shard_map/attention_back/pallas_call | solution.py:721
  441.7 36.4 %norm_backward.2 = (f32[512,768]{1,0:T(8,128)}, bf16[1024,768]{1,0:T(8,128)(2,1)}, bf16[3,768,192]{2,1,0:T(8,128)(2,1)}, f32[1,768]{1,0:T(1,128)}, bf16[4,96,768...) custom-call(bf16[3,1024,192]{2,1,0:T(8,128)(2,1)} %get-tuple-element.131.refs_0_, ...), custom_call_target="tpu_custom_call" | custom-call | tf_op jit(solution)/shard_map/norm_backward/pallas_call | solution.py:721
  478.1 47.3 %ffn_backward.3 = (f32[512,768]{1,0:T(8,128)}, bf16[1024,768]{1,0:T(8,128)(2,1)}, bf16[1024,192]{1,0:T(8,128)(2,1)}, bf16[768,768]{1,0:T(8,128)(2,1)}, bf16[768,...) custom-call(f32[512,768]{1,0:T(8,128)} %get-tuple-element.136.refs_0, ...), custom_call_target="tpu_custom_call" | custom-call | tf_op jit(solution)/shard_map/ffn_backward/pallas_call | solution.py:721
  525.5 22.9 %attention_back.3 = (bf16[3,1024,192]{2,1,0:T(8,128)(2,1)}, bf16[4,96,768]{2,1,0:T(8,128)(2,1)}, f32[3,96,192]{2,1,0:T(8,128)}) custom-call(bf16[3,1024,192]{2,1,0:T(8,128)(2,1)} %get-tuple-element.105.refs_0_, bf16[1024,192]{1,0:T(8,128)(2,1)} %get-tuple-element.146.refs_1_, s32[1024,1]{1,0:T(8,128)} %copy.51.key_seg.refs_2_, s32[1,1024]{1,0:T(1,128)} %refs_3_.3, ...), custom_call_target="tpu_custom_call" | custom-call | tf_op jit(solution)/shard_map/attention_back/pallas_call | solution.py:721
  548.3 30.3 %norm_backward.3 = (f32[512,768]{1,0:T(8,128)}, bf16[1024,768]{1,0:T(8,128)(2,1)}, bf16[3,768,192]{2,1,0:T(8,128)(2,1)}, f32[1,768]{1,0:T(1,128)}, bf16[4,96,768...) custom-call(bf16[3,1024,192]{2,1,0:T(8,128)(2,1)} %get-tuple-element.149.refs_0_, ...), custom_call_target="tpu_custom_call" | custom-call | tf_op jit(solution)/shard_map/norm_backward/pallas_call | solution.py:721
  578.7 6.9 fusion.4
  586.4 71.9 %scatter_grads.1 = (f32[3,96,192]{2,1,0:T(8,128)}, f32[96,2048]{1,0:T(8,128)}, f32[8,128]{1,0:T(8,128)}, f32[96,768]{1,0:T(8,128)}, f32[96,192]{1,0:T(8,128)}) custom-call(bf16[3,8,96,192]{3,2,1,0:T(8,128)(2,1)} %bitcast.90, bf16[8,96,2048]{2,1,0:T(8,128)(2,1)} %bitcast.70, f32[8,8,128]{2,1,0:T(8,128)} %pad.10.refs_2_, ...), custom_call_target="tpu_custom_call" | custom-call | tf_op jit(solution)/shard_map/scatter_grads/pallas_call | solution.py:721
  658.3 1.8 multiply_reduce_fusion.3
  660.2 1.6 multiply_reduce_fusion.4
  663.1 1.7 multiply_reduce_fusion.2
  665.5 0.8 multiply_reduce_fusion.1
  666.9 1.0 multiply_reduce_fusion
  670.4 12.1 %sum_scalars.1 = f32[8,128]{1,0:T(8,128)} custom-call(f32[8,128]{1,0:T(8,128)} %broadcast_select_fusion.given), custom_call_target="tpu_custom_call" | custom-call | tf_op jit(solution)/shard_map/sum_scalars/pallas_call | solution.py:1640
  682.6 1.3 fusion.26
  684.7 3.0 fusion.24
  687.8 0.9 fusion.22
  689.3 1.6 fusion.20
  691.4 1.6 fusion.18
  693.5 0.6 copy-done.10
  694.2 3.3 fusion.16
  (101 shorter events, 5.0 us)
Async XLA Ops:
  5.9 1.3 copy-start.30
  5.9 1.3 copy-start.28
  5.9 3.2 copy-start
  7.2 2.8 copy-start.2
  7.2 3.6 copy-start.12
  7.2 4.2 copy-start.4
  7.2 4.2 copy-start.6
  111.5 30.1 %copy-start.27 = (s32[1,1024]{1,0:T(1,128)S(1)}, s32[1,1024]{1,0:T(1,128)}, u32[]{:S(2)}) copy-start(s32[1,1024]{1,0:T(1,128)} %refs_3_.3) | copy-start | bytes 12292
  247.3 63.6 %copy-start.29 = (s32[1,1024]{1,0:T(1,128)S(1)}, s32[1,1024]{1,0:T(1,128)}, u32[]{:S(2)}) copy-start(s32[1,1024]{1,0:T(1,128)} %param.23) | copy-start | bytes 12292
  247.3 63.7 %copy-start.35 = (s32[1,1024]{1,0:T(1,128)S(1)}, s32[1,1024]{1,0:T(1,128)}, u32[]{:S(2)}) copy-start(s32[1,1024]{1,0:T(1,128)} %param.24) | copy-start | bytes 12292
  247.3 63.7 %copy-start.32 = (s32[1,1024]{1,0:T(1,128)S(1)}, s32[1,1024]{1,0:T(1,128)}, u32[]{:S(2)}) copy-start(s32[1,1024]{1,0:T(1,128)} %param.25) | copy-start | bytes 12292
  578.6 6.9 copy-start.36
  578.6 6.9 copy-start.37
  578.7 6.9 copy-start.38
  578.7 6.9 copy-start.39
  578.7 6.9 copy-start.40
  586.4 72.0 %copy-start.17 = (f32[3,96,192]{2,1,0:T(8,128)S(1)}, f32[3,96,192]{2,1,0:T(8,128)}, u32[]{:S(2)}) copy-start(f32[3,96,192]{2,1,0:T(8,128)} %get-tuple-element.164) | copy-start | bytes 663556
  586.4 73.8 %copy-start.23 = (f32[96,192]{1,0:T(8,128)S(1)}, f32[96,192]{1,0:T(8,128)}, u32[]{:S(2)}) copy-start(f32[96,192]{1,0:T(8,128)} %get-tuple-element.166) | copy-start | bytes 221188
  586.4 76.7 %copy-start.15 = (f32[96,768]{1,0:T(8,128)S(1)}, f32[96,768]{1,0:T(8,128)}, u32[]{:S(2)}) copy-start(f32[96,768]{1,0:T(8,128)} %get-tuple-element.168) | copy-start | bytes 884740
  586.4 79.1 %copy-start.14 = (f32[96,768]{1,0:T(8,128)S(1)}, f32[96,768]{1,0:T(8,128)}, u32[]{:S(2)}) copy-start(f32[96,768]{1,0:T(8,128)} %get-tuple-element.170) | copy-start | bytes 884740
  586.4 79.1 %copy-start.16 = (f32[96,768]{1,0:T(8,128)S(1)}, f32[96,768]{1,0:T(8,128)}, u32[]{:S(2)}) copy-start(f32[96,768]{1,0:T(8,128)} %get-tuple-element.169) | copy-start | bytes 884740
  658.3 8.6 %copy-start.8 = (f32[96,2048]{1,0:T(8,128)S(1)}, f32[96,2048]{1,0:T(8,128)}, u32[]{:S(2)}) copy-start(f32[96,2048]{1,0:T(8,128)} %get-tuple-element.172) | copy-start | bytes 2359300
  658.3 8.6 %copy-start.9 = (f32[96,2048]{1,0:T(8,128)S(1)}, f32[96,2048]{1,0:T(8,128)}, u32[]{:S(2)}) copy-start(f32[96,2048]{1,0:T(8,128)} %get-tuple-element.171) | copy-start | bytes 2359300
  660.2 8.4 %copy-start.31 = (f32[8,128]{1,0:T(8,128)S(1)}, f32[8,128]{1,0:T(8,128)}, u32[]{:S(2)}) copy-start(f32[8,128]{1,0:T(8,128)} %get-tuple-element.173) | copy-start | bytes 12292
  660.2 24.5 %copy-start.3 = (f32[2,3,96,192]{3,2,1,0:T(8,128)S(1)}, f32[2,3,96,192]{3,2,1,0:T(8,128)}, u32[]{:S(2)}) copy-start(f32[2,3,96,192]{3,2,1,0:T(8,128)} %refs_7_.2) | copy-start | bytes 1327108
  684.6 3.1 copy-start.13
  684.6 3.1 copy-start.24
  684.7 3.1 copy-start.25
  684.7 3.1 copy-start.26
  684.7 4.0 copy-start.20
  687.7 1.2 copy-start.5
  687.7 1.4 copy-start.18
  687.7 1.6 copy-start.19
  689.3 1.6 copy-start.7
  689.3 1.6 copy-start.21
  689.3 2.1 copy-start.22
  689.3 3.7 copy-start.11
  691.4 2.1 copy-start.1
  691.4 2.7 copy-start.10
  694.2 3.3 copy-start.33
  694.2 3.3 copy-start.34

commit v4 on v3

--- a/solution.py
+++ b/solution.py
@@ -23,14 +23,15 @@
 ADAM_EPS = 1e-08
 WEIGHT_DECAY = 0.01
 CLIP_NORM = 0.005
+WIDE, NARROW = "wide", "narrow"
 
 
 def add_heads(partial_value):
-    return lax.psum(partial_value, "narrow")
+    return lax.psum(partial_value, NARROW)
 
 
 def back_heads(partial_value):
-    return lax.psum(partial_value, "narrow")
+    return lax.psum(partial_value, NARROW)
 
 
 def rms_forward(value, gain):
@@ -233,21 +234,21 @@
 ):
     layers = attn_in.shape[0]
     mask = counted.reshape(-1).astype(jnp.float32)
-    token_total = lax.psum(jnp.sum(mask), "wide")
+    token_total = lax.psum(jnp.sum(mask), WIDE)
     query_w, output_w, expand_w, reduce_w, table_w, gain_low = (
-        lax.all_gather(attn_in.astype(jnp.bfloat16), "wide", axis=2, tiled=True),
-        lax.all_gather(attn_out.astype(jnp.bfloat16), "wide", axis=1, tiled=True),
-        lax.all_gather(ffn_in.astype(jnp.bfloat16), "wide", axis=1, tiled=True),
-        lax.all_gather(ffn_out.astype(jnp.bfloat16), "wide", axis=1, tiled=True),
-        lax.all_gather(tables.astype(jnp.bfloat16), "wide", axis=1, tiled=True),
-        lax.all_gather(gains.astype(jnp.bfloat16), "wide", axis=1, tiled=True),
+        lax.all_gather(attn_in.astype(jnp.bfloat16), WIDE, axis=2, tiled=True),
+        lax.all_gather(attn_out.astype(jnp.bfloat16), WIDE, axis=1, tiled=True),
+        lax.all_gather(ffn_in.astype(jnp.bfloat16), WIDE, axis=1, tiled=True),
+        lax.all_gather(ffn_out.astype(jnp.bfloat16), WIDE, axis=1, tiled=True),
+        lax.all_gather(tables.astype(jnp.bfloat16), WIDE, axis=1, tiled=True),
+        lax.all_gather(gains.astype(jnp.bfloat16), WIDE, axis=1, tiled=True),
     )
     gain_w = gain_low.astype(jnp.float32)
     noised_flat = noised.reshape(-1)
     clean_flat = clean.reshape(-1)
     step_flat = timesteps.reshape(-1)
     vocab_local = table_w.shape[2]
-    vocab_ids = lax.axis_index("narrow") * vocab_local + jnp.arange(vocab_local, dtype=jnp.int32)
+    vocab_ids = lax.axis_index(NARROW) * vocab_local + jnp.arange(vocab_local, dtype=jnp.int32)
     picks = (noised_flat[:, None] == vocab_ids[None, :]).astype(jnp.bfloat16)
     looked = add_heads(
         jnp.einsum("sv,dv->sd", picks, table_w[0], preferred_element_type=jnp.float32)
@@ -270,8 +271,8 @@
     final_low = final.astype(jnp.bfloat16)
     logits = jnp.dot(final_low, table_w[1], preferred_element_type=jnp.float32)
     local_top = jnp.max(logits, axis=1)
-    row_top = lax.pmax(local_top, "narrow")
-    row_total = lax.psum(jnp.sum(jnp.exp(logits - row_top[:, None]), axis=1), "narrow")
+    row_top = lax.pmax(local_top, NARROW)
+    row_total = lax.psum(jnp.sum(jnp.exp(logits - row_top[:, None]), axis=1), NARROW)
     log_probs = logits - (row_top + jnp.log(row_total))[:, None]
     probs = jnp.exp(log_probs)
     clamped = jnp.maximum(step_flat, 2).astype(jnp.float32)[:, None]
@@ -293,7 +294,7 @@
             jnp.sum(forward_fac * probs, axis=1),
             jnp.sum(at_clean * log_probs, axis=1),
         ),
-        "narrow",
+        NARROW,
     )
     divergence = cross / joint_total - jnp.log(joint_total) + jnp.log(model_total)
     first_step = step_flat == 1
@@ -334,19 +335,19 @@
     gain_layers = stacked[4].reshape(2 * layers, -1)
     grad_tables_all = jnp.stack([grad_table_in, grad_table_out])
     grad_attn_in, grad_attn_out, grad_ffn_in, grad_ffn_out, grad_tables, grad_gains = (
-        lax.psum_scatter(stacked[0], "wide", scatter_dimension=2, tiled=True),
-        lax.psum_scatter(stacked[1], "wide", scatter_dimension=1, tiled=True),
-        lax.psum_scatter(stacked[2], "wide", scatter_dimension=1, tiled=True),
-        lax.psum_scatter(stacked[3], "wide", scatter_dimension=1, tiled=True),
-        lax.psum_scatter(grad_tables_all, "wide", scatter_dimension=1, tiled=True),
+        lax.psum_scatter(stacked[0], WIDE, scatter_dimension=2, tiled=True),
+        lax.psum_scatter(stacked[1], WIDE, scatter_dimension=1, tiled=True),
+        lax.psum_scatter(stacked[2], WIDE, scatter_dimension=1, tiled=True),
+        lax.psum_scatter(stacked[3], WIDE, scatter_dimension=1, tiled=True),
+        lax.psum_scatter(grad_tables_all, WIDE, scatter_dimension=1, tiled=True),
         lax.psum_scatter(
             jnp.concatenate([gain_layers, grad_gain_final[None, :]], axis=0),
-            "wide",
+            WIDE,
             scatter_dimension=1,
             tiled=True,
         ),
     )
-    narrow_first = (lax.axis_index("narrow") == 0).astype(jnp.float32)
+    narrow_first = (lax.axis_index(NARROW) == 0).astype(jnp.float32)
     squares = (
         jnp.sum(grad_attn_in * grad_attn_in)
         + jnp.sum(grad_attn_out * grad_attn_out)
@@ -356,7 +357,7 @@
         + narrow_first * jnp.sum(grad_gains * grad_gains)
     )
     squares, loss_sum = lax.psum(
-        (squares, narrow_first * jnp.sum(mask * losses)), ("wide", "narrow")
+        (squares, narrow_first * jnp.sum(mask * losses)), (WIDE, NARROW)
     )
     grad_norm = jnp.sqrt(squares)
     factor = jnp.minimum(1.0, CLIP_NORM / (grad_norm + 1e-06))
@@ -410,6 +411,8 @@
 
 
 MESH = pl.DeviceIdType.MESH
+SLOW, FAST = 1, 2
+EARLY, MIDDLE, LAST = 1, 2, 3
 F32 = jnp.float32
 BF16 = jnp.bfloat16
 CHUNKS = 4
@@ -449,12 +452,12 @@
 
 
 def group_places(seq_len):
-    me = lax.axis_index("narrow")
+    me = lax.axis_index(NARROW)
     core = lax.rem(me, 2)
     half = seq_len // 2
     mine = pl.multiple_of(core * half, half)
     other = pl.multiple_of((1 - core) * half, half)
-    return ({"narrow": me + 1 - 2 * core}, {"narrow": lax.rem(me + 2, 4)}, mine, other)
+    return ({NARROW: me + 1 - 2 * core}, {NARROW: lax.rem(me + 2, 4)}, mine, other)
 
 
 class Exchange:
@@ -530,11 +533,16 @@
             self.piece(j).wait_send()
 
 
+def wide_places(count):
+    me = lax.axis_index(WIDE)
+    fast = lax.rem(me, 2)
+    slow = me // 2
+    return (me, slow, fast, count // 2)
+
+
 class Carry:
     def __init__(self, loads):
         self.loads = loads
-        self.pieces = [(load, piece) for load in loads for piece in range(load.pieces)]
-        self.relayed = 0
 
     def peers(self):
         ways = []
@@ -542,98 +550,162 @@
             ways += [way for way in load.ways if way not in ways]
         me, slow, fast, slows = wide_places(self.loads[0].count) if self.loads else (0, 0, 0, 0)
         found = []
-        if "slow" in ways:
-            found += [{"wide": 2 * lax.rem(slow + step, slows) + fast} for step in range(1, slows)]
-        if "fast" in ways:
-            found.append({"wide": me + 1 - 2 * fast})
+        if SLOW in ways:
+            found += [{WIDE: 2 * lax.rem(slow + step, slows) + fast} for step in range(1, slows)]
+        if FAST in ways:
+            found.append({WIDE: me + 1 - 2 * fast})
         return found
 
-    def start(self):
+    def start(self, late=False):
         for load in self.loads:
-            load.start()
-
-    def relay(self, part):
-        until = int(part * len(self.pieces) + 0.5)
-        for load, piece in self.pieces[self.relayed : until]:
-            load.relay(piece)
-        self.relayed = max(self.relayed, until)
+            if load.late == late:
+                load.start()
+
+    def relay(self, stage):
+        for load in self.loads:
+            if load.stage == stage:
+                load.relay()
 
     def finish(self):
-        self.relay(1.0)
+        self.relay(LAST)
         for load in self.loads:
             load.finish()
 
 
-class GatherLoad:
-    ways = ("slow", "fast")
-
-    def __init__(self, weights, index, lead, count, pieces=1):
-        self.index, self.lead, self.count, self.pieces = index, lead, count, pieces
-        shape, slows = weights.shape[1:], count // 2
-        self.rows = shape[-2] // pieces
+def part_of(weights, index, window):
+    shape = weights.shape[1:]
+    return shape if window is None else shape[:-1] + (window[1],)
+
+
+class SlowLoad:
+    ways, late, stage = (SLOW,), False, None
+
+    def __init__(self, weights, index, lead, count, window=None):
+        self.index, self.lead, self.count, self.window = index, lead, count, window
+        shape, slows = part_of(weights, index, window), count // 2
         self.operands, self.in_specs = [weights], [whole_vmem()]
+        self.outs = [jax.ShapeDtypeStruct((slows,) + shape, BF16)]
+        self.out_specs = [pl.BlockSpec(memory_space=pl.ANY)]
+        self.scratch = [pltpu.VMEM(shape, BF16), pltpu.SemaphoreType.DMA] + [pltpu.SemaphoreType.DMA((slows,))] * 2
+
+    def bind(self, given, out, scratch):
+        self.shard, self.out = given[0], out[0]
+        self.low, self.local, self.send, self.recv = scratch
+        self.me, self.slow, self.fast, self.slows = wide_places(self.count)
+
+    def cast(self):
+        if self.window is None:
+            self.low[...] = self.shard[self.index].astype(BF16)
+        else:
+            self.low[...] = self.shard[self.index, :, self.window[0] : self.window[0] + self.window[1]].astype(BF16)
+
+    def target(self):
+        return self.out.at[self.slow]
+
+    def slow_copy(self, step):
+        return remote(
+            self.low, self.target(), self.send.at[step], self.recv.at[step],
+            {WIDE: 2 * lax.rem(self.slow + step, self.slows) + self.fast},
+        )
+
+    def own_copy(self):
+        return pltpu.make_async_copy(self.low, self.target(), self.local)
+
+    def start(self):
+        self.cast()
+        for step in range(1, self.slows):
+            self.slow_copy(step).start()
+        self.own_copy().start()
+
+    def finish(self):
+        for step in range(1, self.slows):
+            self.slow_copy(step).wait()
+        self.own_copy().wait()
+
+
+class FastLoad:
+    ways, late, stage = (FAST,), False, None
+
+    def __init__(self, blocks, lead, count):
+        self.lead, self.count = lead, count
+        shape, slows = blocks.shape[1:], count // 2
+        self.operands, self.in_specs = [blocks], [pl.BlockSpec(memory_space=pl.ANY)]
         self.outs = [jax.ShapeDtypeStruct(shape[:lead] + (count,) + shape[lead:], BF16)]
         self.out_specs = [pl.BlockSpec(memory_space=pl.ANY)]
-        self.scratch = [pltpu.VMEM(shape, BF16), pltpu.SemaphoreType.DMA] + [
-            pltpu.SemaphoreType.DMA((pieces, slows))
-        ] * 4
+        self.scratch = [pltpu.SemaphoreType.DMA((slows,))] * 3
 
     def bind(self, given, out, scratch):
-        self.shard, self.out = given[0], out[0]
-        self.low, self.local, self.slow_send, self.slow_recv, self.fast_send, self.fast_recv = scratch
+        self.blocks, self.out = given[0], out[0]
+        self.local, self.send, self.recv = scratch
         self.me, self.slow, self.fast, self.slows = wide_places(self.count)
 
-    def cut(self, ref, piece):
-        if self.pieces == 1:
-            return ref
-        return ref.at[(slice(None),) * (len(ref.shape) - 2) + (pl.ds(piece * self.rows, self.rows),)]
+    def copies(self, step):
+        target = self.out.at[(slice(None),) * self.lead + (2 * step + self.fast,)]
+        return (
+            remote(
+                self.blocks.at[step], target, self.send.at[step], self.recv.at[step],
+                {WIDE: self.me + 1 - 2 * self.fast},
+            ),
+            pltpu.make_async_copy(self.blocks.at[step], target, self.local.at[step]),
+        )
+
+    def start(self):
+        for step in range(self.slows):
+            for copy in self.copies(step):
+                copy.start()
+
+    def finish(self):
+        for step in range(self.slows):
+            for copy in self.copies(step):
+                copy.wait()
+
+
+class GatherLoad(SlowLoad):
+    ways = (SLOW, FAST)
+
+    def __init__(self, weights, index, lead, count, stage, window=None, late=False):
+        super().__init__(weights, index, lead, count, window)
+        self.stage, self.late = stage, late
+        shape, slows = part_of(weights, index, window), count // 2
+        self.outs = [jax.ShapeDtypeStruct(shape[:lead] + (count,) + shape[lead:], BF16)]
+        self.scratch = self.scratch + [pltpu.SemaphoreType.DMA((slows,))] * 2
+
+    def bind(self, given, out, scratch):
+        super().bind(given, out, scratch[:-2])
+        self.fast_send, self.fast_recv = scratch[-2:]
 
     def at(self, owner):
         return self.out.at[(slice(None),) * self.lead + (owner,)]
 
-    def slow_copy(self, piece, step):
+    def target(self):
+        return self.at(self.me)
+
+    def fast_copy(self, step):
+        block = self.at(2 * lax.rem(self.slow + self.slows - step, self.slows) + self.fast)
         return remote(
-            self.cut(self.low, piece), self.cut(self.at(self.me), piece),
-            self.slow_send.at[piece, step], self.slow_recv.at[piece, step],
-            {"wide": 2 * lax.rem(self.slow + step, self.slows) + self.fast},
+            self.low if step == 0 else block, block, self.fast_send.at[step], self.fast_recv.at[step],
+            {WIDE: self.me + 1 - 2 * self.fast},
         )
 
-    def fast_copy(self, piece, step):
-        block = self.cut(self.at(2 * lax.rem(self.slow + self.slows - step, self.slows) + self.fast), piece)
-        return remote(
-            self.cut(self.low, piece) if step == 0 else block, block,
-            self.fast_send.at[piece, step], self.fast_recv.at[piece, step],
-            {"wide": self.me + 1 - 2 * self.fast},
-        )
-
-    def own_copy(self):
-        return pltpu.make_async_copy(self.low, self.at(self.me), self.local)
-
     def start(self):
-        self.low[...] = self.shard[self.index].astype(BF16)
-        for piece in range(self.pieces):
-            for step in range(1, self.slows):
-                self.slow_copy(piece, step).start()
-            self.fast_copy(piece, 0).start()
-        self.own_copy().start()
-
-    def relay(self, piece):
+        super().start()
+        self.fast_copy(0).start()
+
+    def relay(self):
         for step in range(1, self.slows):
-            self.slow_copy(piece, step).wait_recv()
-            self.fast_copy(piece, step).start()
+            self.slow_copy(step).wait_recv()
+            self.fast_copy(step).start()
 
     def finish(self):
-        for piece in range(self.pieces):
-            for step in range(self.slows):
-                self.fast_copy(piece, step).wait()
-                if step:
-                    self.slow_copy(piece, step).wait_send()
+        for step in range(self.slows):
+            self.fast_copy(step).wait()
+            if step:
+                self.slow_copy(step).wait_send()
         self.own_copy().wait()
 
 
 class PairLoad:
-    ways = ("fast",)
-    pieces = 0
+    ways, late, stage = (FAST,), False, None
 
     def __init__(self, full, lead, count):
         self.lead, self.count = lead, count
@@ -654,7 +726,7 @@
     def copy(self, step):
         return remote(
             self.block(step, 1 - self.fast), self.came.at[step], self.send.at[step], self.recv.at[step],
-            {"wide": self.me + 1 - 2 * self.fast},
+            {WIDE: self.me + 1 - 2 * self.fast},
         )
 
     def start(self):
@@ -669,25 +741,25 @@
 
 
 class LineLoad:
-    ways = ("slow",)
-    pieces = 0
+    ways, late, stage = (SLOW,), False, None
 
     def __init__(self, sums, count):
         self.count = count
         slows = count // 2
         self.operands, self.in_specs = [sums], [whole_vmem()]
-        self.outs, self.out_specs = [jax.ShapeDtypeStruct(sums.shape[1:], F32)], [whole_vmem()]
+        self.outs = [jax.ShapeDtypeStruct(sums.shape[1:], F32), jax.ShapeDtypeStruct((8, 128), F32)]
+        self.out_specs = [whole_vmem()] * 2
         self.scratch = [pltpu.VMEM(sums.shape, BF16)] + [pltpu.SemaphoreType.DMA((slows,))] * 2
 
     def bind(self, given, out, scratch):
-        self.sums, self.out = given[0], out[0]
+        self.sums, (self.out, self.squares) = given[0], out
         self.came, self.send, self.recv = scratch
         self.me, self.slow, self.fast, self.slows = wide_places(self.count)
 
     def copy(self, step):
         return remote(
             self.sums.at[step], self.came.at[step], self.send.at[step], self.recv.at[step],
-            {"wide": 2 * lax.rem(self.slow + step, self.slows) + self.fast},
+            {WIDE: 2 * lax.rem(self.slow + step, self.slows) + self.fast},
         )
 
     def start(self):
@@ -700,6 +772,7 @@
             self.copy(step).wait()
             total = total + self.came[step].astype(F32)
         self.out[...] = total
+        self.squares[...] = jnp.full(self.squares.shape, jnp.sum(total * total), F32)
 
 
 def run(body, name, operands, outs, scratch, collective_id=None, loads=()):
@@ -769,59 +842,221 @@
     return pl.ds(pl.multiple_of(start + j * chunk, chunk), chunk)
 
 
-def embed_kernel(ids, extra, table, gain, resid, normed, near_out, near_in, far_out, far_in, send, recv):
+LANES = 128
+
+
+def spread(row):
+    return jnp.transpose(jnp.broadcast_to(row, (LANES, LANES)))
+
+
+def feature_places(owner, width, share):
+    lane = lax.broadcasted_iota(jnp.int32, (LANES, width), 0)
+    feature = lax.broadcasted_iota(jnp.int32, (LANES, width), 1)
+    return ((feature == lane + owner * share) & (lane < share)).astype(F32).astype(BF16)
+
+
+def token_picks(ids, vocab, first):
+    here = spread(ids.astype(F32) - first.astype(F32))
+    lane = lax.broadcasted_iota(jnp.int32, (LANES, LANES), 1).astype(F32)
+    return [jnp.where(here == lane + float(t * LANES), 1.0, 0.0).astype(BF16) for t in range(vocab // LANES)]
+
+
+def embed_kernel(
+    ids, counted, gains, extra, table,
+    resid, normed, gain_all, count_all, ids_all,
+    low, picks, small, near_out, near_in, own, far_out, far_in, wide_out, wide_in, part_out, part_in,
+    id_send, id_recv, small_send, small_recv, near_send, near_recv, far_send, far_recv, wide_send, wide_recv,
+    part_send, part_recv, send, recv, carry,
+):
     seq_len, width = normed.shape
     chunk = seq_len // 2 // CHUNKS
+    quarter = seq_len // 4
+    share, vocab = table.shape[1:]
+    owners = ids_all.shape[0]
+    id_rows = ids.shape[0]
     sibling, partner, mine, other = group_places(seq_len)
-    vocab = table.shape[1]
-    first = lax.axis_index("narrow") * vocab
-    greet([sibling, partner])
-    trade = Exchange((near_out, near_in, far_out, far_in), (send, recv), 0, sibling, partner)
-    share = Share(normed, (send, recv), 2, sibling, mine, chunk)
-
-    def partial(start, j):
-        here = ids[rows_at(start, j, chunk), :] - first
-        columns = lax.broadcasted_iota(jnp.int32, (chunk, vocab), 1)
-        picks = (here == columns).astype(F32).astype(BF16)
-        return dot_nt(picks, table[...])
-
-    trade.give(0, partial(other, 0))
-    for j in range(CHUNKS):
-        if j + 1 < CHUNKS:
-            trade.give(j + 1, partial(other, j + 1))
-        trade.pass_on(j, partial(mine, j))
-    for j in range(CHUNKS):
-        x = math.sqrt(width) * trade.take(j) + extra[rows_at(0, j, chunk), :]
-        resid[rows_at(0, j, chunk), :] = x
-        share.put(j, norm_of(x, gain[...]).astype(BF16))
-    for j in range(CHUNKS):
-        share.arrived(j)
-    trade.close()
-    share.close()
-
-
-def embed(ids, extra, table, gain, collective_id):
-    seq_len, width = ids.shape[0], table.shape[0]
-    chunk = seq_len // 2 // CHUNKS
-    return pl.pallas_call(
+    place = lax.axis_index(NARROW)
+    side = lax.div(place, 2)
+    me = lax.axis_index(WIDE)
+    first = place * vocab
+    around = [lax.rem(me + step, owners) for step in range(owners)]
+
+    def id_copy(step):
+        return remote(ids_all.at[me], ids_all.at[me], id_send.at[step], id_recv.at[step], {WIDE: around[step]})
+
+    def small_copy(step):
+        return remote(small.at[me], small.at[me], small_send.at[step], small_recv.at[step], {WIDE: around[step]})
+
+    def near_copy(step):
+        return remote(near_out.at[step], near_in.at[step], near_send.at[step], near_recv.at[step], sibling)
+
+    def far_copy(step):
+        return remote(far_out.at[step], far_in.at[step], far_send.at[step], far_recv.at[step], partner)
+
+    def wide_copy(step):
+        return remote(wide_out.at[step], wide_in.at[me], wide_send.at[step], wide_recv.at[step], {WIDE: around[step]})
+
+    def part_copy(piece):
+        rows = pl.ds(piece * LANES, LANES)
+        return remote(part_out.at[rows], part_in.at[rows], part_send.at[piece], part_recv.at[piece], partner)
+
+    ids_all[me] = ids[...]
+    small[me] = jnp.zeros(small.shape[1:], F32)
+    small[me, : gains.shape[0], : gains.shape[1]] = gains[...].astype(BF16).astype(F32)
+    count = jnp.sum(counted[...].astype(F32), keepdims=True)
+    small[me, gains.shape[0] : gains.shape[0] + 1, :] = jnp.broadcast_to(count, (1, small.shape[2]))
+    greet([{WIDE: device} for device in around[1:]] + [sibling, partner])
+    for step in range(1, owners):
+        id_copy(step).start()
+    for step in range(1, owners):
+        small_copy(step).start()
+    carry.start()
+    low[...] = jnp.zeros(low.shape, BF16)
+    low[:share, :] = table[0].astype(BF16)
+
+    def look_up(step):
+        row = lax.rem(me + step, owners)
+
+        def block(start, b):
+            place_of = start // LANES + b
+            for t, pick in enumerate(token_picks(ids_all[row, pl.ds(place_of, 1), :], vocab, first)):
+                picks[:, t * LANES : (t + 1) * LANES] = pick
+            return dot_nt(picks[...], low[...]).astype(BF16)
+
+        def theirs(b, _):
+            near_out[step, rows_at(0, b, LANES), :] = block(other, b)
+            return 0
+
+        def ours(b, _):
+            own[step, rows_at(0, b, LANES), :] = block(mine, b)
+            return 0
+
+        lax.fori_loop(0, seq_len // 2 // LANES, theirs, 0)
+        near_copy(step).start()
+        lax.fori_loop(0, seq_len // 2 // LANES, ours, 0)
+
+    def halve(step):
+        near_copy(step).wait_recv()
+        total = own[step] + near_in[step]
+        own[step] = total
+        far_out[step] = own[step, pl.ds(pl.multiple_of((1 - side) * quarter, quarter), quarter), :]
+        far_copy(step).start()
+
+    def deliver(step):
+        far_copy(step).wait_recv()
+        total = own[step, pl.ds(pl.multiple_of(side * quarter, quarter), quarter), :] + far_in[step]
+        if step % owners == 0:
+            wide_in[me] = total
+        else:
+            wide_out[step] = total
+            wide_copy(step).start()
+
+    order = list(range(1, owners)) + [0]
+    for turn in range(owners + 2):
+        if turn < owners:
+            if order[turn]:
+                id_copy(owners - order[turn]).wait_recv()
+            look_up(order[turn])
+        if 1 <= turn < owners + 1:
+            halve(order[turn - 1])
+        if turn >= 2:
+            deliver(order[turn - 2])
+    carry.start(True)
+    for step in range(1, owners):
+        small_copy(step).wait_recv()
+    total = None
+    for owner in range(owners):
+        part = dot_nn(small[owner].astype(BF16), feature_places(owner, width, share))
+        total = part if total is None else total + part
+    gain_all[...] = total
+    count_all[...] = jnp.sum(small[...], axis=0)
+    for step in range(1, owners):
+        wide_copy(step).wait_recv()
+    pieces = quarter // LANES
+    at_side = pl.multiple_of(side * quarter, quarter)
+    at_other = pl.multiple_of((1 - side) * quarter, quarter)
+    for piece in range(pieces):
+        rows = pl.ds(piece * LANES, LANES)
+        found = None
+        for owner in range(owners):
+            part = dot_nn(wide_in[owner, rows, :], feature_places(owner, width, share))
+            found = part if found is None else found + part
+        part_out[rows, :] = found.astype(BF16)
+        part_copy(piece).start()
+    carry.relay(EARLY)
+    give = Share(normed, (send, recv), 0, sibling, mine, chunk)
+
+    def finish(start, source, piece):
+        rows = rows_at(start, piece, LANES)
+        x = math.sqrt(width) * source[pl.ds(piece * LANES, LANES), :].astype(F32) + extra[rows, :]
+        resid[rows, :] = x
+        here = rows_at(mine + start, piece, LANES)
+        normed[here, :] = norm_of(x, gain_all[0:1, :]).astype(BF16)
+        give_rows(here, piece if source is part_out else pieces + piece).start()
+
+    def give_rows(here, k):
+        return remote(normed.at[here], normed.at[here], send.at[0, k], recv.at[0, k], sibling)
+
+    for piece in range(pieces):
+        finish(at_side, part_out, piece)
+    for piece in range(pieces):
+        part_copy(piece).wait_recv()
+        finish(at_other, part_in, piece)
+    carry.relay(MIDDLE)
+    for k in range(2 * pieces):
+        give_rows(rows_at(mine, k % pieces, LANES), k).wait()
+    for step in range(owners):
+        near_copy(step).wait_send()
+        far_copy(step).wait_send()
+        if step:
+            id_copy(step).wait_send()
+            small_copy(step).wait_send()
+            wide_copy(step).wait_send()
+    for piece in range(pieces):
+        part_copy(piece).wait_send()
+    carry.finish()
+
+
+def embed(ids, counted, gains, extra, tables, owners, collective_id, loads):
+    seq_len = ids.size
+    half, width = extra.shape
+    share, vocab = tables.shape[1:]
+    dma = pltpu.SemaphoreType.DMA
+    return run(
         embed_kernel,
-        out_shape=(
-            jax.ShapeDtypeStruct((seq_len // 2, width), F32),
+        "embed",
+        [ids, counted, gains, extra, tables],
+        [
+            jax.ShapeDtypeStruct((half, width), F32),
             jax.ShapeDtypeStruct((seq_len, width), BF16),
-        ),
-        in_specs=[whole_vmem()] * 4,
-        out_specs=(whole_vmem(),) * 2,
-        scratch_shapes=Exchange.scratch(chunk, width, FORWARD_KIND)
-        + [pltpu.SemaphoreType.DMA((3, CHUNKS)), pltpu.SemaphoreType.DMA((3, CHUNKS))],
-        compiler_params=pltpu.CompilerParams(
-            collective_id=collective_id, has_side_effects=True, vmem_limit_bytes=VMEM_LIMIT
-        ),
-        name="embed",
-    )(ids, extra, table, gain)
+            jax.ShapeDtypeStruct((8, width), F32),
+            jax.ShapeDtypeStruct((8, LANES), F32),
+            jax.ShapeDtypeStruct((owners,) + ids.shape, jnp.int32),
+        ],
+        [
+            pltpu.VMEM((LANES, vocab), BF16),
+            pltpu.VMEM((LANES, vocab), BF16),
+            pltpu.VMEM((owners, 8, LANES), F32),
+            pltpu.VMEM((owners, half, LANES), BF16),
+            pltpu.VMEM((owners, half, LANES), BF16),
+            pltpu.VMEM((owners, half, LANES), BF16),
+            pltpu.VMEM((owners, half // 2, LANES), BF16),
+            pltpu.VMEM((owners, half // 2, LANES), BF16),
+            pltpu.VMEM((owners, half // 2, LANES), BF16),
+            pltpu.VMEM((owners, half // 2, LANES), BF16),
+            pltpu.VMEM((half // 2, width), BF16),
+            pltpu.VMEM((half // 2, width), BF16),
+        ]
+        + [dma((owners,))] * 10
+        + [dma((half // 2 // LANES,))] * 2
+        + [dma((1, half // LANES))] * 2,
+        collective_id,
+        loads,
+    )
 
 
 def ffn_kernel(
-    mixed, resid, w_out, w_in, w_red, gain, gain_next,
+    layer, mixed, resid, w_out, w_in, w_red, gains,
     middle, normed, before, after, result, normed_next,
     near_out, near_in, far_out, far_in, near_out2, near_in2, far_out2, far_in2, own2, send, recv, carry,
 ):
@@ -855,21 +1090,21 @@
         rows = rows_at(0, j, chunk)
         mid = resid[rows, :] + first.take(j)
         middle[rows, :] = mid
-        share.put(j, norm_of(mid, gain[...]).astype(BF16))
+        share.put(j, norm_of(mid, gains[2 * layer + 1 : 2 * layer + 2, :]).astype(BF16))
         own2[j] = feed(rows_at(mine, j, chunk))
         share.arrived(j)
         second.give(j, feed(rows_at(other, j, chunk)))
         if j >= 1:
             second.pass_on(j - 1, own2[j - 1])
     second.pass_on(CHUNKS - 1, own2[CHUNKS - 1])
-    carry.relay(0.5)
+    carry.relay(EARLY)
     for j in range(CHUNKS):
         rows = rows_at(0, j, chunk)
         x = middle[rows, :] + second.take(j)
         result[rows, :] = x
-        share_next.put(j, norm_of(x, gain_next[...]).astype(BF16))
+        share_next.put(j, norm_of(x, gains[2 * layer + 2 : 2 * layer + 3, :]).astype(BF16))
         if j == CHUNKS - 2:
-            carry.relay(0.75)
+            carry.relay(MIDDLE)
     for j in range(CHUNKS):
         share_next.arrived(j)
     for part in (first, second, share, share_next):
@@ -877,13 +1112,13 @@
     carry.finish()
 
 
-def ffn_forward(mixed, resid, w_out, w_in, w_red, gain, gain_next, collective_id, loads):
+def ffn_forward(layer, mixed, resid, w_out, w_in, w_red, gains, collective_id, loads):
     seq_len, width, hidden = mixed.shape[0], w_in.shape[0], w_in.shape[1]
     half, chunk = seq_len // 2, seq_len // 2 // CHUNKS
     return run(
-        ffn_kernel,
+        functools.partial(ffn_kernel, layer),
         "ffn_forward",
-        [mixed, resid, w_out, w_in, w_red, gain, gain_next],
+        [mixed, resid, w_out, w_in, w_red, gains],
         [
             jax.ShapeDtypeStruct((half, width), F32),
             jax.ShapeDtypeStruct((seq_len, width), BF16),
@@ -920,7 +1155,7 @@
 
 
 def ffn_back_kernel(
-    grad, branch, w_red, w_in, w_out, before, after, normed, middle, gain, mixed,
+    row, grad, branch, w_red, w_in, w_out, before, after, normed, middle, gain, mixed,
     grad_middle, grad_attn, grad_mixed, d_red, d_in, d_out, d_gain,
     grad_before, turned, near_out, near_in, far_out, far_in, send, recv, carry,
 ):
@@ -949,10 +1184,10 @@
     weight_grad(turned, after, d_red)
     turned[...] = jnp.transpose(normed[...])
     weight_grad(turned, grad_before, d_in)
-    gain_total = jnp.zeros(gain.shape, F32)
+    gain_total = jnp.zeros((1, gain.shape[1]), F32)
     for j in range(CHUNKS):
         rows = rows_at(0, j, chunk)
-        back, gain_part = norm_back(trade.take(j), middle[rows, :], gain[...])
+        back, gain_part = norm_back(trade.take(j), middle[rows, :], gain[row : row + 1, :])
         gain_total = gain_total + gain_part
         total = back + grad[rows, :]
         grad_middle[rows, :] = total
@@ -971,11 +1206,11 @@
     carry.finish()
 
 
-def ffn_backward(grad, branch, w_red, w_in, w_out, before, after, normed, middle, gain, mixed, collective_id, loads):
+def ffn_backward(row, grad, branch, w_red, w_in, w_out, before, after, normed, middle, gain, mixed, collective_id, loads):
     seq_len, width = normed.shape
     half, chunk = seq_len // 2, seq_len // 2 // CHUNKS
     return run(
-        ffn_back_kernel,
+        functools.partial(ffn_back_kernel, row),
         "ffn_backward",
         [grad, branch, w_red, w_in, w_out, before, after, normed, middle, gain, mixed],
         [
@@ -985,7 +1220,7 @@
             jax.ShapeDtypeStruct(w_red.shape, BF16),
             jax.ShapeDtypeStruct(w_in.shape, BF16),
             jax.ShapeDtypeStruct(w_out.shape, BF16),
-            jax.ShapeDtypeStruct(gain.shape, F32),
+            jax.ShapeDtypeStruct((1, gain.shape[1]), F32),
         ],
         [pltpu.VMEM(before.shape, BF16), pltpu.VMEM((width, seq_len), BF16)]
         + Exchange.scratch(chunk, width, BACKWARD_KIND)
@@ -996,7 +1231,7 @@
 
 
 def norm_back_kernel(
-    scale, grads, weights, normed, value, gain, upstream,
+    scale, row, grads, weights, normed, value, gain, upstream,
     grad_out, branch, d_weights, d_gain,
     turned, near_out, near_in, far_out, far_in, send, recv, carry,
 ):
@@ -1025,10 +1260,10 @@
     turned[...] = jnp.transpose(normed[...])
     for which in range(grads.shape[0]):
         weight_grad(turned, grads.at[which], d_weights.at[which])
-    gain_total = jnp.zeros(gain.shape, F32)
+    gain_total = jnp.zeros((1, gain.shape[1]), F32)
     for j in range(CHUNKS):
         rows = rows_at(0, j, chunk)
-        back, gain_part = norm_back(trade.take(j), value[rows, :], gain[...])
+        back, gain_part = norm_back(trade.take(j), value[rows, :], gain[row : row + 1, :])
         gain_total = gain_total + gain_part
         back = back + upstream[rows, :]
         grad_out[rows, :] = back
@@ -1041,18 +1276,18 @@
     carry.finish()
 
 
-def norm_backward(grads, weights, normed, value, gain, upstream, scale, collective_id, loads):
+def norm_backward(row, grads, weights, normed, value, gain, upstream, scale, collective_id, loads):
     seq_len, width = normed.shape
     half, chunk = seq_len // 2, seq_len // 2 // CHUNKS
     return run(
-        functools.partial(norm_back_kernel, scale),
+        functools.partial(norm_back_kernel, scale, row),
         "norm_backward",
         [grads, weights, normed, value, gain, upstream],
         [
             jax.ShapeDtypeStruct((half, width), F32),
             jax.ShapeDtypeStruct((seq_len, width), BF16),
             jax.ShapeDtypeStruct(weights.shape, BF16),
-            jax.ShapeDtypeStruct(gain.shape, F32),
+            jax.ShapeDtypeStruct((1, gain.shape[1]), F32),
         ],
         [pltpu.VMEM((width, seq_len), BF16)] + Exchange.scratch(chunk, width, BACKWARD_KIND) + sems(3),
         collective_id,
@@ -1060,192 +1295,20 @@
     )
 
 
-def wide_places(count):
-    me = lax.axis_index("wide")
-    fast = lax.rem(me, 2)
-    slow = me // 2
-    return (me, slow, fast, count // 2)
-
-
-def gather_kernel(arrays, lead, *refs):
-    shards, outs = refs[:arrays], refs[arrays : 2 * arrays]
-    lows = refs[2 * arrays : 3 * arrays]
-    local, slow_send, slow_recv, fast_send, fast_recv = refs[3 * arrays :]
-    count = outs[0].shape[lead[0]]
-    me, slow, fast, slows = wide_places(count)
-    beside = me + 1 - 2 * fast
-
-    def at(which, owner):
-        out = outs[which]
-        return out.at[(slice(None),) * lead[which] + (owner,)]
-
-    def along(step):
-        return 2 * lax.rem(slow + step, slows) + fast
-
-    def back(step):
-        return 2 * lax.rem(slow + slows - step, slows) + fast
-
-    def slow_copy(which, step):
-        return remote(
-            lows[which], at(which, me), slow_send.at[which, step - 1], slow_recv.at[which, step - 1],
-            {"wide": along(step)},
-        )
-
-    def fast_copy(which, step):
-        block = at(which, back(step))
-        return remote(
-            lows[which] if step == 0 else block, block, fast_send.at[which, step], fast_recv.at[which, step],
-            {"wide": beside},
-        )
-
-    greet([{"wide": along(step)} for step in range(1, slows)] + [{"wide": beside}])
-    for which in range(arrays):
-        lows[which][...] = shards[which][...].astype(lows[which].dtype)
-        for step in range(1, slows):
-            slow_copy(which, step).start()
-        fast_copy(which, 0).start()
-        pltpu.make_async_copy(lows[which], at(which, me), local.at[which]).start()
-    for which in range(arrays):
-        for step in range(1, slows):
-            slow_copy(which, step).wait_recv()
-            fast_copy(which, step).start()
-    for which in range(arrays):
-        for step in range(slows):
-            fast_copy(which, step).wait()
-            if step:
-                slow_copy(which, step).wait_send()
-        pltpu.make_async_copy(lows[which], at(which, me), local.at[which]).wait()
-
-
-def gather_wide(shards, leads, kinds, count, collective_id):
-    arrays = len(shards)
-    slows = count // 2
-    return pl.pallas_call(
-        functools.partial(gather_kernel, arrays, leads),
-        out_shape=tuple(
-            jax.ShapeDtypeStruct(s.shape[:lead] + (count,) + s.shape[lead:], kind)
-            for s, lead, kind in zip(shards, leads, kinds)
-        ),
-        in_specs=[whole_vmem()] * arrays,
-        out_specs=(pl.BlockSpec(memory_space=pl.ANY),) * arrays,
-        scratch_shapes=[pltpu.VMEM(s.shape, kind) for s, kind in zip(shards, kinds)]
-        + [
-            pltpu.SemaphoreType.DMA((arrays,)),
-            pltpu.SemaphoreType.DMA((arrays, slows - 1)),
-            pltpu.SemaphoreType.DMA((arrays, slows - 1)),
-            pltpu.SemaphoreType.DMA((arrays, slows)),
-            pltpu.SemaphoreType.DMA((arrays, slows)),
-        ],
-        compiler_params=pltpu.CompilerParams(
-            collective_id=collective_id, has_side_effects=True, vmem_limit_bytes=VMEM_LIMIT
-        ),
-        name="gather_weights",
-    )(*shards)
-
-
-def scatter_kernel(arrays, lead, *refs, carry):
-    fulls, outs = refs[:arrays], refs[arrays : 2 * arrays]
-    fast_in = refs[2 * arrays : 3 * arrays]
-    sums = refs[3 * arrays : 4 * arrays]
-    slow_in = refs[4 * arrays : 5 * arrays]
-    paired, paired_in, fast_send, fast_recv, slow_send, slow_recv, near_send, near_recv = refs[5 * arrays :]
-    count = fulls[0].shape[lead[0]]
-    me, slow, fast, slows = wide_places(count)
-    beside = me + 1 - 2 * fast
-    place = lax.axis_index("narrow")
-    sibling = {"narrow": place + 1 - 2 * lax.rem(place, 2)}
-    sources = list(fulls[:-1]) + [paired]
-
-    def block(which, owner):
-        return sources[which].at[(slice(None),) * lead[which] + (owner,)]
-
-    def along(step):
-        return lax.rem(slow + step, slows)
-
-    def fast_copy(which, step):
-        owner = 2 * along(step) + 1 - fast
-        return remote(
-            block(which, owner), fast_in[which].at[step], fast_send.at[which, step], fast_recv.at[which, step],
-            {"wide": beside},
-        )
-
-    def slow_copy(which, step):
-        return remote(
-            sums[which].at[step - 1], slow_in[which].at[step - 1],
-            slow_send.at[which, step - 1], slow_recv.at[which, step - 1],
-            {"wide": 2 * along(step) + fast},
-        )
-
-    greet([{"wide": 2 * along(step) + fast} for step in range(1, slows)] + [{"wide": beside}, sibling])
-    carry.start()
-    near = remote(fulls[-1], paired_in, near_send, near_recv, sibling)
-    near.start()
-    for which in range(arrays):
-        if which == arrays - 1:
-            near.wait()
-            paired[...] = fulls[-1][...] + paired_in[...]
-        for step in list(range(1, slows)) + [0]:
-            fast_copy(which, step).start()
-    for which in range(arrays):
-        for step in range(1, slows):
-            fast_copy(which, step).wait_recv()
-            owner = 2 * along(step) + fast
-            total = block(which, owner)[...].astype(F32) + fast_in[which][step].astype(F32)
-            sums[which][step - 1] = total.astype(sums[which].dtype)
-            slow_copy(which, step).start()
-    for which in range(arrays):
-        fast_copy(which, 0).wait_recv()
-        total = block(which, me)[...].astype(F32) + fast_in[which][0].astype(F32)
-        for step in range(1, slows):
-            slow_copy(which, step).wait_recv()
-            total = total + slow_in[which][step - 1].astype(F32)
-        outs[which][...] = total
-    for which in range(arrays):
-        for step in range(slows):
-            fast_copy(which, step).wait_send()
-            if step:
-                slow_copy(which, step).wait_send()
-    carry.finish()
-
-
-def scatter_wide(fulls, leads, collective_id, loads):
-    arrays = len(fulls)
-    slows = fulls[0].shape[leads[0]] // 2
-    shapes = [f.shape[:lead] + f.shape[lead + 1 :] for f, lead in zip(fulls, leads)]
-    kinds = [f.dtype for f in fulls]
-    return run(
-        functools.partial(scatter_kernel, arrays, leads),
-        "scatter_grads",
-        fulls,
-        [jax.ShapeDtypeStruct(shape, F32) for shape in shapes],
-        [pltpu.VMEM((slows,) + shape, kind) for shape, kind in zip(shapes, kinds)]
-        + [pltpu.VMEM((slows - 1,) + shape, kind) for shape, kind in zip(shapes, kinds)]
-        + [pltpu.VMEM((slows - 1,) + shape, kind) for shape, kind in zip(shapes, kinds)]
-        + [pltpu.VMEM(fulls[-1].shape, F32)] * 2
-        + [
-            pltpu.SemaphoreType.DMA((arrays, slows)),
-            pltpu.SemaphoreType.DMA((arrays, slows)),
-            pltpu.SemaphoreType.DMA((arrays, slows - 1)),
-            pltpu.SemaphoreType.DMA((arrays, slows - 1)),
-            pltpu.SemaphoreType.DMA,
-            pltpu.SemaphoreType.DMA,
-        ],
-        collective_id,
-        loads,
-    )
-
-
 def head_lanes(value, head, size):
     lanes = lax.broadcasted_iota(jnp.int32, value.shape, 1)
     inside = (lanes >= head * size) & (lanes < (head + 1) * size)
     return jnp.where(inside, value, jnp.zeros_like(value))
 
 
-def attention_kernel(normed, weights, key_seg, query_seg, projected, mixed, bias, values_t):
+def attention_kernel(normed, weights, key_seg, query_seg, projected, mixed, bias, values_t, carry):
     seq_len = normed.shape[0]
     width = mixed.shape[1]
     block = bias.shape[1]
     heads = width // HD
+    if carry.loads:
+        greet(carry.peers())
+    carry.start()
 
     def project(i, _):
         rows = rows_at(0, i, block)
@@ -1270,26 +1333,27 @@
         return 0
 
     lax.fori_loop(0, seq_len // block, queries, 0)
+    carry.finish()
 
 
 QUERY_BLOCK = 256
 
 
-def attention(normed, weights, key_seg, query_seg):
+def attention(normed, weights, key_seg, query_seg, collective_id, loads):
     seq_len, width = normed.shape[0], weights.shape[2]
     block = min(QUERY_BLOCK, seq_len)
-    return pl.pallas_call(
+    return run(
         attention_kernel,
-        out_shape=(
+        "attention",
+        [normed, weights, key_seg, query_seg],
+        [
             jax.ShapeDtypeStruct((3, seq_len, width), BF16),
             jax.ShapeDtypeStruct((seq_len, width), BF16),
-        ),
-        in_specs=[whole_vmem()] * 4,
-        out_specs=(whole_vmem(),) * 2,
-        scratch_shapes=[pltpu.VMEM((seq_len, block), F32), pltpu.VMEM((width, seq_len), BF16)],
-        compiler_params=pltpu.CompilerParams(vmem_limit_bytes=VMEM_LIMIT),
-        name="attention",
-    )(normed, weights, key_seg, query_seg)
+        ],
+        [pltpu.VMEM((seq_len, block), F32), pltpu.VMEM((width, seq_len), BF16)],
+        collective_id if loads else None,
+        loads,
+    )
 
 
 def attention_back_kernel(projected, grad_mixed, key_seg, query_seg, out, bias, keys_t, grad_keys, grad_values, carry):
@@ -1350,13 +1414,6 @@
     )
 
 
-LANES = 128
-
-
-def spread(row):
-    return jnp.transpose(jnp.broadcast_to(row, (LANES, LANES)))
-
-
 def to_rows(columns):
     lanes = lax.broadcasted_iota(jnp.int32, (LANES, LANES), 1)
     total = jnp.zeros((LANES, LANES), F32)
@@ -1366,20 +1423,30 @@
 
 
 def loss_kernel(
-    normed, table, info, value, gain,
-    grad_out, branch, d_table, d_gain, losses,
+    pieces, row, normed, info, value, gain, *refs, carry,
+):
+    tables, refs = refs[:pieces], refs[pieces:]
+    (grad_out, branch, d_gain, losses), refs = refs[:4], refs[4:]
+    d_tables, refs = refs[:pieces], refs[pieces:]
+    loss_body(row, normed, info, value, gain, tables, grad_out, branch, d_gain, losses, d_tables, *refs, carry)
+
+
+def loss_body(
+    row, normed, info, value, gain, tables, grad_out, branch, d_gain, losses, d_tables,
     logits, grads, places, turned, stat_out, stat_in, sum_out, sum_in,
-    near_out, near_in, far_out, far_in, send, recv, stat_send, stat_recv, sum_send, sum_recv,
+    near_out, near_in, far_out, far_in, send, recv, stat_send, stat_recv, sum_send, sum_recv, carry,
 ):
     seq_len, width = normed.shape
     chunk = seq_len // 2 // CHUNKS
-    vocab = table.shape[1]
+    piece_width = tables[0].shape[1]
+    vocab = piece_width * len(tables)
     tiles = vocab // LANES
     blocks = seq_len // LANES
-    me = lax.axis_index("narrow")
+    me = lax.axis_index(NARROW)
     sibling, partner, mine, other = group_places(seq_len)
-    peers = [{"narrow": lax.rem(me + k, 4)} for k in range(1, 4)]
-    greet(peers)
+    peers = [{NARROW: lax.rem(me + k, 4)} for k in range(1, 4)]
+    greet(peers + carry.peers())
+    carry.start()
     sems = (send, recv)
     trade = Exchange((near_out, near_in, far_out, far_in), sems, 0, sibling, partner)
     share = Share(branch, sems, 2, sibling, mine, chunk)
@@ -1398,7 +1465,8 @@
 
     def ask(b, _):
         rows = rows_at(0, b, LANES)
-        logits[rows, :] = dot_nn(normed[rows, :], table[...])
+        for k, table in enumerate(tables):
+            logits[rows, k * piece_width : (k + 1) * piece_width] = dot_nn(normed[rows, :], table[...])
         here = info[:, rows]
         at_noised = spread(here[0:1] - first)
         at_clean = spread(here[1:2] - first)
@@ -1528,7 +1596,11 @@
         base = start // LANES + j * (chunk // LANES)
         for b in range(chunk // LANES):
             pull(base + b)
-        return dot_nt(grads[rows_at(start, j, chunk), :], table[...])
+        total = None
+        for k, table in enumerate(tables):
+            part = dot_nt(grads[rows_at(start, j, chunk), k * piece_width : (k + 1) * piece_width], table[...])
+            total = part if total is None else total + part
+        return total
 
     trade.give(0, partial(other, 0))
     for j in range(CHUNKS):
@@ -1536,11 +1608,12 @@
             trade.give(j + 1, partial(other, j + 1))
         trade.pass_on(j, partial(mine, j))
     turned[...] = jnp.transpose(normed[...])
-    weight_grad(turned, grads, d_table)
-    gain_total = jnp.zeros(gain.shape, F32)
+    for k, d_table in enumerate(d_tables):
+        weight_grad(turned, grads.at[:, k * piece_width : (k + 1) * piece_width], d_table)
+    gain_total = jnp.zeros((1, gain.shape[1]), F32)
     for j in range(CHUNKS):
         rows = rows_at(0, j, chunk)
-        back, gain_part = norm_back(trade.take(j), value[rows, :], gain[...])
+        back, gain_part = norm_back(trade.take(j), value[rows, :], gain[row : row + 1, :])
         gain_total = gain_total + gain_part
         grad_out[rows, :] = back
         share.put(j, back.astype(BF16))
@@ -1557,24 +1630,25 @@
         return 0
 
     lax.fori_loop(0, blocks, finish, 0)
-
-
-def loss_and_back(normed, table, info, value, gain, collective_id):
+    carry.finish()
+
+
+def loss_and_back(row, normed, tables, info, value, gain, collective_id, loads):
     seq_len, width = normed.shape
-    vocab = table.shape[1]
+    vocab = sum(table.shape[1] for table in tables)
     half, chunk, blocks = seq_len // 2, seq_len // 2 // CHUNKS, seq_len // LANES
-    return pl.pallas_call(
-        loss_kernel,
-        out_shape=(
+    return run(
+        functools.partial(loss_kernel, len(tables), row),
+        "loss_and_back",
+        [normed, info, value, gain, *tables],
+        [
             jax.ShapeDtypeStruct((half, width), F32),
             jax.ShapeDtypeStruct((seq_len, width), BF16),
-            jax.ShapeDtypeStruct(table.shape, BF16),
-            jax.ShapeDtypeStruct(gain.shape, F32),
+            jax.ShapeDtypeStruct((1, width), F32),
             jax.ShapeDtypeStruct((1, seq_len), F32),
-        ),
-        in_specs=[whole_vmem()] * 5,
-        out_specs=(whole_vmem(),) * 5,
-        scratch_shapes=[
+        ]
+        + [jax.ShapeDtypeStruct(table.shape, BF16) for table in tables],
+        [
             pltpu.VMEM((seq_len, vocab), F32),
             pltpu.VMEM((seq_len, vocab), BF16),
             pltpu.VMEM((blocks, 2, LANES, LANES), F32),
@@ -1585,76 +1659,271 @@
             pltpu.VMEM((3, blocks, 8, LANES), F32),
         ]
         + Exchange.scratch(chunk, width, BACKWARD_KIND)
-        + [pltpu.SemaphoreType.DMA((3, CHUNKS)), pltpu.SemaphoreType.DMA((3, CHUNKS))]
+        + sems(3)
         + [pltpu.SemaphoreType.DMA((3, blocks))] * 4,
-        compiler_params=pltpu.CompilerParams(
-            collective_id=collective_id, has_side_effects=True, vmem_limit_bytes=VMEM_LIMIT
-        ),
-        name="loss_and_back",
-    )(normed, table, info, value, gain)
-
-
-def scalars_kernel(given, out, near, along, across, send, recv):
-    count = 2 * along.shape[0]
-    me, slow, fast, slows = wide_places(count)
-    place = lax.axis_index("narrow")
-    beside = me + 1 - 2 * fast
+        collective_id,
+        loads,
+    )
+
+
+def sum_ways(place, me, slow, fast, slows, group):
+    near = [{NARROW: lax.rem(place + step, group)} for step in range(1, group)]
+    return near, {WIDE: me + 1 - 2 * fast}
+
+
+def tail_kernel(
+    layers, branch, ids_all, losses, full, *refs, carry,
+):
+    gain_parts, refs = refs[: 2 * layers + 1], refs[2 * layers + 1 :]
+    squares, refs = refs[: len(refs) - 31], refs[len(refs) - 31 :]
+    tail_body(branch, ids_all, losses, full, gain_parts, squares, *refs, carry)
+
+
+def tail_body(
+    branch, ids_all, losses, full, gain_parts, squares,
+    d_table, d_full, d_small, scalars,
+    out_blocks, all_in, picks, total, gains_out, gains_in, blocks, block_in, line_out, line_in,
+    fast_in, sums, slow_in, near, along, across,
+    wide_send, wide_recv, far_send, far_recv, near_send, near_recv,
+    pair_send, pair_recv, line_send, line_recv, sum_sems,
+    carry,
+):
+    seq_len, width = branch.shape
+    quarter, half = seq_len // 4, seq_len // 2
+    owners = ids_all.shape[0]
+    share, vocab = d_table.shape
+    sibling, partner, mine, other = group_places(seq_len)
+    place = lax.axis_index(NARROW)
+    side = lax.div(place, 2)
+    me, slow, fast, slows = wide_places(owners)
+    beside = {WIDE: me + 1 - 2 * fast}
     group = near.shape[0]
+    first = place * vocab
+    around = [lax.rem(me + step, owners) for step in range(owners)]
+    at_quarter = pl.multiple_of(mine + side * quarter, quarter)
+    across_quarter = pl.multiple_of(mine + (1 - side) * quarter, quarter)
+
+    def along_way(step):
+        return {WIDE: 2 * lax.rem(slow + step, slows) + fast}
+
+    def wide_copy(step):
+        return remote(
+            out_blocks.at[around[step]], all_in.at[me, pl.ds(at_quarter, quarter)],
+            wide_send.at[step], wide_recv.at[step], {WIDE: around[step]},
+        )
+
+    def far_copy(step):
+        rows = all_in.at[around[step], pl.ds(at_quarter, quarter)]
+        return remote(rows, rows, far_send.at[step], far_recv.at[step], partner)
 
     def near_copy(step):
+        rows = all_in.at[around[step], pl.ds(mine, half)]
+        return remote(rows, rows, near_send.at[step], near_recv.at[step], sibling)
+
+    def block(owner):
+        return full.at[:, owner]
+
+    def pair_copy(step):
         return remote(
-            near.at[place], near.at[place], send.at[0, step - 1], recv.at[0, step - 1],
-            {"narrow": lax.rem(place + step, group)},
+            block(2 * lax.rem(slow + step, slows) + 1 - fast), fast_in.at[step],
+            pair_send.at[step], pair_recv.at[step], beside,
         )
 
-    def along_copy(step):
+    def line_copy(step):
+        return remote(sums.at[step], slow_in.at[step], line_send.at[step], line_recv.at[step], along_way(step))
+
+    def gain_near():
+        return remote(gains_out, gains_in, sum_sems.at[0, 0], sum_sems.at[1, 0], sibling)
+
+    def gain_pair(step):
         return remote(
-            along.at[slow], along.at[slow], send.at[1, step - 1], recv.at[1, step - 1],
-            {"wide": 2 * lax.rem(slow + step, slows) + fast},
+            blocks.at[2 * lax.rem(slow + step, slows) + 1 - fast], block_in.at[step],
+            sum_sems.at[2, step], sum_sems.at[3, step], beside,
         )
 
-    greet(
-        [{"narrow": lax.rem(place + step, group)} for step in range(1, group)]
-        + [{"wide": 2 * lax.rem(slow + step, slows) + fast} for step in range(1, slows)]
-        + [{"wide": beside}]
-    )
-    near[place] = given[...]
+    def gain_line(step):
+        return remote(line_out.at[step], line_in.at[step], sum_sems.at[4, step], sum_sems.at[5, step], along_way(step))
+
+    near_ways = [{NARROW: lax.rem(place + step, group)} for step in range(1, group)]
+    greet([{WIDE: device} for device in around[1:]] + near_ways)
+    for step in range(slows):
+        pair_copy(step).start()
+    gains_out[...] = jnp.zeros(gains_out.shape, F32)
+    for row, part in enumerate(gain_parts):
+        gains_out[row : row + 1, :] = part[...]
+    gain_near().start()
+    for owner in range(owners):
+        out_blocks[owner] = dot_nt(
+            branch[pl.ds(at_quarter, quarter), :], feature_places(owner, width, share)
+        ).astype(BF16)
+    for step in range(1, owners):
+        wide_copy(step).start()
+    all_in[me, pl.ds(at_quarter, quarter), :] = out_blocks[me]
+    carry.start()
+    gain_near().wait_recv()
+    both = gains_out[...] + gains_in[...]
+    for owner in range(owners):
+        blocks[owner] = lax.dot_general(
+            both, feature_places(owner, width, share).astype(F32), (((1,), (1,)), ((), ())),
+            precision=lax.Precision.HIGHEST, preferred_element_type=F32,
+        )
+    for step in range(slows):
+        gain_pair(step).start()
+
+    def hand_on(step):
+        if step:
+            wide_copy(owners - step).wait_recv()
+        far_copy(step).start()
+
+    def hand_over(step):
+        far_copy(step).wait_recv()
+        near_copy(step).start()
+
+    def gather_grad(step, first_turn):
+        near_copy(step).wait_recv()
+        row = around[step]
+
+        def make(b, _):
+            rows = rows_at(0, b, LANES)
+            for t, pick in enumerate(token_picks(ids_all[row, pl.ds(b, 1), :], vocab, first)):
+                picks[rows, t * LANES : (t + 1) * LANES] = pick
+            return 0
+
+        lax.fori_loop(0, seq_len // LANES, make, 0)
+        turned = jnp.transpose(all_in[row])
+
+        def columns(i, _):
+            where = pl.ds(pl.multiple_of(i * TILE, TILE), TILE)
+            part = dot_nn(turned, picks[:, where])
+            total[:, where] = part if first_turn else total[:, where] + part
+            return 0
+
+        lax.fori_loop(0, vocab // TILE, columns, 0)
+
+    order = [0] + list(range(1, owners))
+    for turn in range(owners + 2):
+        if turn < owners:
+            hand_on(order[turn])
+        if 1 <= turn < owners + 1:
+            hand_over(order[turn - 1])
+        if turn == 1:
+            for step in list(range(1, slows)) + [0]:
+                pair_copy(step).wait_recv()
+                owner = 2 * lax.rem(slow + step, slows) + fast
+                sums[step] = (block(owner)[...].astype(F32) + fast_in[step].astype(F32)).astype(BF16)
+                if step:
+                    line_copy(step).start()
+            for step in list(range(1, slows)) + [0]:
+                gain_pair(step).wait_recv()
+                line_out[step] = blocks[2 * lax.rem(slow + step, slows) + fast] + block_in[step]
+                if step:
+                    gain_line(step).start()
+        if turn >= 2:
+            gather_grad(order[turn - 2], turn == 2)
+    d_table[...] = total[:share, :]
+    result = sums[0].astype(F32)
+    small = line_out[0]
+    for step in range(1, slows):
+        line_copy(step).wait_recv()
+        result = result + slow_in[step].astype(F32)
+        gain_line(step).wait_recv()
+        small = small + line_in[step]
+    d_full[...] = result
+    d_small[...] = small
+    carry.finish()
+    square = jnp.sum(result * result) + jnp.sum(d_table[...] * d_table[...])
+    for part in squares:
+        square = square + part[0, 0]
+    for load in carry.loads:
+        square = square + load.squares[0, 0]
+    lead = (place == 0).astype(F32)
+    square = square + lead * jnp.sum(small * small)
+    lanes = lax.broadcasted_iota(jnp.int32, (8, LANES), 1)
+    given = jnp.where(lanes == 0, square, jnp.where(lanes == 1, lead * jnp.sum(losses[...]), 0.0))
+
+    def scalar_near(step):
+        return remote(near.at[place], near.at[place], sum_sems.at[6, step], sum_sems.at[7, step], near_ways[step - 1])
+
+    def scalar_line(step):
+        return remote(along.at[slow], along.at[slow], sum_sems.at[8, step], sum_sems.at[9, step], along_way(step))
+
+    near[place] = given
     for step in range(1, group):
-        near_copy(step).start()
+        scalar_near(step).start()
     for step in range(1, group):
-        near_copy(step).wait()
+        scalar_near(step).wait()
     along[slow] = jnp.sum(near[...], axis=0)
     for step in range(1, slows):
-        along_copy(step).start()
+        scalar_line(step).start()
     for step in range(1, slows):
-        along_copy(step).wait()
+        scalar_line(step).wait()
     across[0] = jnp.sum(along[...], axis=0)
-    last = remote(across.at[0], across.at[1], send.at[2, 0], recv.at[2, 0], {"wide": beside})
+    last = remote(across.at[0], across.at[1], sum_sems.at[10, 0], sum_sems.at[11, 0], beside)
     last.start()
     last.wait()
-    out[...] = across[0] + across[1]
-
-
-def sum_scalars(given, wide, narrow, collective_id):
-    steps = max(wide // 2, narrow) - 1
-    return pl.pallas_call(
-        scalars_kernel,
-        out_shape=jax.ShapeDtypeStruct(given.shape, F32),
-        in_specs=[whole_vmem()],
-        out_specs=whole_vmem(),
-        scratch_shapes=[
-            pltpu.VMEM((narrow,) + given.shape, F32),
-            pltpu.VMEM((wide // 2,) + given.shape, F32),
-            pltpu.VMEM((2,) + given.shape, F32),
-            pltpu.SemaphoreType.DMA((3, steps)),
-            pltpu.SemaphoreType.DMA((3, steps)),
+    scalars[...] = across[0] + across[1]
+    gain_near().wait_send()
+    for step in range(owners):
+        far_copy(step).wait_send()
+        near_copy(step).wait_send()
+        if step:
+            wide_copy(step).wait_send()
+    for step in range(slows):
+        pair_copy(step).wait_send()
+        gain_pair(step).wait_send()
+        if step:
+            line_copy(step).wait_send()
+            gain_line(step).wait_send()
+
+
+def tail(branch, ids_all, losses, full, gain_parts, squares, share, vocab, group, collective_id, loads):
+    seq_len, width = branch.shape
+    owners = ids_all.shape[0]
+    slows = owners // 2
+    shape = full.shape[:1] + full.shape[2:]
+    dma = pltpu.SemaphoreType.DMA
+    small = (8, LANES)
+    return run(
+        functools.partial(tail_kernel, (len(gain_parts) - 1) // 2),
+        "tail",
+        [branch, ids_all, losses, full, *gain_parts, *squares],
+        [
+            jax.ShapeDtypeStruct((share, vocab), F32),
+            jax.ShapeDtypeStruct(shape, F32),
+            jax.ShapeDtypeStruct(small, F32),
+            jax.ShapeDtypeStruct(small, F32),
         ],
-        compiler_params=pltpu.CompilerParams(collective_id=collective_id, has_side_effects=True),
-        name="sum_scalars",
-    )(given)
-
-
-def shares_tile(wide, narrow, noised, attn_in, attn_out, ffn_in):
+        [
+            pltpu.VMEM((owners, seq_len // 4, LANES), BF16),
+            pltpu.VMEM((owners, seq_len, LANES), BF16),
+            pltpu.VMEM((seq_len, vocab), BF16),
+            pltpu.VMEM((LANES, vocab), F32),
+            pltpu.VMEM((8, width), F32),
+            pltpu.VMEM((8, width), F32),
+            pltpu.VMEM((owners,) + small, F32),
+            pltpu.VMEM((slows,) + small, F32),
+            pltpu.VMEM((slows,) + small, F32),
+            pltpu.VMEM((slows,) + small, F32),
+            pltpu.VMEM((slows,) + shape, BF16),
+            pltpu.VMEM((slows,) + shape, BF16),
+            pltpu.VMEM((slows,) + shape, BF16),
+            pltpu.VMEM((group,) + small, F32),
+            pltpu.VMEM((slows,) + small, F32),
+            pltpu.VMEM((2,) + small, F32),
+        ]
+        + [dma((owners,))] * 6
+        + [dma((slows,))] * 4
+        + [dma((12, max(slows, group)))],
+        collective_id,
+        loads,
+    )
+
+
+PIECES = 4
+TABLE, ATTN_IN, ATTN_OUT, FFN_IN, FFN_OUT = range(5)
+
+
+def shares_tile(wide, narrow, noised, attn_out, ffn_in, tables):
     rows, seq_len = noised.shape
     return (
         narrow == 4
@@ -1662,13 +1931,16 @@
         and rows == 1
         and seq_len % (2 * CHUNKS * 128) == 0
         and attn_out.shape[1] % 16 == 0
+        and attn_out.shape[1] <= LANES
         and ffn_in.shape[2] % 128 == 0
+        and tables.shape[1] == attn_out.shape[1]
+        and tables.shape[2] % (PIECES * TILE) == 0
     )
 
 
 def per_device(wide, narrow, *arrays):
-    noised, attn_in, attn_out, ffn_in = arrays[0], arrays[5], arrays[6], arrays[7]
-    if shares_tile(wide, narrow, noised, attn_in, attn_out, ffn_in):
+    noised, attn_out, ffn_in, tables = arrays[0], arrays[6], arrays[7], arrays[9]
+    if shares_tile(wide, narrow, noised, attn_out, ffn_in, tables):
         return tiled_device(wide, *arrays)
     return general_device(*arrays)
 
@@ -1704,65 +1976,88 @@
     mask = counted.reshape(-1).astype(jnp.float32)
     seq_len = mask.shape[0]
     half = seq_len // 2
-    core = lax.rem(lax.axis_index("narrow"), 2)
-    small = jnp.pad(
-        jnp.concatenate(
-            [
-                lax.reduce_precision(gains, 8, 7),
-                jnp.full((1, gain_cols), jnp.sum(mask), jnp.float32),
-            ]
-        ),
-        ((0, -(gain_rows + 1) % 8), (0, -gain_cols % 128)),
-    )
-    first_layer = [attn_in[0], attn_out[0], ffn_in[0], ffn_out[0]]
+    core = lax.rem(lax.axis_index(NARROW), 2)
+    share, vocab = tables.shape[1:]
     leads = (1, 0, 0, 0)
-    small_all, table_first, *weights = gather_wide(
-        [small, tables[0]] + first_layer, (0, 0) + leads, [F32] + [BF16] * 5, wide, 0
-    )
-    token_total = jnp.sum(small_all[:, gain_rows, 0])
-    gain_w = small_all[:, :gain_rows, :gain_cols].transpose(1, 0, 2).reshape(gain_rows, 1, -1)
-    table_first = table_first.reshape(-1, tables.shape[2])
+    four = (attn_in, attn_out, ffn_in, ffn_out)
 
     def joined(value, lead):
         return value.reshape(value.shape[:lead] + (-1,) + value.shape[lead + 2 :])
 
-    noised_flat = noised.reshape(-1)
-    clean_flat = clean.reshape(-1)
     step_flat = timesteps.reshape(-1)
-    vocab_local = tables.shape[2]
-    vocab_ids = lax.axis_index("narrow") * vocab_local + jnp.arange(vocab_local, dtype=jnp.int32)
     extra = time_features(lax.dynamic_slice(step_flat, (core * half,), (half,)))
-    residual, normed = embed(noised_flat[:, None], extra, table_first, gain_w[0], 1)
+    ids = noised.reshape(-1, LANES)
+    quarter = vocab // PIECES
+    windows = [(k * quarter, quarter) for k in range(PIECES)]
+    (residual, normed, gain_w, counts, ids_all), carried = embed(
+        ids, counted, gains, extra, tables, wide, 0,
+        [
+            GatherLoad(attn_in, 0, 1, wide, EARLY),
+            GatherLoad(attn_out, 0, 0, wide, MIDDLE),
+            GatherLoad(ffn_in, 0, 0, wide, LAST, late=True),
+            SlowLoad(ffn_out, 0, 0, wide),
+        ],
+    )
+    token_total = counts[gain_rows, 0]
+    query_w, output_w, expand_w, reduce_line = carried
+    next_id = 1
+    tables_w = []
+    table_lines = []
     key_seg, query_seg = segments.reshape(-1, 1), segments.reshape(1, -1)
     kept = []
     for layer in range(layers):
-        query_w, output_w, expand_w, reduce_w = four = [joined(value, lead) for value, lead in zip(weights, leads)]
-        if layer + 1 < layers:
+        more = layer + 1 < layers
+        loads = [FastLoad(reduce_line, 0, wide)]
+        if more:
+            loads.append(SlowLoad(ffn_in, layer + 1, 0, wide))
+        else:
+            loads.append(SlowLoad(tables, 1, 0, wide, windows[1]))
+        query_w, output_w, expand_w = joined(query_w, 1), joined(output_w, 0), joined(expand_w, 0)
+        (projected, mixed), carried = attention(normed, query_w, key_seg, query_seg, next_id, loads)
+        reduce_w = joined(carried[0], 0)
+        if more:
             loads = [
-                GatherLoad(value, layer + 1, lead, wide)
-                for value, lead in zip((attn_in, attn_out, ffn_in, ffn_out), leads)
+                FastLoad(carried[1], 0, wide),
+                GatherLoad(attn_in, layer + 1, 1, wide, EARLY),
+                GatherLoad(attn_out, layer + 1, 0, wide, EARLY),
+                SlowLoad(ffn_out, layer + 1, 0, wide),
             ]
+            if layer + 2 == layers:
+                loads.append(SlowLoad(tables, 1, 0, wide, windows[0]))
         else:
-            loads = [GatherLoad(tables, 1, 0, wide, 3)]
-        projected, mixed = attention(normed, query_w, key_seg, query_seg)
-        (middle, normed_two, before, after, result, normed_next), weights = ffn_forward(
-            mixed, residual, output_w, expand_w, reduce_w,
-            gain_w[2 * layer + 1], gain_w[2 * layer + 2], 2 + layer, loads,
+            loads = [
+                FastLoad(table_line, 0, wide),
+                FastLoad(carried[1], 0, wide),
+                GatherLoad(tables, 1, 0, wide, EARLY, windows[2]),
+                GatherLoad(tables, 1, 0, wide, MIDDLE, windows[3]),
+            ]
+        (middle, normed_two, before, after, result, normed_next), carried = ffn_forward(
+            layer, mixed, residual, output_w, expand_w, reduce_w, gain_w, next_id + 1, loads
         )
-        kept.append((residual, normed, projected, mixed, middle, normed_two, before, after, four))
+        next_id += 2
+        kept.append(
+            (residual, normed, projected, mixed, middle, normed_two, before, after)
+            + (query_w, output_w, expand_w, reduce_w)
+        )
         residual, normed = result, normed_next
-    table_last = joined(weights[0], 0)
-
+        if more:
+            expand_w, query_w, output_w, reduce_line, *rest = carried
+            if rest:
+                table_line = rest[0]
+        else:
+            tables_w = [joined(value, 0) for value in carried]
+
+    noised_flat, clean_flat = noised.reshape(-1), clean.reshape(-1)
     info = jnp.stack(
         [noised_flat.astype(F32), clean_flat.astype(F32), step_flat.astype(F32), mask / token_total, mask]
         + [jnp.zeros_like(mask)] * 3
     )
-    grad, branch, d_last, gain_final, losses = loss_and_back(
-        normed, table_last, info, residual, gain_w[2 * layers], 2 + layers
-    )
-    next_id = 3 + layers
+    (grad, branch, gain_final, losses, *d_last), _ = loss_and_back(
+        2 * layers, normed, tables_w, info, residual, gain_w, next_id, []
+    )
+    next_id += 1
     gain_grads = [None] * (2 * layers) + [gain_final]
-    own = {}
+    own, squares = {}, []
 
     def by_owner(value, lead):
         shape = value.shape
@@ -1781,73 +2076,51 @@
         def back(self, results):
             pairs, lines = self.now
             self.halfway = self.halfway + [(key, sums) for (key, _, _), sums in zip(pairs, results)]
-            for (key, _), total in zip(lines, results[len(pairs) :]):
-                own[key] = total
+            for k, (key, _) in enumerate(lines):
+                own[key] = results[len(pairs) + 2 * k]
+                squares.append(results[len(pairs) + 2 * k + 1])
 
     route = Route()
-    route.waiting = [(("tables", 1), d_last, 0)]
+    route.waiting = [((TABLE, k), piece, 0) for k, piece in enumerate(d_last)]
     for layer in reversed(range(layers)):
-        residual, normed, projected, mixed, middle, normed_two, before, after, four = kept[layer]
-        query_w, output_w, expand_w, reduce_w = four
+        residual, normed, projected, mixed, middle, normed_two, before, after, *four_w = kept[layer]
+        query_w, output_w, expand_w, reduce_w = four_w
         top = layer == layers - 1
-        loads = route.take(1, 3)
+        loads = route.take(3 if top else 2, 3)
         (grad_middle, grad_attn, grad_mixed, d_red, d_in, d_out, gain_two), carried = ffn_backward(
-            grad, branch, reduce_w, expand_w, output_w, before, after,
-            normed_two, middle, gain_w[2 * layer + 1], mixed, next_id, loads,
+            2 * layer + 1, grad, branch, reduce_w, expand_w, output_w, before, after,
+            normed_two, middle, gain_w, mixed, next_id, loads,
         )
         route.back(carried)
-        route.waiting += [(("ffn_out", layer), d_red, 0), (("ffn_in", layer), d_in, 0)]
-        loads = route.take(1, 0 if top else 1)
+        route.waiting += [((FFN_OUT, layer), d_red, 0), ((FFN_IN, layer), d_in, 0)]
+        loads = route.take(1, 2)
         (grad_projected,), carried = attention_back(projected, grad_mixed, key_seg, query_seg, next_id + 1, loads)
         route.back(carried)
-        route.waiting += [(("attn_out", layer), d_out, 0)]
-        loads = route.take(3, 1)
+        route.waiting += [((ATTN_OUT, layer), d_out, 0)]
+        loads = route.take(2, 2)
         (grad, branch, d_query, gain_one), carried = norm_backward(
-            grad_projected, query_w, normed, residual, gain_w[2 * layer], grad_middle,
+            2 * layer, grad_projected, query_w, normed, residual, gain_w, grad_middle,
             math.sqrt(D) if layer == 0 else None, next_id + 2, loads,
         )
         route.back(carried)
-        route.waiting += [(("attn_in", layer), d_query, 1)]
+        route.waiting += [((ATTN_IN, layer), d_query, 1)]
         next_id += 3
         gain_grads[2 * layer], gain_grads[2 * layer + 1] = gain_one, gain_two
-    picks = (noised_flat[:, None] == vocab_ids[None, :]).astype(jnp.bfloat16)
-    d_first = jnp.einsum("sd,sv->dv", branch, picks, preferred_element_type=jnp.float32)
-
-    small_grad = jnp.pad(
-        jnp.concatenate(gain_grads).reshape(gain_rows, wide, gain_cols).transpose(1, 0, 2),
-        ((0, 0), (0, -gain_rows % 8), (0, -gain_cols % 128)),
-    )
-    rest = route.waiting + [(("tables", 0), d_first.astype(BF16), 0)]
+    (key, last_full, _), = route.waiting
     lines = route.halfway
-    (*sums, total_small), carried = scatter_wide(
-        [by_owner(value, lead) for _, value, lead in rest] + [small_grad],
-        [lead for _, _, lead in rest] + [0],
-        next_id,
+    (own_first, own[key], total_small, scalars), carried = tail(
+        branch, ids_all, losses, by_owner(last_full, 1), gain_grads, squares, share, vocab, 4, next_id,
         [LineLoad(value, wide) for _, value in lines],
     )
-    for (key, _, _), total in zip(rest, sums):
-        own[key] = total
-    for (key, _), total in zip(lines, carried):
-        own[key] = total
-    grad_attn_in, grad_attn_out, grad_ffn_in, grad_ffn_out, grad_tables = [
-        jnp.stack([own[name, index] for index in range(2)])
-        for name in ("attn_in", "attn_out", "ffn_in", "ffn_out", "tables")
+    for k, (key, _) in enumerate(lines):
+        own[key] = carried[2 * k]
+    grad_attn_in, grad_attn_out, grad_ffn_in, grad_ffn_out = [
+        jnp.stack([own[name, index] for index in range(layers)]) for name in (ATTN_IN, ATTN_OUT, FFN_IN, FFN_OUT)
     ]
+    grad_tables = jnp.stack([own_first, jnp.concatenate([own[TABLE, k] for k in range(PIECES)], axis=1)])
     grad_gains = total_small[:gain_rows, :gain_cols]
-    narrow_first = (lax.axis_index("narrow") == 0).astype(jnp.float32)
-    squares = (
-        jnp.sum(grad_attn_in * grad_attn_in)
-        + jnp.sum(grad_attn_out * grad_attn_out)
-        + jnp.sum(grad_ffn_in * grad_ffn_in)
-        + jnp.sum(grad_ffn_out * grad_ffn_out)
-        + jnp.sum(grad_tables * grad_tables)
-        + narrow_first * jnp.sum(grad_gains * grad_gains)
-    )
-    lanes = lax.broadcasted_iota(jnp.int32, (8, 128), 1)
-    both = jnp.where(lanes == 0, squares, jnp.where(lanes == 1, narrow_first * jnp.sum(losses), 0.0))
-    both = sum_scalars(both, wide, 4, next_id + 1)
-    squares, loss_sum = both[0, 0], both[0, 1]
-    grad_norm = jnp.sqrt(squares)
+    total_square, loss_sum = scalars[0, 0], scalars[0, 1]
+    grad_norm = jnp.sqrt(total_square)
     factor = jnp.minimum(1.0, CLIP_NORM / (grad_norm + 1e-06))
     results = [loss_sum, token_total, grad_norm]
     for weight, gradient, first, second, decay, rate in (
@@ -1863,31 +2136,31 @@
 
 
 def solution(mesh):
-    wide, narrow = mesh.shape["wide"], mesh.shape["narrow"]
+    wide, narrow = mesh.shape[WIDE], mesh.shape[NARROW]
     placed = (
-        P("wide", None),
-        P("wide", None),
-        P("wide", None),
-        P("wide", None),
-        P("wide", None),
-        P(None, None, "wide", "narrow"),
-        P(None, "wide", "narrow"),
-        P(None, "wide", "narrow"),
-        P(None, "wide", "narrow"),
-        P(None, "wide", "narrow"),
-        P(None, "wide"),
-        P(None, None, "wide", "narrow"),
-        P(None, "wide", "narrow"),
-        P(None, "wide", "narrow"),
-        P(None, "wide", "narrow"),
-        P(None, "wide", "narrow"),
-        P(None, "wide"),
-        P(None, None, "wide", "narrow"),
-        P(None, "wide", "narrow"),
-        P(None, "wide", "narrow"),
-        P(None, "wide", "narrow"),
-        P(None, "wide", "narrow"),
-        P(None, "wide"),
+        P(WIDE, None),
+        P(WIDE, None),
+        P(WIDE, None),
+        P(WIDE, None),
+        P(WIDE, None),
+        P(None, None, WIDE, NARROW),
+        P(None, WIDE, NARROW),
+        P(None, WIDE, NARROW),
+        P(None, WIDE, NARROW),
+        P(None, WIDE, NARROW),
+        P(None, WIDE),
+        P(None, None, WIDE, NARROW),
+        P(None, WIDE, NARROW),
+        P(None, WIDE, NARROW),
+        P(None, WIDE, NARROW),
+        P(None, WIDE, NARROW),
+        P(None, WIDE),
+        P(None, None, WIDE, NARROW),
+        P(None, WIDE, NARROW),
+        P(None, WIDE, NARROW),
+        P(None, WIDE, NARROW),
+        P(None, WIDE, NARROW),
+        P(None, WIDE),
     )
     return jax.shard_map(
         functools.partial(per_device, wide, narrow),
@@ -1897,30 +2170,30 @@
             P(),
             P(),
             P(),
-            P(None, None, "wide", "narrow"),
-            P(None, None, "wide", "narrow"),
-            P(None, None, "wide", "narrow"),
-            P(None, None, "wide", "narrow"),
-            P(None, "wide", "narrow"),
-            P(None, "wide", "narrow"),
-            P(None, "wide", "narrow"),
-            P(None, "wide", "narrow"),
-            P(None, "wide", "narrow"),
-            P(None, "wide", "narrow"),
-            P(None, "wide", "narrow"),
-            P(None, "wide", "narrow"),
-            P(None, "wide", "narrow"),
-            P(None, "wide", "narrow"),
-            P(None, "wide", "narrow"),
-            P(None, "wide", "narrow"),
-            P(None, "wide", "narrow"),
-            P(None, "wide", "narrow"),
-            P(None, "wide", "narrow"),
-            P(None, "wide", "narrow"),
-            P(None, "wide"),
-            P(None, "wide"),
-            P(None, "wide"),
-            P(None, "wide"),
+            P(None, None, WIDE, NARROW),
+            P(None, None, WIDE, NARROW),
+            P(None, None, WIDE, NARROW),
+            P(None, None, WIDE, NARROW),
+            P(None, WIDE, NARROW),
+            P(None, WIDE, NARROW),
+            P(None, WIDE, NARROW),
+            P(None, WIDE, NARROW),
+            P(None, WIDE, NARROW),
+            P(None, WIDE, NARROW),
+            P(None, WIDE, NARROW),
+            P(None, WIDE, NARROW),
+            P(None, WIDE, NARROW),
+            P(None, WIDE, NARROW),
+            P(None, WIDE, NARROW),
+            P(None, WIDE, NARROW),
+            P(None, WIDE, NARROW),
+            P(None, WIDE, NARROW),
+            P(None, WIDE, NARROW),
+            P(None, WIDE, NARROW),
+            P(None, WIDE),
+            P(None, WIDE),
+            P(None, WIDE),
+            P(None, WIDE),
         ),
         check_vma=False,
     )

time: 709 us -> 591 us (0.83)
  Pallas kernels: 640 us -> 557 us
  other arithmetic: 29.2 us -> 18.8 us
    pallas_call x6 -> x0, Pallas kernels: 226 us -> none  [the longest x1 97.8 us: gather_wide(): pl.pallas_call(functools.partial(gather_kernel, arrays, leads), out_shape...]
    pallas_call x9 -> x13, Pallas kernels: 414 us -> 557 us  [run(): pl.pallas_call(kernel, out_shape=tuple(outs) + tuple((out for load in loa...]
    reduce_sum x9 -> x0, other arithmetic: 10.8 us -> none  [the longest x1 1.83 us: tiled_device(): jnp.sum(grad_attn_in * grad_attn_in)]
where the time goes in v4:
time: 591 us; the launch traced here: 587 us
  Pallas kernels  557 us (94%)
  other arithmetic  18.8 us (3%)
  local copies, waits for them, and re-layouts  8.06 us (1%)
    pallas_call x13, Pallas kernels, run(): pl.pallas_call(kernel, out_shape=tuple(outs) + tuple((out for load in loa...  557 us

profile of v4, /device:TPU:0, one launch (start us, length us, event | category | flops | bytes accessed | tf_op | source)
XLA Modules:
  0.0 587.3 jit_solution(1316631119018855617)
XLA Ops:
  0.7 0.7 dynamic-slice_convert_fusion
  1.4 0.7 convert_element_type.48
  2.1 0.7 convert_element_type.47
  2.8 0.7 convert_element_type.49
  3.5 0.7 convert_element_type.50
  4.1 1.7 copy.50.refs_2_
  5.8 2.8 multiply_sine_fusion
  8.7 1.3 pad_maximum_fusion.refs_3_
  9.9 84.2 %embed.1 = (f32[512,768]{1,0:T(8,128)}, bf16[1024,768]{1,0:T(8,128)(2,1)}, f32[8,768]{1,0:T(8,128)}, f32[8,128]{1,0:T(8,128)}, s32[8,8,128]{2,1,0:T(8,128)}, /*i...) custom-call(s32[8,128]{1,0:T(8,128)} %bitcast.83, ...), custom_call_target="tpu_custom_call" | custom-call | tf_op jit(solution)/shard_map/embed/pallas_call | solution.py:794
  94.2 1.2 slice.12
  95.4 0.7 broadcast_divide_fusion
  96.0 0.7 stack.57.refs_1_
  96.7 26.2 %attention.2 = (bf16[3,1024,192]{2,1,0:T(8,128)(2,1)}, bf16[1024,192]{1,0:T(8,128)(2,1)}, bf16[8,96,768]{2,1,0:T(8,128)(2,1)}, bf16[4,96,768]{2,1,0:T(8,128)(2,1)}) custom-call(bf16[1024,768]{1,0:T(8,128)(2,1)} %get-tuple-element.129.refs_0_.refs_2_, bf16[3,768,192]{2,1,0:T(8,128)(2,1)} %bitcast.51, s32[1024,1]{1,0:T(8,128)} %copy.50.refs_2_, ...), custom_call_target="tpu_custom_call" | custom-call | tf_op jit(solution)/shard_map/attention/pallas_call | solution.py:794
  123.0 49.5 %ffn_forward.2 = (f32[512,768]{1,0:T(8,128)}, bf16[1024,768]{1,0:T(8,128)(2,1)}, f32[1024,768]{1,0:T(8,128)}, bf16[1024,768]{1,0:T(8,128)(2,1)}, f32[512,768]{1,...) custom-call(bf16[1024,192]{1,0:T(8,128)(2,1)} %get-tuple-element.133, ...), custom_call_target="tpu_custom_call" | custom-call | tf_op jit(solution)/shard_map/ffn_forward/pallas_call | solution.py:794
  172.5 24.9 %attention.3 = (bf16[3,1024,192]{2,1,0:T(8,128)(2,1)}, bf16[1024,192]{1,0:T(8,128)(2,1)}, bf16[8,96,768]{2,1,0:T(8,128)(2,1)}, bf16[4,96,512]{2,1,0:T(8,128)(2,1)}) custom-call(bf16[1024,768]{1,0:T(8,128)(2,1)} %get-tuple-element.140.refs_0_.refs_2_, bf16[3,768,192]{2,1,0:T(8,128)(2,1)} %bitcast.49, s32[1024,1]{1,0:T(8,128)} %copy.50.refs_2_, ...), custom_call_target="tpu_custom_call" | custom-call | tf_op jit(solution)/shard_map/attention/pallas_call | solution.py:794
  197.4 53.4 %ffn_forward.3 = (f32[512,768]{1,0:T(8,128)}, bf16[1024,768]{1,0:T(8,128)(2,1)}, f32[1024,768]{1,0:T(8,128)}, bf16[1024,768]{1,0:T(8,128)(2,1)}, f32[512,768]{1,...) custom-call(bf16[1024,192]{1,0:T(8,128)(2,1)} %get-tuple-element.144, ...), custom_call_target="tpu_custom_call" | custom-call | tf_op jit(solution)/shard_map/ffn_forward/pallas_call | solution.py:794
  250.8 61.1 %loss_and_back.1 = (f32[512,768]{1,0:T(8,128)}, bf16[1024,768]{1,0:T(8,128)(2,1)}, f32[1,768]{1,0:T(1,128)}, f32[1,1024]{1,0:T(1,128)}, bf16[768,512]{1,0:T(8,12...) custom-call(bf16[1024,768]{1,0:T(8,128)(2,1)} %get-tuple-element.151.refs_0_, ...), custom_call_target="tpu_custom_call" | custom-call | tf_op jit(solution)/shard_map/loss_and_back/pallas_call | solution.py:794
  312.0 37.5 %ffn_backward.2 = (f32[512,768]{1,0:T(8,128)}, bf16[1024,768]{1,0:T(8,128)(2,1)}, bf16[1024,192]{1,0:T(8,128)(2,1)}, bf16[768,768]{1,0:T(8,128)(2,1)}, bf16[768,...) custom-call(f32[512,768]{1,0:T(8,128)} %get-tuple-element.158.refs_0, ...), custom_call_target="tpu_custom_call" | custom-call | tf_op jit(solution)/shard_map/ffn_backward/pallas_call | solution.py:794
  349.5 22.7 %attention_back.2 = (bf16[3,1024,192]{2,1,0:T(8,128)(2,1)}, bf16[4,96,512]{2,1,0:T(8,128)(2,1)}, f32[96,512]{1,0:T(8,128)}, f32[8,128]{1,0:T(8,128)}, f32[96,512]{1,0:T(8,128)}, /*index=5*/f32[8,128]{1,0:T(8,128)}) custom-call(bf16[3,1024,192]{2,1,0:T(8,128)(2,1)} %get-tuple-element.143.refs_0_, bf16[1024,192]{1,0:T(8,128)(2,1)} %get-tuple-element.167.refs_1_, ...), custom_call_target="tpu_custom_call" | custom-call | tf_op jit(solution)/shard_map/attention_back/pallas_call | solution.py:794
  372.2 35.9 %norm_backward.2 = (f32[512,768]{1,0:T(8,128)}, bf16[1024,768]{1,0:T(8,128)(2,1)}, bf16[3,768,192]{2,1,0:T(8,128)(2,1)}, f32[1,768]{1,0:T(1,128)}, bf16[4,96,768...) custom-call(bf16[3,1024,192]{2,1,0:T(8,128)(2,1)} %get-tuple-element, ...), custom_call_target="tpu_custom_call" | custom-call | tf_op jit(solution)/shard_map/norm_backward/pallas_call | solution.py:794
  408.1 36.3 %ffn_backward.3 = (f32[512,768]{1,0:T(8,128)}, bf16[1024,768]{1,0:T(8,128)(2,1)}, bf16[1024,192]{1,0:T(8,128)(2,1)}, bf16[768,768]{1,0:T(8,128)(2,1)}, bf16[768,...) custom-call(f32[512,768]{1,0:T(8,128)} %get-tuple-element.177.refs_0, ...), custom_call_target="tpu_custom_call" | custom-call | tf_op jit(solution)/shard_map/ffn_backward/pallas_call | solution.py:794
  444.4 23.9 %attention_back.3 = (bf16[3,1024,192]{2,1,0:T(8,128)(2,1)}, bf16[4,96,768]{2,1,0:T(8,128)(2,1)}, f32[96,192]{1,0:T(8,128)}, f32[8,128]{1,0:T(8,128)}, f32[3,96,192]{2,1,0:T(8,128)}, /*index=5*/f32[8,128]{1,0:T(8,128)}) custom-call(bf16[3,1024,192]{2,1,0:T(8,128)(2,1)} %get-tuple-element.132.refs_0_, bf16[1024,192]{1,0:T(8,128)(2,1)} %get-tuple-element.187.refs_1_, ...), custom_call_target="tpu_custom_call" | custom-call | tf_op jit(solution)/shard_map/attention_back/pallas_call | solution.py:794
  468.3 31.9 %norm_backward.3 = (f32[512,768]{1,0:T(8,128)}, bf16[1024,768]{1,0:T(8,128)(2,1)}, bf16[3,768,192]{2,1,0:T(8,128)(2,1)}, f32[1,768]{1,0:T(1,128)}, bf16[4,96,768...) custom-call(bf16[3,1024,192]{2,1,0:T(8,128)(2,1)} %get-tuple-element.191.refs_0_, ...), custom_call_target="tpu_custom_call" | custom-call | tf_op jit(solution)/shard_map/norm_backward/pallas_call | solution.py:794
  500.3 0.0 copy-start.27
  500.3 0.0 copy-start.28
  500.4 69.5 %tail.1 = (f32[96,2048]{1,0:T(8,128)}, f32[3,96,192]{2,1,0:T(8,128)}, f32[8,128]{1,0:T(8,128)}, f32[8,128]{1,0:T(8,128)}, f32[96,768]{1,0:T(8,128)}, /*index=5*/...) custom-call(bf16[1024,768]{1,0:T(8,128)(2,1)} %get-tuple-element.196.refs_0_, ...), custom_call_target="tpu_custom_call" | custom-call | tf_op jit(solution)/shard_map/tail/pallas_call | solution.py:794
  569.9 0.0 copy-start.4
  569.9 0.0 copy-start.1
  570.0 1.4 fusion.18
  572.1 1.3 fusion.6
  573.5 0.1 maximum_bitcast_fusion
  573.6 2.0 fusion.14
  575.6 0.0 copy-start.2
  575.6 0.0 copy-start.11
  575.6 0.0 copy-start.12
  575.7 1.6 fusion.16
  577.3 0.2 copy-done.10
  577.5 0.4 copy-done.11
  577.9 0.2 copy-done.12
  578.1 0.2 copy-done.13
  578.3 0.1 copy-done.14
  578.4 0.1 copy-done.15
  578.5 0.1 copy-done.17
  578.6 2.3 fusion.10
  580.9 1.0 copy-done.5
  581.9 0.5 copy-done.6
  582.4 0.2 copy-done.7
  582.6 3.3 fusion.8
  (44 shorter events, 0.1 us)
Async XLA Ops:
  9.9 85.4 %copy-start.25 = (s32[1,1024]{1,0:T(1,128)S(1)}, s32[1,1024]{1,0:T(1,128)}, u32[]{:S(2)}) copy-start(s32[1,1024]{1,0:T(1,128)} %refs_1_.1) | copy-start | bytes 12292
  500.3 71.8 %copy-start.26 = (f32[5,96]{1,0:T(8,128)S(1)}, f32[5,96]{1,0:T(8,128)}, u32[]{:S(2)}) copy-start(f32[5,96]{1,0:T(8,128)} %refs_2_.1) | copy-start | bytes 5764
  500.3 71.8 %copy-start.27 = (f32[5,96]{1,0:T(8,128)S(1)}, f32[5,96]{1,0:T(8,128)}, u32[]{:S(2)}) copy-start(f32[5,96]{1,0:T(8,128)} %param.39) | copy-start | bytes 5764
  500.3 71.8 %copy-start.28 = (f32[5,96]{1,0:T(8,128)S(1)}, f32[5,96]{1,0:T(8,128)}, u32[]{:S(2)}) copy-start(f32[5,96]{1,0:T(8,128)} %param.45) | copy-start | bytes 5764
  500.3 73.1 %copy-start.20 = (f32[96,512]{1,0:T(8,128)S(1)}, f32[96,512]{1,0:T(8,128)}, u32[]{:S(2)}) copy-start(f32[96,512]{1,0:T(8,128)} %get-tuple-element.226) | copy-start | bytes 589828
  500.3 73.1 %copy-start.21 = (f32[96,512]{1,0:T(8,128)S(1)}, f32[96,512]{1,0:T(8,128)}, u32[]{:S(2)}) copy-start(f32[96,512]{1,0:T(8,128)} %get-tuple-element.227) | copy-start | bytes 589828
  500.3 73.1 %copy-start.22 = (f32[96,512]{1,0:T(8,128)S(1)}, f32[96,512]{1,0:T(8,128)}, u32[]{:S(2)}) copy-start(f32[96,512]{1,0:T(8,128)} %get-tuple-element.228) | copy-start | bytes 589828
  500.3 73.1 %copy-start.23 = (f32[96,512]{1,0:T(8,128)S(1)}, f32[96,512]{1,0:T(8,128)}, u32[]{:S(2)}) copy-start(f32[96,512]{1,0:T(8,128)} %get-tuple-element.229) | copy-start | bytes 589828
  500.3 73.2 %copy-start.24 = (f32[2,96,192]{2,1,0:T(8,128)S(1)}, f32[2,96,192]{2,1,0:T(8,128)}, u32[]{:S(2)}) copy-start(f32[2,96,192]{2,1,0:T(8,128)} %param.35) | copy-start | bytes 442372
  569.9 3.7 copy-start.4
  569.9 5.7 copy-start.1
  569.9 5.7 copy-start.8
  569.9 5.6 copy-start.9
  569.9 5.6 copy-start.16
  569.9 5.6 copy-start.19
  573.6 3.8 copy-start.18
  575.6 1.7 copy-start.2
  575.6 1.7 copy-start.3
  575.6 1.9 copy-start.10
  575.6 2.3 copy-start.11
  575.6 2.5 copy-start.12
  575.7 2.7 copy-start.13
  575.7 2.7 copy-start.14
  575.7 2.8 copy-start.15
  575.7 2.9 copy-start.17
  578.6 2.3 copy-start
  578.6 3.4 copy-start.5
  578.6 3.8 copy-start.6
  578.6 4.0 copy-start.7

commit v5 on v4

--- a/solution.py
+++ b/solution.py
@@ -412,7 +412,7 @@
 
 MESH = pl.DeviceIdType.MESH
 SLOW, FAST = 1, 2
-EARLY, MIDDLE, LAST = 1, 2, 3
+FIRST, SECOND, THIRD, LAST = 1, 2, 3, 4
 F32 = jnp.float32
 BF16 = jnp.bfloat16
 CHUNKS = 4
@@ -556,10 +556,15 @@
             found.append({WIDE: me + 1 - 2 * fast})
         return found
 
-    def start(self, late=False):
+    def start(self, late=0):
         for load in self.loads:
             if load.late == late:
                 load.start()
+
+    def need(self):
+        for load in self.loads:
+            if load.needed:
+                load.finish()
 
     def relay(self, stage):
         for load in self.loads:
@@ -569,7 +574,8 @@
     def finish(self):
         self.relay(LAST)
         for load in self.loads:
-            load.finish()
+            if not load.needed:
+                load.finish()
 
 
 def part_of(weights, index, window):
@@ -578,7 +584,7 @@
 
 
 class SlowLoad:
-    ways, late, stage = (SLOW,), False, None
+    ways, late, stage, needed = (SLOW,), 0, None, False
 
     def __init__(self, weights, index, lead, count, window=None):
         self.index, self.lead, self.count, self.window = index, lead, count, window
@@ -624,7 +630,7 @@
 
 
 class FastLoad:
-    ways, late, stage = (FAST,), False, None
+    ways, late, stage, needed = (FAST,), 0, None, False
 
     def __init__(self, blocks, lead, count):
         self.lead, self.count = lead, count
@@ -663,11 +669,13 @@
 class GatherLoad(SlowLoad):
     ways = (SLOW, FAST)
 
-    def __init__(self, weights, index, lead, count, stage, window=None, late=False):
+    def __init__(self, weights, index, lead, count, stage, window=None, late=0, needed=False):
         super().__init__(weights, index, lead, count, window)
-        self.stage, self.late = stage, late
+        self.stage, self.late, self.needed = stage, late, needed
         shape, slows = part_of(weights, index, window), count // 2
         self.outs = [jax.ShapeDtypeStruct(shape[:lead] + (count,) + shape[lead:], BF16)]
+        if needed:
+            self.out_specs = [whole_vmem()]
         self.scratch = self.scratch + [pltpu.SemaphoreType.DMA((slows,))] * 2
 
     def bind(self, given, out, scratch):
@@ -705,7 +713,7 @@
 
 
 class PairLoad:
-    ways, late, stage = (FAST,), False, None
+    ways, late, stage, needed = (FAST,), 0, None, False
 
     def __init__(self, full, lead, count):
         self.lead, self.count = lead, count
@@ -741,7 +749,7 @@
 
 
 class LineLoad:
-    ways, late, stage = (SLOW,), False, None
+    ways, late, stage, needed = (SLOW,), 0, None, False
 
     def __init__(self, sums, count):
         self.count = count
@@ -911,29 +919,25 @@
     for step in range(1, owners):
         small_copy(step).start()
     carry.start()
-    low[...] = jnp.zeros(low.shape, BF16)
-    low[:share, :] = table[0].astype(BF16)
+    padded = jnp.concatenate([table[0], jnp.zeros((LANES - share, vocab), F32)], axis=0)
+    low[...] = jnp.transpose(padded).astype(BF16)
 
     def look_up(step):
         row = lax.rem(me + step, owners)
 
-        def block(start, b):
-            place_of = start // LANES + b
-            for t, pick in enumerate(token_picks(ids_all[row, pl.ds(place_of, 1), :], vocab, first)):
-                picks[:, t * LANES : (t + 1) * LANES] = pick
-            return dot_nt(picks[...], low[...]).astype(BF16)
-
-        def theirs(b, _):
-            near_out[step, rows_at(0, b, LANES), :] = block(other, b)
-            return 0
-
-        def ours(b, _):
-            own[step, rows_at(0, b, LANES), :] = block(mine, b)
-            return 0
-
-        lax.fori_loop(0, seq_len // 2 // LANES, theirs, 0)
+        def find(start):
+            def block(b, _):
+                place_of = start // LANES + b
+                for t, pick in enumerate(token_picks(ids_all[row, pl.ds(place_of, 1), :], vocab, first)):
+                    picks[rows_at(0, b, LANES), t * LANES : (t + 1) * LANES] = pick
+                return 0
+
+            lax.fori_loop(0, seq_len // 2 // LANES, block, 0)
+            return dot_nn(picks[...], low[...]).astype(BF16)
+
+        near_out[step] = find(other)
         near_copy(step).start()
-        lax.fori_loop(0, seq_len // 2 // LANES, ours, 0)
+        own[step] = find(mine)
 
     def halve(step):
         near_copy(step).wait_recv()
@@ -961,7 +965,7 @@
             halve(order[turn - 1])
         if turn >= 2:
             deliver(order[turn - 2])
-    carry.start(True)
+    carry.start(1)
     for step in range(1, owners):
         small_copy(step).wait_recv()
     total = None
@@ -983,8 +987,7 @@
             found = part if found is None else found + part
         part_out[rows, :] = found.astype(BF16)
         part_copy(piece).start()
-    carry.relay(EARLY)
-    give = Share(normed, (send, recv), 0, sibling, mine, chunk)
+    carry.relay(FIRST)
 
     def finish(start, source, piece):
         rows = rows_at(start, piece, LANES)
@@ -1002,7 +1005,7 @@
     for piece in range(pieces):
         part_copy(piece).wait_recv()
         finish(at_other, part_in, piece)
-    carry.relay(MIDDLE)
+    carry.relay(SECOND)
     for k in range(2 * pieces):
         give_rows(rows_at(mine, k % pieces, LANES), k).wait()
     for step in range(owners):
@@ -1034,8 +1037,8 @@
             jax.ShapeDtypeStruct((owners,) + ids.shape, jnp.int32),
         ],
         [
-            pltpu.VMEM((LANES, vocab), BF16),
-            pltpu.VMEM((LANES, vocab), BF16),
+            pltpu.VMEM((vocab, LANES), BF16),
+            pltpu.VMEM((half, vocab), BF16),
             pltpu.VMEM((owners, 8, LANES), F32),
             pltpu.VMEM((owners, half, LANES), BF16),
             pltpu.VMEM((owners, half, LANES), BF16),
@@ -1050,87 +1053,6 @@
         + [dma((owners,))] * 10
         + [dma((half // 2 // LANES,))] * 2
         + [dma((1, half // LANES))] * 2,
-        collective_id,
-        loads,
-    )
-
-
-def ffn_kernel(
-    layer, mixed, resid, w_out, w_in, w_red, gains,
-    middle, normed, before, after, result, normed_next,
-    near_out, near_in, far_out, far_in, near_out2, near_in2, far_out2, far_in2, own2, send, recv, carry,
-):
-    seq_len = normed.shape[0]
-    chunk = seq_len // 2 // CHUNKS
-    sibling, partner, mine, other = group_places(seq_len)
-    greet([sibling, partner] + carry.peers())
-    carry.start()
-    sems = (send, recv)
-    first = Exchange((near_out, near_in, far_out, far_in), sems, 0, sibling, partner)
-    second = Exchange((near_out2, near_in2, far_out2, far_in2), sems, 2, sibling, partner)
-    share = Share(normed, sems, 4, sibling, mine, chunk)
-    share_next = Share(normed_next, sems, 5, sibling, mine, chunk)
-
-    def project(start, j):
-        return dot_nt(mixed[rows_at(start, j, chunk), :], w_out[...])
-
-    def feed(rows):
-        pre = dot_nn(normed[rows, :], w_in[...])
-        before[rows, :] = pre
-        act = gelu_of(pre).astype(BF16)
-        after[rows, :] = act
-        return dot_nt(act, w_red[...])
-
-    first.give(0, project(other, 0))
-    for j in range(CHUNKS):
-        if j + 1 < CHUNKS:
-            first.give(j + 1, project(other, j + 1))
-        first.pass_on(j, project(mine, j))
-    for j in range(CHUNKS):
-        rows = rows_at(0, j, chunk)
-        mid = resid[rows, :] + first.take(j)
-        middle[rows, :] = mid
-        share.put(j, norm_of(mid, gains[2 * layer + 1 : 2 * layer + 2, :]).astype(BF16))
-        own2[j] = feed(rows_at(mine, j, chunk))
-        share.arrived(j)
-        second.give(j, feed(rows_at(other, j, chunk)))
-        if j >= 1:
-            second.pass_on(j - 1, own2[j - 1])
-    second.pass_on(CHUNKS - 1, own2[CHUNKS - 1])
-    carry.relay(EARLY)
-    for j in range(CHUNKS):
-        rows = rows_at(0, j, chunk)
-        x = middle[rows, :] + second.take(j)
-        result[rows, :] = x
-        share_next.put(j, norm_of(x, gains[2 * layer + 2 : 2 * layer + 3, :]).astype(BF16))
-        if j == CHUNKS - 2:
-            carry.relay(MIDDLE)
-    for j in range(CHUNKS):
-        share_next.arrived(j)
-    for part in (first, second, share, share_next):
-        part.close()
-    carry.finish()
-
-
-def ffn_forward(layer, mixed, resid, w_out, w_in, w_red, gains, collective_id, loads):
-    seq_len, width, hidden = mixed.shape[0], w_in.shape[0], w_in.shape[1]
-    half, chunk = seq_len // 2, seq_len // 2 // CHUNKS
-    return run(
-        functools.partial(ffn_kernel, layer),
-        "ffn_forward",
-        [mixed, resid, w_out, w_in, w_red, gains],
-        [
-            jax.ShapeDtypeStruct((half, width), F32),
-            jax.ShapeDtypeStruct((seq_len, width), BF16),
-            jax.ShapeDtypeStruct((seq_len, hidden), F32),
-            jax.ShapeDtypeStruct((seq_len, hidden), BF16),
-            jax.ShapeDtypeStruct((half, width), F32),
-            jax.ShapeDtypeStruct((seq_len, width), BF16),
-        ],
-        Exchange.scratch(chunk, width, FORWARD_KIND)
-        + Exchange.scratch(chunk, width, FORWARD_KIND)
-        + [pltpu.VMEM((CHUNKS, chunk, width), F32)]
-        + sems(6),
         collective_id,
         loads,
     )
@@ -1301,26 +1223,39 @@
     return jnp.where(inside, value, jnp.zeros_like(value))
 
 
-def attention_kernel(normed, weights, key_seg, query_seg, projected, mixed, bias, values_t, carry):
-    seq_len = normed.shape[0]
-    width = mixed.shape[1]
+QUERY_BLOCK = 256
+
+
+def forward_kernel(
+    layer, normed, w_query, key_seg, query_seg, resid, w_out, w_in, gains,
+    projected, mixed, middle, normed_two, before, after, result, normed_next,
+    bias, values_t, near_out, near_in, far_out, far_in, near_out2, near_in2, far_out2, far_in2, own2, send, recv,
+    carry,
+):
+    seq_len, width = normed.shape
+    chunk = seq_len // 2 // CHUNKS
     block = bias.shape[1]
-    heads = width // HD
-    if carry.loads:
-        greet(carry.peers())
+    heads = mixed.shape[1] // HD
+    sibling, partner, mine, other = group_places(seq_len)
+    greet([sibling, partner] + carry.peers())
     carry.start()
-
-    def project(i, _):
+    pair = (send, recv)
+    first = Exchange((near_out, near_in, far_out, far_in), pair, 0, sibling, partner)
+    second = Exchange((near_out2, near_in2, far_out2, far_in2), pair, 2, sibling, partner)
+    share = Share(normed_two, pair, 4, sibling, mine, chunk)
+    share_next = Share(normed_next, pair, 5, sibling, mine, chunk)
+
+    def ask(i, _):
         rows = rows_at(0, i, block)
         for which in range(3):
-            projected[which, rows, :] = dot_nn(normed[rows, :], weights[which]).astype(BF16)
+            projected[which, rows, :] = dot_nn(normed[rows, :], w_query[which]).astype(BF16)
         return 0
 
-    lax.fori_loop(0, seq_len // block, project, 0)
+    lax.fori_loop(0, seq_len // block, ask, 0)
     values_t[...] = jnp.transpose(projected[2])
 
-    def queries(i, _):
-        rows = rows_at(0, i, block)
+    def attend_rows(start):
+        rows = pl.ds(pl.multiple_of(start, block), block)
         bias[...] = jnp.where(key_seg[...] == query_seg[:, rows], 0.0, -1e30)
         asked = projected[0, rows, :] * HD ** (-0.5)
         parts = []
@@ -1330,28 +1265,89 @@
             probs = (powers * (1.0 / jnp.sum(powers, axis=0, keepdims=True))).astype(BF16)
             parts.append(dot_nn(values_t[head * HD : (head + 1) * HD, :], probs))
         mixed[rows, :] = jnp.transpose(jnp.concatenate(parts, axis=0)).astype(BF16)
-        return 0
-
-    lax.fori_loop(0, seq_len // block, queries, 0)
+
+    def project(start, j):
+        return dot_nt(mixed[rows_at(start, j, chunk), :], w_out[...])
+
+    def feed(rows):
+        pre = dot_nn(normed_two[rows, :], w_in[...])
+        before[rows, :] = pre
+        act = gelu_of(pre).astype(BF16)
+        after[rows, :] = act
+        return dot_nt(act, w_red())
+
+    per_block = block // chunk
+    for part in range(CHUNKS // per_block):
+
+        def both(i, _):
+            attend_rows(jnp.where(i == 0, other, mine) + part * block)
+            return 0
+
+        lax.fori_loop(0, 2, both, 0)
+        for j in range(part * per_block, (part + 1) * per_block):
+            first.give(j, project(other, j))
+        if part == 0:
+            carry.relay(FIRST)
+            carry.start(1)
+        for j in range(part * per_block, (part + 1) * per_block):
+            first.pass_on(j, project(mine, j))
+    carry.need()
+    reduced = [load.out for load in carry.loads if load.needed][0]
+
+    def w_red():
+        return reduced[...].reshape(w_in.shape)
+
+    for j in range(CHUNKS):
+        rows = rows_at(0, j, chunk)
+        mid = resid[rows, :] + first.take(j)
+        middle[rows, :] = mid
+        share.put(j, norm_of(mid, gains[2 * layer + 1 : 2 * layer + 2, :]).astype(BF16))
+        own2[j] = feed(rows_at(mine, j, chunk))
+        share.arrived(j)
+        second.give(j, feed(rows_at(other, j, chunk)))
+        if j >= 1:
+            second.pass_on(j - 1, own2[j - 1])
+    second.pass_on(CHUNKS - 1, own2[CHUNKS - 1])
+    carry.relay(SECOND)
+    for j in range(CHUNKS):
+        rows = rows_at(0, j, chunk)
+        x = middle[rows, :] + second.take(j)
+        result[rows, :] = x
+        share_next.put(j, norm_of(x, gains[2 * layer + 2 : 2 * layer + 3, :]).astype(BF16))
+        if j == CHUNKS - 2:
+            carry.relay(THIRD)
+    for j in range(CHUNKS):
+        share_next.arrived(j)
+    for part in (first, second, share, share_next):
+        part.close()
     carry.finish()
 
 
-QUERY_BLOCK = 256
-
-
-def attention(normed, weights, key_seg, query_seg, collective_id, loads):
-    seq_len, width = normed.shape[0], weights.shape[2]
-    block = min(QUERY_BLOCK, seq_len)
+def forward_block(layer, normed, w_query, key_seg, query_seg, resid, w_out, w_in, gains, collective_id, loads):
+    seq_len, width = normed.shape
+    hidden, heads_width = w_in.shape[1], w_query.shape[2]
+    half, chunk = seq_len // 2, seq_len // 2 // CHUNKS
+    block = max(chunk, min(QUERY_BLOCK, half))
     return run(
-        attention_kernel,
-        "attention",
-        [normed, weights, key_seg, query_seg],
+        functools.partial(forward_kernel, layer),
+        "forward_block",
+        [normed, w_query, key_seg, query_seg, resid, w_out, w_in, gains],
         [
-            jax.ShapeDtypeStruct((3, seq_len, width), BF16),
+            jax.ShapeDtypeStruct((3, seq_len, heads_width), BF16),
+            jax.ShapeDtypeStruct((seq_len, heads_width), BF16),
+            jax.ShapeDtypeStruct((half, width), F32),
+            jax.ShapeDtypeStruct((seq_len, width), BF16),
+            jax.ShapeDtypeStruct((seq_len, hidden), F32),
+            jax.ShapeDtypeStruct((seq_len, hidden), BF16),
+            jax.ShapeDtypeStruct((half, width), F32),
             jax.ShapeDtypeStruct((seq_len, width), BF16),
         ],
-        [pltpu.VMEM((seq_len, block), F32), pltpu.VMEM((width, seq_len), BF16)],
-        collective_id if loads else None,
+        [pltpu.VMEM((seq_len, block), F32), pltpu.VMEM((heads_width, seq_len), BF16)]
+        + Exchange.scratch(chunk, width, FORWARD_KIND)
+        + Exchange.scratch(chunk, width, FORWARD_KIND)
+        + [pltpu.VMEM((CHUNKS, chunk, width), F32)]
+        + sems(6),
+        collective_id,
         loads,
     )
 
@@ -1463,10 +1459,8 @@
     def tile_at(t):
         return pl.ds(pl.multiple_of(t * LANES, LANES), LANES)
 
-    def ask(b, _):
+    def ask(b):
         rows = rows_at(0, b, LANES)
-        for k, table in enumerate(tables):
-            logits[rows, k * piece_width : (k + 1) * piece_width] = dot_nn(normed[rows, :], table[...])
         here = info[:, rows]
         at_noised = spread(here[0:1] - first)
         at_clean = spread(here[1:2] - first)
@@ -1491,13 +1485,20 @@
             )
 
         zero = jnp.zeros((LANES, LANES), F32)
-        totals = lax.fori_loop(0, tiles, sum_step, (zero, zero, zero))
+        totals = lax.fori_loop(0, tiles, sum_step, (zero, zero, zero), unroll=2)
         stat_out[b] = to_rows([top] + [jnp.sum(total, axis=1, keepdims=True) for total in totals])
         for k in range(3):
             stat_copy(b, k).start()
+
+    def product(i, _):
+        rows = rows_at(0, i, TILE)
+        for k, table in enumerate(tables):
+            logits[rows, k * piece_width : (k + 1) * piece_width] = dot_nn(normed[rows, :], table[...])
+        for b in range(TILE // LANES):
+            ask(i * (TILE // LANES) + b)
         return 0
 
-    lax.fori_loop(0, blocks, ask, 0)
+    lax.fori_loop(0, seq_len // TILE, product, 0)
 
     def scalars(b):
         here = info[:, rows_at(0, b, LANES)]
@@ -1534,7 +1535,7 @@
             return (logs + jnp.log(grown), shares + probs / grown)
 
         zero = jnp.zeros((LANES, LANES), F32)
-        totals = lax.fori_loop(0, tiles, step, (zero, zero))
+        totals = lax.fori_loop(0, tiles, step, (zero, zero), unroll=2)
         sum_out[b] = to_rows([jnp.sum(total, axis=1, keepdims=True) for total in totals])
         for k in range(3):
             sum_copy(b, k).start()
@@ -1590,7 +1591,7 @@
             grads[rows, tile_at(t)] = grad.astype(BF16)
             return 0
 
-        lax.fori_loop(0, tiles, step, 0)
+        lax.fori_loop(0, tiles, step, 0, unroll=2)
 
     def partial(start, j):
         base = start // LANES + j * (chunk // LANES)
@@ -1675,14 +1676,14 @@
     layers, branch, ids_all, losses, full, *refs, carry,
 ):
     gain_parts, refs = refs[: 2 * layers + 1], refs[2 * layers + 1 :]
-    squares, refs = refs[: len(refs) - 31], refs[len(refs) - 31 :]
+    squares, refs = refs[: len(refs) - 32], refs[len(refs) - 32 :]
     tail_body(branch, ids_all, losses, full, gain_parts, squares, *refs, carry)
 
 
 def tail_body(
     branch, ids_all, losses, full, gain_parts, squares,
     d_table, d_full, d_small, scalars,
-    out_blocks, all_in, picks, total, gains_out, gains_in, blocks, block_in, line_out, line_in,
+    out_blocks, all_in, masked, picks, total, gains_out, gains_in, blocks, block_in, line_out, line_in,
     fast_in, sums, slow_in, near, along, across,
     wide_send, wide_recv, far_send, far_recv, near_send, near_recv,
     pair_send, pair_recv, line_send, line_recv, sum_sems,
@@ -1785,20 +1786,27 @@
 
         def make(b, _):
             rows = rows_at(0, b, LANES)
-            for t, pick in enumerate(token_picks(ids_all[row, pl.ds(b, 1), :], vocab, first)):
-                picks[rows, t * LANES : (t + 1) * LANES] = pick
+            here = ids_all[row, pl.ds(b, 1), :] - first
+            high = lax.shift_right_arithmetic(here, 7)
+            rest = spread((here - high * LANES).astype(F32))
+            lane = lax.broadcasted_iota(jnp.int32, (LANES, LANES), 1).astype(F32)
+            picks[rows, :] = jnp.where(rest == lane, 1.0, 0.0).astype(BF16)
+            turned = jnp.transpose(all_in[row, rows, :])
+            for t in range(vocab // LANES):
+                inside = jnp.where(high == t, 1.0, 0.0).astype(BF16)
+                masked[t * LANES : (t + 1) * LANES, rows] = turned * inside
             return 0
 
         lax.fori_loop(0, seq_len // LANES, make, 0)
-        turned = jnp.transpose(all_in[row])
-
-        def columns(i, _):
-            where = pl.ds(pl.multiple_of(i * TILE, TILE), TILE)
-            part = dot_nn(turned, picks[:, where])
-            total[:, where] = part if first_turn else total[:, where] + part
+        span = 2 * TILE
+
+        def some(i, _):
+            rows = rows_at(0, i, span)
+            part = dot_nn(masked[rows, :], picks[...])
+            total[rows, :] = part if first_turn else total[rows, :] + part
             return 0
 
-        lax.fori_loop(0, vocab // TILE, columns, 0)
+        lax.fori_loop(0, vocab // span, some, 0)
 
     order = [0] + list(range(1, owners))
     for turn in range(owners + 2):
@@ -1820,7 +1828,8 @@
                     gain_line(step).start()
         if turn >= 2:
             gather_grad(order[turn - 2], turn == 2)
-    d_table[...] = total[:share, :]
+    for t in range(vocab // LANES):
+        d_table[:, t * LANES : (t + 1) * LANES] = total[t * LANES : t * LANES + share, :]
     result = sums[0].astype(F32)
     small = line_out[0]
     for step in range(1, slows):
@@ -1896,8 +1905,9 @@
         [
             pltpu.VMEM((owners, seq_len // 4, LANES), BF16),
             pltpu.VMEM((owners, seq_len, LANES), BF16),
-            pltpu.VMEM((seq_len, vocab), BF16),
-            pltpu.VMEM((LANES, vocab), F32),
+            pltpu.VMEM((vocab, seq_len), BF16),
+            pltpu.VMEM((seq_len, LANES), BF16),
+            pltpu.VMEM((vocab, LANES), F32),
             pltpu.VMEM((8, width), F32),
             pltpu.VMEM((8, width), F32),
             pltpu.VMEM((owners,) + small, F32),
@@ -1992,60 +2002,40 @@
     (residual, normed, gain_w, counts, ids_all), carried = embed(
         ids, counted, gains, extra, tables, wide, 0,
         [
-            GatherLoad(attn_in, 0, 1, wide, EARLY),
-            GatherLoad(attn_out, 0, 0, wide, MIDDLE),
-            GatherLoad(ffn_in, 0, 0, wide, LAST, late=True),
-            SlowLoad(ffn_out, 0, 0, wide),
+            GatherLoad(attn_in, 0, 1, wide, FIRST),
+            GatherLoad(attn_out, 0, 0, wide, FIRST),
+            GatherLoad(ffn_in, 0, 0, wide, LAST, late=1),
         ],
     )
     token_total = counts[gain_rows, 0]
-    query_w, output_w, expand_w, reduce_line = carried
     next_id = 1
-    tables_w = []
-    table_lines = []
     key_seg, query_seg = segments.reshape(-1, 1), segments.reshape(1, -1)
     kept = []
     for layer in range(layers):
-        more = layer + 1 < layers
-        loads = [FastLoad(reduce_line, 0, wide)]
-        if more:
-            loads.append(SlowLoad(ffn_in, layer + 1, 0, wide))
+        query_w, output_w, expand_w = [joined(value, lead) for value, lead in zip(carried, leads)]
+        loads = [GatherLoad(ffn_out, layer, 0, wide, FIRST, needed=True)]
+        if layer + 1 < layers:
+            loads += [
+                GatherLoad(attn_in, layer + 1, 1, wide, SECOND, late=1),
+                GatherLoad(attn_out, layer + 1, 0, wide, SECOND, late=1),
+                GatherLoad(ffn_in, layer + 1, 0, wide, THIRD, late=1),
+            ]
         else:
-            loads.append(SlowLoad(tables, 1, 0, wide, windows[1]))
-        query_w, output_w, expand_w = joined(query_w, 1), joined(output_w, 0), joined(expand_w, 0)
-        (projected, mixed), carried = attention(normed, query_w, key_seg, query_seg, next_id, loads)
-        reduce_w = joined(carried[0], 0)
-        if more:
-            loads = [
-                FastLoad(carried[1], 0, wide),
-                GatherLoad(attn_in, layer + 1, 1, wide, EARLY),
-                GatherLoad(attn_out, layer + 1, 0, wide, EARLY),
-                SlowLoad(ffn_out, layer + 1, 0, wide),
+            loads += [
+                GatherLoad(tables, 1, 0, wide, stage, window, late)
+                for window, stage, late in zip(windows, (SECOND, SECOND, THIRD, LAST), (0, 1, 1, 1))
             ]
-            if layer + 2 == layers:
-                loads.append(SlowLoad(tables, 1, 0, wide, windows[0]))
-        else:
-            loads = [
-                FastLoad(table_line, 0, wide),
-                FastLoad(carried[1], 0, wide),
-                GatherLoad(tables, 1, 0, wide, EARLY, windows[2]),
-                GatherLoad(tables, 1, 0, wide, MIDDLE, windows[3]),
-            ]
-        (middle, normed_two, before, after, result, normed_next), carried = ffn_forward(
-            layer, mixed, residual, output_w, expand_w, reduce_w, gain_w, next_id + 1, loads
+        (projected, mixed, middle, normed_two, before, after, result, normed_next), carried = forward_block(
+            layer, normed, query_w, key_seg, query_seg, residual, output_w, expand_w, gain_w, next_id, loads
         )
-        next_id += 2
+        next_id += 1
+        reduce_w, *carried = carried
         kept.append(
             (residual, normed, projected, mixed, middle, normed_two, before, after)
-            + (query_w, output_w, expand_w, reduce_w)
+            + (query_w, output_w, expand_w, joined(reduce_w, 0))
         )
         residual, normed = result, normed_next
-        if more:
-            expand_w, query_w, output_w, reduce_line, *rest = carried
-            if rest:
-                table_line = rest[0]
-        else:
-            tables_w = [joined(value, 0) for value in carried]
+    tables_w = [joined(value, 0) for value in carried]
 
     noised_flat, clean_flat = noised.reshape(-1), clean.reshape(-1)
     info = jnp.stack(

time: 591 us -> 591 us (level)
    pallas_call x13 -> x11, Pallas kernels: 557 us -> 557 us  [run(): pl.pallas_call(kernel, out_shape=tuple(outs) + tuple((out for load in loa...]
where the time goes in v5:
time: 591 us; the launch traced here: 588 us
  Pallas kernels  557 us (94%)
  other arithmetic  18.8 us (3%)
  local copies, waits for them, and re-layouts  8.05 us (1%)
    pallas_call x11, Pallas kernels, run(): pl.pallas_call(kernel, out_shape=tuple(outs) + tuple((out for load in loa...  557 us

profile of v5, /device:TPU:0, one launch (start us, length us, event | category | flops | bytes accessed | tf_op | source)
XLA Modules:
  0.0 587.5 jit_solution(13633079695347917479)
XLA Ops:
  0.7 0.7 dynamic-slice_convert_fusion
  1.4 0.7 convert_element_type.48
  2.1 0.7 convert_element_type.47
  2.8 0.7 convert_element_type.49
  3.5 0.7 convert_element_type.50
  4.1 1.7 copy.50.refs_2_
  5.8 2.8 multiply_sine_fusion
  8.7 1.3 pad_maximum_fusion.refs_3_
  9.9 79.4 %embed.1 = (f32[512,768]{1,0:T(8,128)}, bf16[1024,768]{1,0:T(8,128)(2,1)}, f32[8,768]{1,0:T(8,128)}, f32[8,128]{1,0:T(8,128)}, s32[8,8,128]{2,1,0:T(8,128)}, /*i...) custom-call(s32[8,128]{1,0:T(8,128)} %bitcast.81, s32[1,1024]{1,0:T(1,128)} %refs_1_.1, ...), custom_call_target="tpu_custom_call" | custom-call | tf_op jit(solution)/shard_map/embed/pallas_call | solution.py:802
  89.3 1.2 slice.12
  90.5 0.7 broadcast_divide_fusion
  91.2 0.7 stack.57.refs_1_
  91.8 70.0 %forward_block.2 = (bf16[3,1024,192]{2,1,0:T(8,128)(2,1)}, bf16[1024,192]{1,0:T(8,128)(2,1)}, f32[512,768]{1,0:T(8,128)}, bf16[1024,768]{1,0:T(8,128)(2,1)}, f32...) custom-call(bf16[1024,768]{1,0:T(8,128)(2,1)} %get-tuple-element.124, ...), custom_call_target="tpu_custom_call" | custom-call | tf_op jit(solution)/shard_map/forward_block/pallas_call | solution.py:802
  161.9 85.5 %forward_block.3 = (bf16[3,1024,192]{2,1,0:T(8,128)(2,1)}, bf16[1024,192]{1,0:T(8,128)(2,1)}, f32[512,768]{1,0:T(8,128)}, bf16[1024,768]{1,0:T(8,128)(2,1)}, f32...) custom-call(bf16[1024,768]{1,0:T(8,128)(2,1)} %get-tuple-element.131, ...), custom_call_target="tpu_custom_call" | custom-call | tf_op jit(solution)/shard_map/forward_block/pallas_call | solution.py:802
  247.4 61.1 %loss_and_back.1 = (f32[512,768]{1,0:T(8,128)}, bf16[1024,768]{1,0:T(8,128)(2,1)}, f32[1,768]{1,0:T(1,128)}, f32[1,1024]{1,0:T(1,128)}, bf16[768,512]{1,0:T(8,12...) custom-call(bf16[1024,768]{1,0:T(8,128)(2,1)} %get-tuple-element.137.refs_0_, ...), custom_call_target="tpu_custom_call" | custom-call | tf_op jit(solution)/shard_map/loss_and_back/pallas_call | solution.py:802
  308.5 37.5 %ffn_backward.2 = (f32[512,768]{1,0:T(8,128)}, bf16[1024,768]{1,0:T(8,128)(2,1)}, bf16[1024,192]{1,0:T(8,128)(2,1)}, bf16[768,768]{1,0:T(8,128)(2,1)}, bf16[768,...) custom-call(f32[512,768]{1,0:T(8,128)} %get-tuple-element.144.refs_0, ...), custom_call_target="tpu_custom_call" | custom-call | tf_op jit(solution)/shard_map/ffn_backward/pallas_call | solution.py:802
  346.0 28.0 %attention_back.2 = (bf16[3,1024,192]{2,1,0:T(8,128)(2,1)}, bf16[4,96,512]{2,1,0:T(8,128)(2,1)}, f32[96,512]{1,0:T(8,128)}, f32[8,128]{1,0:T(8,128)}, f32[96,512]{1,0:T(8,128)}, /*index=5*/f32[8,128]{1,0:T(8,128)}) custom-call(bf16[3,1024,192]{2,1,0:T(8,128)(2,1)} %get-tuple-element.136.refs_0_, bf16[1024,192]{1,0:T(8,128)(2,1)} %get-tuple-element.155.refs_1_, ...), custom_call_target="tpu_custom_call" | custom-call | tf_op jit(solution)/shard_map/attention_back/pallas_call | solution.py:802
  374.0 36.7 %norm_backward.2 = (f32[512,768]{1,0:T(8,128)}, bf16[1024,768]{1,0:T(8,128)(2,1)}, bf16[3,768,192]{2,1,0:T(8,128)(2,1)}, f32[1,768]{1,0:T(1,128)}, bf16[4,96,768...) custom-call(bf16[3,1024,192]{2,1,0:T(8,128)(2,1)} %get-tuple-element, ...), custom_call_target="tpu_custom_call" | custom-call | tf_op jit(solution)/shard_map/norm_backward/pallas_call | solution.py:802
  410.7 36.1 %ffn_backward.3 = (f32[512,768]{1,0:T(8,128)}, bf16[1024,768]{1,0:T(8,128)(2,1)}, bf16[1024,192]{1,0:T(8,128)(2,1)}, bf16[768,768]{1,0:T(8,128)(2,1)}, bf16[768,...) custom-call(f32[512,768]{1,0:T(8,128)} %get-tuple-element.165.refs_0, ...), custom_call_target="tpu_custom_call" | custom-call | tf_op jit(solution)/shard_map/ffn_backward/pallas_call | solution.py:802
  446.8 24.4 %attention_back.3 = (bf16[3,1024,192]{2,1,0:T(8,128)(2,1)}, bf16[4,96,768]{2,1,0:T(8,128)(2,1)}, f32[96,192]{1,0:T(8,128)}, f32[8,128]{1,0:T(8,128)}, f32[3,96,192]{2,1,0:T(8,128)}, /*index=5*/f32[8,128]{1,0:T(8,128)}) custom-call(bf16[3,1024,192]{2,1,0:T(8,128)(2,1)} %get-tuple-element.130.refs_0_, bf16[1024,192]{1,0:T(8,128)(2,1)} %get-tuple-element.177.refs_1_, ...), custom_call_target="tpu_custom_call" | custom-call | tf_op jit(solution)/shard_map/attention_back/pallas_call | solution.py:802
  471.2 31.6 %norm_backward.3 = (f32[512,768]{1,0:T(8,128)}, bf16[1024,768]{1,0:T(8,128)(2,1)}, bf16[3,768,192]{2,1,0:T(8,128)(2,1)}, f32[1,768]{1,0:T(1,128)}, bf16[4,96,768...) custom-call(bf16[3,1024,192]{2,1,0:T(8,128)(2,1)} %get-tuple-element.181.refs_0_, ...), custom_call_target="tpu_custom_call" | custom-call | tf_op jit(solution)/shard_map/norm_backward/pallas_call | solution.py:802
  502.8 0.0 copy-start.26
  502.9 0.0 copy-start.27
  502.9 0.0 copy-start.28
  502.9 0.0 copy-start.24
  502.9 66.9 %tail.1 = (f32[96,2048]{1,0:T(8,128)}, f32[3,96,192]{2,1,0:T(8,128)}, f32[8,128]{1,0:T(8,128)}, f32[8,128]{1,0:T(8,128)}, f32[96,768]{1,0:T(8,128)}, /*index=5*/...) custom-call(bf16[1024,768]{1,0:T(8,128)(2,1)} %get-tuple-element.186.refs_0_, ...), custom_call_target="tpu_custom_call" | custom-call | tf_op jit(solution)/shard_map/tail/pallas_call | solution.py:802
  569.9 0.0 copy-start.4
  569.9 0.0 copy-start.9
  569.9 1.4 fusion.18
  572.1 1.3 fusion.6
  573.4 0.1 maximum_bitcast_fusion
  573.5 2.0 fusion.14
  575.6 0.0 copy-start.10
  575.6 0.0 copy-start.11
  575.6 0.0 copy-start.13
  575.6 1.6 fusion.16
  577.3 0.2 copy-done.10
  577.5 0.4 copy-done.11
  577.9 0.2 copy-done.12
  578.1 0.2 copy-done.13
  578.3 0.1 copy-done.14
  578.3 0.1 copy-done.15
  578.4 0.1 copy-done.17
  578.5 2.3 fusion.10
  580.8 1.0 copy-done.5
  581.9 0.5 copy-done.6
  582.4 0.2 copy-done.7
  582.5 3.3 fusion.8
  (42 shorter events, 0.1 us)
Async XLA Ops:
  9.9 80.6 %copy-start.25 = (s32[1,1024]{1,0:T(1,128)S(1)}, s32[1,1024]{1,0:T(1,128)}, u32[]{:S(2)}) copy-start(s32[1,1024]{1,0:T(1,128)} %refs_1_.1) | copy-start | bytes 12292
  502.8 69.2 %copy-start.26 = (f32[5,96]{1,0:T(8,128)S(1)}, f32[5,96]{1,0:T(8,128)}, u32[]{:S(2)}) copy-start(f32[5,96]{1,0:T(8,128)} %refs_2_.1) | copy-start | bytes 5764
  502.9 69.2 %copy-start.27 = (f32[5,96]{1,0:T(8,128)S(1)}, f32[5,96]{1,0:T(8,128)}, u32[]{:S(2)}) copy-start(f32[5,96]{1,0:T(8,128)} %param.39) | copy-start | bytes 5764
  502.9 69.2 %copy-start.28 = (f32[5,96]{1,0:T(8,128)S(1)}, f32[5,96]{1,0:T(8,128)}, u32[]{:S(2)}) copy-start(f32[5,96]{1,0:T(8,128)} %param.45) | copy-start | bytes 5764
  502.9 70.5 %copy-start.20 = (f32[96,512]{1,0:T(8,128)S(1)}, f32[96,512]{1,0:T(8,128)}, u32[]{:S(2)}) copy-start(f32[96,512]{1,0:T(8,128)} %get-tuple-element.216) | copy-start | bytes 589828
  502.9 70.5 %copy-start.21 = (f32[96,512]{1,0:T(8,128)S(1)}, f32[96,512]{1,0:T(8,128)}, u32[]{:S(2)}) copy-start(f32[96,512]{1,0:T(8,128)} %get-tuple-element.217) | copy-start | bytes 589828
  502.9 70.5 %copy-start.22 = (f32[96,512]{1,0:T(8,128)S(1)}, f32[96,512]{1,0:T(8,128)}, u32[]{:S(2)}) copy-start(f32[96,512]{1,0:T(8,128)} %get-tuple-element.218) | copy-start | bytes 589828
  502.9 70.5 %copy-start.23 = (f32[96,512]{1,0:T(8,128)S(1)}, f32[96,512]{1,0:T(8,128)}, u32[]{:S(2)}) copy-start(f32[96,512]{1,0:T(8,128)} %get-tuple-element.219) | copy-start | bytes 589828
  502.9 70.6 %copy-start.24 = (f32[2,96,192]{2,1,0:T(8,128)S(1)}, f32[2,96,192]{2,1,0:T(8,128)}, u32[]{:S(2)}) copy-start(f32[2,96,192]{2,1,0:T(8,128)} %param.35) | copy-start | bytes 442372
  569.9 3.6 copy-start.4
  569.9 5.6 copy-start.1
  569.9 5.6 copy-start.8
  569.9 5.6 copy-start.9
  569.9 5.6 copy-start.16
  569.9 5.6 copy-start.19
  573.5 3.8 copy-start.18
  575.5 1.7 copy-start.2
  575.6 1.7 copy-start.3
  575.6 1.9 copy-start.10
  575.6 2.3 copy-start.11
  575.6 2.5 copy-start.12
  575.6 2.7 copy-start.13
  575.6 2.7 copy-start.14
  575.6 2.8 copy-start.15
  575.6 2.9 copy-start.17
  578.5 2.3 copy-start
  578.5 3.4 copy-start.5
  578.5 3.8 copy-start.6
  578.5 4.0 copy-start.7

commit v6 on v5

--- a/solution.py
+++ b/solution.py
@@ -412,11 +412,11 @@
 
 MESH = pl.DeviceIdType.MESH
 SLOW, FAST = 1, 2
-FIRST, SECOND, THIRD, LAST = 1, 2, 3, 4
+HBM, KEPT, LOCAL = 1, 2, 3
 F32 = jnp.float32
 BF16 = jnp.bfloat16
 CHUNKS = 4
-VMEM_LIMIT = 56 * 1024 * 1024
+VMEM_LIMIT = 61 * 1024 * 1024
 FORWARD_KIND = BF16
 BACKWARD_KIND = BF16
 
@@ -556,26 +556,20 @@
             found.append({WIDE: me + 1 - 2 * fast})
         return found
 
-    def start(self, late=0):
-        for load in self.loads:
-            if load.late == late:
-                load.start()
-
-    def need(self):
-        for load in self.loads:
-            if load.needed:
-                load.finish()
-
-    def relay(self, stage):
-        for load in self.loads:
-            if load.stage == stage:
-                load.relay()
-
-    def finish(self):
-        self.relay(LAST)
-        for load in self.loads:
-            if not load.needed:
-                load.finish()
+    def begin(self, *which):
+        for k in which:
+            self.loads[k].start()
+
+    def hand_on(self, *which):
+        for k in which:
+            self.loads[k].relay()
+
+    def end(self, *which):
+        for k in which:
+            self.loads[k].finish()
+
+    def all(self):
+        return range(len(self.loads))
 
 
 def part_of(weights, index, window):
@@ -584,7 +578,7 @@
 
 
 class SlowLoad:
-    ways, late, stage, needed = (SLOW,), 0, None, False
+    ways = (SLOW,)
 
     def __init__(self, weights, index, lead, count, window=None):
         self.index, self.lead, self.count, self.window = index, lead, count, window
@@ -630,15 +624,18 @@
 
 
 class FastLoad:
-    ways, late, stage, needed = (FAST,), 0, None, False
+    ways = (FAST,)
 
     def __init__(self, blocks, lead, count):
         self.lead, self.count = lead, count
         shape, slows = blocks.shape[1:], count // 2
         self.operands, self.in_specs = [blocks], [pl.BlockSpec(memory_space=pl.ANY)]
         self.outs = [jax.ShapeDtypeStruct(shape[:lead] + (count,) + shape[lead:], BF16)]
-        self.out_specs = [pl.BlockSpec(memory_space=pl.ANY)]
+        self.out_specs = [whole_vmem()]
         self.scratch = [pltpu.SemaphoreType.DMA((slows,))] * 3
+
+    def value(self):
+        return self.out[...].reshape((-1, self.out.shape[-1]))
 
     def bind(self, given, out, scratch):
         self.blocks, self.out = given[0], out[0]
@@ -669,18 +666,28 @@
 class GatherLoad(SlowLoad):
     ways = (SLOW, FAST)
 
-    def __init__(self, weights, index, lead, count, stage, window=None, late=0, needed=False):
+    def __init__(self, weights, index, lead, count, window=None, place=HBM):
         super().__init__(weights, index, lead, count, window)
-        self.stage, self.late, self.needed = stage, late, needed
         shape, slows = part_of(weights, index, window), count // 2
-        self.outs = [jax.ShapeDtypeStruct(shape[:lead] + (count,) + shape[lead:], BF16)]
-        if needed:
+        whole = shape[:lead] + (count,) + shape[lead:]
+        self.outs = [jax.ShapeDtypeStruct(whole, BF16)]
+        self.scratch = self.scratch + [pltpu.SemaphoreType.DMA((slows,))] * 2
+        if place == KEPT:
             self.out_specs = [whole_vmem()]
-        self.scratch = self.scratch + [pltpu.SemaphoreType.DMA((slows,))] * 2
+        self.local_out = place == LOCAL
+        if self.local_out:
+            self.outs, self.out_specs = [], []
+            self.scratch = self.scratch + [pltpu.VMEM(whole, BF16)]
 
     def bind(self, given, out, scratch):
+        if self.local_out:
+            out, scratch = scratch[-1:], scratch[:-1]
         super().bind(given, out, scratch[:-2])
         self.fast_send, self.fast_recv = scratch[-2:]
+
+    def value(self, *index):
+        found = self.out[index] if index else self.out[...]
+        return found.reshape((-1, found.shape[-1]))
 
     def at(self, owner):
         return self.out.at[(slice(None),) * self.lead + (owner,)]
@@ -713,7 +720,7 @@
 
 
 class PairLoad:
-    ways, late, stage, needed = (FAST,), 0, None, False
+    ways = (FAST,)
 
     def __init__(self, full, lead, count):
         self.lead, self.count = lead, count
@@ -749,7 +756,7 @@
 
 
 class LineLoad:
-    ways, late, stage, needed = (SLOW,), 0, None, False
+    ways = (SLOW,)
 
     def __init__(self, sums, count):
         self.count = count
@@ -784,8 +791,18 @@
 
 
 def run(body, name, operands, outs, scratch, collective_id=None, loads=()):
-    counts = [len(operands)] + [len(load.operands) for load in loads]
-    counts += [len(outs)] + [len(load.outs) for load in loads]
+    given, in_specs, taken = list(operands), [whole_vmem()] * len(operands), []
+    for load in loads:
+        places = []
+        for operand, spec in zip(load.operands, load.in_specs):
+            known = [k for k, other in enumerate(given) if other is operand]
+            if not known:
+                known = [len(given)]
+                given.append(operand)
+                in_specs.append(spec)
+            places.append(known[0])
+        taken.append(places)
+    counts = [len(given), len(outs)] + [len(load.outs) for load in loads]
     counts += [len(scratch)] + [len(load.scratch) for load in loads]
     parts = 1 + len(loads)
 
@@ -794,15 +811,14 @@
         for count in counts:
             groups.append(refs[place : place + count])
             place += count
-        for k, load in enumerate(loads, 1):
-            load.bind(groups[k], groups[parts + k], groups[2 * parts + k])
-        main = groups[0] + groups[parts] + groups[2 * parts]
-        body(*main, carry=Carry(list(loads)))
+        for k, load in enumerate(loads):
+            load.bind([groups[0][p] for p in taken[k]], groups[2 + k], groups[2 + parts + k])
+        body(*groups[0][: len(operands)], *groups[1], *groups[1 + parts], carry=Carry(list(loads)))
 
     results = pl.pallas_call(
         kernel,
         out_shape=tuple(outs) + tuple(out for load in loads for out in load.outs),
-        in_specs=[whole_vmem()] * len(operands) + [spec for load in loads for spec in load.in_specs],
+        in_specs=in_specs,
         out_specs=(whole_vmem(),) * len(outs) + tuple(spec for load in loads for spec in load.out_specs),
         scratch_shapes=list(scratch) + [s for load in loads for s in load.scratch],
         compiler_params=pltpu.CompilerParams(
@@ -811,7 +827,7 @@
             vmem_limit_bytes=VMEM_LIMIT,
         ),
         name=name,
-    )(*operands, *[operand for load in loads for operand in load.operands])
+    )(*given)
     return results[: len(outs)], results[len(outs) :]
 
 
@@ -869,7 +885,7 @@
     return [jnp.where(here == lane + float(t * LANES), 1.0, 0.0).astype(BF16) for t in range(vocab // LANES)]
 
 
-def embed_kernel(
+def embed_part(
     ids, counted, gains, extra, table,
     resid, normed, gain_all, count_all, ids_all,
     low, picks, small, near_out, near_in, own, far_out, far_in, wide_out, wide_in, part_out, part_in,
@@ -918,7 +934,7 @@
         id_copy(step).start()
     for step in range(1, owners):
         small_copy(step).start()
-    carry.start()
+    carry.begin(0, 1)
     padded = jnp.concatenate([table[0], jnp.zeros((LANES - share, vocab), F32)], axis=0)
     low[...] = jnp.transpose(padded).astype(BF16)
 
@@ -965,7 +981,10 @@
             halve(order[turn - 1])
         if turn >= 2:
             deliver(order[turn - 2])
-    carry.start(1)
+        if turn == 1:
+            carry.begin(2)
+    carry.begin(3)
+    carry.hand_on(0, 1)
     for step in range(1, owners):
         small_copy(step).wait_recv()
     total = None
@@ -987,7 +1006,6 @@
             found = part if found is None else found + part
         part_out[rows, :] = found.astype(BF16)
         part_copy(piece).start()
-    carry.relay(FIRST)
 
     def finish(start, source, piece):
         rows = rows_at(start, piece, LANES)
@@ -1005,7 +1023,7 @@
     for piece in range(pieces):
         part_copy(piece).wait_recv()
         finish(at_other, part_in, piece)
-    carry.relay(SECOND)
+    carry.hand_on(2)
     for k in range(2 * pieces):
         give_rows(rows_at(mine, k % pieces, LANES), k).wait()
     for step in range(owners):
@@ -1017,25 +1035,169 @@
             wide_copy(step).wait_send()
     for piece in range(pieces):
         part_copy(piece).wait_send()
-    carry.finish()
-
-
-def embed(ids, counted, gains, extra, tables, owners, collective_id, loads):
+
+
+QUERY_BLOCK = 256
+
+
+def forward_part(
+    layer, weights, points, normed, key_seg, query_seg, resid, gains,
+    projected, mixed, middle, normed_two, result, normed_next,
+    bias, values_t, near_out, near_in, far_out, far_in, near_out2, near_in2, far_out2, far_in2, own2, send, recv,
+):
+    w_query, w_out, w_in, w_red = weights
+    at_half, at_feed, at_sent, at_last = points
+    seq_len, width = normed.shape
+    chunk = seq_len // 2 // CHUNKS
+    block = bias.shape[1]
+    heads = mixed.shape[1] // HD
+    sibling, partner, mine, other = group_places(seq_len)
+    pair = (send, recv)
+    first = Exchange((near_out, near_in, far_out, far_in), pair, 0, sibling, partner)
+    second = Exchange((near_out2, near_in2, far_out2, far_in2), pair, 2, sibling, partner)
+    share = Share(normed_two, pair, 4, sibling, mine, chunk)
+    share_next = Share(normed_next, pair, 5, sibling, mine, chunk)
+
+    def ask(i, _):
+        rows = rows_at(0, i, block)
+        for which in range(3):
+            projected[which, rows, :] = dot_nn(normed[rows, :], w_query(which)).astype(BF16)
+        return 0
+
+    lax.fori_loop(0, seq_len // block, ask, 0)
+    values_t[...] = jnp.transpose(projected[2])
+
+    def attend_rows(start):
+        rows = pl.ds(pl.multiple_of(start, block), block)
+        bias[...] = jnp.where(key_seg[...] == query_seg[:, rows], 0.0, -1e30)
+        asked = projected[0, rows, :] * HD ** (-0.5)
+        parts = []
+        for head in range(heads):
+            scores = dot_nt(projected[1], head_lanes(asked, head, HD)) + bias[...]
+            powers = jnp.exp(scores - jnp.max(scores, axis=0, keepdims=True))
+            probs = (powers * (1.0 / jnp.sum(powers, axis=0, keepdims=True))).astype(BF16)
+            parts.append(dot_nn(values_t[head * HD : (head + 1) * HD, :], probs))
+        mixed[rows, :] = jnp.transpose(jnp.concatenate(parts, axis=0)).astype(BF16)
+
+    def project(start, j):
+        return dot_nt(mixed[rows_at(start, j, chunk), :], w_out())
+
+    def feed(rows):
+        pre = dot_nn(normed_two[rows, :], w_in())
+        return dot_nt(gelu_of(pre).astype(BF16), w_red())
+
+    per_block = block // chunk
+    for part in range(CHUNKS // per_block):
+
+        def both(i, _):
+            attend_rows(jnp.where(i == 0, other, mine) + part * block)
+            return 0
+
+        lax.fori_loop(0, 2, both, 0)
+        for j in range(part * per_block, (part + 1) * per_block):
+            first.give(j, project(other, j))
+        if part == 0:
+            at_half()
+        for j in range(part * per_block, (part + 1) * per_block):
+            first.pass_on(j, project(mine, j))
+    at_feed()
+    for j in range(CHUNKS):
+        rows = rows_at(0, j, chunk)
+        mid = resid[rows, :] + first.take(j)
+        middle[rows, :] = mid
+        share.put(j, norm_of(mid, gains[2 * layer + 1 : 2 * layer + 2, :]).astype(BF16))
+        own2[j] = feed(rows_at(mine, j, chunk))
+        share.arrived(j)
+        second.give(j, feed(rows_at(other, j, chunk)))
+        if j >= 1:
+            second.pass_on(j - 1, own2[j - 1])
+    second.pass_on(CHUNKS - 1, own2[CHUNKS - 1])
+    at_sent()
+    for j in range(CHUNKS):
+        rows = rows_at(0, j, chunk)
+        x = middle[rows, :] + second.take(j)
+        result[rows, :] = x
+        share_next.put(j, norm_of(x, gains[2 * layer + 2 : 2 * layer + 3, :]).astype(BF16))
+        if j == CHUNKS - 2:
+            at_last()
+    for j in range(CHUNKS):
+        share_next.arrived(j)
+    for part in (first, second, share, share_next):
+        part.close()
+
+
+def layer_outs(seq_len, width, heads_width):
+    return [
+        jax.ShapeDtypeStruct((3, seq_len, heads_width), BF16),
+        jax.ShapeDtypeStruct((seq_len, heads_width), BF16),
+        jax.ShapeDtypeStruct((seq_len // 2, width), F32),
+        jax.ShapeDtypeStruct((seq_len, width), BF16),
+    ]
+
+
+def layer_scratch(seq_len, width, heads_width):
+    half, chunk = seq_len // 2, seq_len // 2 // CHUNKS
+    block = max(chunk, min(QUERY_BLOCK, half))
+    return (
+        [pltpu.VMEM((seq_len, block), F32), pltpu.VMEM((heads_width, seq_len), BF16)]
+        + Exchange.scratch(chunk, width, FORWARD_KIND)
+        + Exchange.scratch(chunk, width, FORWARD_KIND)
+        + [pltpu.VMEM((CHUNKS, chunk, width), F32)]
+        + sems(6)
+    )
+
+
+LAYER_SCRATCH = 13
+
+
+def front_kernel(
+    ids, counted, gains, extra, table, key_seg, query_seg,
+    resid, normed, gain_all, count_all, ids_all, projected, mixed, middle, normed_two, result, normed_next,
+    *scratch, carry,
+):
+    embed_part(
+        ids, counted, gains, extra, table, resid, normed, gain_all, count_all, ids_all,
+        *scratch[:-LAYER_SCRATCH], carry,
+    )
+    carry.end(0, 1)
+    later = list(carry.all())[4:]
+
+    def at_half():
+        carry.hand_on(3)
+        carry.begin(*later[:2])
+
+    def at_feed():
+        carry.end(2, 3)
+        carry.begin(*later[2:])
+
+    forward_part(
+        0,
+        [carry.loads[0].value] + [load.value for load in carry.loads[1:4]],
+        (at_half, at_feed, lambda: carry.hand_on(*later[:2]), lambda: carry.hand_on(*later[2:3])),
+        normed, key_seg, query_seg, resid, gain_all,
+        projected, mixed, middle, normed_two, result, normed_next, *scratch[-LAYER_SCRATCH:],
+    )
+    carry.end(*later)
+
+
+def front(ids, counted, gains, extra, tables, key_seg, query_seg, owners, heads_width, collective_id, loads):
     seq_len = ids.size
     half, width = extra.shape
     share, vocab = tables.shape[1:]
     dma = pltpu.SemaphoreType.DMA
     return run(
-        embed_kernel,
-        "embed",
-        [ids, counted, gains, extra, tables],
+        front_kernel,
+        "front",
+        [ids, counted, gains, extra, tables, key_seg, query_seg],
         [
             jax.ShapeDtypeStruct((half, width), F32),
             jax.ShapeDtypeStruct((seq_len, width), BF16),
             jax.ShapeDtypeStruct((8, width), F32),
             jax.ShapeDtypeStruct((8, LANES), F32),
             jax.ShapeDtypeStruct((owners,) + ids.shape, jnp.int32),
-        ],
+        ]
+        + layer_outs(seq_len, width, heads_width)
+        + [jax.ShapeDtypeStruct((half, width), F32), jax.ShapeDtypeStruct((seq_len, width), BF16)],
         [
             pltpu.VMEM((vocab, LANES), BF16),
             pltpu.VMEM((half, vocab), BF16),
@@ -1052,7 +1214,8 @@
         ]
         + [dma((owners,))] * 10
         + [dma((half // 2 // LANES,))] * 2
-        + [dma((1, half // LANES))] * 2,
+        + [dma((1, half // LANES))] * 2
+        + layer_scratch(seq_len, width, heads_width),
         collective_id,
         loads,
     )
@@ -1077,23 +1240,24 @@
 
 
 def ffn_back_kernel(
-    row, grad, branch, w_red, w_in, w_out, before, after, normed, middle, gain, mixed,
+    row, grad, branch, w_red, w_in, w_out, normed, middle, gain, mixed,
     grad_middle, grad_attn, grad_mixed, d_red, d_in, d_out, d_gain,
-    grad_before, turned, near_out, near_in, far_out, far_in, send, recv, carry,
+    grad_before, after, turned, near_out, near_in, far_out, far_in, send, recv, carry,
 ):
     seq_len = normed.shape[0]
     chunk = seq_len // 2 // CHUNKS
     sibling, partner, mine, other = group_places(seq_len)
     greet([sibling, partner] + carry.peers())
-    carry.start()
+    carry.begin(*carry.all())
     sems = (send, recv)
     trade = Exchange((near_out, near_in, far_out, far_in), sems, 0, sibling, partner)
     share = Share(grad_attn, sems, 2, sibling, mine, chunk)
 
     def partial(start, j):
         rows = rows_at(start, j, chunk)
-        back = dot_nn(branch[rows, :], w_red[...])
-        low = (back * gelu_slope(before[rows, :])).astype(BF16)
+        pre = dot_nn(normed[rows, :], w_in[...])
+        after[rows, :] = gelu_of(pre).astype(BF16)
+        low = (dot_nn(branch[rows, :], w_red[...]) * gelu_slope(pre)).astype(BF16)
         grad_before[rows, :] = low
         return dot_nt(low, w_in[...])
 
@@ -1125,16 +1289,16 @@
     weight_grad(turned, mixed, d_out)
     trade.close()
     share.close()
-    carry.finish()
-
-
-def ffn_backward(row, grad, branch, w_red, w_in, w_out, before, after, normed, middle, gain, mixed, collective_id, loads):
+    carry.end(*carry.all())
+
+
+def ffn_backward(row, grad, branch, w_red, w_in, w_out, normed, middle, gain, mixed, collective_id, loads):
     seq_len, width = normed.shape
     half, chunk = seq_len // 2, seq_len // 2 // CHUNKS
     return run(
         functools.partial(ffn_back_kernel, row),
         "ffn_backward",
-        [grad, branch, w_red, w_in, w_out, before, after, normed, middle, gain, mixed],
+        [grad, branch, w_red, w_in, w_out, normed, middle, gain, mixed],
         [
             jax.ShapeDtypeStruct((half, width), F32),
             jax.ShapeDtypeStruct((seq_len, width), BF16),
@@ -1144,7 +1308,7 @@
             jax.ShapeDtypeStruct(w_out.shape, BF16),
             jax.ShapeDtypeStruct((1, gain.shape[1]), F32),
         ],
-        [pltpu.VMEM(before.shape, BF16), pltpu.VMEM((width, seq_len), BF16)]
+        [pltpu.VMEM((seq_len, w_in.shape[1]), BF16)] * 2 + [pltpu.VMEM((width, seq_len), BF16)]
         + Exchange.scratch(chunk, width, BACKWARD_KIND)
         + sems(3),
         collective_id,
@@ -1161,7 +1325,7 @@
     chunk = seq_len // 2 // CHUNKS
     sibling, partner, mine, other = group_places(seq_len)
     greet([sibling, partner] + carry.peers())
-    carry.start()
+    carry.begin(*carry.all())
     sems = (send, recv)
     trade = Exchange((near_out, near_in, far_out, far_in), sems, 0, sibling, partner)
     share = Share(branch, sems, 2, sibling, mine, chunk)
@@ -1195,7 +1359,7 @@
         share.arrived(j)
     trade.close()
     share.close()
-    carry.finish()
+    carry.end(*carry.all())
 
 
 def norm_backward(row, grads, weights, normed, value, gain, upstream, scale, collective_id, loads):
@@ -1223,135 +1387,6 @@
     return jnp.where(inside, value, jnp.zeros_like(value))
 
 
-QUERY_BLOCK = 256
-
-
-def forward_kernel(
-    layer, normed, w_query, key_seg, query_seg, resid, w_out, w_in, gains,
-    projected, mixed, middle, normed_two, before, after, result, normed_next,
-    bias, values_t, near_out, near_in, far_out, far_in, near_out2, near_in2, far_out2, far_in2, own2, send, recv,
-    carry,
-):
-    seq_len, width = normed.shape
-    chunk = seq_len // 2 // CHUNKS
-    block = bias.shape[1]
-    heads = mixed.shape[1] // HD
-    sibling, partner, mine, other = group_places(seq_len)
-    greet([sibling, partner] + carry.peers())
-    carry.start()
-    pair = (send, recv)
-    first = Exchange((near_out, near_in, far_out, far_in), pair, 0, sibling, partner)
-    second = Exchange((near_out2, near_in2, far_out2, far_in2), pair, 2, sibling, partner)
-    share = Share(normed_two, pair, 4, sibling, mine, chunk)
-    share_next = Share(normed_next, pair, 5, sibling, mine, chunk)
-
-    def ask(i, _):
-        rows = rows_at(0, i, block)
-        for which in range(3):
-            projected[which, rows, :] = dot_nn(normed[rows, :], w_query[which]).astype(BF16)
-        return 0
-
-    lax.fori_loop(0, seq_len // block, ask, 0)
-    values_t[...] = jnp.transpose(projected[2])
-
-    def attend_rows(start):
-        rows = pl.ds(pl.multiple_of(start, block), block)
-        bias[...] = jnp.where(key_seg[...] == query_seg[:, rows], 0.0, -1e30)
-        asked = projected[0, rows, :] * HD ** (-0.5)
-        parts = []
-        for head in range(heads):
-            scores = dot_nt(projected[1], head_lanes(asked, head, HD)) + bias[...]
-            powers = jnp.exp(scores - jnp.max(scores, axis=0, keepdims=True))
-            probs = (powers * (1.0 / jnp.sum(powers, axis=0, keepdims=True))).astype(BF16)
-            parts.append(dot_nn(values_t[head * HD : (head + 1) * HD, :], probs))
-        mixed[rows, :] = jnp.transpose(jnp.concatenate(parts, axis=0)).astype(BF16)
-
-    def project(start, j):
-        return dot_nt(mixed[rows_at(start, j, chunk), :], w_out[...])
-
-    def feed(rows):
-        pre = dot_nn(normed_two[rows, :], w_in[...])
-        before[rows, :] = pre
-        act = gelu_of(pre).astype(BF16)
-        after[rows, :] = act
-        return dot_nt(act, w_red())
-
-    per_block = block // chunk
-    for part in range(CHUNKS // per_block):
-
-        def both(i, _):
-            attend_rows(jnp.where(i == 0, other, mine) + part * block)
-            return 0
-
-        lax.fori_loop(0, 2, both, 0)
-        for j in range(part * per_block, (part + 1) * per_block):
-            first.give(j, project(other, j))
-        if part == 0:
-            carry.relay(FIRST)
-            carry.start(1)
-        for j in range(part * per_block, (part + 1) * per_block):
-            first.pass_on(j, project(mine, j))
-    carry.need()
-    reduced = [load.out for load in carry.loads if load.needed][0]
-
-    def w_red():
-        return reduced[...].reshape(w_in.shape)
-
-    for j in range(CHUNKS):
-        rows = rows_at(0, j, chunk)
-        mid = resid[rows, :] + first.take(j)
-        middle[rows, :] = mid
-        share.put(j, norm_of(mid, gains[2 * layer + 1 : 2 * layer + 2, :]).astype(BF16))
-        own2[j] = feed(rows_at(mine, j, chunk))
-        share.arrived(j)
-        second.give(j, feed(rows_at(other, j, chunk)))
-        if j >= 1:
-            second.pass_on(j - 1, own2[j - 1])
-    second.pass_on(CHUNKS - 1, own2[CHUNKS - 1])
-    carry.relay(SECOND)
-    for j in range(CHUNKS):
-        rows = rows_at(0, j, chunk)
-        x = middle[rows, :] + second.take(j)
-        result[rows, :] = x
-        share_next.put(j, norm_of(x, gains[2 * layer + 2 : 2 * layer + 3, :]).astype(BF16))
-        if j == CHUNKS - 2:
-            carry.relay(THIRD)
-    for j in range(CHUNKS):
-        share_next.arrived(j)
-    for part in (first, second, share, share_next):
-        part.close()
-    carry.finish()
-
-
-def forward_block(layer, normed, w_query, key_seg, query_seg, resid, w_out, w_in, gains, collective_id, loads):
-    seq_len, width = normed.shape
-    hidden, heads_width = w_in.shape[1], w_query.shape[2]
-    half, chunk = seq_len // 2, seq_len // 2 // CHUNKS
-    block = max(chunk, min(QUERY_BLOCK, half))
-    return run(
-        functools.partial(forward_kernel, layer),
-        "forward_block",
-        [normed, w_query, key_seg, query_seg, resid, w_out, w_in, gains],
-        [
-            jax.ShapeDtypeStruct((3, seq_len, heads_width), BF16),
-            jax.ShapeDtypeStruct((seq_len, heads_width), BF16),
-            jax.ShapeDtypeStruct((half, width), F32),
-            jax.ShapeDtypeStruct((seq_len, width), BF16),
-            jax.ShapeDtypeStruct((seq_len, hidden), F32),
-            jax.ShapeDtypeStruct((seq_len, hidden), BF16),
-            jax.ShapeDtypeStruct((half, width), F32),
-            jax.ShapeDtypeStruct((seq_len, width), BF16),
-        ],
-        [pltpu.VMEM((seq_len, block), F32), pltpu.VMEM((heads_width, seq_len), BF16)]
-        + Exchange.scratch(chunk, width, FORWARD_KIND)
-        + Exchange.scratch(chunk, width, FORWARD_KIND)
-        + [pltpu.VMEM((CHUNKS, chunk, width), F32)]
-        + sems(6),
-        collective_id,
-        loads,
-    )
-
-
 def attention_back_kernel(projected, grad_mixed, key_seg, query_seg, out, bias, keys_t, grad_keys, grad_values, carry):
     seq_len, width = grad_mixed.shape
     block = bias.shape[1]
@@ -1359,7 +1394,7 @@
     scale = HD ** (-0.5)
     if carry.loads:
         greet(carry.peers())
-    carry.start()
+    carry.begin(*carry.all())
     keys_t[...] = jnp.transpose(projected[1])
     grad_keys[...] = jnp.zeros(grad_keys.shape, F32)
     grad_values[...] = jnp.zeros(grad_values.shape, F32)
@@ -1388,7 +1423,7 @@
     lax.fori_loop(0, seq_len // block, queries, 0)
     out[1] = grad_keys[...].astype(BF16)
     out[2] = grad_values[...].astype(BF16)
-    carry.finish()
+    carry.end(*carry.all())
 
 
 def attention_back(projected, grad_mixed, key_seg, query_seg, collective_id, loads):
@@ -1418,31 +1453,20 @@
     return jnp.transpose(total)[:8, :]
 
 
-def loss_kernel(
-    pieces, row, normed, info, value, gain, *refs, carry,
-):
-    tables, refs = refs[:pieces], refs[pieces:]
-    (grad_out, branch, d_gain, losses), refs = refs[:4], refs[4:]
-    d_tables, refs = refs[:pieces], refs[pieces:]
-    loss_body(row, normed, info, value, gain, tables, grad_out, branch, d_gain, losses, d_tables, *refs, carry)
-
-
-def loss_body(
-    row, normed, info, value, gain, tables, grad_out, branch, d_gain, losses, d_tables,
+def loss_part(
+    row, normed, info, value, gain, table_loads, grad_out, branch, d_gain, losses, d_tables,
     logits, grads, places, turned, stat_out, stat_in, sum_out, sum_in,
-    near_out, near_in, far_out, far_in, send, recv, stat_send, stat_recv, sum_send, sum_recv, carry,
+    stat_send, stat_recv, sum_send, sum_recv, near_out, near_in, far_out, far_in, send, recv,
 ):
     seq_len, width = normed.shape
     chunk = seq_len // 2 // CHUNKS
-    piece_width = tables[0].shape[1]
-    vocab = piece_width * len(tables)
+    piece_width = table_loads[0].out.shape[-1]
+    vocab = piece_width * len(table_loads)
     tiles = vocab // LANES
     blocks = seq_len // LANES
     me = lax.axis_index(NARROW)
     sibling, partner, mine, other = group_places(seq_len)
     peers = [{NARROW: lax.rem(me + k, 4)} for k in range(1, 4)]
-    greet(peers + carry.peers())
-    carry.start()
     sems = (send, recv)
     trade = Exchange((near_out, near_in, far_out, far_in), sems, 0, sibling, partner)
     share = Share(branch, sems, 2, sibling, mine, chunk)
@@ -1459,7 +1483,7 @@
     def tile_at(t):
         return pl.ds(pl.multiple_of(t * LANES, LANES), LANES)
 
-    def ask(b):
+    def ask(b, _):
         rows = rows_at(0, b, LANES)
         here = info[:, rows]
         at_noised = spread(here[0:1] - first)
@@ -1489,16 +1513,19 @@
         stat_out[b] = to_rows([top] + [jnp.sum(total, axis=1, keepdims=True) for total in totals])
         for k in range(3):
             stat_copy(b, k).start()
-
-    def product(i, _):
-        rows = rows_at(0, i, TILE)
-        for k, table in enumerate(tables):
-            logits[rows, k * piece_width : (k + 1) * piece_width] = dot_nn(normed[rows, :], table[...])
-        for b in range(TILE // LANES):
-            ask(i * (TILE // LANES) + b)
         return 0
 
-    lax.fori_loop(0, seq_len // TILE, product, 0)
+    for k, table in enumerate(table_loads):
+        if k == len(table_loads) - 1:
+            table.finish()
+
+        def product(i, _):
+            rows = rows_at(0, i, TILE)
+            logits[rows, k * piece_width : (k + 1) * piece_width] = dot_nn(normed[rows, :], table.value())
+            return 0
+
+        lax.fori_loop(0, seq_len // TILE, product, 0)
+    lax.fori_loop(0, blocks, ask, 0)
 
     def scalars(b):
         here = info[:, rows_at(0, b, LANES)]
@@ -1598,8 +1625,8 @@
         for b in range(chunk // LANES):
             pull(base + b)
         total = None
-        for k, table in enumerate(tables):
-            part = dot_nt(grads[rows_at(start, j, chunk), k * piece_width : (k + 1) * piece_width], table[...])
+        for k, table in enumerate(table_loads):
+            part = dot_nt(grads[rows_at(start, j, chunk), k * piece_width : (k + 1) * piece_width], table.value())
             total = part if total is None else total + part
         return total
 
@@ -1631,25 +1658,72 @@
         return 0
 
     lax.fori_loop(0, blocks, finish, 0)
-    carry.finish()
-
-
-def loss_and_back(row, normed, tables, info, value, gain, collective_id, loads):
+
+
+def back_kernel(
+    layer, normed, key_seg, query_seg, resid, w_query, w_out, w_in, gains, info,
+    projected, mixed, middle, normed_two, grad_out, branch, d_gain, losses, *refs, carry,
+):
+    pieces = len(carry.loads) - 1
+    d_tables, refs = refs[:pieces], refs[pieces:]
+    (result, normed_next), refs = refs[:2], refs[2:]
+    loss_scratch, layer_refs = refs[:-LAYER_SCRATCH], refs[-LAYER_SCRATCH:]
+    me = lax.axis_index(NARROW)
+    greet([{NARROW: lax.rem(me + k, 4)} for k in range(1, 4)] + carry.peers())
+    carry.begin(0, 1)
+
+    def at_half():
+        carry.begin(2)
+
+    def at_feed():
+        carry.end(0)
+        carry.hand_on(1)
+        carry.begin(3)
+
+    def at_sent():
+        carry.hand_on(2)
+        carry.begin(4)
+
+    def at_last():
+        carry.hand_on(3)
+
+    forward_part(
+        layer,
+        [lambda which: w_query[which], lambda: w_out[...], lambda: w_in[...], carry.loads[0].value],
+        (at_half, at_feed, at_sent, at_last),
+        normed, key_seg, query_seg, resid, gains,
+        projected, mixed, middle, normed_two, result, normed_next, *layer_refs,
+    )
+    carry.hand_on(4)
+    carry.end(1, 2, 3)
+    loss_part(
+        2 * layer + 2, normed_next, info, result, gains, carry.loads[1:], grad_out, branch, d_gain, losses, d_tables,
+        *loss_scratch, *layer_refs[2:6], *layer_refs[-2:],
+    )
+
+
+def last_and_loss(
+    layer, normed, key_seg, query_seg, resid, w_query, w_out, w_in, gains, info, vocab, collective_id, loads
+):
     seq_len, width = normed.shape
-    vocab = sum(table.shape[1] for table in tables)
-    half, chunk, blocks = seq_len // 2, seq_len // 2 // CHUNKS, seq_len // LANES
+    heads_width = w_query.shape[2]
+    half, blocks = seq_len // 2, seq_len // LANES
+    pieces = len(loads) - 1
     return run(
-        functools.partial(loss_kernel, len(tables), row),
-        "loss_and_back",
-        [normed, info, value, gain, *tables],
-        [
+        functools.partial(back_kernel, layer),
+        "last_and_loss",
+        [normed, key_seg, query_seg, resid, w_query, w_out, w_in, gains, info],
+        layer_outs(seq_len, width, heads_width)
+        + [
             jax.ShapeDtypeStruct((half, width), F32),
             jax.ShapeDtypeStruct((seq_len, width), BF16),
             jax.ShapeDtypeStruct((1, width), F32),
             jax.ShapeDtypeStruct((1, seq_len), F32),
         ]
-        + [jax.ShapeDtypeStruct(table.shape, BF16) for table in tables],
+        + [jax.ShapeDtypeStruct((width, vocab // pieces), BF16)] * pieces,
         [
+            pltpu.VMEM((half, width), F32),
+            pltpu.VMEM((seq_len, width), BF16),
             pltpu.VMEM((seq_len, vocab), F32),
             pltpu.VMEM((seq_len, vocab), BF16),
             pltpu.VMEM((blocks, 2, LANES, LANES), F32),
@@ -1659,9 +1733,8 @@
             pltpu.VMEM((blocks, 8, LANES), F32),
             pltpu.VMEM((3, blocks, 8, LANES), F32),
         ]
-        + Exchange.scratch(chunk, width, BACKWARD_KIND)
-        + sems(3)
-        + [pltpu.SemaphoreType.DMA((3, blocks))] * 4,
+        + [pltpu.SemaphoreType.DMA((3, blocks))] * 4
+        + layer_scratch(seq_len, width, heads_width),
         collective_id,
         loads,
     )
@@ -1760,7 +1833,7 @@
     for step in range(1, owners):
         wide_copy(step).start()
     all_in[me, pl.ds(at_quarter, quarter), :] = out_blocks[me]
-    carry.start()
+    carry.begin(*carry.all())
     gain_near().wait_recv()
     both = gains_out[...] + gains_in[...]
     for owner in range(owners):
@@ -1839,7 +1912,7 @@
         small = small + line_in[step]
     d_full[...] = result
     d_small[...] = small
-    carry.finish()
+    carry.end(*carry.all())
     square = jnp.sum(result * result) + jnp.sum(d_table[...] * d_table[...])
     for part in squares:
         square = square + part[0, 0]
@@ -1936,7 +2009,8 @@
 def shares_tile(wide, narrow, noised, attn_out, ffn_in, tables):
     rows, seq_len = noised.shape
     return (
-        narrow == 4
+        attn_out.shape[0] == 2
+        and narrow == 4
         and wide % 2 == 0
         and rows == 1
         and seq_len % (2 * CHUNKS * 128) == 0
@@ -1999,53 +2073,32 @@
     ids = noised.reshape(-1, LANES)
     quarter = vocab // PIECES
     windows = [(k * quarter, quarter) for k in range(PIECES)]
-    (residual, normed, gain_w, counts, ids_all), carried = embed(
-        ids, counted, gains, extra, tables, wide, 0,
-        [
-            GatherLoad(attn_in, 0, 1, wide, FIRST),
-            GatherLoad(attn_out, 0, 0, wide, FIRST),
-            GatherLoad(ffn_in, 0, 0, wide, LAST, late=1),
-        ],
+    key_seg, query_seg = segments.reshape(-1, 1), segments.reshape(1, -1)
+    weights = (attn_in, attn_out, ffn_in, ffn_out)
+    (residual, normed, gain_w, counts, ids_all, projected, mixed, middle, normed_two, result, normed_next), carried = front(
+        ids, counted, gains, extra, tables, key_seg, query_seg, wide, attn_out.shape[2], 0,
+        [GatherLoad(value, 0, lead, wide, place=KEPT) for value, lead in zip(weights, leads)]
+        + [GatherLoad(value, 1, lead, wide) for value, lead in zip(weights[:3], leads)]
+        + [SlowLoad(ffn_out, 1, 0, wide)],
     )
     token_total = counts[gain_rows, 0]
-    next_id = 1
-    key_seg, query_seg = segments.reshape(-1, 1), segments.reshape(1, -1)
-    kept = []
-    for layer in range(layers):
-        query_w, output_w, expand_w = [joined(value, lead) for value, lead in zip(carried, leads)]
-        loads = [GatherLoad(ffn_out, layer, 0, wide, FIRST, needed=True)]
-        if layer + 1 < layers:
-            loads += [
-                GatherLoad(attn_in, layer + 1, 1, wide, SECOND, late=1),
-                GatherLoad(attn_out, layer + 1, 0, wide, SECOND, late=1),
-                GatherLoad(ffn_in, layer + 1, 0, wide, THIRD, late=1),
-            ]
-        else:
-            loads += [
-                GatherLoad(tables, 1, 0, wide, stage, window, late)
-                for window, stage, late in zip(windows, (SECOND, SECOND, THIRD, LAST), (0, 1, 1, 1))
-            ]
-        (projected, mixed, middle, normed_two, before, after, result, normed_next), carried = forward_block(
-            layer, normed, query_w, key_seg, query_seg, residual, output_w, expand_w, gain_w, next_id, loads
-        )
-        next_id += 1
-        reduce_w, *carried = carried
-        kept.append(
-            (residual, normed, projected, mixed, middle, normed_two, before, after)
-            + (query_w, output_w, expand_w, joined(reduce_w, 0))
-        )
-        residual, normed = result, normed_next
-    tables_w = [joined(value, 0) for value in carried]
-
+    first_w = [joined(value, lead) for value, lead in zip(carried[:4], leads)]
+    query_w, output_w, expand_w = [joined(value, lead) for value, lead in zip(carried[4:7], leads)]
+    kept = [(residual, normed, projected, mixed, middle, normed_two, *first_w)]
     noised_flat, clean_flat = noised.reshape(-1), clean.reshape(-1)
     info = jnp.stack(
         [noised_flat.astype(F32), clean_flat.astype(F32), step_flat.astype(F32), mask / token_total, mask]
         + [jnp.zeros_like(mask)] * 3
     )
-    (grad, branch, gain_final, losses, *d_last), _ = loss_and_back(
-        2 * layers, normed, tables_w, info, residual, gain_w, next_id, []
-    )
-    next_id += 1
+    (projected, mixed, middle, normed_two, grad, branch, gain_final, losses, *d_last), (reduce_w,) = last_and_loss(
+        1, normed_next, key_seg, query_seg, result, query_w, output_w, expand_w, gain_w, info, vocab, 1,
+        [FastLoad(carried[7], 0, wide)]
+        + [GatherLoad(tables, 1, 0, wide, window, place=LOCAL) for window in windows],
+    )
+    kept.append(
+        (result, normed_next, projected, mixed, middle, normed_two, query_w, output_w, expand_w, joined(reduce_w, 0))
+    )
+    next_id = 2
     gain_grads = [None] * (2 * layers) + [gain_final]
     own, squares = {}, []
 
@@ -2073,12 +2126,12 @@
     route = Route()
     route.waiting = [((TABLE, k), piece, 0) for k, piece in enumerate(d_last)]
     for layer in reversed(range(layers)):
-        residual, normed, projected, mixed, middle, normed_two, before, after, *four_w = kept[layer]
+        residual, normed, projected, mixed, middle, normed_two, *four_w = kept[layer]
         query_w, output_w, expand_w, reduce_w = four_w
         top = layer == layers - 1
         loads = route.take(3 if top else 2, 3)
         (grad_middle, grad_attn, grad_mixed, d_red, d_in, d_out, gain_two), carried = ffn_backward(
-            2 * layer + 1, grad, branch, reduce_w, expand_w, output_w, before, after,
+            2 * layer + 1, grad, branch, reduce_w, expand_w, output_w,
             normed_two, middle, gain_w, mixed, next_id, loads,
         )
         route.back(carried)

time: 591 us -> 535 us (0.905)
  Pallas kernels: 557 us -> 502 us
    pallas_call x11 -> x9, Pallas kernels: 557 us -> 502 us  [run(): pl.pallas_call(kernel, out_shape=tuple(outs) + tuple((out for load in loa...]
where the time goes in v6:
time: 535 us; the launch traced here: 532 us
  Pallas kernels  502 us (94%)
  other arithmetic  18.8 us (4%)
  local copies, waits for them, and re-layouts  8.06 us (2%)
    pallas_call x9, Pallas kernels, run(): pl.pallas_call(kernel, out_shape=tuple(outs) + tuple((out for load in loa...  502 us

profile of v6, /device:TPU:0, one launch (start us, length us, event | category | flops | bytes accessed | tf_op | source)
XLA Modules:
  0.0 532.0 jit_solution(6284364910710425847)
XLA Ops:
  0.7 0.7 dynamic-slice_convert_fusion
  1.4 0.7 convert_element_type.48
  2.1 0.7 convert_element_type.47
  2.8 0.7 convert_element_type.49
  3.5 0.7 convert_element_type.50
  4.1 1.7 copy.50.refs_5_.refs_1_.refs_2_
  5.8 2.8 multiply_sine_fusion
  8.7 1.3 pad_maximum_fusion.refs_3_
  9.9 132.3 %front.1 = (f32[512,768]{1,0:T(8,128)}, bf16[1024,768]{1,0:T(8,128)(2,1)}, f32[8,768]{1,0:T(8,128)}, f32[8,128]{1,0:T(8,128)}, s32[8,8,128]{2,1,0:T(8,128)}, /*i...) custom-call(s32[8,128]{1,0:T(8,128)} %bitcast.70, ...), custom_call_target="tpu_custom_call" | custom-call | tf_op jit(solution)/shard_map/front/pallas_call | solution.py:818
  142.3 1.2 slice.12
  143.5 0.7 broadcast_divide_fusion
  144.2 0.7 stack.57.refs_8_
  144.8 116.5 %last_and_loss.1 = (bf16[3,1024,192]{2,1,0:T(8,128)(2,1)}, bf16[1024,192]{1,0:T(8,128)(2,1)}, f32[512,768]{1,0:T(8,128)}, bf16[1024,768]{1,0:T(8,128)(2,1)}, f32...) custom-call(bf16[1024,768]{1,0:T(8,128)(2,1)} %get-tuple-element.116, ...), custom_call_target="tpu_custom_call" | custom-call | tf_op jit(solution)/shard_map/last_and_loss/pallas_call | solution.py:818
  261.3 36.9 %ffn_backward.2 = (f32[512,768]{1,0:T(8,128)}, bf16[1024,768]{1,0:T(8,128)(2,1)}, bf16[1024,192]{1,0:T(8,128)(2,1)}, bf16[768,768]{1,0:T(8,128)(2,1)}, bf16[768,...) custom-call(f32[512,768]{1,0:T(8,128)} %get-tuple-element.125.refs_0, ...), custom_call_target="tpu_custom_call" | custom-call | tf_op jit(solution)/shard_map/ffn_backward/pallas_call | solution.py:818
  298.2 22.7 %attention_back.2 = (bf16[3,1024,192]{2,1,0:T(8,128)(2,1)}, bf16[4,96,512]{2,1,0:T(8,128)(2,1)}, f32[96,512]{1,0:T(8,128)}, f32[8,128]{1,0:T(8,128)}, f32[96,512]{1,0:T(8,128)}, /*index=5*/f32[8,128]{1,0:T(8,128)}) custom-call(bf16[3,1024,192]{2,1,0:T(8,128)(2,1)} %get-tuple-element.124.refs_0_, bf16[1024,192]{1,0:T(8,128)(2,1)} %get-tuple-element.134.refs_1_, ...), custom_call_target="tpu_custom_call" | custom-call | tf_op jit(solution)/shard_map/attention_back/pallas_call | solution.py:818
  320.9 35.5 %norm_backward.2 = (f32[512,768]{1,0:T(8,128)}, bf16[1024,768]{1,0:T(8,128)(2,1)}, bf16[3,768,192]{2,1,0:T(8,128)(2,1)}, f32[1,768]{1,0:T(1,128)}, bf16[4,96,768...) custom-call(bf16[3,1024,192]{2,1,0:T(8,128)(2,1)} %get-tuple-element, ...), custom_call_target="tpu_custom_call" | custom-call | tf_op jit(solution)/shard_map/norm_backward/pallas_call | solution.py:818
  356.5 35.6 %ffn_backward.3 = (f32[512,768]{1,0:T(8,128)}, bf16[1024,768]{1,0:T(8,128)(2,1)}, bf16[1024,192]{1,0:T(8,128)(2,1)}, bf16[768,768]{1,0:T(8,128)(2,1)}, bf16[768,...) custom-call(f32[512,768]{1,0:T(8,128)} %get-tuple-element.144.refs_0, ...), custom_call_target="tpu_custom_call" | custom-call | tf_op jit(solution)/shard_map/ffn_backward/pallas_call | solution.py:818
  392.1 23.0 %attention_back.3 = (bf16[3,1024,192]{2,1,0:T(8,128)(2,1)}, bf16[4,96,768]{2,1,0:T(8,128)(2,1)}, f32[96,192]{1,0:T(8,128)}, f32[8,128]{1,0:T(8,128)}, f32[3,96,192]{2,1,0:T(8,128)}, /*index=5*/f32[8,128]{1,0:T(8,128)}) custom-call(bf16[3,1024,192]{2,1,0:T(8,128)(2,1)} %get-tuple-element.115.refs_0_, bf16[1024,192]{1,0:T(8,128)(2,1)} %get-tuple-element.156.refs_1_, ...), custom_call_target="tpu_custom_call" | custom-call | tf_op jit(solution)/shard_map/attention_back/pallas_call | solution.py:818
  415.1 32.5 %norm_backward.3 = (f32[512,768]{1,0:T(8,128)}, bf16[1024,768]{1,0:T(8,128)(2,1)}, bf16[3,768,192]{2,1,0:T(8,128)(2,1)}, f32[1,768]{1,0:T(1,128)}, bf16[4,96,768...) custom-call(bf16[3,1024,192]{2,1,0:T(8,128)(2,1)} %get-tuple-element.160.refs_0_, ...), custom_call_target="tpu_custom_call" | custom-call | tf_op jit(solution)/shard_map/norm_backward/pallas_call | solution.py:818
  447.6 0.0 copy-start.26
  447.7 0.0 copy-start.27
  447.7 0.0 copy-start.28
  447.7 0.0 copy-start.24
  447.7 66.8 %tail.1 = (f32[96,2048]{1,0:T(8,128)}, f32[3,96,192]{2,1,0:T(8,128)}, f32[8,128]{1,0:T(8,128)}, f32[8,128]{1,0:T(8,128)}, f32[96,768]{1,0:T(8,128)}, /*index=5*/...) custom-call(bf16[1024,768]{1,0:T(8,128)(2,1)} %get-tuple-element.168.refs_0_, ...), custom_call_target="tpu_custom_call" | custom-call | tf_op jit(solution)/shard_map/tail/pallas_call | solution.py:818
  514.6 0.0 copy-start.6
  514.6 0.0 copy-start.1
  514.6 0.0 copy-start.8
  514.6 0.0 copy-start.9
  514.7 1.4 fusion.18
  516.8 1.3 fusion.6
  518.2 0.1 maximum_bitcast_fusion
  518.3 2.0 fusion.14
  520.3 0.0 copy-start.2
  520.3 0.0 copy-start.10
  520.3 0.0 copy-start.11
  520.4 1.6 fusion.16
  522.0 0.2 copy-done.10
  522.2 0.4 copy-done.11
  522.6 0.2 copy-done.12
  522.8 0.2 copy-done.13
  523.0 0.1 copy-done.14
  523.1 0.1 copy-done.15
  523.2 0.1 copy-done.17
  523.3 2.3 fusion.10
  525.6 1.0 copy-done.4
  526.6 0.5 copy-done.5
  527.1 0.2 copy-done.7
  527.3 3.3 fusion.8
  (40 shorter events, 0.1 us)
Async XLA Ops:
  9.9 133.6 %copy-start.25 = (s32[1,1024]{1,0:T(1,128)S(1)}, s32[1,1024]{1,0:T(1,128)}, u32[]{:S(2)}) copy-start(s32[1,1024]{1,0:T(1,128)} %refs_1_.1) | copy-start | bytes 12292
  447.6 69.2 %copy-start.26 = (f32[5,96]{1,0:T(8,128)S(1)}, f32[5,96]{1,0:T(8,128)}, u32[]{:S(2)}) copy-start(f32[5,96]{1,0:T(8,128)} %refs_2_.2) | copy-start | bytes 5764
  447.7 69.2 %copy-start.27 = (f32[5,96]{1,0:T(8,128)S(1)}, f32[5,96]{1,0:T(8,128)}, u32[]{:S(2)}) copy-start(f32[5,96]{1,0:T(8,128)} %param.39) | copy-start | bytes 5764
  447.7 69.2 %copy-start.28 = (f32[5,96]{1,0:T(8,128)S(1)}, f32[5,96]{1,0:T(8,128)}, u32[]{:S(2)}) copy-start(f32[5,96]{1,0:T(8,128)} %param.45) | copy-start | bytes 5764
  447.7 70.5 %copy-start.20 = (f32[96,512]{1,0:T(8,128)S(1)}, f32[96,512]{1,0:T(8,128)}, u32[]{:S(2)}) copy-start(f32[96,512]{1,0:T(8,128)} %get-tuple-element.198) | copy-start | bytes 589828
  447.7 70.5 %copy-start.21 = (f32[96,512]{1,0:T(8,128)S(1)}, f32[96,512]{1,0:T(8,128)}, u32[]{:S(2)}) copy-start(f32[96,512]{1,0:T(8,128)} %get-tuple-element.199) | copy-start | bytes 589828
  447.7 70.4 %copy-start.22 = (f32[96,512]{1,0:T(8,128)S(1)}, f32[96,512]{1,0:T(8,128)}, u32[]{:S(2)}) copy-start(f32[96,512]{1,0:T(8,128)} %get-tuple-element.200) | copy-start | bytes 589828
  447.7 70.4 %copy-start.23 = (f32[96,512]{1,0:T(8,128)S(1)}, f32[96,512]{1,0:T(8,128)}, u32[]{:S(2)}) copy-start(f32[96,512]{1,0:T(8,128)} %get-tuple-element.201) | copy-start | bytes 589828
  447.7 70.5 %copy-start.24 = (f32[2,96,192]{2,1,0:T(8,128)S(1)}, f32[2,96,192]{2,1,0:T(8,128)}, u32[]{:S(2)}) copy-start(f32[2,96,192]{2,1,0:T(8,128)} %param.35) | copy-start | bytes 442372
  514.6 3.6 copy-start.6
  514.6 5.7 %copy-start.1 = (f32[2,3,96,192]{3,2,1,0:T(8,128)S(1)}, f32[2,3,96,192]{3,2,1,0:T(8,128)}, u32[]{:S(2)}) copy-start(f32[2,3,96,192]{3,2,1,0:T(8,128)} %refs_7_.1) | copy-start | bytes 1327108
  514.6 5.6 %copy-start.8 = (f32[2,3,96,192]{3,2,1,0:T(8,128)S(1)}, f32[2,3,96,192]{3,2,1,0:T(8,128)}, u32[]{:S(2)}) copy-start(f32[2,3,96,192]{3,2,1,0:T(8,128)} %param.34) | copy-start | bytes 1327108
  514.6 5.6 %copy-start.9 = (f32[2,3,96,192]{3,2,1,0:T(8,128)S(1)}, f32[2,3,96,192]{3,2,1,0:T(8,128)}, u32[]{:S(2)}) copy-start(f32[2,3,96,192]{3,2,1,0:T(8,128)} %param.40) | copy-start | bytes 1327108
  514.6 5.6 %copy-start.16 = (f32[3,96,192]{2,1,0:T(8,128)S(1)}, f32[3,96,192]{2,1,0:T(8,128)}, u32[]{:S(2)}) copy-start(f32[3,96,192]{2,1,0:T(8,128)} %get-tuple-element.190) | copy-start | bytes 663556
  514.6 5.6 %copy-start.19 = (f32[3,96,192]{2,1,0:T(8,128)S(1)}, f32[3,96,192]{2,1,0:T(8,128)}, u32[]{:S(2)}) copy-start(f32[3,96,192]{2,1,0:T(8,128)} %get-tuple-element.189) | copy-start | bytes 663556
  518.2 3.8 copy-start.18
  520.3 1.7 copy-start.2
  520.3 1.7 copy-start.3
  520.3 1.9 copy-start.10
  520.3 2.3 copy-start.11
  520.3 2.5 copy-start.12
  520.3 2.7 copy-start.13
  520.4 2.7 copy-start.14
  520.4 2.8 copy-start.15
  520.4 2.9 copy-start.17
  523.3 2.3 copy-start
  523.3 3.4 copy-start.4
  523.3 3.8 copy-start.5
  523.3 4.0 copy-start.7

commit v7 on v6

--- a/solution.py
+++ b/solution.py
@@ -722,15 +722,16 @@
 class PairLoad:
     ways = (FAST,)
 
-    def __init__(self, full, lead, count):
-        self.lead, self.count = lead, count
-        shape, slows = full.shape[:lead] + full.shape[lead + 1 :], count // 2
-        self.operands, self.in_specs = [full], [whole_vmem()]
-        self.outs, self.out_specs = [jax.ShapeDtypeStruct((slows,) + shape, BF16)], [whole_vmem()]
-        self.scratch = [pltpu.VMEM((slows,) + shape, BF16)] + [pltpu.SemaphoreType.DMA((slows,))] * 2
+    def __init__(self, full, lead, inside=False):
+        self.lead, self.count, self.inside = lead, full.shape[lead], inside
+        self.shape, self.slows = full.shape[:lead] + full.shape[lead + 1 :], self.count // 2
+        self.operands, self.in_specs = ([], []) if inside else ([full], [whole_vmem()])
+        self.outs, self.out_specs = [jax.ShapeDtypeStruct((self.slows,) + self.shape, BF16)], [whole_vmem()]
+        self.scratch = [pltpu.VMEM((self.slows,) + self.shape, BF16)] + [pltpu.SemaphoreType.DMA((self.slows,))] * 2
 
     def bind(self, given, out, scratch):
-        self.full, self.out = given[0], out[0]
+        self.full = None if self.inside else given[0]
+        self.out = out[0]
         self.came, self.send, self.recv = scratch
         self.me, self.slow, self.fast, self.slows = wide_places(self.count)
 
@@ -745,7 +746,7 @@
         )
 
     def start(self):
-        for step in range(self.slows):
+        for step in list(range(1, self.slows)) + [0]:
             self.copy(step).start()
 
     def finish(self):
@@ -753,6 +754,47 @@
             self.copy(step).wait()
             total = self.block(step, self.fast)[...].astype(F32) + self.came[step].astype(F32)
             self.out[step] = total.astype(BF16)
+
+
+class ReduceLoad(PairLoad):
+    ways = (SLOW, FAST)
+
+    def __init__(self, full, lead, inside=False):
+        super().__init__(full, lead, inside)
+        self.outs = [jax.ShapeDtypeStruct(self.shape, F32), jax.ShapeDtypeStruct((8, 128), F32)]
+        self.out_specs = [whole_vmem()] * 2
+        self.scratch = (
+            self.scratch
+            + [pltpu.VMEM((self.slows - 1,) + self.shape, BF16)]
+            + [pltpu.SemaphoreType.DMA((self.slows,))] * 2
+        )
+
+    def bind(self, given, out, scratch):
+        super().bind(given, out[:1], scratch[:3])
+        self.squares = out[1]
+        self.landed, self.line_send, self.line_recv = scratch[3:]
+
+    def line_copy(self, step):
+        return remote(
+            self.came.at[step], self.landed.at[step - 1], self.line_send.at[step], self.line_recv.at[step],
+            {WIDE: 2 * lax.rem(self.slow + step, self.slows) + self.fast},
+        )
+
+    def relay(self):
+        for step in list(range(1, self.slows)) + [0]:
+            self.copy(step).wait()
+            total = self.block(step, self.fast)[...].astype(F32) + self.came[step].astype(F32)
+            self.came[step] = total.astype(BF16)
+            if step:
+                self.line_copy(step).start()
+
+    def finish(self):
+        total = self.came[0].astype(F32)
+        for step in range(1, self.slows):
+            self.line_copy(step).wait()
+            total = total + self.landed[step - 1].astype(F32)
+        self.out[...] = total
+        self.squares[...] = jnp.full(self.squares.shape, jnp.sum(total * total), F32)
 
 
 class LineLoad:
@@ -790,8 +832,11 @@
         self.squares[...] = jnp.full(self.squares.shape, jnp.sum(total * total), F32)
 
 
-def run(body, name, operands, outs, scratch, collective_id=None, loads=()):
-    given, in_specs, taken = list(operands), [whole_vmem()] * len(operands), []
+def run(body, name, operands, outs, scratch, collective_id=None, loads=(), far_operands=()):
+    given, taken = list(operands), []
+    in_specs = [
+        pl.BlockSpec(memory_space=pl.ANY) if k in far_operands else whole_vmem() for k in range(len(operands))
+    ]
     for load in loads:
         places = []
         for operand, spec in zip(load.operands, load.in_specs):
@@ -1228,133 +1273,150 @@
     columns = right.shape[1]
     tile = TILE if columns % TILE == 0 else columns
 
+    def put(where):
+        value = dot_nn(left_t[...], right[:, where]).astype(out.dtype)
+        if len(out.shape) == 3:
+            out[:, :, where] = value.reshape(out.shape[:2] + (tile,))
+        else:
+            out[:, where] = value
+
     def step(i, _):
-        where = pl.ds(pl.multiple_of(i * tile, tile), tile)
-        out[:, where] = dot_nn(left_t[...], right[:, where]).astype(out.dtype)
+        put(pl.ds(pl.multiple_of(i * tile, tile), tile))
         return 0
 
     if tile == columns:
-        out[...] = dot_nn(left_t[...], right[...]).astype(out.dtype)
+        put(slice(None))
     else:
         lax.fori_loop(0, columns // tile, step, 0)
 
 
-def ffn_back_kernel(
-    row, grad, branch, w_red, w_in, w_out, normed, middle, gain, mixed,
-    grad_middle, grad_attn, grad_mixed, d_red, d_in, d_out, d_gain,
-    grad_before, after, turned, near_out, near_in, far_out, far_in, send, recv, carry,
+def head_lanes(value, head, size):
+    lanes = lax.broadcasted_iota(jnp.int32, value.shape, 1)
+    inside = (lanes >= head * size) & (lanes < (head + 1) * size)
+    return jnp.where(inside, value, jnp.zeros_like(value))
+
+
+def backward_kernel(
+    layer, scale, points, grad, branch, w_red, w_in, w_out, normed_two, middle, gains, mixed,
+    projected, key_seg, query_seg, w_query, resid, normed,
+    grad_out, branch_out, d_out, d_query, gain_two, gain_one,
+    d_red, d_in, grad_middle, grad_attn, grad_mixed, grad_projected, grad_before, after, turned,
+    bias, keys_t, grad_keys, grad_values,
+    near_out, near_in, far_out, far_in, far_out2, far_in2, send, recv, loaded, carry,
 ):
-    seq_len = normed.shape[0]
+    at_start, at_made, at_summed, at_attended, at_sent = points
+    seq_len, width = normed_two.shape
     chunk = seq_len // 2 // CHUNKS
     sibling, partner, mine, other = group_places(seq_len)
     greet([sibling, partner] + carry.peers())
-    carry.begin(*carry.all())
-    sems = (send, recv)
-    trade = Exchange((near_out, near_in, far_out, far_in), sems, 0, sibling, partner)
-    share = Share(grad_attn, sems, 2, sibling, mine, chunk)
-
-    def partial(start, j):
+    at_start(carry, d_red, d_in)
+    pair = (send, recv)
+    trade = Exchange((near_out, near_in, far_out, far_in), pair, 0, sibling, partner)
+    share = Share(grad_attn, pair, 2, sibling, mine, chunk)
+
+    def ffn_partial(start, j):
         rows = rows_at(start, j, chunk)
-        pre = dot_nn(normed[rows, :], w_in[...])
+        pre = dot_nn(normed_two[rows, :], w_in[...])
         after[rows, :] = gelu_of(pre).astype(BF16)
         low = (dot_nn(branch[rows, :], w_red[...]) * gelu_slope(pre)).astype(BF16)
         grad_before[rows, :] = low
         return dot_nt(low, w_in[...])
 
-    trade.give(0, partial(other, 0))
+    trade.give(0, ffn_partial(other, 0))
     for j in range(CHUNKS):
         if j + 1 < CHUNKS:
-            trade.give(j + 1, partial(other, j + 1))
-        trade.pass_on(j, partial(mine, j))
+            trade.give(j + 1, ffn_partial(other, j + 1))
+        trade.pass_on(j, ffn_partial(mine, j))
     turned[...] = jnp.transpose(branch[...])
     weight_grad(turned, after, d_red)
-    turned[...] = jnp.transpose(normed[...])
+    turned[...] = jnp.transpose(normed_two[...])
     weight_grad(turned, grad_before, d_in)
-    gain_total = jnp.zeros((1, gain.shape[1]), F32)
+    at_made(carry)
+    fetch = pltpu.make_async_copy(normed, after, loaded)
+    fetch.start()
+    total = jnp.zeros((1, width), F32)
     for j in range(CHUNKS):
         rows = rows_at(0, j, chunk)
-        back, gain_part = norm_back(trade.take(j), middle[rows, :], gain[row : row + 1, :])
-        gain_total = gain_total + gain_part
-        total = back + grad[rows, :]
-        grad_middle[rows, :] = total
-        share.put(j, total.astype(BF16))
+        back, part = norm_back(trade.take(j), middle[rows, :], gains[2 * layer + 1 : 2 * layer + 2, :])
+        total = total + part
+        back = back + grad[rows, :]
+        grad_middle[rows, :] = back
+        share.put(j, back.astype(BF16))
         here = rows_at(mine, j, chunk)
         grad_mixed[here, :] = dot_nn(grad_attn[here, :], w_out[...]).astype(BF16)
+    gain_two[...] = total
     for j in range(CHUNKS):
         share.arrived(j)
         here = rows_at(other, j, chunk)
         grad_mixed[here, :] = dot_nn(grad_attn[here, :], w_out[...]).astype(BF16)
-    d_gain[...] = gain_total
+    trade.close()
+    share.close()
+    at_summed(carry)
+
+    block = bias.shape[1]
+    heads = grad_mixed.shape[1] // HD
+    keys_t[...] = jnp.transpose(projected[1])
+    grad_keys[...] = jnp.zeros(grad_keys.shape, F32)
+    grad_values[...] = jnp.zeros(grad_values.shape, F32)
+
+    def queries(i, _):
+        rows = rows_at(0, i, block)
+        bias[...] = jnp.where(key_seg[...] == query_seg[:, rows], 0.0, -1e30)
+        asked = projected[0, rows, :] * HD ** (-0.5)
+        given = grad_mixed[rows, :]
+        parts = []
+        for head in range(heads):
+            query = head_lanes(asked, head, HD)
+            wanted = head_lanes(given, head, HD)
+            scores = dot_nt(projected[1], query) + bias[...]
+            powers = jnp.exp(scores - jnp.max(scores, axis=0, keepdims=True))
+            probs = powers * (1.0 / jnp.sum(powers, axis=0, keepdims=True))
+            grad_probs = dot_nt(projected[2], wanted)
+            centre = jnp.sum(probs * grad_probs, axis=0, keepdims=True)
+            grad_scores = (probs * (grad_probs - centre)).astype(BF16)
+            parts.append(dot_nn(keys_t[head * HD : (head + 1) * HD, :], grad_scores))
+            grad_keys[...] += dot_nn(grad_scores, query)
+            grad_values[...] += dot_nn(probs.astype(BF16), wanted)
+        grad_projected[0, rows, :] = (jnp.transpose(jnp.concatenate(parts, axis=0)) * HD ** (-0.5)).astype(BF16)
+        return 0
+
+    lax.fori_loop(0, seq_len // block, queries, 0)
+    grad_projected[1] = grad_keys[...].astype(BF16)
+    grad_projected[2] = grad_values[...].astype(BF16)
+    at_attended(carry)
+
+    trade = Exchange((near_out, near_in, far_out2, far_in2), pair, 3, sibling, partner)
+    share = Share(branch_out, pair, 5, sibling, mine, chunk)
+
+    def query_partial(start, j):
+        rows = rows_at(start, j, chunk)
+        found = None
+        for which in range(3):
+            part = dot_nt(grad_projected[which, rows, :], w_query[which])
+            found = part if found is None else found + part
+        return found
+
+    trade.give(0, query_partial(other, 0))
+    for j in range(CHUNKS):
+        if j + 1 < CHUNKS:
+            trade.give(j + 1, query_partial(other, j + 1))
+        trade.pass_on(j, query_partial(mine, j))
     turned[...] = jnp.transpose(grad_attn[...])
     weight_grad(turned, mixed, d_out)
-    trade.close()
-    share.close()
-    carry.end(*carry.all())
-
-
-def ffn_backward(row, grad, branch, w_red, w_in, w_out, normed, middle, gain, mixed, collective_id, loads):
-    seq_len, width = normed.shape
-    half, chunk = seq_len // 2, seq_len // 2 // CHUNKS
-    return run(
-        functools.partial(ffn_back_kernel, row),
-        "ffn_backward",
-        [grad, branch, w_red, w_in, w_out, normed, middle, gain, mixed],
-        [
-            jax.ShapeDtypeStruct((half, width), F32),
-            jax.ShapeDtypeStruct((seq_len, width), BF16),
-            jax.ShapeDtypeStruct(mixed.shape, BF16),
-            jax.ShapeDtypeStruct(w_red.shape, BF16),
-            jax.ShapeDtypeStruct(w_in.shape, BF16),
-            jax.ShapeDtypeStruct(w_out.shape, BF16),
-            jax.ShapeDtypeStruct((1, gain.shape[1]), F32),
-        ],
-        [pltpu.VMEM((seq_len, w_in.shape[1]), BF16)] * 2 + [pltpu.VMEM((width, seq_len), BF16)]
-        + Exchange.scratch(chunk, width, BACKWARD_KIND)
-        + sems(3),
-        collective_id,
-        loads,
-    )
-
-
-def norm_back_kernel(
-    scale, row, grads, weights, normed, value, gain, upstream,
-    grad_out, branch, d_weights, d_gain,
-    turned, near_out, near_in, far_out, far_in, send, recv, carry,
-):
-    seq_len, width = normed.shape
-    chunk = seq_len // 2 // CHUNKS
-    sibling, partner, mine, other = group_places(seq_len)
-    greet([sibling, partner] + carry.peers())
-    carry.begin(*carry.all())
-    sems = (send, recv)
-    trade = Exchange((near_out, near_in, far_out, far_in), sems, 0, sibling, partner)
-    share = Share(branch, sems, 2, sibling, mine, chunk)
-
-    def partial(start, j):
-        rows = rows_at(start, j, chunk)
-        total = None
-        for which in range(grads.shape[0]):
-            part = dot_nt(grads[which, rows, :], weights[which])
-            total = part if total is None else total + part
-        return total
-
-    trade.give(0, partial(other, 0))
-    for j in range(CHUNKS):
-        if j + 1 < CHUNKS:
-            trade.give(j + 1, partial(other, j + 1))
-        trade.pass_on(j, partial(mine, j))
-    turned[...] = jnp.transpose(normed[...])
-    for which in range(grads.shape[0]):
-        weight_grad(turned, grads.at[which], d_weights.at[which])
-    gain_total = jnp.zeros((1, gain.shape[1]), F32)
+    fetch.wait()
+    turned[...] = jnp.transpose(after[...])
+    for which in range(3):
+        weight_grad(turned, grad_projected.at[which], d_query.at[which])
+    at_sent(carry, d_out)
+    total = jnp.zeros((1, width), F32)
     for j in range(CHUNKS):
         rows = rows_at(0, j, chunk)
-        back, gain_part = norm_back(trade.take(j), value[rows, :], gain[row : row + 1, :])
-        gain_total = gain_total + gain_part
-        back = back + upstream[rows, :]
+        back, part = norm_back(trade.take(j), resid[rows, :], gains[2 * layer : 2 * layer + 1, :])
+        total = total + part
+        back = back + grad_middle[rows, :]
         grad_out[rows, :] = back
         share.put(j, (back if scale is None else scale * back).astype(BF16))
-    d_gain[...] = gain_total
+    gain_one[...] = total
     for j in range(CHUNKS):
         share.arrived(j)
     trade.close()
@@ -1362,86 +1424,49 @@
     carry.end(*carry.all())
 
 
-def norm_backward(row, grads, weights, normed, value, gain, upstream, scale, collective_id, loads):
-    seq_len, width = normed.shape
+def backward_block(
+    layer, scale, points, grad, branch, w_red, w_in, w_out, normed_two, middle, gains, mixed,
+    projected, key_seg, query_seg, w_query, resid, normed, owners, collective_id, loads,
+):
+    seq_len, width = normed_two.shape
+    hidden, heads_width = w_in.shape[1], w_query.shape[2]
     half, chunk = seq_len // 2, seq_len // 2 // CHUNKS
+    block = min(QUERY_BLOCK, seq_len)
+    far = pltpu.VMEM((CHUNKS, chunk, width), BACKWARD_KIND)
     return run(
-        functools.partial(norm_back_kernel, scale, row),
-        "norm_backward",
-        [grads, weights, normed, value, gain, upstream],
+        functools.partial(backward_kernel, layer, scale, points),
+        "backward_block",
+        [grad, branch, w_red, w_in, w_out, normed_two, middle, gains, mixed]
+        + [projected, key_seg, query_seg, w_query, resid, normed],
         [
             jax.ShapeDtypeStruct((half, width), F32),
             jax.ShapeDtypeStruct((seq_len, width), BF16),
-            jax.ShapeDtypeStruct(weights.shape, BF16),
-            jax.ShapeDtypeStruct((1, gain.shape[1]), F32),
+            jax.ShapeDtypeStruct((owners, width // owners, heads_width), BF16),
+            jax.ShapeDtypeStruct((3, owners, width // owners, heads_width), BF16),
+            jax.ShapeDtypeStruct((1, width), F32),
+            jax.ShapeDtypeStruct((1, width), F32),
         ],
-        [pltpu.VMEM((width, seq_len), BF16)] + Exchange.scratch(chunk, width, BACKWARD_KIND) + sems(3),
+        [pltpu.VMEM((owners, width // owners, hidden), BF16)] * 2
+        + [
+            pltpu.VMEM((half, width), F32),
+            pltpu.VMEM((seq_len, width), BF16),
+            pltpu.VMEM((seq_len, heads_width), BF16),
+            pltpu.VMEM((3, seq_len, heads_width), BF16),
+            pltpu.VMEM((seq_len, hidden), BF16),
+            pltpu.VMEM((seq_len, width), BF16),
+            pltpu.VMEM((width, seq_len), BF16),
+            pltpu.VMEM((seq_len, block), F32),
+            pltpu.VMEM((heads_width, seq_len), BF16),
+            pltpu.VMEM((seq_len, heads_width), F32),
+            pltpu.VMEM((seq_len, heads_width), F32),
+        ]
+        + Exchange.scratch(chunk, width, BACKWARD_KIND)
+        + [far, far]
+        + sems(6)
+        + [pltpu.SemaphoreType.DMA],
         collective_id,
         loads,
-    )
-
-
-def head_lanes(value, head, size):
-    lanes = lax.broadcasted_iota(jnp.int32, value.shape, 1)
-    inside = (lanes >= head * size) & (lanes < (head + 1) * size)
-    return jnp.where(inside, value, jnp.zeros_like(value))
-
-
-def attention_back_kernel(projected, grad_mixed, key_seg, query_seg, out, bias, keys_t, grad_keys, grad_values, carry):
-    seq_len, width = grad_mixed.shape
-    block = bias.shape[1]
-    heads = width // HD
-    scale = HD ** (-0.5)
-    if carry.loads:
-        greet(carry.peers())
-    carry.begin(*carry.all())
-    keys_t[...] = jnp.transpose(projected[1])
-    grad_keys[...] = jnp.zeros(grad_keys.shape, F32)
-    grad_values[...] = jnp.zeros(grad_values.shape, F32)
-
-    def queries(i, _):
-        rows = rows_at(0, i, block)
-        bias[...] = jnp.where(key_seg[...] == query_seg[:, rows], 0.0, -1e30)
-        asked = projected[0, rows, :] * scale
-        given = grad_mixed[rows, :]
-        parts = []
-        for head in range(heads):
-            query = head_lanes(asked, head, HD)
-            grad = head_lanes(given, head, HD)
-            scores = dot_nt(projected[1], query) + bias[...]
-            powers = jnp.exp(scores - jnp.max(scores, axis=0, keepdims=True))
-            probs = powers * (1.0 / jnp.sum(powers, axis=0, keepdims=True))
-            grad_probs = dot_nt(projected[2], grad)
-            centre = jnp.sum(probs * grad_probs, axis=0, keepdims=True)
-            grad_scores = (probs * (grad_probs - centre)).astype(BF16)
-            parts.append(dot_nn(keys_t[head * HD : (head + 1) * HD, :], grad_scores))
-            grad_keys[...] += dot_nn(grad_scores, query)
-            grad_values[...] += dot_nn(probs.astype(BF16), grad)
-        out[0, rows, :] = (jnp.transpose(jnp.concatenate(parts, axis=0)) * scale).astype(BF16)
-        return 0
-
-    lax.fori_loop(0, seq_len // block, queries, 0)
-    out[1] = grad_keys[...].astype(BF16)
-    out[2] = grad_values[...].astype(BF16)
-    carry.end(*carry.all())
-
-
-def attention_back(projected, grad_mixed, key_seg, query_seg, collective_id, loads):
-    seq_len, width = grad_mixed.shape
-    block = min(QUERY_BLOCK, seq_len)
-    return run(
-        attention_back_kernel,
-        "attention_back",
-        [projected, grad_mixed, key_seg, query_seg],
-        [jax.ShapeDtypeStruct(projected.shape, BF16)],
-        [
-            pltpu.VMEM((seq_len, block), F32),
-            pltpu.VMEM((width, seq_len), BF16),
-            pltpu.VMEM((seq_len, width), F32),
-            pltpu.VMEM((seq_len, width), F32),
-        ],
-        collective_id if loads else None,
-        loads,
+        far_operands=(14,),
     )
 
 
@@ -2098,65 +2123,77 @@
     kept.append(
         (result, normed_next, projected, mixed, middle, normed_two, query_w, output_w, expand_w, joined(reduce_w, 0))
     )
-    next_id = 2
-    gain_grads = [None] * (2 * layers) + [gain_final]
     own, squares = {}, []
 
     def by_owner(value, lead):
         shape = value.shape
         return value.reshape(shape[:lead] + (wide, shape[lead] // wide) + shape[lead + 1 :])
 
-    class Route:
-        waiting, halfway = [], []
-
-        def take(self, pairs, lines):
-            self.now = self.waiting[:pairs], self.halfway[:lines]
-            self.waiting, self.halfway = self.waiting[pairs:], self.halfway[lines:]
-            return [PairLoad(by_owner(value, lead), lead, wide) for _, value, lead in self.now[0]] + [
-                LineLoad(sums, wide) for _, sums in self.now[1]
-            ]
-
-        def back(self, results):
-            pairs, lines = self.now
-            self.halfway = self.halfway + [(key, sums) for (key, _, _), sums in zip(pairs, results)]
-            for k, (key, _) in enumerate(lines):
-                own[key] = results[len(pairs) + 2 * k]
-                squares.append(results[len(pairs) + 2 * k + 1])
-
-    route = Route()
-    route.waiting = [((TABLE, k), piece, 0) for k, piece in enumerate(d_last)]
-    for layer in reversed(range(layers)):
-        residual, normed, projected, mixed, middle, normed_two, *four_w = kept[layer]
-        query_w, output_w, expand_w, reduce_w = four_w
-        top = layer == layers - 1
-        loads = route.take(3 if top else 2, 3)
-        (grad_middle, grad_attn, grad_mixed, d_red, d_in, d_out, gain_two), carried = ffn_backward(
-            2 * layer + 1, grad, branch, reduce_w, expand_w, output_w,
-            normed_two, middle, gain_w, mixed, next_id, loads,
-        )
-        route.back(carried)
-        route.waiting += [((FFN_OUT, layer), d_red, 0), ((FFN_IN, layer), d_in, 0)]
-        loads = route.take(1, 2)
-        (grad_projected,), carried = attention_back(projected, grad_mixed, key_seg, query_seg, next_id + 1, loads)
-        route.back(carried)
-        route.waiting += [((ATTN_OUT, layer), d_out, 0)]
-        loads = route.take(2, 2)
-        (grad, branch, d_query, gain_one), carried = norm_backward(
-            2 * layer, grad_projected, query_w, normed, residual, gain_w, grad_middle,
-            math.sqrt(D) if layer == 0 else None, next_id + 2, loads,
-        )
-        route.back(carried)
-        route.waiting += [((ATTN_IN, layer), d_query, 1)]
-        next_id += 3
-        gain_grads[2 * layer], gain_grads[2 * layer + 1] = gain_one, gain_two
-    (key, last_full, _), = route.waiting
-    lines = route.halfway
-    (own_first, own[key], total_small, scalars), carried = tail(
-        branch, ids_all, losses, by_owner(last_full, 1), gain_grads, squares, share, vocab, 4, next_id,
-        [LineLoad(value, wide) for _, value in lines],
-    )
-    for k, (key, _) in enumerate(lines):
-        own[key] = carried[2 * k]
+    def landed(key, results):
+        own[key] = results[0]
+        squares.append(results[1])
+        return results[2:]
+
+    hidden = ffn_in.shape[2]
+    made = jax.ShapeDtypeStruct((wide, share, hidden), BF16)
+    made_out = jax.ShapeDtypeStruct((wide, share, attn_out.shape[2]), BF16)
+
+    def start_last(carry, d_red, d_in):
+        carry.loads[PIECES].full, carry.loads[PIECES + 1].full = d_red, d_in
+        carry.begin(*range(PIECES))
+
+    half_pieces = PIECES // 2
+    points = (
+        start_last,
+        lambda carry: carry.begin(PIECES, PIECES + 1),
+        lambda carry: carry.hand_on(*range(half_pieces)),
+        lambda carry: carry.hand_on(*range(half_pieces, PIECES)),
+        lambda carry, d_out: None,
+    )
+    residual, normed, projected, mixed, middle, normed_two, query_w, output_w, expand_w, reduce_w = kept[1]
+    (grad, branch, d_out, d_query, gain_two, gain_one), carried = backward_block(
+        1, None, points, grad, branch, reduce_w, expand_w, output_w, normed_two, middle, gain_w, mixed,
+        projected, key_seg, query_seg, query_w, residual, normed, wide, 2,
+        [ReduceLoad(by_owner(piece, 0), 0) for piece in d_last]
+        + [PairLoad(made, 0, True), PairLoad(made, 0, True)],
+    )
+    for k in range(PIECES):
+        carried = landed((TABLE, k), carried)
+    red_sums, in_sums = carried
+    gain_grads = [None, None, gain_one, gain_two, gain_final]
+
+    def start_first(carry, d_red, d_in):
+        carry.loads[4].full, carry.loads[5].full = d_red, d_in
+        carry.begin(0, 1, 2, 3)
+
+    def sent_first(carry, d_out):
+        carry.loads[6].full = d_out
+        carry.begin(6)
+
+    points = (
+        start_first,
+        lambda carry: carry.begin(4, 5),
+        lambda carry: carry.hand_on(2, 3),
+        lambda carry: carry.hand_on(4),
+        sent_first,
+    )
+    residual, normed, projected, mixed, middle, normed_two, query_w, output_w, expand_w, reduce_w = kept[0]
+    (grad, branch, _, d_query, gain_two, gain_one), carried = backward_block(
+        0, math.sqrt(D), points, grad, branch, reduce_w, expand_w, output_w, normed_two, middle, gain_w, mixed,
+        projected, key_seg, query_seg, query_w, residual, normed, wide, 3,
+        [LineLoad(red_sums, wide), LineLoad(in_sums, wide), ReduceLoad(d_out, 0), ReduceLoad(d_query, 1)]
+        + [ReduceLoad(made, 0, True), PairLoad(made, 0, True), PairLoad(made_out, 0, True)],
+    )
+    for key in ((FFN_OUT, 1), (FFN_IN, 1), (ATTN_OUT, 1), (ATTN_IN, 1), (FFN_OUT, 0)):
+        carried = landed(key, carried)
+    in_sums, out_sums = carried
+    gain_grads[:2] = gain_one, gain_two
+
+    (own_first, own[ATTN_IN, 0], total_small, scalars), carried = tail(
+        branch, ids_all, losses, d_query, gain_grads, squares, share, vocab, 4, 4,
+        [LineLoad(in_sums, wide), LineLoad(out_sums, wide)],
+    )
+    own[FFN_IN, 0], own[ATTN_OUT, 0] = carried[0], carried[2]
     grad_attn_in, grad_attn_out, grad_ffn_in, grad_ffn_out = [
         jnp.stack([own[name, index] for index in range(layers)]) for name in (ATTN_IN, ATTN_OUT, FFN_IN, FFN_OUT)
     ]

time: 535 us -> 501 us (0.936)
  Pallas kernels: 502 us -> 468 us
    pallas_call x9 -> x5, Pallas kernels: 502 us -> 468 us  [run(): pl.pallas_call(kernel, out_shape=tuple(outs) + tuple((out for load in loa...]
where the time goes in v7:
time: 501 us; the launch traced here: 497 us
  Pallas kernels  468 us (93%)
  other arithmetic  18.8 us (4%)
  local copies, waits for them, and re-layouts  8.07 us (2%)
    pallas_call x5, Pallas kernels, run(): pl.pallas_call(kernel, out_shape=tuple(outs) + tuple((out for load in loa...  468 us
    convert_element_type x5, other arithmetic, adam(): return (weight_new, first_new, second_new, weight_new.astype(jnp.bfloat16))  10.5 us

profile of v7, /device:TPU:0, one launch (start us, length us, event | category | flops | bytes accessed | tf_op | source)
XLA Modules:
  0.0 497.5 jit_solution(17864309681399933242)
XLA Ops:
  0.7 0.7 dynamic-slice_convert_fusion
  1.4 0.7 convert_element_type.48
  2.1 0.7 convert_element_type.47
  2.8 0.7 convert_element_type.49
  3.5 0.7 convert_element_type.50
  4.1 1.7 copy.50.refs_5_.refs_1_.refs_10_
  5.8 2.8 multiply_sine_fusion
  8.7 1.3 pad_maximum_fusion.refs_3_
  9.9 132.2 %front.1 = (f32[512,768]{1,0:T(8,128)}, bf16[1024,768]{1,0:T(8,128)(2,1)}, f32[8,768]{1,0:T(8,128)}, f32[8,128]{1,0:T(8,128)}, s32[8,8,128]{2,1,0:T(8,128)}, /*i...) custom-call(s32[8,128]{1,0:T(8,128)} %bitcast.54, ...), custom_call_target="tpu_custom_call" | custom-call | tf_op jit(solution)/shard_map/front/pallas_call | solution.py:863
  142.1 1.2 slice.12
  143.3 0.7 broadcast_divide_fusion
  144.0 0.7 stack.57.refs_8_
  144.7 116.5 %last_and_loss.1 = (bf16[3,1024,192]{2,1,0:T(8,128)(2,1)}, bf16[1024,192]{1,0:T(8,128)(2,1)}, f32[512,768]{1,0:T(8,128)}, bf16[1024,768]{1,0:T(8,128)(2,1)}, f32...) custom-call(bf16[1024,768]{1,0:T(8,128)(2,1)} %get-tuple-element.97., ...), custom_call_target="tpu_custom_call" | custom-call | tf_op jit(solution)/shard_map/last_and_loss/pallas_call | solution.py:863
  261.2 76.0 %backward_block.2 = (f32[512,768]{1,0:T(8,128)}, bf16[1024,768]{1,0:T(8,128)(2,1)}, bf16[8,96,192]{2,1,0:T(8,128)(2,1)}, bf16[3,8,96,192]{3,2,1,0:T(8,128)(2,1)}...) custom-call(f32[512,768]{1,0:T(8,128)} %get-tuple-element.105.refs_0, ...), custom_call_target="tpu_custom_call" | custom-call | tf_op jit(solution)/shard_map/backward_block/pallas_call | solution.py:863
  337.2 75.7 %backward_block.3 = (f32[512,768]{1,0:T(8,128)}, bf16[1024,768]{1,0:T(8,128)(2,1)}, bf16[8,96,192]{2,1,0:T(8,128)(2,1)}, bf16[3,8,96,192]{3,2,1,0:T(8,128)(2,1)}...) custom-call(f32[512,768]{1,0:T(8,128)} %get-tuple-element.116.refs_0, ...), custom_call_target="tpu_custom_call" | custom-call | tf_op jit(solution)/shard_map/backward_block/pallas_call | solution.py:863
  412.8 0.0 copy-start.26
  412.9 0.0 copy-start.27
  412.9 0.0 copy-start.28
  412.9 0.0 copy-start.6
  412.9 0.0 copy-start.24
  412.9 67.2 %tail.1 = (f32[96,2048]{1,0:T(8,128)}, f32[3,96,192]{2,1,0:T(8,128)}, f32[8,128]{1,0:T(8,128)}, f32[8,128]{1,0:T(8,128)}, f32[96,768]{1,0:T(8,128)}, /*index=5*/...) custom-call(bf16[1024,768]{1,0:T(8,128)(2,1)} %get-tuple-element.132.refs_0_, ...), custom_call_target="tpu_custom_call" | custom-call | tf_op jit(solution)/shard_map/tail/pallas_call | solution.py:863
  480.1 0.0 copy-start.1
  480.2 0.0 copy-start.8
  480.2 0.0 copy-start.9
  480.2 1.4 fusion.18
  482.3 0.0 copy-done.26
  482.4 1.3 fusion.6
  483.7 2.0 fusion.14
  485.7 0.1 maximum_bitcast_fusion
  485.8 0.0 copy-start.2
  485.8 0.0 copy-start.3
  485.8 0.0 copy-start.10
  485.8 0.0 copy-start.11
  485.8 0.0 copy-start.12
  485.8 0.0 copy-start.13
  485.9 1.6 fusion.16
  487.5 0.2 copy-done.10
  487.7 0.4 copy-done.11
  488.1 0.2 copy-done.12
  488.3 0.2 copy-done.13
  488.5 0.1 copy-done.14
  488.6 0.1 copy-done.15
  488.7 0.1 copy-done.16
  488.8 2.3 fusion.10
  491.1 1.0 copy-done.4
  492.1 0.5 copy-done.5
  492.6 0.2 copy-done.7
  492.8 3.3 fusion.8
  (36 shorter events, 0.1 us)
Async XLA Ops:
  9.9 133.4 %copy-start.25 = (s32[1,1024]{1,0:T(1,128)S(1)}, s32[1,1024]{1,0:T(1,128)}, u32[]{:S(2)}) copy-start(s32[1,1024]{1,0:T(1,128)} %refs_1_.1) | copy-start | bytes 12292
  412.8 69.5 %copy-start.26 = (f32[5,96]{1,0:T(8,128)S(1)}, f32[5,96]{1,0:T(8,128)}, u32[]{:S(2)}) copy-start(f32[5,96]{1,0:T(8,128)} %refs_2_.2) | copy-start | bytes 5764
  412.9 69.5 %copy-start.27 = (f32[5,96]{1,0:T(8,128)S(1)}, f32[5,96]{1,0:T(8,128)}, u32[]{:S(2)}) copy-start(f32[5,96]{1,0:T(8,128)} %param.39) | copy-start | bytes 5764
  412.9 69.5 %copy-start.28 = (f32[5,96]{1,0:T(8,128)S(1)}, f32[5,96]{1,0:T(8,128)}, u32[]{:S(2)}) copy-start(f32[5,96]{1,0:T(8,128)} %param.45) | copy-start | bytes 5764
  412.9 70.8 %copy-start.6 = (f32[2,96,192]{2,1,0:T(8,128)S(1)}, f32[2,96,192]{2,1,0:T(8,128)}, u32[]{:S(2)}) copy-start(f32[2,96,192]{2,1,0:T(8,128)} %refs_8_.1) | copy-start | bytes 442372
  412.9 70.8 %copy-start.24 = (f32[2,96,192]{2,1,0:T(8,128)S(1)}, f32[2,96,192]{2,1,0:T(8,128)}, u32[]{:S(2)}) copy-start(f32[2,96,192]{2,1,0:T(8,128)} %param.35) | copy-start | bytes 442372
  412.9 72.7 %copy-start.20 = (f32[96,512]{1,0:T(8,128)S(1)}, f32[96,512]{1,0:T(8,128)}, u32[]{:S(2)}) copy-start(f32[96,512]{1,0:T(8,128)} %get-tuple-element.162) | copy-start | bytes 589828
  412.9 72.7 %copy-start.21 = (f32[96,512]{1,0:T(8,128)S(1)}, f32[96,512]{1,0:T(8,128)}, u32[]{:S(2)}) copy-start(f32[96,512]{1,0:T(8,128)} %get-tuple-element.163) | copy-start | bytes 589828
  412.9 72.7 %copy-start.22 = (f32[96,512]{1,0:T(8,128)S(1)}, f32[96,512]{1,0:T(8,128)}, u32[]{:S(2)}) copy-start(f32[96,512]{1,0:T(8,128)} %get-tuple-element.164) | copy-start | bytes 589828
  412.9 72.7 %copy-start.23 = (f32[96,512]{1,0:T(8,128)S(1)}, f32[96,512]{1,0:T(8,128)}, u32[]{:S(2)}) copy-start(f32[96,512]{1,0:T(8,128)} %get-tuple-element.165) | copy-start | bytes 589828
  480.1 5.6 %copy-start.1 = (f32[2,3,96,192]{3,2,1,0:T(8,128)S(1)}, f32[2,3,96,192]{3,2,1,0:T(8,128)}, u32[]{:S(2)}) copy-start(f32[2,3,96,192]{3,2,1,0:T(8,128)} %refs_7_.1) | copy-start | bytes 1327108
  480.2 5.6 %copy-start.8 = (f32[2,3,96,192]{3,2,1,0:T(8,128)S(1)}, f32[2,3,96,192]{3,2,1,0:T(8,128)}, u32[]{:S(2)}) copy-start(f32[2,3,96,192]{3,2,1,0:T(8,128)} %param.34) | copy-start | bytes 1327108
  480.2 5.6 %copy-start.9 = (f32[2,3,96,192]{3,2,1,0:T(8,128)S(1)}, f32[2,3,96,192]{3,2,1,0:T(8,128)}, u32[]{:S(2)}) copy-start(f32[2,3,96,192]{3,2,1,0:T(8,128)} %param.40) | copy-start | bytes 1327108
  480.2 5.6 %copy-start.17 = (f32[3,96,192]{2,1,0:T(8,128)S(1)}, f32[3,96,192]{2,1,0:T(8,128)}, u32[]{:S(2)}) copy-start(f32[3,96,192]{2,1,0:T(8,128)} %get-tuple-element.154) | copy-start | bytes 663556
  480.2 5.6 %copy-start.19 = (f32[3,96,192]{2,1,0:T(8,128)S(1)}, f32[3,96,192]{2,1,0:T(8,128)}, u32[]{:S(2)}) copy-start(f32[3,96,192]{2,1,0:T(8,128)} %get-tuple-element.153) | copy-start | bytes 663556
  485.6 1.8 copy-start.18
  485.8 1.7 copy-start.2
  485.8 1.7 copy-start.3
  485.8 1.9 copy-start.10
  485.8 2.3 copy-start.11
  485.8 2.5 copy-start.12
  485.8 2.7 copy-start.13
  485.8 2.7 copy-start.14
  485.9 2.8 copy-start.15
  485.9 2.9 copy-start.16
  488.8 2.3 copy-start
  488.8 3.4 copy-start.4
  488.8 3.8 copy-start.5
  488.8 4.0 copy-start.7

commit v8 on v7

--- a/solution.py
+++ b/solution.py
@@ -924,16 +924,17 @@
     return ((feature == lane + owner * share) & (lane < share)).astype(F32).astype(BF16)
 
 
-def token_picks(ids, vocab, first):
-    here = spread(ids.astype(F32) - first.astype(F32))
-    lane = lax.broadcasted_iota(jnp.int32, (LANES, LANES), 1).astype(F32)
-    return [jnp.where(here == lane + float(t * LANES), 1.0, 0.0).astype(BF16) for t in range(vocab // LANES)]
+def token_parts(ids, first):
+    here = ids - first
+    high = lax.shift_right_arithmetic(here, 7)
+    place = lax.broadcasted_iota(jnp.int32, (LANES, ids.shape[1]), 0)
+    return high, jnp.where(place == here - high * LANES, 1.0, 0.0).astype(BF16)
 
 
 def embed_part(
-    ids, counted, gains, extra, table,
+    ids, counted, gains, steps, rates, table,
     resid, normed, gain_all, count_all, ids_all,
-    low, picks, small, near_out, near_in, own, far_out, far_in, wide_out, wide_in, part_out, part_in,
+    low, extra, small, near_out, near_in, own, far_out, far_in, wide_out, wide_in, part_out, part_in,
     id_send, id_recv, small_send, small_recv, near_send, near_recv, far_send, far_recv, wide_send, wide_recv,
     part_send, part_recv, send, recv, carry,
 ):
@@ -942,7 +943,6 @@
     quarter = seq_len // 4
     share, vocab = table.shape[1:]
     owners = ids_all.shape[0]
-    id_rows = ids.shape[0]
     sibling, partner, mine, other = group_places(seq_len)
     place = lax.axis_index(NARROW)
     side = lax.div(place, 2)
@@ -980,36 +980,37 @@
     for step in range(1, owners):
         small_copy(step).start()
     carry.begin(0, 1)
-    padded = jnp.concatenate([table[0], jnp.zeros((LANES - share, vocab), F32)], axis=0)
-    low[...] = jnp.transpose(padded).astype(BF16)
+    parts = vocab // LANES
+    for part in range(parts):
+        low[part * share : (part + 1) * share, :] = table[0, :, part * LANES : (part + 1) * LANES].astype(BF16)
+    core = lax.rem(place, 2)
 
     def look_up(step):
         row = lax.rem(me + step, owners)
 
-        def find(start):
-            def block(b, _):
-                place_of = start // LANES + b
-                for t, pick in enumerate(token_picks(ids_all[row, pl.ds(place_of, 1), :], vocab, first)):
-                    picks[rows_at(0, b, LANES), t * LANES : (t + 1) * LANES] = pick
-                return 0
-
-            lax.fori_loop(0, seq_len // 2 // LANES, block, 0)
-            return dot_nn(picks[...], low[...]).astype(BF16)
-
-        near_out[step] = find(other)
+        def find(which):
+            high, picks = token_parts(ids_all[row, pl.ds(which, 1), :], first)
+            found = dot_nn(low[...], picks)
+            total = jnp.zeros((share, quarter), F32)
+            for part in range(parts):
+                total = total + jnp.where(high == part, found[part * share : (part + 1) * share, :], 0.0)
+            return total.astype(BF16)
+
+        for k in range(2):
+            near_out[step, k] = find(2 * (1 - core) + k)
         near_copy(step).start()
-        own[step] = find(mine)
+        for k in range(2):
+            own[step, k] = find(2 * core + k)
 
     def halve(step):
         near_copy(step).wait_recv()
-        total = own[step] + near_in[step]
-        own[step] = total
-        far_out[step] = own[step, pl.ds(pl.multiple_of((1 - side) * quarter, quarter), quarter), :]
+        own[step] = own[step] + near_in[step]
+        far_out[step] = own[step, 1 - side]
         far_copy(step).start()
 
     def deliver(step):
         far_copy(step).wait_recv()
-        total = own[step, pl.ds(pl.multiple_of(side * quarter, quarter), quarter), :] + far_in[step]
+        total = own[step, side] + far_in[step]
         if step % owners == 0:
             wide_in[me] = total
         else:
@@ -1038,18 +1039,24 @@
         total = part if total is None else total + part
     gain_all[...] = total
     count_all[...] = jnp.sum(small[...], axis=0)
+    half_width = width // 2
+    for k in range(seq_len // 2 // LANES):
+        when = spread(steps[pl.ds(mine // LANES + k, 1), :].astype(F32))
+        for t in range(half_width // LANES):
+            columns = slice(t * LANES, (t + 1) * LANES)
+            angles = when * rates[:, columns]
+            rows = slice(k * LANES, (k + 1) * LANES)
+            extra[rows, t * LANES : (t + 1) * LANES] = jnp.sin(angles)
+            extra[rows, half_width + t * LANES : half_width + (t + 1) * LANES] = jnp.cos(angles)
     for step in range(1, owners):
         wide_copy(step).wait_recv()
+    found = jnp.transpose(wide_in[...].reshape(width, quarter))
     pieces = quarter // LANES
     at_side = pl.multiple_of(side * quarter, quarter)
     at_other = pl.multiple_of((1 - side) * quarter, quarter)
     for piece in range(pieces):
         rows = pl.ds(piece * LANES, LANES)
-        found = None
-        for owner in range(owners):
-            part = dot_nn(wide_in[owner, rows, :], feature_places(owner, width, share))
-            found = part if found is None else found + part
-        part_out[rows, :] = found.astype(BF16)
+        part_out[rows, :] = found[piece * LANES : (piece + 1) * LANES, :]
         part_copy(piece).start()
 
     def finish(start, source, piece):
@@ -1196,12 +1203,12 @@
 
 
 def front_kernel(
-    ids, counted, gains, extra, table, key_seg, query_seg,
+    ids, counted, gains, steps, rates, table, key_seg, query_seg,
     resid, normed, gain_all, count_all, ids_all, projected, mixed, middle, normed_two, result, normed_next,
     *scratch, carry,
 ):
     embed_part(
-        ids, counted, gains, extra, table, resid, normed, gain_all, count_all, ids_all,
+        ids, counted, gains, steps, rates, table, resid, normed, gain_all, count_all, ids_all,
         *scratch[:-LAYER_SCRATCH], carry,
     )
     carry.end(0, 1)
@@ -1225,15 +1232,15 @@
     carry.end(*later)
 
 
-def front(ids, counted, gains, extra, tables, key_seg, query_seg, owners, heads_width, collective_id, loads):
+def front(ids, counted, gains, steps, rates, tables, key_seg, query_seg, owners, heads_width, collective_id, loads):
     seq_len = ids.size
-    half, width = extra.shape
     share, vocab = tables.shape[1:]
+    half, width = seq_len // 2, owners * share
     dma = pltpu.SemaphoreType.DMA
     return run(
         front_kernel,
         "front",
-        [ids, counted, gains, extra, tables, key_seg, query_seg],
+        [ids, counted, gains, steps, rates, tables, key_seg, query_seg],
         [
             jax.ShapeDtypeStruct((half, width), F32),
             jax.ShapeDtypeStruct((seq_len, width), BF16),
@@ -1244,16 +1251,13 @@
         + layer_outs(seq_len, width, heads_width)
         + [jax.ShapeDtypeStruct((half, width), F32), jax.ShapeDtypeStruct((seq_len, width), BF16)],
         [
-            pltpu.VMEM((vocab, LANES), BF16),
-            pltpu.VMEM((half, vocab), BF16),
+            pltpu.VMEM((vocab // LANES * share, LANES), BF16),
+            pltpu.VMEM((half, width), F32),
             pltpu.VMEM((owners, 8, LANES), F32),
-            pltpu.VMEM((owners, half, LANES), BF16),
-            pltpu.VMEM((owners, half, LANES), BF16),
-            pltpu.VMEM((owners, half, LANES), BF16),
-            pltpu.VMEM((owners, half // 2, LANES), BF16),
-            pltpu.VMEM((owners, half // 2, LANES), BF16),
-            pltpu.VMEM((owners, half // 2, LANES), BF16),
-            pltpu.VMEM((owners, half // 2, LANES), BF16),
+        ]
+        + [pltpu.VMEM((owners, 2, share, half // 2), BF16)] * 3
+        + [pltpu.VMEM((owners, share, half // 2), BF16)] * 4
+        + [
             pltpu.VMEM((half // 2, width), BF16),
             pltpu.VMEM((half // 2, width), BF16),
         ]
@@ -1800,23 +1804,23 @@
     first = place * vocab
     around = [lax.rem(me + step, owners) for step in range(owners)]
     at_quarter = pl.multiple_of(mine + side * quarter, quarter)
-    across_quarter = pl.multiple_of(mine + (1 - side) * quarter, quarter)
+    held = 2 * lax.rem(place, 2) + side
 
     def along_way(step):
         return {WIDE: 2 * lax.rem(slow + step, slows) + fast}
 
     def wide_copy(step):
         return remote(
-            out_blocks.at[around[step]], all_in.at[me, pl.ds(at_quarter, quarter)],
+            out_blocks.at[around[step]], all_in.at[me, held],
             wide_send.at[step], wide_recv.at[step], {WIDE: around[step]},
         )
 
     def far_copy(step):
-        rows = all_in.at[around[step], pl.ds(at_quarter, quarter)]
+        rows = all_in.at[around[step], held]
         return remote(rows, rows, far_send.at[step], far_recv.at[step], partner)
 
     def near_copy(step):
-        rows = all_in.at[around[step], pl.ds(mine, half)]
+        rows = all_in.at[around[step], pl.ds(2 * lax.rem(place, 2), 2)]
         return remote(rows, rows, near_send.at[step], near_recv.at[step], sibling)
 
     def block(owner):
@@ -1851,13 +1855,10 @@
     for row, part in enumerate(gain_parts):
         gains_out[row : row + 1, :] = part[...]
     gain_near().start()
-    for owner in range(owners):
-        out_blocks[owner] = dot_nt(
-            branch[pl.ds(at_quarter, quarter), :], feature_places(owner, width, share)
-        ).astype(BF16)
+    out_blocks[...] = jnp.transpose(branch[pl.ds(at_quarter, quarter), :]).reshape(out_blocks.shape)
     for step in range(1, owners):
         wide_copy(step).start()
-    all_in[me, pl.ds(at_quarter, quarter), :] = out_blocks[me]
+    all_in[me, held] = out_blocks[me]
     carry.begin(*carry.all())
     gain_near().wait_recv()
     both = gains_out[...] + gains_in[...]
@@ -1882,29 +1883,23 @@
         near_copy(step).wait_recv()
         row = around[step]
 
-        def make(b, _):
-            rows = rows_at(0, b, LANES)
-            here = ids_all[row, pl.ds(b, 1), :] - first
-            high = lax.shift_right_arithmetic(here, 7)
-            rest = spread((here - high * LANES).astype(F32))
-            lane = lax.broadcasted_iota(jnp.int32, (LANES, LANES), 1).astype(F32)
-            picks[rows, :] = jnp.where(rest == lane, 1.0, 0.0).astype(BF16)
-            turned = jnp.transpose(all_in[row, rows, :])
-            for t in range(vocab // LANES):
-                inside = jnp.where(high == t, 1.0, 0.0).astype(BF16)
-                masked[t * LANES : (t + 1) * LANES, rows] = turned * inside
-            return 0
-
-        lax.fori_loop(0, seq_len // LANES, make, 0)
-        span = 2 * TILE
+        for k in range(seq_len // quarter):
+            columns = slice(k * quarter, (k + 1) * quarter)
+            high, found = token_parts(ids_all[row, k : k + 1, :], first)
+            picks[:, columns] = found
+            grads = all_in[row, k]
+            for part in range(vocab // LANES):
+                inside = jnp.where(high == part, 1.0, 0.0).astype(BF16)
+                masked[part * share : (part + 1) * share, columns] = grads * inside
+        span = 4 * share
 
         def some(i, _):
             rows = rows_at(0, i, span)
-            part = dot_nn(masked[rows, :], picks[...])
+            part = dot_nt(masked[rows, :], picks[...])
             total[rows, :] = part if first_turn else total[rows, :] + part
             return 0
 
-        lax.fori_loop(0, vocab // span, some, 0)
+        lax.fori_loop(0, total.shape[0] // span, some, 0)
 
     order = [0] + list(range(1, owners))
     for turn in range(owners + 2):
@@ -1927,7 +1922,7 @@
         if turn >= 2:
             gather_grad(order[turn - 2], turn == 2)
     for t in range(vocab // LANES):
-        d_table[:, t * LANES : (t + 1) * LANES] = total[t * LANES : t * LANES + share, :]
+        d_table[:, t * LANES : (t + 1) * LANES] = total[t * share : (t + 1) * share, :]
     result = sums[0].astype(F32)
     small = line_out[0]
     for step in range(1, slows):
@@ -2001,11 +1996,11 @@
             jax.ShapeDtypeStruct(small, F32),
         ],
         [
-            pltpu.VMEM((owners, seq_len // 4, LANES), BF16),
-            pltpu.VMEM((owners, seq_len, LANES), BF16),
-            pltpu.VMEM((vocab, seq_len), BF16),
-            pltpu.VMEM((seq_len, LANES), BF16),
-            pltpu.VMEM((vocab, LANES), F32),
+            pltpu.VMEM((owners, share, seq_len // 4), BF16),
+            pltpu.VMEM((owners, 4, share, seq_len // 4), BF16),
+            pltpu.VMEM((vocab // LANES * share, seq_len), BF16),
+            pltpu.VMEM((LANES, seq_len), BF16),
+            pltpu.VMEM((vocab // LANES * share, LANES), F32),
             pltpu.VMEM((8, width), F32),
             pltpu.VMEM((8, width), F32),
             pltpu.VMEM((owners,) + small, F32),
@@ -2039,6 +2034,7 @@
         and wide % 2 == 0
         and rows == 1
         and seq_len % (2 * CHUNKS * 128) == 0
+        and tables.shape[1] * wide % 256 == 0
         and attn_out.shape[1] % 16 == 0
         and attn_out.shape[1] <= LANES
         and ffn_in.shape[2] % 128 == 0
@@ -2094,14 +2090,16 @@
         return value.reshape(value.shape[:lead] + (-1,) + value.shape[lead + 2 :])
 
     step_flat = timesteps.reshape(-1)
-    extra = time_features(lax.dynamic_slice(step_flat, (core * half,), (half,)))
-    ids = noised.reshape(-1, LANES)
+    ids = noised.reshape(4, -1)
+    steps = timesteps.reshape(-1, LANES)
+    half_width = D // 2
+    rates = jnp.exp(-math.log(10000.0) * jnp.arange(half_width, dtype=F32) / half_width)[None, :]
     quarter = vocab // PIECES
     windows = [(k * quarter, quarter) for k in range(PIECES)]
     key_seg, query_seg = segments.reshape(-1, 1), segments.reshape(1, -1)
     weights = (attn_in, attn_out, ffn_in, ffn_out)
     (residual, normed, gain_w, counts, ids_all, projected, mixed, middle, normed_two, result, normed_next), carried = front(
-        ids, counted, gains, extra, tables, key_seg, query_seg, wide, attn_out.shape[2], 0,
+        ids, counted, gains, steps, rates, tables, key_seg, query_seg, wide, attn_out.shape[2], 0,
         [GatherLoad(value, 0, lead, wide, place=KEPT) for value, lead in zip(weights, leads)]
         + [GatherLoad(value, 1, lead, wide) for value, lead in zip(weights[:3], leads)]
         + [SlowLoad(ffn_out, 1, 0, wide)],

time: 501 us -> 488 us (0.974)
  Pallas kernels: 468 us -> 454 us
    pallas_call x5, Pallas kernels: 468 us -> 454 us  [run(): pl.pallas_call(kernel, out_shape=tuple(outs) + tuple((out for load in loa...]
where the time goes in v8:
time: 488 us; the launch traced here: 481 us
  Pallas kernels  454 us (93%)
  other arithmetic  15.3 us (3%)
  local copies, waits for them, and re-layouts  9.17 us (2%)
    pallas_call x5, Pallas kernels, run(): pl.pallas_call(kernel, out_shape=tuple(outs) + tuple((out for load in loa...  454 us
    convert_element_type x5, other arithmetic, adam(): return (weight_new, first_new, second_new, weight_new.astype(jnp.bfloat16))  10.5 us

profile of v8, /device:TPU:0, one launch (start us, length us, event | category | flops | bytes accessed | tf_op | source)
XLA Modules:
  0.0 481.5 jit_solution(6890574255450610584)
XLA Ops:
  0.7 0.6 multiply_exponential_fusion.refs_4_
  1.2 0.7 convert_element_type.36
  1.9 0.7 convert_element_type.37
  2.6 0.7 convert_element_type.38
  3.3 0.5 broadcast.80
  3.8 1.4 fusion.19
  5.3 0.6 reshape.114.refs_0_
  5.9 1.7 copy.50.refs_6_.refs_1_.refs_10_
  7.6 128.8 %front.1 = (f32[512,768]{1,0:T(8,128)}, bf16[1024,768]{1,0:T(8,128)(2,1)}, f32[8,768]{1,0:T(8,128)}, f32[8,128]{1,0:T(8,128)}, s32[8,4,256]{2,1,0:T(4,128)}, /*i...) custom-call(s32[4,256]{1,0:T(4,128)} %reshape.114.refs_0_, ...), custom_call_target="tpu_custom_call" | custom-call | tf_op jit(solution)/shard_map/front/pallas_call | solution.py:863
  136.3 1.2 slice.12
  137.5 0.7 broadcast_divide_fusion
  138.2 0.7 stack.57.refs_8_
  138.9 116.9 %last_and_loss.1 = (bf16[3,1024,192]{2,1,0:T(8,128)(2,1)}, bf16[1024,192]{1,0:T(8,128)(2,1)}, f32[512,768]{1,0:T(8,128)}, bf16[1024,768]{1,0:T(8,128)(2,1)}, f32...) custom-call(bf16[1024,768]{1,0:T(8,128)(2,1)} %get-tuple-element.97., ...), custom_call_target="tpu_custom_call" | custom-call | tf_op jit(solution)/shard_map/last_and_loss/pallas_call | solution.py:863
  255.7 75.4 %backward_block.2 = (f32[512,768]{1,0:T(8,128)}, bf16[1024,768]{1,0:T(8,128)(2,1)}, bf16[8,96,192]{2,1,0:T(8,128)(2,1)}, bf16[3,8,96,192]{3,2,1,0:T(8,128)(2,1)}...) custom-call(f32[512,768]{1,0:T(8,128)} %get-tuple-element.105.refs_0, ...), custom_call_target="tpu_custom_call" | custom-call | tf_op jit(solution)/shard_map/backward_block/pallas_call | solution.py:863
  331.1 76.1 %backward_block.3 = (f32[512,768]{1,0:T(8,128)}, bf16[1024,768]{1,0:T(8,128)(2,1)}, bf16[8,96,192]{2,1,0:T(8,128)(2,1)}, bf16[3,8,96,192]{3,2,1,0:T(8,128)(2,1)}...) custom-call(f32[512,768]{1,0:T(8,128)} %get-tuple-element.116.refs_0, ...), custom_call_target="tpu_custom_call" | custom-call | tf_op jit(solution)/shard_map/backward_block/pallas_call | solution.py:863
  407.2 0.0 copy-start.26
  407.2 0.0 copy-start.27
  407.2 0.0 copy-start.28
  407.2 0.0 copy-start.6
  407.2 0.0 copy-start.24
  407.3 56.8 %tail.1 = (f32[96,2048]{1,0:T(8,128)}, f32[3,96,192]{2,1,0:T(8,128)}, f32[8,128]{1,0:T(8,128)}, f32[8,128]{1,0:T(8,128)}, f32[96,768]{1,0:T(8,128)}, /*index=5*/...) custom-call(bf16[1024,768]{1,0:T(8,128)(2,1)} %get-tuple-element.132.refs_0_, ...), custom_call_target="tpu_custom_call" | custom-call | tf_op jit(solution)/shard_map/tail/pallas_call | solution.py:863
  464.1 0.0 copy-start.1
  464.2 0.0 copy-start.8
  464.2 0.0 copy-start.9
  464.2 1.4 fusion.18
  466.4 1.3 fusion.6
  467.7 2.0 fusion.14
  469.6 0.0 copy-done.21
  469.7 0.1 maximum_bitcast_fusion
  469.8 0.0 copy-start.2
  469.8 0.0 copy-start.3
  469.8 0.0 copy-start.10
  469.8 0.0 copy-start.11
  469.8 0.0 copy-start.12
  469.8 0.0 copy-start.13
  469.9 1.6 fusion.16
  471.5 0.2 copy-done.10
  471.7 0.4 copy-done.11
  472.2 0.2 copy-done.12
  472.3 0.2 copy-done.13
  472.5 0.1 copy-done.14
  472.6 0.1 copy-done.15
  472.7 0.1 copy-done.16
  472.8 2.3 fusion.10
  475.1 1.0 copy-done.4
  476.1 0.5 copy-done.5
  476.6 0.2 copy-done.7
  476.8 3.3 fusion.8
  (35 shorter events, 0.1 us)
Async XLA Ops:
  7.6 130.0 %copy-start.25 = (s32[1,1024]{1,0:T(1,128)S(1)}, s32[1,1024]{1,0:T(1,128)}, u32[]{:S(2)}) copy-start(s32[1,1024]{1,0:T(1,128)} %refs_1_.1) | copy-start | bytes 12292
  407.2 59.2 %copy-start.26 = (f32[5,96]{1,0:T(8,128)S(1)}, f32[5,96]{1,0:T(8,128)}, u32[]{:S(2)}) copy-start(f32[5,96]{1,0:T(8,128)} %refs_2_.2) | copy-start | bytes 5764
  407.2 59.2 %copy-start.27 = (f32[5,96]{1,0:T(8,128)S(1)}, f32[5,96]{1,0:T(8,128)}, u32[]{:S(2)}) copy-start(f32[5,96]{1,0:T(8,128)} %param.39) | copy-start | bytes 5764
  407.2 59.2 %copy-start.28 = (f32[5,96]{1,0:T(8,128)S(1)}, f32[5,96]{1,0:T(8,128)}, u32[]{:S(2)}) copy-start(f32[5,96]{1,0:T(8,128)} %param.45) | copy-start | bytes 5764
  407.2 60.5 %copy-start.6 = (f32[2,96,192]{2,1,0:T(8,128)S(1)}, f32[2,96,192]{2,1,0:T(8,128)}, u32[]{:S(2)}) copy-start(f32[2,96,192]{2,1,0:T(8,128)} %refs_9_.1) | copy-start | bytes 442372
  407.2 60.4 %copy-start.24 = (f32[2,96,192]{2,1,0:T(8,128)S(1)}, f32[2,96,192]{2,1,0:T(8,128)}, u32[]{:S(2)}) copy-start(f32[2,96,192]{2,1,0:T(8,128)} %param.35) | copy-start | bytes 442372
  407.2 62.4 %copy-start.20 = (f32[96,512]{1,0:T(8,128)S(1)}, f32[96,512]{1,0:T(8,128)}, u32[]{:S(2)}) copy-start(f32[96,512]{1,0:T(8,128)} %get-tuple-element.162) | copy-start | bytes 589828
  407.3 62.4 %copy-start.21 = (f32[96,512]{1,0:T(8,128)S(1)}, f32[96,512]{1,0:T(8,128)}, u32[]{:S(2)}) copy-start(f32[96,512]{1,0:T(8,128)} %get-tuple-element.163) | copy-start | bytes 589828
  407.3 62.4 %copy-start.22 = (f32[96,512]{1,0:T(8,128)S(1)}, f32[96,512]{1,0:T(8,128)}, u32[]{:S(2)}) copy-start(f32[96,512]{1,0:T(8,128)} %get-tuple-element.164) | copy-start | bytes 589828
  407.3 62.4 %copy-start.23 = (f32[96,512]{1,0:T(8,128)S(1)}, f32[96,512]{1,0:T(8,128)}, u32[]{:S(2)}) copy-start(f32[96,512]{1,0:T(8,128)} %get-tuple-element.165) | copy-start | bytes 589828
  464.1 5.6 %copy-start.1 = (f32[2,3,96,192]{3,2,1,0:T(8,128)S(1)}, f32[2,3,96,192]{3,2,1,0:T(8,128)}, u32[]{:S(2)}) copy-start(f32[2,3,96,192]{3,2,1,0:T(8,128)} %refs_8_.1) | copy-start | bytes 1327108
  464.2 5.6 %copy-start.8 = (f32[2,3,96,192]{3,2,1,0:T(8,128)S(1)}, f32[2,3,96,192]{3,2,1,0:T(8,128)}, u32[]{:S(2)}) copy-start(f32[2,3,96,192]{3,2,1,0:T(8,128)} %param.34) | copy-start | bytes 1327108
  464.2 5.6 %copy-start.9 = (f32[2,3,96,192]{3,2,1,0:T(8,128)S(1)}, f32[2,3,96,192]{3,2,1,0:T(8,128)}, u32[]{:S(2)}) copy-start(f32[2,3,96,192]{3,2,1,0:T(8,128)} %param.40) | copy-start | bytes 1327108
  464.2 5.6 %copy-start.17 = (f32[3,96,192]{2,1,0:T(8,128)S(1)}, f32[3,96,192]{2,1,0:T(8,128)}, u32[]{:S(2)}) copy-start(f32[3,96,192]{2,1,0:T(8,128)} %get-tuple-element.154) | copy-start | bytes 663556
  464.2 5.6 %copy-start.19 = (f32[3,96,192]{2,1,0:T(8,128)S(1)}, f32[3,96,192]{2,1,0:T(8,128)}, u32[]{:S(2)}) copy-start(f32[3,96,192]{2,1,0:T(8,128)} %get-tuple-element.153) | copy-start | bytes 663556
  469.7 1.8 copy-start.18
  469.8 1.7 copy-start.2
  469.8 1.7 copy-start.3
  469.8 1.9 copy-start.10
  469.8 2.3 copy-start.11
  469.8 2.5 copy-start.12
  469.8 2.7 copy-start.13
  469.9 2.7 copy-start.14
  469.9 2.8 copy-start.15
  469.9 2.9 copy-start.16
  472.8 2.3 copy-start
  472.8 3.4 copy-start.4
  472.8 3.8 copy-start.5
  472.8 4.0 copy-start.7

commit v9 on v8

--- a/solution.py
+++ b/solution.py
@@ -541,8 +541,27 @@
 
 
 class Carry:
-    def __init__(self, loads):
-        self.loads = loads
+    def __init__(self, loads, fetches, leaves):
+        self.loads, self.fetches, self.leaves = loads, fetches, leaves
+        self.left = []
+
+    def fetch(self):
+        for copy in self.fetches:
+            copy.start()
+
+    def fetched(self):
+        for copy in self.fetches:
+            copy.wait()
+
+    def leave(self, *which):
+        for k in which:
+            self.leaves[k].start()
+            self.left.append(k)
+
+    def gone(self):
+        self.leave(*[k for k in self.leaves if k not in self.left])
+        for k in self.left:
+            self.leaves[k].wait()
 
     def peers(self):
         ways = []
@@ -832,11 +851,10 @@
         self.squares[...] = jnp.full(self.squares.shape, jnp.sum(total * total), F32)
 
 
-def run(body, name, operands, outs, scratch, collective_id=None, loads=(), far_operands=()):
+def run(body, name, operands, outs, scratch, collective_id=None, loads=(), away=(), lazy=(), early=()):
+    any_place = pl.BlockSpec(memory_space=pl.ANY)
     given, taken = list(operands), []
-    in_specs = [
-        pl.BlockSpec(memory_space=pl.ANY) if k in far_operands else whole_vmem() for k in range(len(operands))
-    ]
+    in_specs = [any_place if k in away or k in lazy else whole_vmem() for k in range(len(operands))]
     for load in loads:
         places = []
         for operand, spec in zip(load.operands, load.in_specs):
@@ -847,8 +865,9 @@
                 in_specs.append(spec)
             places.append(known[0])
         taken.append(places)
+    moved = [operands[k] for k in lazy] + [outs[k] for k in early]
     counts = [len(given), len(outs)] + [len(load.outs) for load in loads]
-    counts += [len(scratch)] + [len(load.scratch) for load in loads]
+    counts += [len(scratch)] + [len(load.scratch) for load in loads] + [len(moved), len(moved)]
     parts = 1 + len(loads)
 
     def kernel(*refs):
@@ -858,14 +877,26 @@
             place += count
         for k, load in enumerate(loads):
             load.bind([groups[0][p] for p in taken[k]], groups[2 + k], groups[2 + parts + k])
-        body(*groups[0][: len(operands)], *groups[1], *groups[1 + parts], carry=Carry(list(loads)))
+        mine, results = list(groups[0][: len(operands)]), list(groups[1])
+        fetches, leaves = [], {}
+        for k, buffer, sem in zip(lazy, groups[-2], groups[-1]):
+            fetches.append(pltpu.make_async_copy(mine[k], buffer, sem))
+            mine[k] = buffer
+        for k, buffer, sem in zip(early, groups[-2][len(lazy) :], groups[-1][len(lazy) :]):
+            leaves[k] = pltpu.make_async_copy(buffer, results[k], sem)
+            results[k] = buffer
+        body(*mine, *results, *groups[1 + parts], carry=Carry(list(loads), fetches, leaves))
 
     results = pl.pallas_call(
         kernel,
         out_shape=tuple(outs) + tuple(out for load in loads for out in load.outs),
         in_specs=in_specs,
-        out_specs=(whole_vmem(),) * len(outs) + tuple(spec for load in loads for spec in load.out_specs),
-        scratch_shapes=list(scratch) + [s for load in loads for s in load.scratch],
+        out_specs=tuple(any_place if k in early else whole_vmem() for k in range(len(outs)))
+        + tuple(spec for load in loads for spec in load.out_specs),
+        scratch_shapes=list(scratch)
+        + [s for load in loads for s in load.scratch]
+        + [pltpu.VMEM(value.shape, value.dtype) for value in moved]
+        + [pltpu.SemaphoreType.DMA] * len(moved),
         compiler_params=pltpu.CompilerParams(
             collective_id=collective_id,
             has_side_effects=collective_id is not None,
@@ -973,7 +1004,7 @@
     small[me] = jnp.zeros(small.shape[1:], F32)
     small[me, : gains.shape[0], : gains.shape[1]] = gains[...].astype(BF16).astype(F32)
     count = jnp.sum(counted[...].astype(F32), keepdims=True)
-    small[me, gains.shape[0] : gains.shape[0] + 1, :] = jnp.broadcast_to(count, (1, small.shape[2]))
+    small[me, COUNT_ROW : COUNT_ROW + 1, :] = jnp.broadcast_to(count, (1, small.shape[2]))
     greet([{WIDE: device} for device in around[1:]] + [sibling, partner])
     for step in range(1, owners):
         id_copy(step).start()
@@ -1027,9 +1058,7 @@
             halve(order[turn - 1])
         if turn >= 2:
             deliver(order[turn - 2])
-        if turn == 1:
-            carry.begin(2)
-    carry.begin(3)
+    carry.begin(2, 3)
     carry.hand_on(0, 1)
     for step in range(1, owners):
         small_copy(step).wait_recv()
@@ -1200,6 +1229,7 @@
 
 
 LAYER_SCRATCH = 13
+COUNT_ROW = 5
 
 
 def front_kernel(
@@ -1221,15 +1251,21 @@
     def at_feed():
         carry.end(2, 3)
         carry.begin(*later[2:])
+        carry.leave(0, 1, 5, 6)
+
+    def at_sent():
+        carry.hand_on(*later[:2])
+        carry.leave(7, 8)
 
     forward_part(
         0,
         [carry.loads[0].value] + [load.value for load in carry.loads[1:4]],
-        (at_half, at_feed, lambda: carry.hand_on(*later[:2]), lambda: carry.hand_on(*later[2:3])),
+        (at_half, at_feed, at_sent, lambda: carry.hand_on(*later[2:3])),
         normed, key_seg, query_seg, resid, gain_all,
         projected, mixed, middle, normed_two, result, normed_next, *scratch[-LAYER_SCRATCH:],
     )
     carry.end(*later)
+    carry.gone()
 
 
 def front(ids, counted, gains, steps, rates, tables, key_seg, query_seg, owners, heads_width, collective_id, loads):
@@ -1267,6 +1303,7 @@
         + layer_scratch(seq_len, width, heads_width),
         collective_id,
         loads,
+        early=(0, 1, 5, 6, 7, 8),
     )
 
 
@@ -1312,6 +1349,7 @@
     seq_len, width = normed_two.shape
     chunk = seq_len // 2 // CHUNKS
     sibling, partner, mine, other = group_places(seq_len)
+    carry.fetch()
     greet([sibling, partner] + carry.peers())
     at_start(carry, d_red, d_in)
     pair = (send, recv)
@@ -1338,6 +1376,7 @@
     at_made(carry)
     fetch = pltpu.make_async_copy(normed, after, loaded)
     fetch.start()
+    carry.fetched()
     total = jnp.zeros((1, width), F32)
     for j in range(CHUNKS):
         rows = rows_at(0, j, chunk)
@@ -1411,7 +1450,7 @@
     turned[...] = jnp.transpose(after[...])
     for which in range(3):
         weight_grad(turned, grad_projected.at[which], d_query.at[which])
-    at_sent(carry, d_out)
+    at_sent(carry, d_out, d_query)
     total = jnp.zeros((1, width), F32)
     for j in range(CHUNKS):
         rows = rows_at(0, j, chunk)
@@ -1470,7 +1509,8 @@
         + [pltpu.SemaphoreType.DMA],
         collective_id,
         loads,
-        far_operands=(14,),
+        away=(14,),
+        lazy=(0, 4, 6, 8, 9, 10, 12, 13),
     )
 
 
@@ -1485,7 +1525,7 @@
 def loss_part(
     row, normed, info, value, gain, table_loads, grad_out, branch, d_gain, losses, d_tables,
     logits, grads, places, turned, stat_out, stat_in, sum_out, sum_in,
-    stat_send, stat_recv, sum_send, sum_recv, near_out, near_in, far_out, far_in, send, recv,
+    stat_send, stat_recv, sum_send, sum_recv, near_out, near_in, far_out, far_in, send, recv, made,
 ):
     seq_len, width = normed.shape
     chunk = seq_len // 2 // CHUNKS
@@ -1667,6 +1707,7 @@
     turned[...] = jnp.transpose(normed[...])
     for k, d_table in enumerate(d_tables):
         weight_grad(turned, grads.at[:, k * piece_width : (k + 1) * piece_width], d_table)
+    made()
     gain_total = jnp.zeros((1, gain.shape[1]), F32)
     for j in range(CHUNKS):
         rows = rows_at(0, j, chunk)
@@ -1690,14 +1731,21 @@
 
 
 def back_kernel(
-    layer, normed, key_seg, query_seg, resid, w_query, w_out, w_in, gains, info,
+    layer, normed, key_seg, query_seg, resid, w_query, w_out, w_in, gains, noised, clean, steps, counted, counts,
     projected, mixed, middle, normed_two, grad_out, branch, d_gain, losses, *refs, carry,
 ):
     pieces = len(carry.loads) - 1
     d_tables, refs = refs[:pieces], refs[pieces:]
-    (result, normed_next), refs = refs[:2], refs[2:]
+    (result, normed_next, info), refs = refs[:3], refs[3:]
     loss_scratch, layer_refs = refs[:-LAYER_SCRATCH], refs[-LAYER_SCRATCH:]
     me = lax.axis_index(NARROW)
+    carry.fetch()
+    info[...] = jnp.zeros(info.shape, F32)
+    mask = counted[...].astype(F32)
+    for row, value in enumerate((noised[...], clean[...], steps[...])):
+        info[row : row + 1, :] = value.astype(F32)
+    info[3:4, :] = mask / counts[COUNT_ROW : COUNT_ROW + 1, 0:1]
+    info[4:5, :] = mask
     greet([{NARROW: lax.rem(me + k, 4)} for k in range(1, 4)] + carry.peers())
     carry.begin(0, 1)
 
@@ -1705,11 +1753,13 @@
         carry.begin(2)
 
     def at_feed():
+        carry.fetched()
         carry.end(0)
         carry.hand_on(1)
         carry.begin(3)
 
     def at_sent():
+        carry.leave(0, 1, 2, 3)
         carry.hand_on(2)
         carry.begin(4)
 
@@ -1727,12 +1777,13 @@
     carry.end(1, 2, 3)
     loss_part(
         2 * layer + 2, normed_next, info, result, gains, carry.loads[1:], grad_out, branch, d_gain, losses, d_tables,
-        *loss_scratch, *layer_refs[2:6], *layer_refs[-2:],
-    )
+        *loss_scratch, *layer_refs[2:6], *layer_refs[-2:], made=lambda: carry.leave(*range(8, 8 + pieces)),
+    )
+    carry.gone()
 
 
 def last_and_loss(
-    layer, normed, key_seg, query_seg, resid, w_query, w_out, w_in, gains, info, vocab, collective_id, loads
+    layer, normed, key_seg, query_seg, resid, w_query, w_out, w_in, gains, tokens, counts, vocab, collective_id, loads
 ):
     seq_len, width = normed.shape
     heads_width = w_query.shape[2]
@@ -1741,7 +1792,7 @@
     return run(
         functools.partial(back_kernel, layer),
         "last_and_loss",
-        [normed, key_seg, query_seg, resid, w_query, w_out, w_in, gains, info],
+        [normed, key_seg, query_seg, resid, w_query, w_out, w_in, gains, *tokens, counts],
         layer_outs(seq_len, width, heads_width)
         + [
             jax.ShapeDtypeStruct((half, width), F32),
@@ -1753,6 +1804,7 @@
         [
             pltpu.VMEM((half, width), F32),
             pltpu.VMEM((seq_len, width), BF16),
+            pltpu.VMEM((8, seq_len), F32),
             pltpu.VMEM((seq_len, vocab), F32),
             pltpu.VMEM((seq_len, vocab), BF16),
             pltpu.VMEM((blocks, 2, LANES, LANES), F32),
@@ -1766,6 +1818,8 @@
         + layer_scratch(seq_len, width, heads_width),
         collective_id,
         loads,
+        lazy=(3, 6),
+        early=(0, 1, 2, 3) + tuple(range(8, 8 + pieces)),
     )
 
 
@@ -1775,20 +1829,20 @@
 
 
 def tail_kernel(
-    layers, branch, ids_all, losses, full, *refs, carry,
+    layers, branch, ids_all, losses, *refs, carry,
 ):
     gain_parts, refs = refs[: 2 * layers + 1], refs[2 * layers + 1 :]
-    squares, refs = refs[: len(refs) - 32], refs[len(refs) - 32 :]
-    tail_body(branch, ids_all, losses, full, gain_parts, squares, *refs, carry)
+    squares, refs = refs[: len(refs) - 24], refs[len(refs) - 24 :]
+    tail_body(branch, ids_all, losses, gain_parts, squares, *refs, carry)
 
 
 def tail_body(
-    branch, ids_all, losses, full, gain_parts, squares,
-    d_table, d_full, d_small, scalars,
+    branch, ids_all, losses, gain_parts, squares,
+    d_table, d_small, scalars,
     out_blocks, all_in, masked, picks, total, gains_out, gains_in, blocks, block_in, line_out, line_in,
-    fast_in, sums, slow_in, near, along, across,
+    near, along, across,
     wide_send, wide_recv, far_send, far_recv, near_send, near_recv,
-    pair_send, pair_recv, line_send, line_recv, sum_sems,
+    sum_sems,
     carry,
 ):
     seq_len, width = branch.shape
@@ -1823,18 +1877,6 @@
         rows = all_in.at[around[step], pl.ds(2 * lax.rem(place, 2), 2)]
         return remote(rows, rows, near_send.at[step], near_recv.at[step], sibling)
 
-    def block(owner):
-        return full.at[:, owner]
-
-    def pair_copy(step):
-        return remote(
-            block(2 * lax.rem(slow + step, slows) + 1 - fast), fast_in.at[step],
-            pair_send.at[step], pair_recv.at[step], beside,
-        )
-
-    def line_copy(step):
-        return remote(sums.at[step], slow_in.at[step], line_send.at[step], line_recv.at[step], along_way(step))
-
     def gain_near():
         return remote(gains_out, gains_in, sum_sems.at[0, 0], sum_sems.at[1, 0], sibling)
 
@@ -1849,8 +1891,6 @@
 
     near_ways = [{NARROW: lax.rem(place + step, group)} for step in range(1, group)]
     greet([{WIDE: device} for device in around[1:]] + near_ways)
-    for step in range(slows):
-        pair_copy(step).start()
     gains_out[...] = jnp.zeros(gains_out.shape, F32)
     for row, part in enumerate(gain_parts):
         gains_out[row : row + 1, :] = part[...]
@@ -1909,12 +1949,6 @@
             hand_over(order[turn - 1])
         if turn == 1:
             for step in list(range(1, slows)) + [0]:
-                pair_copy(step).wait_recv()
-                owner = 2 * lax.rem(slow + step, slows) + fast
-                sums[step] = (block(owner)[...].astype(F32) + fast_in[step].astype(F32)).astype(BF16)
-                if step:
-                    line_copy(step).start()
-            for step in list(range(1, slows)) + [0]:
                 gain_pair(step).wait_recv()
                 line_out[step] = blocks[2 * lax.rem(slow + step, slows) + fast] + block_in[step]
                 if step:
@@ -1923,17 +1957,13 @@
             gather_grad(order[turn - 2], turn == 2)
     for t in range(vocab // LANES):
         d_table[:, t * LANES : (t + 1) * LANES] = total[t * share : (t + 1) * share, :]
-    result = sums[0].astype(F32)
     small = line_out[0]
     for step in range(1, slows):
-        line_copy(step).wait_recv()
-        result = result + slow_in[step].astype(F32)
         gain_line(step).wait_recv()
         small = small + line_in[step]
-    d_full[...] = result
     d_small[...] = small
     carry.end(*carry.all())
-    square = jnp.sum(result * result) + jnp.sum(d_table[...] * d_table[...])
+    square = jnp.sum(d_table[...] * d_table[...])
     for part in squares:
         square = square + part[0, 0]
     for load in carry.loads:
@@ -1971,27 +2001,23 @@
         if step:
             wide_copy(step).wait_send()
     for step in range(slows):
-        pair_copy(step).wait_send()
         gain_pair(step).wait_send()
         if step:
-            line_copy(step).wait_send()
             gain_line(step).wait_send()
 
 
-def tail(branch, ids_all, losses, full, gain_parts, squares, share, vocab, group, collective_id, loads):
+def tail(branch, ids_all, losses, gain_parts, squares, share, vocab, group, collective_id, loads):
     seq_len, width = branch.shape
     owners = ids_all.shape[0]
     slows = owners // 2
-    shape = full.shape[:1] + full.shape[2:]
     dma = pltpu.SemaphoreType.DMA
     small = (8, LANES)
     return run(
         functools.partial(tail_kernel, (len(gain_parts) - 1) // 2),
         "tail",
-        [branch, ids_all, losses, full, *gain_parts, *squares],
+        [branch, ids_all, losses, *gain_parts, *squares],
         [
             jax.ShapeDtypeStruct((share, vocab), F32),
-            jax.ShapeDtypeStruct(shape, F32),
             jax.ShapeDtypeStruct(small, F32),
             jax.ShapeDtypeStruct(small, F32),
         ],
@@ -2007,15 +2033,11 @@
             pltpu.VMEM((slows,) + small, F32),
             pltpu.VMEM((slows,) + small, F32),
             pltpu.VMEM((slows,) + small, F32),
-            pltpu.VMEM((slows,) + shape, BF16),
-            pltpu.VMEM((slows,) + shape, BF16),
-            pltpu.VMEM((slows,) + shape, BF16),
             pltpu.VMEM((group,) + small, F32),
             pltpu.VMEM((slows,) + small, F32),
             pltpu.VMEM((2,) + small, F32),
         ]
         + [dma((owners,))] * 6
-        + [dma((slows,))] * 4
         + [dma((12, max(slows, group)))],
         collective_id,
         loads,
@@ -2078,10 +2100,6 @@
 ):
     layers = attn_in.shape[0]
     gain_rows, gain_cols = gains.shape
-    mask = counted.reshape(-1).astype(jnp.float32)
-    seq_len = mask.shape[0]
-    half = seq_len // 2
-    core = lax.rem(lax.axis_index(NARROW), 2)
     share, vocab = tables.shape[1:]
     leads = (1, 0, 0, 0)
     four = (attn_in, attn_out, ffn_in, ffn_out)
@@ -2089,7 +2107,6 @@
     def joined(value, lead):
         return value.reshape(value.shape[:lead] + (-1,) + value.shape[lead + 2 :])
 
-    step_flat = timesteps.reshape(-1)
     ids = noised.reshape(4, -1)
     steps = timesteps.reshape(-1, LANES)
     half_width = D // 2
@@ -2108,13 +2125,9 @@
     first_w = [joined(value, lead) for value, lead in zip(carried[:4], leads)]
     query_w, output_w, expand_w = [joined(value, lead) for value, lead in zip(carried[4:7], leads)]
     kept = [(residual, normed, projected, mixed, middle, normed_two, *first_w)]
-    noised_flat, clean_flat = noised.reshape(-1), clean.reshape(-1)
-    info = jnp.stack(
-        [noised_flat.astype(F32), clean_flat.astype(F32), step_flat.astype(F32), mask / token_total, mask]
-        + [jnp.zeros_like(mask)] * 3
-    )
     (projected, mixed, middle, normed_two, grad, branch, gain_final, losses, *d_last), (reduce_w,) = last_and_loss(
-        1, normed_next, key_seg, query_seg, result, query_w, output_w, expand_w, gain_w, info, vocab, 1,
+        1, normed_next, key_seg, query_seg, result, query_w, output_w, expand_w, gain_w,
+        (noised, clean, timesteps, counted), counts, vocab, 1,
         [FastLoad(carried[7], 0, wide)]
         + [GatherLoad(tables, 1, 0, wide, window, place=LOCAL) for window in windows],
     )
@@ -2134,6 +2147,7 @@
 
     hidden = ffn_in.shape[2]
     made = jax.ShapeDtypeStruct((wide, share, hidden), BF16)
+    made_in = jax.ShapeDtypeStruct((3, wide, share, attn_in.shape[3]), BF16)
     made_out = jax.ShapeDtypeStruct((wide, share, attn_out.shape[2]), BF16)
 
     def start_last(carry, d_red, d_in):
@@ -2146,7 +2160,7 @@
         lambda carry: carry.begin(PIECES, PIECES + 1),
         lambda carry: carry.hand_on(*range(half_pieces)),
         lambda carry: carry.hand_on(*range(half_pieces, PIECES)),
-        lambda carry, d_out: None,
+        lambda carry, d_out, d_query: None,
     )
     residual, normed, projected, mixed, middle, normed_two, query_w, output_w, expand_w, reduce_w = kept[1]
     (grad, branch, d_out, d_query, gain_two, gain_one), carried = backward_block(
@@ -2164,9 +2178,10 @@
         carry.loads[4].full, carry.loads[5].full = d_red, d_in
         carry.begin(0, 1, 2, 3)
 
-    def sent_first(carry, d_out):
-        carry.loads[6].full = d_out
-        carry.begin(6)
+    def sent_first(carry, d_out, d_query):
+        carry.hand_on(5)
+        carry.loads[6].full, carry.loads[7].full = d_out, d_query
+        carry.begin(6, 7)
 
     points = (
         start_first,
@@ -2180,18 +2195,18 @@
         0, math.sqrt(D), points, grad, branch, reduce_w, expand_w, output_w, normed_two, middle, gain_w, mixed,
         projected, key_seg, query_seg, query_w, residual, normed, wide, 3,
         [LineLoad(red_sums, wide), LineLoad(in_sums, wide), ReduceLoad(d_out, 0), ReduceLoad(d_query, 1)]
-        + [ReduceLoad(made, 0, True), PairLoad(made, 0, True), PairLoad(made_out, 0, True)],
-    )
-    for key in ((FFN_OUT, 1), (FFN_IN, 1), (ATTN_OUT, 1), (ATTN_IN, 1), (FFN_OUT, 0)):
+        + [ReduceLoad(made, 0, True), ReduceLoad(made, 0, True), PairLoad(made_out, 0, True), PairLoad(made_in, 1, True)],
+    )
+    for key in ((FFN_OUT, 1), (FFN_IN, 1), (ATTN_OUT, 1), (ATTN_IN, 1), (FFN_OUT, 0), (FFN_IN, 0)):
         carried = landed(key, carried)
-    in_sums, out_sums = carried
+    out_sums, in_sums = carried
     gain_grads[:2] = gain_one, gain_two
 
-    (own_first, own[ATTN_IN, 0], total_small, scalars), carried = tail(
-        branch, ids_all, losses, d_query, gain_grads, squares, share, vocab, 4, 4,
-        [LineLoad(in_sums, wide), LineLoad(out_sums, wide)],
-    )
-    own[FFN_IN, 0], own[ATTN_OUT, 0] = carried[0], carried[2]
+    (own_first, total_small, scalars), carried = tail(
+        branch, ids_all, losses, gain_grads, squares, share, vocab, 4, 4,
+        [LineLoad(out_sums, wide), LineLoad(in_sums, wide)],
+    )
+    own[ATTN_OUT, 0], own[ATTN_IN, 0] = carried[0], carried[2]
     grad_attn_in, grad_attn_out, grad_ffn_in, grad_ffn_out = [
         jnp.stack([own[name, index] for index in range(layers)]) for name in (ATTN_IN, ATTN_OUT, FFN_IN, FFN_OUT)
     ]

time: 488 us -> 470 us (0.963)
  Pallas kernels: 454 us -> 440 us
    pallas_call x5, Pallas kernels: 454 us -> 440 us  [run(): pl.pallas_call(kernel, out_shape=tuple(outs) + tuple((out for load in loa...]
where the time goes in v9:
time: 470 us; the launch traced here: 464 us
  Pallas kernels  440 us (94%)
  other arithmetic  12.5 us (3%)
  local copies, waits for them, and re-layouts  8.51 us (2%)
    pallas_call x5, Pallas kernels, run(): pl.pallas_call(kernel, out_shape=tuple(outs) + tuple((out for load in loa...  440 us
    convert_element_type x5, other arithmetic, adam(): return (weight_new, first_new, second_new, weight_new.astype(jnp.bfloat16))  10.5 us

profile of v9, /device:TPU:0, one launch (start us, length us, event | category | flops | bytes accessed | tf_op | source)
XLA Modules:
  0.0 463.7 jit_solution(16759080149106299317)
XLA Ops:
  0.7 0.6 multiply_exponential_fusion.refs_4_
  1.2 0.5 broadcast.79
  1.8 1.3 reduce.3
  3.1 0.6 reshape.110.refs_0_
  3.7 1.7 copy.50.refs_6_.refs_1_.refs_10_
  5.4 115.9 %front.1 = (f32[512,768]{1,0:T(8,128)}, bf16[1024,768]{1,0:T(8,128)(2,1)}, f32[8,768]{1,0:T(8,128)}, f32[8,128]{1,0:T(8,128)}, s32[8,4,256]{2,1,0:T(4,128)}, /*i...) custom-call(s32[4,256]{1,0:T(4,128)} %reshape.110.refs_0_, ...), custom_call_target="tpu_custom_call" | custom-call | tf_op jit(solution)/shard_map/front/pallas_call | solution.py:890
  121.3 1.2 slice.13
  122.5 115.5 %last_and_loss.1 = (bf16[3,1024,192]{2,1,0:T(8,128)(2,1)}, bf16[1024,192]{1,0:T(8,128)(2,1)}, f32[512,768]{1,0:T(8,128)}, bf16[1024,768]{1,0:T(8,128)(2,1)}, f32...) custom-call(bf16[1024,768]{1,0:T(8,128)(2,1)} %get-tuple-element.97., ...), custom_call_target="tpu_custom_call" | custom-call | tf_op jit(solution)/shard_map/last_and_loss/pallas_call | solution.py:890
  238.0 73.2 %backward_block.2 = (f32[512,768]{1,0:T(8,128)}, bf16[1024,768]{1,0:T(8,128)(2,1)}, bf16[8,96,192]{2,1,0:T(8,128)(2,1)}, bf16[3,8,96,192]{3,2,1,0:T(8,128)(2,1)}...) custom-call(f32[512,768]{1,0:T(8,128)} %get-tuple-element.105.refs_0, ...), custom_call_target="tpu_custom_call" | custom-call | tf_op jit(solution)/shard_map/backward_block/pallas_call | solution.py:890
  311.2 77.3 %backward_block.3 = (f32[512,768]{1,0:T(8,128)}, bf16[1024,768]{1,0:T(8,128)(2,1)}, bf16[8,96,192]{2,1,0:T(8,128)(2,1)}, bf16[3,8,96,192]{3,2,1,0:T(8,128)(2,1)}...) custom-call(f32[512,768]{1,0:T(8,128)} %get-tuple-element.116.refs_0, ...), custom_call_target="tpu_custom_call" | custom-call | tf_op jit(solution)/shard_map/backward_block/pallas_call | solution.py:890
  388.5 0.0 copy-start.25
  388.5 0.0 copy-start.26
  388.5 0.0 copy-start.27
  388.5 0.0 copy-start.6
  388.5 0.0 copy-start.24
  388.6 0.0 copy-start.20
  388.6 0.0 copy-start.21
  388.6 0.0 copy-start.22
  388.6 0.0 copy-start.23
  388.6 57.7 %tail.1 = (f32[96,2048]{1,0:T(8,128)}, f32[8,128]{1,0:T(8,128)}, f32[8,128]{1,0:T(8,128)}, f32[96,192]{1,0:T(8,128)}, f32[8,128]{1,0:T(8,128)}, /*index=5*/f32[3,96,192]{2,1,0:T(8,128)}, f32[8,128]{1,0:T(8,128)}) custom-call(bf16[1024,768]{1,0:T(8,128)(2,1)} %get-tuple-element.132.refs_0_, s32[8,4,256]{2,1,0:T(4,128)} %get-tuple-element.133.refs_1_, ...), custom_call_target="tpu_custom_call" | custom-call | tf_op jit(solution)/shard_map/tail/pallas_call | solution.py:890
  446.3 0.0 copy-start.1
  446.4 0.0 copy-start.8
  446.4 0.0 copy-start.9
  446.4 0.0 copy-start.18
  446.4 0.0 copy-start.19
  446.4 1.4 fusion.18
  448.6 1.3 fusion.6
  449.9 2.0 fusion.14
  451.9 0.1 maximum_bitcast_fusion
  452.0 0.0 copy-start.2
  452.0 0.0 copy-start.3
  452.0 0.0 copy-start.10
  452.0 0.0 copy-start.11
  452.0 0.0 copy-start.12
  452.0 0.0 copy-start.13
  452.1 1.6 fusion.16
  453.7 0.2 copy-done.10
  453.9 0.4 copy-done.11
  454.4 0.2 copy-done.12
  454.5 0.2 copy-done.13
  454.7 0.1 copy-done.14
  454.8 0.1 copy-done.15
  454.9 0.1 copy-done.16
  455.0 2.3 fusion.10
  457.3 1.0 copy-done.4
  458.3 0.5 copy-done.5
  458.8 0.2 copy-done.7
  459.0 3.3 fusion.8
  (26 shorter events, 0.1 us)
Async XLA Ops:
  388.5 60.1 %copy-start.25 = (f32[5,96]{1,0:T(8,128)S(1)}, f32[5,96]{1,0:T(8,128)}, u32[]{:S(2)}) copy-start(f32[5,96]{1,0:T(8,128)} %refs_2_.2) | copy-start | bytes 5764
  388.5 60.1 %copy-start.26 = (f32[5,96]{1,0:T(8,128)S(1)}, f32[5,96]{1,0:T(8,128)}, u32[]{:S(2)}) copy-start(f32[5,96]{1,0:T(8,128)} %param.39) | copy-start | bytes 5764
  388.5 60.1 %copy-start.27 = (f32[5,96]{1,0:T(8,128)S(1)}, f32[5,96]{1,0:T(8,128)}, u32[]{:S(2)}) copy-start(f32[5,96]{1,0:T(8,128)} %param.45) | copy-start | bytes 5764
  388.5 61.4 %copy-start.6 = (f32[2,96,192]{2,1,0:T(8,128)S(1)}, f32[2,96,192]{2,1,0:T(8,128)}, u32[]{:S(2)}) copy-start(f32[2,96,192]{2,1,0:T(8,128)} %refs_9_.2) | copy-start | bytes 442372
  388.5 61.3 %copy-start.24 = (f32[2,96,192]{2,1,0:T(8,128)S(1)}, f32[2,96,192]{2,1,0:T(8,128)}, u32[]{:S(2)}) copy-start(f32[2,96,192]{2,1,0:T(8,128)} %param.35) | copy-start | bytes 442372
  388.6 63.3 %copy-start.20 = (f32[96,512]{1,0:T(8,128)S(1)}, f32[96,512]{1,0:T(8,128)}, u32[]{:S(2)}) copy-start(f32[96,512]{1,0:T(8,128)} %get-tuple-element.162) | copy-start | bytes 589828
  388.6 63.3 %copy-start.21 = (f32[96,512]{1,0:T(8,128)S(1)}, f32[96,512]{1,0:T(8,128)}, u32[]{:S(2)}) copy-start(f32[96,512]{1,0:T(8,128)} %get-tuple-element.163) | copy-start | bytes 589828
  388.6 63.3 %copy-start.22 = (f32[96,512]{1,0:T(8,128)S(1)}, f32[96,512]{1,0:T(8,128)}, u32[]{:S(2)}) copy-start(f32[96,512]{1,0:T(8,128)} %get-tuple-element.164) | copy-start | bytes 589828
  388.6 63.3 %copy-start.23 = (f32[96,512]{1,0:T(8,128)S(1)}, f32[96,512]{1,0:T(8,128)}, u32[]{:S(2)}) copy-start(f32[96,512]{1,0:T(8,128)} %get-tuple-element.165) | copy-start | bytes 589828
  446.3 5.6 %copy-start.1 = (f32[2,3,96,192]{3,2,1,0:T(8,128)S(1)}, f32[2,3,96,192]{3,2,1,0:T(8,128)}, u32[]{:S(2)}) copy-start(f32[2,3,96,192]{3,2,1,0:T(8,128)} %refs_8_.2) | copy-start | bytes 1327108
  446.4 5.6 %copy-start.8 = (f32[2,3,96,192]{3,2,1,0:T(8,128)S(1)}, f32[2,3,96,192]{3,2,1,0:T(8,128)}, u32[]{:S(2)}) copy-start(f32[2,3,96,192]{3,2,1,0:T(8,128)} %param.34) | copy-start | bytes 1327108
  446.4 5.6 %copy-start.9 = (f32[2,3,96,192]{3,2,1,0:T(8,128)S(1)}, f32[2,3,96,192]{3,2,1,0:T(8,128)}, u32[]{:S(2)}) copy-start(f32[2,3,96,192]{3,2,1,0:T(8,128)} %param.40) | copy-start | bytes 1327108
  446.4 5.6 %copy-start.18 = (f32[3,96,192]{2,1,0:T(8,128)S(1)}, f32[3,96,192]{2,1,0:T(8,128)}, u32[]{:S(2)}) copy-start(f32[3,96,192]{2,1,0:T(8,128)} %get-tuple-element.154) | copy-start | bytes 663556
  446.4 5.6 %copy-start.19 = (f32[3,96,192]{2,1,0:T(8,128)S(1)}, f32[3,96,192]{2,1,0:T(8,128)}, u32[]{:S(2)}) copy-start(f32[3,96,192]{2,1,0:T(8,128)} %get-tuple-element.153) | copy-start | bytes 663556
  451.9 1.8 copy-start.17
  452.0 1.7 copy-start.2
  452.0 1.7 copy-start.3
  452.0 1.9 copy-start.10
  452.0 2.3 copy-start.11
  452.0 2.5 copy-start.12
  452.0 2.7 copy-start.13
  452.1 2.7 copy-start.14
  452.1 2.8 copy-start.15
  452.1 2.9 copy-start.16
  455.0 2.3 copy-start
  455.0 3.4 copy-start.4
  455.0 3.8 copy-start.5
  455.0 4.0 copy-start.7

commit v10 on v9

--- a/solution.py
+++ b/solution.py
@@ -416,6 +416,7 @@
 F32 = jnp.float32
 BF16 = jnp.bfloat16
 CHUNKS = 4
+SPAN = 2
 VMEM_LIMIT = 61 * 1024 * 1024
 FORWARD_KIND = BF16
 BACKWARD_KIND = BF16
@@ -487,6 +488,16 @@
     def give(self, j, value):
         self.near_out[j] = value
         self.near(j).start()
+
+    def give_span(self, k, value):
+        chunk = self.near_out.shape[1]
+        for i in range(SPAN):
+            self.give(SPAN * k + i, value[i * chunk : (i + 1) * chunk, :])
+
+    def pass_on_span(self, k, value):
+        chunk = self.near_out.shape[1]
+        for i in range(SPAN):
+            self.pass_on(SPAN * k + i, value[i * chunk : (i + 1) * chunk, :])
 
     def pass_on(self, j, value):
         self.near(j).wait_recv()
@@ -943,6 +954,7 @@
 
 
 LANES = 128
+SUB = 64
 
 
 def spread(row):
@@ -1123,8 +1135,8 @@
 
 def forward_part(
     layer, weights, points, normed, key_seg, query_seg, resid, gains,
-    projected, mixed, middle, normed_two, result, normed_next,
-    bias, values_t, near_out, near_in, far_out, far_in, near_out2, near_in2, far_out2, far_in2, own2, send, recv,
+    projected, mixed, middle, normed_two, log_sums, result, normed_next,
+    bias, values_t, near_out, near_in, far_out, far_in, near_out2, near_in2, far_out2, far_in2, send, recv,
 ):
     w_query, w_out, w_in, w_red = weights
     at_half, at_feed, at_sent, at_last = points
@@ -1155,44 +1167,44 @@
         parts = []
         for head in range(heads):
             scores = dot_nt(projected[1], head_lanes(asked, head, HD)) + bias[...]
-            powers = jnp.exp(scores - jnp.max(scores, axis=0, keepdims=True))
-            probs = (powers * (1.0 / jnp.sum(powers, axis=0, keepdims=True))).astype(BF16)
+            top = jnp.max(scores, axis=0, keepdims=True)
+            powers = jnp.exp(scores - top)
+            total = jnp.sum(powers, axis=0, keepdims=True)
+            log_sums[head : head + 1, rows] = top + jnp.log(total)
+            probs = (powers * (1.0 / total)).astype(BF16)
             parts.append(dot_nn(values_t[head * HD : (head + 1) * HD, :], probs))
         mixed[rows, :] = jnp.transpose(jnp.concatenate(parts, axis=0)).astype(BF16)
 
-    def project(start, j):
-        return dot_nt(mixed[rows_at(start, j, chunk), :], w_out())
+    def project(start, k):
+        return dot_nt(mixed[rows_at(start, k, SPAN * chunk), :], w_out())
 
     def feed(rows):
         pre = dot_nn(normed_two[rows, :], w_in())
         return dot_nt(gelu_of(pre).astype(BF16), w_red())
 
-    per_block = block // chunk
-    for part in range(CHUNKS // per_block):
+    for part in range(CHUNKS // SPAN):
 
         def both(i, _):
             attend_rows(jnp.where(i == 0, other, mine) + part * block)
             return 0
 
         lax.fori_loop(0, 2, both, 0)
-        for j in range(part * per_block, (part + 1) * per_block):
-            first.give(j, project(other, j))
+        first.give_span(part, project(other, part))
         if part == 0:
             at_half()
-        for j in range(part * per_block, (part + 1) * per_block):
-            first.pass_on(j, project(mine, j))
+        first.pass_on_span(part, project(mine, part))
     at_feed()
-    for j in range(CHUNKS):
-        rows = rows_at(0, j, chunk)
-        mid = resid[rows, :] + first.take(j)
-        middle[rows, :] = mid
-        share.put(j, norm_of(mid, gains[2 * layer + 1 : 2 * layer + 2, :]).astype(BF16))
-        own2[j] = feed(rows_at(mine, j, chunk))
-        share.arrived(j)
-        second.give(j, feed(rows_at(other, j, chunk)))
-        if j >= 1:
-            second.pass_on(j - 1, own2[j - 1])
-    second.pass_on(CHUNKS - 1, own2[CHUNKS - 1])
+    for k in range(CHUNKS // SPAN):
+        for j in range(SPAN * k, SPAN * (k + 1)):
+            rows = rows_at(0, j, chunk)
+            mid = resid[rows, :] + first.take(j)
+            middle[rows, :] = mid
+            share.put(j, norm_of(mid, gains[2 * layer + 1 : 2 * layer + 2, :]).astype(BF16))
+        kept = feed(rows_at(mine, k, SPAN * chunk))
+        for j in range(SPAN * k, SPAN * (k + 1)):
+            share.arrived(j)
+        second.give_span(k, feed(rows_at(other, k, SPAN * chunk)))
+        second.pass_on_span(k, kept)
     at_sent()
     for j in range(CHUNKS):
         rows = rows_at(0, j, chunk)
@@ -1213,28 +1225,28 @@
         jax.ShapeDtypeStruct((seq_len, heads_width), BF16),
         jax.ShapeDtypeStruct((seq_len // 2, width), F32),
         jax.ShapeDtypeStruct((seq_len, width), BF16),
+        jax.ShapeDtypeStruct((8, seq_len), F32),
     ]
 
 
 def layer_scratch(seq_len, width, heads_width):
     half, chunk = seq_len // 2, seq_len // 2 // CHUNKS
-    block = max(chunk, min(QUERY_BLOCK, half))
+    block = SPAN * chunk
     return (
         [pltpu.VMEM((seq_len, block), F32), pltpu.VMEM((heads_width, seq_len), BF16)]
         + Exchange.scratch(chunk, width, FORWARD_KIND)
         + Exchange.scratch(chunk, width, FORWARD_KIND)
-        + [pltpu.VMEM((CHUNKS, chunk, width), F32)]
         + sems(6)
     )
 
 
-LAYER_SCRATCH = 13
+LAYER_SCRATCH = 12
 COUNT_ROW = 5
 
 
 def front_kernel(
     ids, counted, gains, steps, rates, table, key_seg, query_seg,
-    resid, normed, gain_all, count_all, ids_all, projected, mixed, middle, normed_two, result, normed_next,
+    resid, normed, gain_all, count_all, ids_all, projected, mixed, middle, normed_two, log_sums, result, normed_next,
     *scratch, carry,
 ):
     embed_part(
@@ -1262,7 +1274,7 @@
         [carry.loads[0].value] + [load.value for load in carry.loads[1:4]],
         (at_half, at_feed, at_sent, lambda: carry.hand_on(*later[2:3])),
         normed, key_seg, query_seg, resid, gain_all,
-        projected, mixed, middle, normed_two, result, normed_next, *scratch[-LAYER_SCRATCH:],
+        projected, mixed, middle, normed_two, log_sums, result, normed_next, *scratch[-LAYER_SCRATCH:],
     )
     carry.end(*later)
     carry.gone()
@@ -1339,7 +1351,7 @@
 
 def backward_kernel(
     layer, scale, points, grad, branch, w_red, w_in, w_out, normed_two, middle, gains, mixed,
-    projected, key_seg, query_seg, w_query, resid, normed,
+    projected, log_sums, key_seg, query_seg, w_query, resid, normed,
     grad_out, branch_out, d_out, d_query, gain_two, gain_one,
     d_red, d_in, grad_middle, grad_attn, grad_mixed, grad_projected, grad_before, after, turned,
     bias, keys_t, grad_keys, grad_values,
@@ -1356,19 +1368,17 @@
     trade = Exchange((near_out, near_in, far_out, far_in), pair, 0, sibling, partner)
     share = Share(grad_attn, pair, 2, sibling, mine, chunk)
 
-    def ffn_partial(start, j):
-        rows = rows_at(start, j, chunk)
+    def ffn_partial(start, k):
+        rows = rows_at(start, k, SPAN * chunk)
         pre = dot_nn(normed_two[rows, :], w_in[...])
         after[rows, :] = gelu_of(pre).astype(BF16)
         low = (dot_nn(branch[rows, :], w_red[...]) * gelu_slope(pre)).astype(BF16)
         grad_before[rows, :] = low
         return dot_nt(low, w_in[...])
 
-    trade.give(0, ffn_partial(other, 0))
-    for j in range(CHUNKS):
-        if j + 1 < CHUNKS:
-            trade.give(j + 1, ffn_partial(other, j + 1))
-        trade.pass_on(j, ffn_partial(mine, j))
+    for k in range(CHUNKS // SPAN):
+        trade.give_span(k, ffn_partial(other, k))
+        trade.pass_on_span(k, ffn_partial(mine, k))
     turned[...] = jnp.transpose(branch[...])
     weight_grad(turned, after, d_red)
     turned[...] = jnp.transpose(normed_two[...])
@@ -1412,8 +1422,7 @@
             query = head_lanes(asked, head, HD)
             wanted = head_lanes(given, head, HD)
             scores = dot_nt(projected[1], query) + bias[...]
-            powers = jnp.exp(scores - jnp.max(scores, axis=0, keepdims=True))
-            probs = powers * (1.0 / jnp.sum(powers, axis=0, keepdims=True))
+            probs = jnp.exp(scores - log_sums[head : head + 1, rows])
             grad_probs = dot_nt(projected[2], wanted)
             centre = jnp.sum(probs * grad_probs, axis=0, keepdims=True)
             grad_scores = (probs * (grad_probs - centre)).astype(BF16)
@@ -1431,19 +1440,17 @@
     trade = Exchange((near_out, near_in, far_out2, far_in2), pair, 3, sibling, partner)
     share = Share(branch_out, pair, 5, sibling, mine, chunk)
 
-    def query_partial(start, j):
-        rows = rows_at(start, j, chunk)
+    def query_partial(start, k):
+        rows = rows_at(start, k, SPAN * chunk)
         found = None
         for which in range(3):
             part = dot_nt(grad_projected[which, rows, :], w_query[which])
             found = part if found is None else found + part
         return found
 
-    trade.give(0, query_partial(other, 0))
-    for j in range(CHUNKS):
-        if j + 1 < CHUNKS:
-            trade.give(j + 1, query_partial(other, j + 1))
-        trade.pass_on(j, query_partial(mine, j))
+    for k in range(CHUNKS // SPAN):
+        trade.give_span(k, query_partial(other, k))
+        trade.pass_on_span(k, query_partial(mine, k))
     turned[...] = jnp.transpose(grad_attn[...])
     weight_grad(turned, mixed, d_out)
     fetch.wait()
@@ -1469,7 +1476,7 @@
 
 def backward_block(
     layer, scale, points, grad, branch, w_red, w_in, w_out, normed_two, middle, gains, mixed,
-    projected, key_seg, query_seg, w_query, resid, normed, owners, collective_id, loads,
+    projected, log_sums, key_seg, query_seg, w_query, resid, normed, owners, collective_id, loads,
 ):
     seq_len, width = normed_two.shape
     hidden, heads_width = w_in.shape[1], w_query.shape[2]
@@ -1480,7 +1487,7 @@
         functools.partial(backward_kernel, layer, scale, points),
         "backward_block",
         [grad, branch, w_red, w_in, w_out, normed_two, middle, gains, mixed]
-        + [projected, key_seg, query_seg, w_query, resid, normed],
+        + [projected, log_sums, key_seg, query_seg, w_query, resid, normed],
         [
             jax.ShapeDtypeStruct((half, width), F32),
             jax.ShapeDtypeStruct((seq_len, width), BF16),
@@ -1509,8 +1516,8 @@
         + [pltpu.SemaphoreType.DMA],
         collective_id,
         loads,
-        away=(14,),
-        lazy=(0, 4, 6, 8, 9, 10, 12, 13),
+        away=(15,),
+        lazy=(0, 4, 6, 8, 9, 11, 13, 14),
     )
 
 
@@ -1560,26 +1567,35 @@
         places[b, 0] = at_noised
         places[b, 1] = at_clean
 
-        def top_step(t, top):
-            return jnp.maximum(top, logits[rows, tile_at(t)])
-
-        top = lax.fori_loop(1, tiles, top_step, logits[rows, tile_at(0)], unroll=4)
-        top = jnp.max(top, axis=1, keepdims=True)
-        top_wide = jnp.broadcast_to(top, (LANES, LANES))
-
-        def sum_step(t, totals):
-            powers, noised, clean = totals
-            piece = logits[rows, tile_at(t)]
-            column = lanes + (t * LANES).astype(F32)
-            return (
-                powers + jnp.exp(piece - top_wide),
-                noised + jnp.where(column == at_noised, piece, 0.0),
-                clean + jnp.where(column == at_clean, piece, 0.0),
-            )
-
-        zero = jnp.zeros((LANES, LANES), F32)
-        totals = lax.fori_loop(0, tiles, sum_step, (zero, zero, zero), unroll=2)
-        stat_out[b] = to_rows([top] + [jnp.sum(total, axis=1, keepdims=True) for total in totals])
+        tops, sums = [], [[], [], []]
+        for k in range(LANES // SUB):
+            part = pl.ds(pl.multiple_of(b * LANES + k * SUB, SUB), SUB)
+            subset = slice(k * SUB, (k + 1) * SUB)
+
+            def top_step(t, top):
+                return jnp.maximum(top, logits[part, tile_at(t)])
+
+            top = lax.fori_loop(1, tiles, top_step, logits[part, tile_at(0)], unroll=5)
+            top = jnp.max(top, axis=1, keepdims=True)
+            top_wide = jnp.broadcast_to(top, (SUB, LANES))
+            noised_at, clean_at = at_noised[subset], at_clean[subset]
+
+            def sum_step(t, totals):
+                powers, noised, clean = totals
+                piece = logits[part, tile_at(t)]
+                column = lanes[subset] + (t * LANES).astype(F32)
+                return (
+                    powers + jnp.exp(piece - top_wide),
+                    noised + jnp.where(column == noised_at, piece, 0.0),
+                    clean + jnp.where(column == clean_at, piece, 0.0),
+                )
+
+            zero = jnp.zeros((SUB, LANES), F32)
+            totals = lax.fori_loop(0, tiles, sum_step, (zero, zero, zero), unroll=4)
+            tops.append(top)
+            for found, total in zip(sums, totals):
+                found.append(jnp.sum(total, axis=1, keepdims=True))
+        stat_out[b] = to_rows([jnp.concatenate(found, axis=0) for found in [tops] + sums])
         for k in range(3):
             stat_copy(b, k).start()
         return 0
@@ -1623,16 +1639,23 @@
         log_wide = spread(log_total)
         ratio = spread(keep / rest)
 
-        def step(t, totals):
-            logs, shares = totals
-            probs = jnp.exp(logits[rows, tile_at(t)] - log_wide)
-            logits[rows, tile_at(t)] = probs
-            grown = 1.0 + probs * ratio
-            return (logs + jnp.log(grown), shares + probs / grown)
-
-        zero = jnp.zeros((LANES, LANES), F32)
-        totals = lax.fori_loop(0, tiles, step, (zero, zero), unroll=2)
-        sum_out[b] = to_rows([jnp.sum(total, axis=1, keepdims=True) for total in totals])
+        sums = [[], []]
+        for k in range(LANES // SUB):
+            part = pl.ds(pl.multiple_of(b * LANES + k * SUB, SUB), SUB)
+            log_part, ratio_part = log_wide[k * SUB : (k + 1) * SUB], ratio[k * SUB : (k + 1) * SUB]
+
+            def step(t, totals):
+                logs, shares = totals
+                probs = jnp.exp(logits[part, tile_at(t)] - log_part)
+                logits[part, tile_at(t)] = probs
+                grown = 1.0 + probs * ratio_part
+                return (logs + jnp.log(grown), shares + probs / grown)
+
+            zero = jnp.zeros((SUB, LANES), F32)
+            totals = lax.fori_loop(0, tiles, step, (zero, zero), unroll=4)
+            for found, total in zip(sums, totals):
+                found.append(jnp.sum(total, axis=1, keepdims=True))
+        sum_out[b] = to_rows([jnp.concatenate(found, axis=0) for found in sums])
         for k in range(3):
             sum_copy(b, k).start()
         return 0
@@ -1678,32 +1701,39 @@
         even, bent, ratio = spread(even), spread(bent), spread(ratio)
         at_noised, at_clean = places[b, 0], places[b, 1]
 
-        def step(t, _):
-            probs = logits[rows, tile_at(t)]
-            column = lanes + (t * LANES).astype(F32)
-            grad = probs * (even + bent / (1.0 + probs * ratio))
-            grad = grad + jnp.where(column == at_noised, extra_n, 0.0)
-            grad = grad + jnp.where(column == at_clean, extra_c, 0.0)
-            grads[rows, tile_at(t)] = grad.astype(BF16)
-            return 0
-
-        lax.fori_loop(0, tiles, step, 0, unroll=2)
-
-    def partial(start, j):
-        base = start // LANES + j * (chunk // LANES)
-        for b in range(chunk // LANES):
+        for k in range(LANES // SUB):
+            part = pl.ds(pl.multiple_of(b * LANES + k * SUB, SUB), SUB)
+            subset = slice(k * SUB, (k + 1) * SUB)
+            even_at, bent_at, ratio_at = even[subset], bent[subset], ratio[subset]
+            n_at, c_at, noised_at, clean_at = extra_n[subset], extra_c[subset], at_noised[subset], at_clean[subset]
+
+            def step(t, _):
+                probs = logits[part, tile_at(t)]
+                column = lanes[subset] + (t * LANES).astype(F32)
+                grad = probs * (even_at + bent_at / (1.0 + probs * ratio_at))
+                grad = grad + jnp.where(column == noised_at, n_at, 0.0)
+                grad = grad + jnp.where(column == clean_at, c_at, 0.0)
+                grads[part, tile_at(t)] = grad.astype(BF16)
+                return 0
+
+            lax.fori_loop(0, tiles, step, 0, unroll=4)
+
+    def partial(start, k):
+        span = SPAN * chunk
+        base = start // LANES + k * (span // LANES)
+        for b in range(span // LANES):
             pull(base + b)
         total = None
-        for k, table in enumerate(table_loads):
-            part = dot_nt(grads[rows_at(start, j, chunk), k * piece_width : (k + 1) * piece_width], table.value())
+        for k_table, table in enumerate(table_loads):
+            part = dot_nt(
+                grads[rows_at(start, k, span), k_table * piece_width : (k_table + 1) * piece_width], table.value()
+            )
             total = part if total is None else total + part
         return total
 
-    trade.give(0, partial(other, 0))
-    for j in range(CHUNKS):
-        if j + 1 < CHUNKS:
-            trade.give(j + 1, partial(other, j + 1))
-        trade.pass_on(j, partial(mine, j))
+    for k in range(CHUNKS // SPAN):
+        trade.give_span(k, partial(other, k))
+        trade.pass_on_span(k, partial(mine, k))
     turned[...] = jnp.transpose(normed[...])
     for k, d_table in enumerate(d_tables):
         weight_grad(turned, grads.at[:, k * piece_width : (k + 1) * piece_width], d_table)
@@ -1732,7 +1762,7 @@
 
 def back_kernel(
     layer, normed, key_seg, query_seg, resid, w_query, w_out, w_in, gains, noised, clean, steps, counted, counts,
-    projected, mixed, middle, normed_two, grad_out, branch, d_gain, losses, *refs, carry,
+    projected, mixed, middle, normed_two, log_sums, grad_out, branch, d_gain, losses, *refs, carry,
 ):
     pieces = len(carry.loads) - 1
     d_tables, refs = refs[:pieces], refs[pieces:]
@@ -1771,13 +1801,13 @@
         [lambda which: w_query[which], lambda: w_out[...], lambda: w_in[...], carry.loads[0].value],
         (at_half, at_feed, at_sent, at_last),
         normed, key_seg, query_seg, resid, gains,
-        projected, mixed, middle, normed_two, result, normed_next, *layer_refs,
+        projected, mixed, middle, normed_two, log_sums, result, normed_next, *layer_refs,
     )
     carry.hand_on(4)
     carry.end(1, 2, 3)
     loss_part(
         2 * layer + 2, normed_next, info, result, gains, carry.loads[1:], grad_out, branch, d_gain, losses, d_tables,
-        *loss_scratch, *layer_refs[2:6], *layer_refs[-2:], made=lambda: carry.leave(*range(8, 8 + pieces)),
+        *loss_scratch, *layer_refs[2:6], *layer_refs[-2:], made=lambda: carry.leave(*range(9, 9 + pieces)),
     )
     carry.gone()
 
@@ -1819,7 +1849,7 @@
         collective_id,
         loads,
         lazy=(3, 6),
-        early=(0, 1, 2, 3) + tuple(range(8, 8 + pieces)),
+        early=(0, 1, 2, 3) + tuple(range(9, 9 + pieces)),
     )
 
 
@@ -1832,7 +1862,7 @@
     layers, branch, ids_all, losses, *refs, carry,
 ):
     gain_parts, refs = refs[: 2 * layers + 1], refs[2 * layers + 1 :]
-    squares, refs = refs[: len(refs) - 24], refs[len(refs) - 24 :]
+    squares, refs = refs[: len(refs) - 25], refs[len(refs) - 25 :]
     tail_body(branch, ids_all, losses, gain_parts, squares, *refs, carry)
 
 
@@ -1840,8 +1870,8 @@
     branch, ids_all, losses, gain_parts, squares,
     d_table, d_small, scalars,
     out_blocks, all_in, masked, picks, total, gains_out, gains_in, blocks, block_in, line_out, line_in,
-    near, along, across,
-    wide_send, wide_recv, far_send, far_recv, near_send, near_recv,
+    near, along,
+    wide_send, wide_recv, far_send, far_recv, near_send, near_recv, all_send, all_recv,
     sum_sems,
     carry,
 ):
@@ -1931,7 +1961,7 @@
             for part in range(vocab // LANES):
                 inside = jnp.where(high == part, 1.0, 0.0).astype(BF16)
                 masked[part * share : (part + 1) * share, columns] = grads * inside
-        span = 4 * share
+        span = 8 * share
 
         def some(i, _):
             rows = rows_at(0, i, span)
@@ -1976,24 +2006,20 @@
     def scalar_near(step):
         return remote(near.at[place], near.at[place], sum_sems.at[6, step], sum_sems.at[7, step], near_ways[step - 1])
 
-    def scalar_line(step):
-        return remote(along.at[slow], along.at[slow], sum_sems.at[8, step], sum_sems.at[9, step], along_way(step))
+    def scalar_wide(step):
+        return remote(along.at[me], along.at[me], all_send.at[step], all_recv.at[step], {WIDE: around[step]})
 
     near[place] = given
     for step in range(1, group):
         scalar_near(step).start()
     for step in range(1, group):
         scalar_near(step).wait()
-    along[slow] = jnp.sum(near[...], axis=0)
-    for step in range(1, slows):
-        scalar_line(step).start()
-    for step in range(1, slows):
-        scalar_line(step).wait()
-    across[0] = jnp.sum(along[...], axis=0)
-    last = remote(across.at[0], across.at[1], sum_sems.at[10, 0], sum_sems.at[11, 0], beside)
-    last.start()
-    last.wait()
-    scalars[...] = across[0] + across[1]
+    along[me] = jnp.sum(near[...], axis=0)
+    for step in range(1, owners):
+        scalar_wide(step).start()
+    for step in range(1, owners):
+        scalar_wide(step).wait()
+    scalars[...] = jnp.sum(along[...], axis=0)
     gain_near().wait_send()
     for step in range(owners):
         far_copy(step).wait_send()
@@ -2034,10 +2060,9 @@
             pltpu.VMEM((slows,) + small, F32),
             pltpu.VMEM((slows,) + small, F32),
             pltpu.VMEM((group,) + small, F32),
-            pltpu.VMEM((slows,) + small, F32),
-            pltpu.VMEM((2,) + small, F32),
+            pltpu.VMEM((owners,) + small, F32),
         ]
-        + [dma((owners,))] * 6
+        + [dma((owners,))] * 8
         + [dma((12, max(slows, group)))],
         collective_id,
         loads,
@@ -2115,7 +2140,7 @@
     windows = [(k * quarter, quarter) for k in range(PIECES)]
     key_seg, query_seg = segments.reshape(-1, 1), segments.reshape(1, -1)
     weights = (attn_in, attn_out, ffn_in, ffn_out)
-    (residual, normed, gain_w, counts, ids_all, projected, mixed, middle, normed_two, result, normed_next), carried = front(
+    (residual, normed, gain_w, counts, ids_all, projected, mixed, middle, normed_two, log_sums, result, normed_next), carried = front(
         ids, counted, gains, steps, rates, tables, key_seg, query_seg, wide, attn_out.shape[2], 0,
         [GatherLoad(value, 0, lead, wide, place=KEPT) for value, lead in zip(weights, leads)]
         + [GatherLoad(value, 1, lead, wide) for value, lead in zip(weights[:3], leads)]
@@ -2124,15 +2149,16 @@
     token_total = counts[gain_rows, 0]
     first_w = [joined(value, lead) for value, lead in zip(carried[:4], leads)]
     query_w, output_w, expand_w = [joined(value, lead) for value, lead in zip(carried[4:7], leads)]
-    kept = [(residual, normed, projected, mixed, middle, normed_two, *first_w)]
-    (projected, mixed, middle, normed_two, grad, branch, gain_final, losses, *d_last), (reduce_w,) = last_and_loss(
+    kept = [(residual, normed, projected, mixed, middle, normed_two, log_sums, *first_w)]
+    (projected, mixed, middle, normed_two, log_sums, grad, branch, gain_final, losses, *d_last), (reduce_w,) = last_and_loss(
         1, normed_next, key_seg, query_seg, result, query_w, output_w, expand_w, gain_w,
         (noised, clean, timesteps, counted), counts, vocab, 1,
         [FastLoad(carried[7], 0, wide)]
         + [GatherLoad(tables, 1, 0, wide, window, place=LOCAL) for window in windows],
     )
     kept.append(
-        (result, normed_next, projected, mixed, middle, normed_two, query_w, output_w, expand_w, joined(reduce_w, 0))
+        (result, normed_next, projected, mixed, middle, normed_two, log_sums)
+        + (query_w, output_w, expand_w, joined(reduce_w, 0))
     )
     own, squares = {}, []
 
@@ -2162,10 +2188,11 @@
         lambda carry: carry.hand_on(*range(half_pieces, PIECES)),
         lambda carry, d_out, d_query: None,
     )
-    residual, normed, projected, mixed, middle, normed_two, query_w, output_w, expand_w, reduce_w = kept[1]
+    residual, normed, projected, mixed, middle, normed_two, log_sums, *four_w = kept[1]
+    query_w, output_w, expand_w, reduce_w = four_w
     (grad, branch, d_out, d_query, gain_two, gain_one), carried = backward_block(
         1, None, points, grad, branch, reduce_w, expand_w, output_w, normed_two, middle, gain_w, mixed,
-        projected, key_seg, query_seg, query_w, residual, normed, wide, 2,
+        projected, log_sums, key_seg, query_seg, query_w, residual, normed, wide, 2,
         [ReduceLoad(by_owner(piece, 0), 0) for piece in d_last]
         + [PairLoad(made, 0, True), PairLoad(made, 0, True)],
     )
@@ -2190,10 +2217,11 @@
         lambda carry: carry.hand_on(4),
         sent_first,
     )
-    residual, normed, projected, mixed, middle, normed_two, query_w, output_w, expand_w, reduce_w = kept[0]
+    residual, normed, projected, mixed, middle, normed_two, log_sums, *four_w = kept[0]
+    query_w, output_w, expand_w, reduce_w = four_w
     (grad, branch, _, d_query, gain_two, gain_one), carried = backward_block(
         0, math.sqrt(D), points, grad, branch, reduce_w, expand_w, output_w, normed_two, middle, gain_w, mixed,
-        projected, key_seg, query_seg, query_w, residual, normed, wide, 3,
+        projected, log_sums, key_seg, query_seg, query_w, residual, normed, wide, 3,
         [LineLoad(red_sums, wide), LineLoad(in_sums, wide), ReduceLoad(d_out, 0), ReduceLoad(d_query, 1)]
         + [ReduceLoad(made, 0, True), ReduceLoad(made, 0, True), PairLoad(made_out, 0, True), PairLoad(made_in, 1, True)],
     )

time: 470 us -> 462 us (0.983)
  Pallas kernels: 440 us -> 431 us
    pallas_call x5, Pallas kernels: 440 us -> 431 us  [run(): pl.pallas_call(kernel, out_shape=tuple(outs) + tuple((out for load in loa...]
where the time goes in v10:
time: 462 us; the launch traced here: 455 us
  Pallas kernels  431 us (93%)
  other arithmetic  12.5 us (3%)
  local copies, waits for them, and re-layouts  8.5 us (2%)
    pallas_call x5, Pallas kernels, run(): pl.pallas_call(kernel, out_shape=tuple(outs) + tuple((out for load in loa...  431 us
    convert_element_type x5, other arithmetic, adam(): return (weight_new, first_new, second_new, weight_new.astype(jnp.bfloat16))  10.5 us

profile of v10, /device:TPU:0, one launch (start us, length us, event | category | flops | bytes accessed | tf_op | source)
XLA Modules:
  0.0 455.3 jit_solution(7041660937142272540)
XLA Ops:
  0.7 0.6 multiply_exponential_fusion.refs_4_
  1.2 0.5 broadcast.79
  1.8 1.3 reduce.3
  3.1 0.6 reshape.110.refs_0_
  3.7 1.7 copy.50.refs_6_.refs_1_.refs_11_
  5.4 115.8 %front.1 = (f32[512,768]{1,0:T(8,128)}, bf16[1024,768]{1,0:T(8,128)(2,1)}, f32[8,768]{1,0:T(8,128)}, f32[8,128]{1,0:T(8,128)}, s32[8,4,256]{2,1,0:T(4,128)}, /*i...) custom-call(s32[4,256]{1,0:T(4,128)} %reshape.110.refs_0_, ...), custom_call_target="tpu_custom_call" | custom-call | tf_op jit(solution)/shard_map/front/pallas_call | solution.py:901
  121.2 1.2 slice.13
  122.4 113.6 %last_and_loss.1 = (bf16[3,1024,192]{2,1,0:T(8,128)(2,1)}, bf16[1024,192]{1,0:T(8,128)(2,1)}, f32[512,768]{1,0:T(8,128)}, bf16[1024,768]{1,0:T(8,128)(2,1)}, f32...) custom-call(bf16[1024,768]{1,0:T(8,128)(2,1)} %get-tuple-element.99., ...), custom_call_target="tpu_custom_call" | custom-call | tf_op jit(solution)/shard_map/last_and_loss/pallas_call | solution.py:901
  236.0 70.5 %backward_block.2 = (f32[512,768]{1,0:T(8,128)}, bf16[1024,768]{1,0:T(8,128)(2,1)}, bf16[8,96,192]{2,1,0:T(8,128)(2,1)}, bf16[3,8,96,192]{3,2,1,0:T(8,128)(2,1)}...) custom-call(f32[512,768]{1,0:T(8,128)} %get-tuple-element.107.refs_0, ...), custom_call_target="tpu_custom_call" | custom-call | tf_op jit(solution)/shard_map/backward_block/pallas_call | solution.py:901
  306.5 77.1 %backward_block.3 = (f32[512,768]{1,0:T(8,128)}, bf16[1024,768]{1,0:T(8,128)(2,1)}, bf16[8,96,192]{2,1,0:T(8,128)(2,1)}, bf16[3,8,96,192]{3,2,1,0:T(8,128)(2,1)}...) custom-call(f32[512,768]{1,0:T(8,128)} %get-tuple-element.119.refs_0, ...), custom_call_target="tpu_custom_call" | custom-call | tf_op jit(solution)/shard_map/backward_block/pallas_call | solution.py:901
  383.6 0.0 copy-start.25
  383.6 0.0 copy-start.26
  383.6 0.0 copy-start.27
  383.6 0.0 copy-start.6
  383.6 0.0 copy-start.24
  383.7 0.0 copy-start.20
  383.7 0.0 copy-start.21
  383.7 54.2 %tail.1 = (f32[96,2048]{1,0:T(8,128)}, f32[8,128]{1,0:T(8,128)}, f32[8,128]{1,0:T(8,128)}, f32[96,192]{1,0:T(8,128)}, f32[8,128]{1,0:T(8,128)}, /*index=5*/f32[3,96,192]{2,1,0:T(8,128)}, f32[8,128]{1,0:T(8,128)}) custom-call(bf16[1024,768]{1,0:T(8,128)(2,1)} %get-tuple-element.136.refs_0_, s32[8,4,256]{2,1,0:T(4,128)} %get-tuple-element.137.refs_1_, ...), custom_call_target="tpu_custom_call" | custom-call | tf_op jit(solution)/shard_map/tail/pallas_call | solution.py:901
  437.9 0.0 copy-start.1
  437.9 0.0 copy-start.8
  438.0 0.0 copy-start.9
  438.0 0.0 copy-start.18
  438.0 0.0 copy-start.19
  438.0 1.4 fusion.18
  440.2 1.3 fusion.6
  441.5 2.0 fusion.14
  443.4 0.0 copy-done.21
  443.5 0.1 maximum_bitcast_fusion
  443.6 0.0 copy-start.2
  443.6 0.0 copy-start.3
  443.6 0.0 copy-start.10
  443.6 0.0 copy-start.11
  443.6 0.0 copy-start.12
  443.6 0.0 copy-start.13
  443.7 1.6 fusion.16
  445.3 0.0 copy-done.2
  445.3 0.2 copy-done.10
  445.5 0.4 copy-done.11
  445.9 0.2 copy-done.12
  446.1 0.2 copy-done.13
  446.3 0.1 copy-done.14
  446.4 0.1 copy-done.15
  446.5 0.1 copy-done.16
  446.6 2.3 fusion.10
  448.9 1.0 copy-done.4
  449.9 0.5 copy-done.5
  450.4 0.2 copy-done.7
  450.6 3.3 fusion.8
  (26 shorter events, 0.1 us)
Async XLA Ops:
  383.6 56.5 %copy-start.25 = (f32[5,96]{1,0:T(8,128)S(1)}, f32[5,96]{1,0:T(8,128)}, u32[]{:S(2)}) copy-start(f32[5,96]{1,0:T(8,128)} %refs_2_.2) | copy-start | bytes 5764
  383.6 56.5 %copy-start.26 = (f32[5,96]{1,0:T(8,128)S(1)}, f32[5,96]{1,0:T(8,128)}, u32[]{:S(2)}) copy-start(f32[5,96]{1,0:T(8,128)} %param.39) | copy-start | bytes 5764
  383.6 56.5 %copy-start.27 = (f32[5,96]{1,0:T(8,128)S(1)}, f32[5,96]{1,0:T(8,128)}, u32[]{:S(2)}) copy-start(f32[5,96]{1,0:T(8,128)} %param.45) | copy-start | bytes 5764
  383.6 57.8 %copy-start.6 = (f32[2,96,192]{2,1,0:T(8,128)S(1)}, f32[2,96,192]{2,1,0:T(8,128)}, u32[]{:S(2)}) copy-start(f32[2,96,192]{2,1,0:T(8,128)} %refs_9_.2) | copy-start | bytes 442372
  383.6 57.8 %copy-start.24 = (f32[2,96,192]{2,1,0:T(8,128)S(1)}, f32[2,96,192]{2,1,0:T(8,128)}, u32[]{:S(2)}) copy-start(f32[2,96,192]{2,1,0:T(8,128)} %param.35) | copy-start | bytes 442372
  383.7 59.8 %copy-start.20 = (f32[96,512]{1,0:T(8,128)S(1)}, f32[96,512]{1,0:T(8,128)}, u32[]{:S(2)}) copy-start(f32[96,512]{1,0:T(8,128)} %get-tuple-element.166) | copy-start | bytes 589828
  383.7 59.8 %copy-start.21 = (f32[96,512]{1,0:T(8,128)S(1)}, f32[96,512]{1,0:T(8,128)}, u32[]{:S(2)}) copy-start(f32[96,512]{1,0:T(8,128)} %get-tuple-element.167) | copy-start | bytes 589828
  383.7 59.8 %copy-start.22 = (f32[96,512]{1,0:T(8,128)S(1)}, f32[96,512]{1,0:T(8,128)}, u32[]{:S(2)}) copy-start(f32[96,512]{1,0:T(8,128)} %get-tuple-element.168) | copy-start | bytes 589828
  383.7 59.7 %copy-start.23 = (f32[96,512]{1,0:T(8,128)S(1)}, f32[96,512]{1,0:T(8,128)}, u32[]{:S(2)}) copy-start(f32[96,512]{1,0:T(8,128)} %get-tuple-element.169) | copy-start | bytes 589828
  437.9 5.6 %copy-start.1 = (f32[2,3,96,192]{3,2,1,0:T(8,128)S(1)}, f32[2,3,96,192]{3,2,1,0:T(8,128)}, u32[]{:S(2)}) copy-start(f32[2,3,96,192]{3,2,1,0:T(8,128)} %refs_8_.2) | copy-start | bytes 1327108
  437.9 5.6 %copy-start.8 = (f32[2,3,96,192]{3,2,1,0:T(8,128)S(1)}, f32[2,3,96,192]{3,2,1,0:T(8,128)}, u32[]{:S(2)}) copy-start(f32[2,3,96,192]{3,2,1,0:T(8,128)} %param.34) | copy-start | bytes 1327108
  438.0 5.6 %copy-start.9 = (f32[2,3,96,192]{3,2,1,0:T(8,128)S(1)}, f32[2,3,96,192]{3,2,1,0:T(8,128)}, u32[]{:S(2)}) copy-start(f32[2,3,96,192]{3,2,1,0:T(8,128)} %param.40) | copy-start | bytes 1327108
  438.0 5.6 %copy-start.18 = (f32[3,96,192]{2,1,0:T(8,128)S(1)}, f32[3,96,192]{2,1,0:T(8,128)}, u32[]{:S(2)}) copy-start(f32[3,96,192]{2,1,0:T(8,128)} %get-tuple-element.158) | copy-start | bytes 663556
  438.0 5.6 %copy-start.19 = (f32[3,96,192]{2,1,0:T(8,128)S(1)}, f32[3,96,192]{2,1,0:T(8,128)}, u32[]{:S(2)}) copy-start(f32[3,96,192]{2,1,0:T(8,128)} %get-tuple-element.157) | copy-start | bytes 663556
  443.4 1.8 copy-start.17
  443.6 1.7 copy-start.2
  443.6 1.7 copy-start.3
  443.6 1.9 copy-start.10
  443.6 2.3 copy-start.11
  443.6 2.5 copy-start.12
  443.6 2.7 copy-start.13
  443.6 2.7 copy-start.14
  443.7 2.8 copy-start.15
  443.7 2.9 copy-start.16
  446.6 2.3 copy-start
  446.6 3.4 copy-start.4
  446.6 3.8 copy-start.5
  446.6 4.0 copy-start.7

commit v11 on v10

--- a/solution.py
+++ b/solution.py
@@ -1737,7 +1737,7 @@
     turned[...] = jnp.transpose(normed[...])
     for k, d_table in enumerate(d_tables):
         weight_grad(turned, grads.at[:, k * piece_width : (k + 1) * piece_width], d_table)
-    made()
+        made(k)
     gain_total = jnp.zeros((1, gain.shape[1]), F32)
     for j in range(CHUNKS):
         rows = rows_at(0, j, chunk)
@@ -1761,11 +1761,15 @@
 
 
 def back_kernel(
-    layer, normed, key_seg, query_seg, resid, w_query, w_out, w_in, gains, noised, clean, steps, counted, counts,
+    layer, pieces, normed, key_seg, query_seg, resid, w_query, w_out, w_in, gains, noised, clean, steps, counted, counts,
     projected, mixed, middle, normed_two, log_sums, grad_out, branch, d_gain, losses, *refs, carry,
 ):
-    pieces = len(carry.loads) - 1
-    d_tables, refs = refs[:pieces], refs[pieces:]
+    outs = 2 * pieces - (len(carry.loads) - 1)
+    d_tables, refs = refs[:outs], refs[outs:]
+    d_tables, refs = refs[: pieces - outs] + d_tables, refs[pieces - outs :]
+    starting = range(pieces + 1, len(carry.loads))
+    for k in starting:
+        carry.loads[k].full = d_tables[k - pieces - 1]
     (result, normed_next, info), refs = refs[:3], refs[3:]
     loss_scratch, layer_refs = refs[:-LAYER_SCRATCH], refs[-LAYER_SCRATCH:]
     me = lax.axis_index(NARROW)
@@ -1796,6 +1800,12 @@
     def at_last():
         carry.hand_on(3)
 
+    def made(piece):
+        if piece == pieces - outs - 1:
+            carry.begin(*starting)
+        if piece == pieces - 1:
+            carry.leave(*range(9, 9 + outs))
+
     forward_part(
         layer,
         [lambda which: w_query[which], lambda: w_out[...], lambda: w_in[...], carry.loads[0].value],
@@ -1806,21 +1816,24 @@
     carry.hand_on(4)
     carry.end(1, 2, 3)
     loss_part(
-        2 * layer + 2, normed_next, info, result, gains, carry.loads[1:], grad_out, branch, d_gain, losses, d_tables,
-        *loss_scratch, *layer_refs[2:6], *layer_refs[-2:], made=lambda: carry.leave(*range(9, 9 + pieces)),
-    )
+        2 * layer + 2, normed_next, info, result, gains, carry.loads[1 : pieces + 1], grad_out, branch, d_gain, losses, d_tables,
+        *loss_scratch, *layer_refs[2:6], *layer_refs[-2:], made=made,
+    )
+    carry.end(*starting)
     carry.gone()
 
 
 def last_and_loss(
-    layer, normed, key_seg, query_seg, resid, w_query, w_out, w_in, gains, tokens, counts, vocab, collective_id, loads
+    layer, normed, key_seg, query_seg, resid, w_query, w_out, w_in, gains, tokens, counts, vocab, pieces, collective_id, loads
 ):
     seq_len, width = normed.shape
     heads_width = w_query.shape[2]
     half, blocks = seq_len // 2, seq_len // LANES
-    pieces = len(loads) - 1
+    outs = 2 * pieces - (len(loads) - 1)
+    owners = loads[1].count
+    table = (owners, width // owners, vocab // pieces)
     return run(
-        functools.partial(back_kernel, layer),
+        functools.partial(back_kernel, layer, pieces),
         "last_and_loss",
         [normed, key_seg, query_seg, resid, w_query, w_out, w_in, gains, *tokens, counts],
         layer_outs(seq_len, width, heads_width)
@@ -1830,8 +1843,9 @@
             jax.ShapeDtypeStruct((1, width), F32),
             jax.ShapeDtypeStruct((1, seq_len), F32),
         ]
-        + [jax.ShapeDtypeStruct((width, vocab // pieces), BF16)] * pieces,
-        [
+        + [jax.ShapeDtypeStruct(table, BF16)] * outs,
+        [pltpu.VMEM(table, BF16)] * (pieces - outs)
+        + [
             pltpu.VMEM((half, width), F32),
             pltpu.VMEM((seq_len, width), BF16),
             pltpu.VMEM((8, seq_len), F32),
@@ -1849,7 +1863,7 @@
         collective_id,
         loads,
         lazy=(3, 6),
-        early=(0, 1, 2, 3) + tuple(range(9, 9 + pieces)),
+        early=(0, 1, 2, 3) + tuple(range(9, 9 + outs)),
     )
 
 
@@ -2150,12 +2164,16 @@
     first_w = [joined(value, lead) for value, lead in zip(carried[:4], leads)]
     query_w, output_w, expand_w = [joined(value, lead) for value, lead in zip(carried[4:7], leads)]
     kept = [(residual, normed, projected, mixed, middle, normed_two, log_sums, *first_w)]
-    (projected, mixed, middle, normed_two, log_sums, grad, branch, gain_final, losses, *d_last), (reduce_w,) = last_and_loss(
+    half_pieces = PIECES // 2
+    piece_made = jax.ShapeDtypeStruct((wide, share, quarter), BF16)
+    (projected, mixed, middle, normed_two, log_sums, grad, branch, gain_final, losses, *d_last), carried = last_and_loss(
         1, normed_next, key_seg, query_seg, result, query_w, output_w, expand_w, gain_w,
-        (noised, clean, timesteps, counted), counts, vocab, 1,
+        (noised, clean, timesteps, counted), counts, vocab, PIECES, 1,
         [FastLoad(carried[7], 0, wide)]
-        + [GatherLoad(tables, 1, 0, wide, window, place=LOCAL) for window in windows],
-    )
+        + [GatherLoad(tables, 1, 0, wide, window, place=LOCAL) for window in windows]
+        + [PairLoad(piece_made, 0, True) for _ in range(half_pieces)],
+    )
+    reduce_w, *table_sums = carried
     kept.append(
         (result, normed_next, projected, mixed, middle, normed_two, log_sums)
         + (query_w, output_w, expand_w, joined(reduce_w, 0))
@@ -2180,12 +2198,11 @@
         carry.loads[PIECES].full, carry.loads[PIECES + 1].full = d_red, d_in
         carry.begin(*range(PIECES))
 
-    half_pieces = PIECES // 2
     points = (
         start_last,
         lambda carry: carry.begin(PIECES, PIECES + 1),
-        lambda carry: carry.hand_on(*range(half_pieces)),
         lambda carry: carry.hand_on(*range(half_pieces, PIECES)),
+        lambda carry: carry.hand_on(PIECES),
         lambda carry, d_out, d_query: None,
     )
     residual, normed, projected, mixed, middle, normed_two, log_sums, *four_w = kept[1]
@@ -2193,39 +2210,40 @@
     (grad, branch, d_out, d_query, gain_two, gain_one), carried = backward_block(
         1, None, points, grad, branch, reduce_w, expand_w, output_w, normed_two, middle, gain_w, mixed,
         projected, log_sums, key_seg, query_seg, query_w, residual, normed, wide, 2,
-        [ReduceLoad(by_owner(piece, 0), 0) for piece in d_last]
-        + [PairLoad(made, 0, True), PairLoad(made, 0, True)],
-    )
-    for k in range(PIECES):
-        carried = landed((TABLE, k), carried)
-    red_sums, in_sums = carried
+        [LineLoad(sums, wide) for sums in table_sums]
+        + [ReduceLoad(piece, 0) for piece in d_last]
+        + [ReduceLoad(made, 0, True), PairLoad(made, 0, True)],
+    )
+    for key in [(TABLE, k) for k in range(PIECES)] + [(FFN_OUT, 1)]:
+        carried = landed(key, carried)
+    (in_sums,) = carried
     gain_grads = [None, None, gain_one, gain_two, gain_final]
 
     def start_first(carry, d_red, d_in):
-        carry.loads[4].full, carry.loads[5].full = d_red, d_in
-        carry.begin(0, 1, 2, 3)
+        carry.loads[3].full, carry.loads[4].full = d_red, d_in
+        carry.begin(0, 1, 2)
 
     def sent_first(carry, d_out, d_query):
-        carry.hand_on(5)
-        carry.loads[6].full, carry.loads[7].full = d_out, d_query
-        carry.begin(6, 7)
+        carry.hand_on(4)
+        carry.loads[5].full, carry.loads[6].full = d_out, d_query
+        carry.begin(5, 6)
 
     points = (
         start_first,
-        lambda carry: carry.begin(4, 5),
-        lambda carry: carry.hand_on(2, 3),
-        lambda carry: carry.hand_on(4),
+        lambda carry: carry.begin(3, 4),
+        lambda carry: carry.hand_on(1, 2),
+        lambda carry: carry.hand_on(3),
         sent_first,
     )
     residual, normed, projected, mixed, middle, normed_two, log_sums, *four_w = kept[0]
     query_w, output_w, expand_w, reduce_w = four_w
-    (grad, branch, _, d_query, gain_two, gain_one), carried = backward_block(
+    (grad, branch, _, _, gain_two, gain_one), carried = backward_block(
         0, math.sqrt(D), points, grad, branch, reduce_w, expand_w, output_w, normed_two, middle, gain_w, mixed,
         projected, log_sums, key_seg, query_seg, query_w, residual, normed, wide, 3,
-        [LineLoad(red_sums, wide), LineLoad(in_sums, wide), ReduceLoad(d_out, 0), ReduceLoad(d_query, 1)]
+        [LineLoad(in_sums, wide), ReduceLoad(d_out, 0), ReduceLoad(d_query, 1)]
         + [ReduceLoad(made, 0, True), ReduceLoad(made, 0, True), PairLoad(made_out, 0, True), PairLoad(made_in, 1, True)],
     )
-    for key in ((FFN_OUT, 1), (FFN_IN, 1), (ATTN_OUT, 1), (ATTN_IN, 1), (FFN_OUT, 0), (FFN_IN, 0)):
+    for key in ((FFN_IN, 1), (ATTN_OUT, 1), (ATTN_IN, 1), (FFN_OUT, 0), (FFN_IN, 0)):
         carried = landed(key, carried)
     out_sums, in_sums = carried
     gain_grads[:2] = gain_one, gain_two

time: 462 us -> 469 us (1.015)
  Pallas kernels: 431 us -> 438 us
    pallas_call x5, Pallas kernels: 431 us -> 438 us  [run(): pl.pallas_call(kernel, out_shape=tuple(outs) + tuple((out for load in loa...]
where the time goes in v11:
time: 469 us; the launch traced here: 462 us
  Pallas kernels  438 us (93%)
  other arithmetic  12.5 us (3%)
  local copies, waits for them, and re-layouts  8.51 us (2%)
    pallas_call x5, Pallas kernels, run(): pl.pallas_call(kernel, out_shape=tuple(outs) + tuple((out for load in loa...  438 us
    convert_element_type x5, other arithmetic, adam(): return (weight_new, first_new, second_new, weight_new.astype(jnp.bfloat16))  10.5 us

profile of v11, /device:TPU:0, one launch (start us, length us, event | category | flops | bytes accessed | tf_op | source)
XLA Modules:
  0.0 462.4 jit_solution(12207169418373840230)
XLA Ops:
  0.7 0.6 multiply_exponential_fusion.refs_4_
  1.2 0.5 broadcast.79
  1.8 1.3 reduce.3
  3.1 0.6 reshape.98.refs_0_
  3.7 1.7 copy.50.refs_6_.refs_1_.refs_11_
  5.4 115.8 %front.1 = (f32[512,768]{1,0:T(8,128)}, bf16[1024,768]{1,0:T(8,128)(2,1)}, f32[8,768]{1,0:T(8,128)}, f32[8,128]{1,0:T(8,128)}, s32[8,4,256]{2,1,0:T(4,128)}, /*i...) custom-call(s32[4,256]{1,0:T(4,128)} %reshape.98.refs_0_, ...), custom_call_target="tpu_custom_call" | custom-call | tf_op jit(solution)/shard_map/front/pallas_call | solution.py:901
  121.2 1.2 slice.13
  122.4 122.6 %last_and_loss.1 = (bf16[3,1024,192]{2,1,0:T(8,128)(2,1)}, bf16[1024,192]{1,0:T(8,128)(2,1)}, f32[512,768]{1,0:T(8,128)}, bf16[1024,768]{1,0:T(8,128)(2,1)}, f32...) custom-call(bf16[1024,768]{1,0:T(8,128)(2,1)} %get-tuple-element.98., ...), custom_call_target="tpu_custom_call" | custom-call | tf_op jit(solution)/shard_map/last_and_loss/pallas_call | solution.py:901
  245.1 69.3 %backward_block.2 = (f32[512,768]{1,0:T(8,128)}, bf16[1024,768]{1,0:T(8,128)(2,1)}, bf16[8,96,192]{2,1,0:T(8,128)(2,1)}, bf16[3,8,96,192]{3,2,1,0:T(8,128)(2,1)}...) custom-call(f32[512,768]{1,0:T(8,128)} %get-tuple-element.106.refs_0, ...), custom_call_target="tpu_custom_call" | custom-call | tf_op jit(solution)/shard_map/backward_block/pallas_call | solution.py:901
  314.4 75.2 %backward_block.3 = (f32[512,768]{1,0:T(8,128)}, bf16[1024,768]{1,0:T(8,128)(2,1)}, bf16[8,96,192]{2,1,0:T(8,128)(2,1)}, bf16[3,8,96,192]{3,2,1,0:T(8,128)(2,1)}...) custom-call(f32[512,768]{1,0:T(8,128)} %get-tuple-element.118.refs_0, ...), custom_call_target="tpu_custom_call" | custom-call | tf_op jit(solution)/shard_map/backward_block/pallas_call | solution.py:901
  389.5 0.0 copy-start.25
  389.5 0.0 copy-start.26
  389.6 0.0 copy-start.27
  389.6 0.0 copy-start.6
  389.6 0.0 copy-start.24
  389.6 0.0 copy-start.20
  389.6 0.0 copy-start.21
  389.6 0.0 copy-start.22
  389.6 0.0 copy-start.23
  389.6 55.5 %tail.1 = (f32[96,2048]{1,0:T(8,128)}, f32[8,128]{1,0:T(8,128)}, f32[8,128]{1,0:T(8,128)}, f32[96,192]{1,0:T(8,128)}, f32[8,128]{1,0:T(8,128)}, /*index=5*/f32[3,96,192]{2,1,0:T(8,128)}, f32[8,128]{1,0:T(8,128)}) custom-call(bf16[1024,768]{1,0:T(8,128)(2,1)} %get-tuple-element.134.refs_0_, s32[8,4,256]{2,1,0:T(4,128)} %get-tuple-element.135.refs_1_, ...), custom_call_target="tpu_custom_call" | custom-call | tf_op jit(solution)/shard_map/tail/pallas_call | solution.py:901
  445.1 0.0 copy-start.1
  445.1 0.0 copy-start.8
  445.1 0.0 copy-start.9
  445.2 1.4 fusion.18
  447.3 0.0 copy-done.25
  447.3 0.0 copy-done.26
  447.4 1.3 fusion.6
  448.7 2.0 fusion.14
  450.6 0.1 maximum_bitcast_fusion
  450.8 0.0 copy-start.2
  450.8 0.0 copy-start.3
  450.8 0.0 copy-start.10
  450.8 0.0 copy-start.11
  450.8 0.0 copy-start.12
  450.8 0.0 copy-start.13
  450.9 1.6 fusion.16
  452.5 0.2 copy-done.10
  452.7 0.4 copy-done.11
  453.1 0.2 copy-done.12
  453.3 0.2 copy-done.13
  453.5 0.1 copy-done.14
  453.6 0.1 copy-done.15
  453.7 0.1 copy-done.16
  453.8 2.3 fusion.10
  456.1 1.0 copy-done.4
  457.1 0.5 copy-done.5
  457.6 0.2 copy-done.7
  457.8 3.3 fusion.8
  (26 shorter events, 0.1 us)
Async XLA Ops:
  389.5 57.8 %copy-start.25 = (f32[5,96]{1,0:T(8,128)S(1)}, f32[5,96]{1,0:T(8,128)}, u32[]{:S(2)}) copy-start(f32[5,96]{1,0:T(8,128)} %refs_2_.2) | copy-start | bytes 5764
  389.5 57.8 %copy-start.26 = (f32[5,96]{1,0:T(8,128)S(1)}, f32[5,96]{1,0:T(8,128)}, u32[]{:S(2)}) copy-start(f32[5,96]{1,0:T(8,128)} %param.39) | copy-start | bytes 5764
  389.6 57.8 %copy-start.27 = (f32[5,96]{1,0:T(8,128)S(1)}, f32[5,96]{1,0:T(8,128)}, u32[]{:S(2)}) copy-start(f32[5,96]{1,0:T(8,128)} %param.45) | copy-start | bytes 5764
  389.6 59.1 %copy-start.6 = (f32[2,96,192]{2,1,0:T(8,128)S(1)}, f32[2,96,192]{2,1,0:T(8,128)}, u32[]{:S(2)}) copy-start(f32[2,96,192]{2,1,0:T(8,128)} %refs_9_.2) | copy-start | bytes 442372
  389.6 59.1 %copy-start.24 = (f32[2,96,192]{2,1,0:T(8,128)S(1)}, f32[2,96,192]{2,1,0:T(8,128)}, u32[]{:S(2)}) copy-start(f32[2,96,192]{2,1,0:T(8,128)} %param.35) | copy-start | bytes 442372
  389.6 61.0 %copy-start.20 = (f32[96,512]{1,0:T(8,128)S(1)}, f32[96,512]{1,0:T(8,128)}, u32[]{:S(2)}) copy-start(f32[96,512]{1,0:T(8,128)} %get-tuple-element.164) | copy-start | bytes 589828
  389.6 61.0 %copy-start.21 = (f32[96,512]{1,0:T(8,128)S(1)}, f32[96,512]{1,0:T(8,128)}, u32[]{:S(2)}) copy-start(f32[96,512]{1,0:T(8,128)} %get-tuple-element.165) | copy-start | bytes 589828
  389.6 61.0 %copy-start.22 = (f32[96,512]{1,0:T(8,128)S(1)}, f32[96,512]{1,0:T(8,128)}, u32[]{:S(2)}) copy-start(f32[96,512]{1,0:T(8,128)} %get-tuple-element.166) | copy-start | bytes 589828
  389.6 61.0 %copy-start.23 = (f32[96,512]{1,0:T(8,128)S(1)}, f32[96,512]{1,0:T(8,128)}, u32[]{:S(2)}) copy-start(f32[96,512]{1,0:T(8,128)} %get-tuple-element.167) | copy-start | bytes 589828
  445.1 5.6 %copy-start.1 = (f32[2,3,96,192]{3,2,1,0:T(8,128)S(1)}, f32[2,3,96,192]{3,2,1,0:T(8,128)}, u32[]{:S(2)}) copy-start(f32[2,3,96,192]{3,2,1,0:T(8,128)} %refs_8_.2) | copy-start | bytes 1327108
  445.1 5.6 %copy-start.8 = (f32[2,3,96,192]{3,2,1,0:T(8,128)S(1)}, f32[2,3,96,192]{3,2,1,0:T(8,128)}, u32[]{:S(2)}) copy-start(f32[2,3,96,192]{3,2,1,0:T(8,128)} %param.34) | copy-start | bytes 1327108
  445.1 5.6 %copy-start.9 = (f32[2,3,96,192]{3,2,1,0:T(8,128)S(1)}, f32[2,3,96,192]{3,2,1,0:T(8,128)}, u32[]{:S(2)}) copy-start(f32[2,3,96,192]{3,2,1,0:T(8,128)} %param.40) | copy-start | bytes 1327108
  445.1 5.6 %copy-start.18 = (f32[3,96,192]{2,1,0:T(8,128)S(1)}, f32[3,96,192]{2,1,0:T(8,128)}, u32[]{:S(2)}) copy-start(f32[3,96,192]{2,1,0:T(8,128)} %get-tuple-element.156) | copy-start | bytes 663556
  445.2 5.6 %copy-start.19 = (f32[3,96,192]{2,1,0:T(8,128)S(1)}, f32[3,96,192]{2,1,0:T(8,128)}, u32[]{:S(2)}) copy-start(f32[3,96,192]{2,1,0:T(8,128)} %get-tuple-element.155) | copy-start | bytes 663556
  450.6 1.8 copy-start.17
  450.8 1.7 copy-start.2
  450.8 1.7 copy-start.3
  450.8 1.9 copy-start.10
  450.8 2.3 copy-start.11
  450.8 2.5 copy-start.12
  450.8 2.7 copy-start.13
  450.8 2.7 copy-start.14
  450.8 2.8 copy-start.15
  450.9 2.9 copy-start.16
  453.7 2.3 copy-start
  453.7 3.4 copy-start.4
  453.8 3.8 copy-start.5
  453.8 4.0 copy-start.7

commit v12 on v10

--- a/solution.py
+++ b/solution.py
@@ -415,8 +415,8 @@
 HBM, KEPT, LOCAL = 1, 2, 3
 F32 = jnp.float32
 BF16 = jnp.bfloat16
-CHUNKS = 4
-SPAN = 2
+CHUNKS = 8
+SPAN = 4
 VMEM_LIMIT = 61 * 1024 * 1024
 FORWARD_KIND = BF16
 BACKWARD_KIND = BF16
@@ -486,7 +486,7 @@
         )
 
     def give(self, j, value):
-        self.near_out[j] = value
+        self.near_out[j] = value.astype(self.near_out.dtype)
         self.near(j).start()
 
     def give_span(self, k, value):
@@ -501,7 +501,7 @@
 
     def pass_on(self, j, value):
         self.near(j).wait_recv()
-        self.far_out[j] = (value + self.near_in[j]).astype(self.far_out.dtype)
+        self.far_out[j] = (value + self.near_in[j].astype(F32)).astype(self.far_out.dtype)
         self.far(j).start()
 
     def take(self, j):
@@ -516,8 +516,8 @@
     @staticmethod
     def scratch(chunk, width, kind):
         return [
-            pltpu.VMEM((CHUNKS, chunk, width), F32),
-            pltpu.VMEM((CHUNKS, chunk, width), F32),
+            pltpu.VMEM((CHUNKS, chunk, width), BF16),
+            pltpu.VMEM((CHUNKS, chunk, width), BF16),
             pltpu.VMEM((CHUNKS, chunk, width), kind),
             pltpu.VMEM((CHUNKS, chunk, width), kind),
         ]
@@ -1355,14 +1355,14 @@
     grad_out, branch_out, d_out, d_query, gain_two, gain_one,
     d_red, d_in, grad_middle, grad_attn, grad_mixed, grad_projected, grad_before, after, turned,
     bias, keys_t, grad_keys, grad_values,
-    near_out, near_in, far_out, far_in, far_out2, far_in2, send, recv, loaded, carry,
+    near_out, near_in, far_out, far_in, far_out2, far_in2, send, recv, loaded, carry, peers=None,
 ):
     at_start, at_made, at_summed, at_attended, at_sent = points
     seq_len, width = normed_two.shape
     chunk = seq_len // 2 // CHUNKS
     sibling, partner, mine, other = group_places(seq_len)
     carry.fetch()
-    greet([sibling, partner] + carry.peers())
+    greet([sibling, partner] + carry.peers() if peers is None else peers)
     at_start(carry, d_red, d_in)
     pair = (send, recv)
     trade = Exchange((near_out, near_in, far_out, far_in), pair, 0, sibling, partner)
@@ -1471,31 +1471,15 @@
         share.arrived(j)
     trade.close()
     share.close()
-    carry.end(*carry.all())
-
-
-def backward_block(
-    layer, scale, points, grad, branch, w_red, w_in, w_out, normed_two, middle, gains, mixed,
-    projected, log_sums, key_seg, query_seg, w_query, resid, normed, owners, collective_id, loads,
-):
-    seq_len, width = normed_two.shape
-    hidden, heads_width = w_in.shape[1], w_query.shape[2]
+    if peers is None:
+        carry.end(*carry.all())
+
+
+def backward_scratch(seq_len, width, hidden, heads_width, owners):
     half, chunk = seq_len // 2, seq_len // 2 // CHUNKS
     block = min(QUERY_BLOCK, seq_len)
     far = pltpu.VMEM((CHUNKS, chunk, width), BACKWARD_KIND)
-    return run(
-        functools.partial(backward_kernel, layer, scale, points),
-        "backward_block",
-        [grad, branch, w_red, w_in, w_out, normed_two, middle, gains, mixed]
-        + [projected, log_sums, key_seg, query_seg, w_query, resid, normed],
-        [
-            jax.ShapeDtypeStruct((half, width), F32),
-            jax.ShapeDtypeStruct((seq_len, width), BF16),
-            jax.ShapeDtypeStruct((owners, width // owners, heads_width), BF16),
-            jax.ShapeDtypeStruct((3, owners, width // owners, heads_width), BF16),
-            jax.ShapeDtypeStruct((1, width), F32),
-            jax.ShapeDtypeStruct((1, width), F32),
-        ],
+    return (
         [pltpu.VMEM((owners, width // owners, hidden), BF16)] * 2
         + [
             pltpu.VMEM((half, width), F32),
@@ -1513,11 +1497,37 @@
         + Exchange.scratch(chunk, width, BACKWARD_KIND)
         + [far, far]
         + sems(6)
-        + [pltpu.SemaphoreType.DMA],
+        + [pltpu.SemaphoreType.DMA]
+    )
+
+
+def backward_outs(seq_len, width, heads_width, owners):
+    return [
+        jax.ShapeDtypeStruct((seq_len // 2, width), F32),
+        jax.ShapeDtypeStruct((seq_len, width), BF16),
+        jax.ShapeDtypeStruct((owners, width // owners, heads_width), BF16),
+        jax.ShapeDtypeStruct((3, owners, width // owners, heads_width), BF16),
+        jax.ShapeDtypeStruct((1, width), F32),
+        jax.ShapeDtypeStruct((1, width), F32),
+    ]
+
+
+AWAY, LAZY = (15,), (0, 4, 6, 8, 9, 11, 13, 14)
+
+
+def backward_block(layer, points, operands, owners, collective_id, loads):
+    seq_len, width = operands[5].shape
+    hidden, heads_width = operands[3].shape[1], operands[13].shape[2]
+    return run(
+        functools.partial(backward_kernel, layer, None, points),
+        "backward_block",
+        operands,
+        backward_outs(seq_len, width, heads_width, owners),
+        backward_scratch(seq_len, width, hidden, heads_width, owners),
         collective_id,
         loads,
-        away=(15,),
-        lazy=(0, 4, 6, 8, 9, 11, 13, 14),
+        away=AWAY,
+        lazy=LAZY,
     )
 
 
@@ -1853,17 +1863,28 @@
     )
 
 
-def sum_ways(place, me, slow, fast, slows, group):
-    near = [{NARROW: lax.rem(place + step, group)} for step in range(1, group)]
-    return near, {WIDE: me + 1 - 2 * fast}
-
-
-def tail_kernel(
-    layers, branch, ids_all, losses, *refs, carry,
-):
-    gain_parts, refs = refs[: 2 * layers + 1], refs[2 * layers + 1 :]
-    squares, refs = refs[: len(refs) - 25], refs[len(refs) - 25 :]
-    tail_body(branch, ids_all, losses, gain_parts, squares, *refs, carry)
+TAIL_SCRATCH = 22
+
+
+def end_kernel(points, scale, gain_count, *refs, carry):
+    operands, refs = refs[:16], refs[16:]
+    (ids_all, losses), refs = refs[:2], refs[2:]
+    gain_parts, refs = refs[:gain_count], refs[gain_count:]
+    count = len(refs) - 3 - 6 - BACK_SCRATCH - TAIL_SCRATCH
+    squares, refs = refs[:count], refs[count:]
+    (d_table, d_small, scalars), refs = refs[:3], refs[3:]
+    made, refs = refs[:6], refs[6:]
+    back_refs, tail_refs = refs[:BACK_SCRATCH], refs[BACK_SCRATCH:]
+    me, owners, place = lax.axis_index(WIDE), ids_all.shape[0], lax.axis_index(NARROW)
+    peers = [{WIDE: lax.rem(me + step, owners)} for step in range(1, owners)]
+    peers += [{NARROW: lax.rem(place + step, 4)} for step in range(1, 4)]
+    backward_kernel(0, scale, points, *operands, *made, *back_refs, carry, peers=peers)
+    tail_body(
+        made[1], ids_all, losses, (made[5], made[4], *gain_parts), squares, d_table, d_small, scalars, *tail_refs, carry
+    )
+
+
+BACK_SCRATCH = 22
 
 
 def tail_body(
@@ -1920,7 +1941,6 @@
         return remote(line_out.at[step], line_in.at[step], sum_sems.at[4, step], sum_sems.at[5, step], along_way(step))
 
     near_ways = [{NARROW: lax.rem(place + step, group)} for step in range(1, group)]
-    greet([{WIDE: device} for device in around[1:]] + near_ways)
     gains_out[...] = jnp.zeros(gains_out.shape, F32)
     for row, part in enumerate(gain_parts):
         gains_out[row : row + 1, :] = part[...]
@@ -1929,7 +1949,7 @@
     for step in range(1, owners):
         wide_copy(step).start()
     all_in[me, held] = out_blocks[me]
-    carry.begin(*carry.all())
+    carry.hand_on(6, 7)
     gain_near().wait_recv()
     both = gains_out[...] + gains_in[...]
     for owner in range(owners):
@@ -2032,40 +2052,48 @@
             gain_line(step).wait_send()
 
 
-def tail(branch, ids_all, losses, gain_parts, squares, share, vocab, group, collective_id, loads):
-    seq_len, width = branch.shape
+def first_and_tail(
+    points, scale, operands, ids_all, losses, gain_parts, squares, share, vocab, group, collective_id, loads
+):
+    seq_len, width = operands[5].shape
+    hidden, heads_width = operands[3].shape[1], operands[13].shape[2]
     owners = ids_all.shape[0]
     slows = owners // 2
     dma = pltpu.SemaphoreType.DMA
     small = (8, LANES)
+    made = [pltpu.VMEM(out.shape, out.dtype) for out in backward_outs(seq_len, width, heads_width, owners)]
+    tail_scratch = [
+        pltpu.VMEM((owners, share, seq_len // 4), BF16),
+        pltpu.VMEM((owners, 4, share, seq_len // 4), BF16),
+        pltpu.VMEM((vocab // LANES * share, seq_len), BF16),
+        pltpu.VMEM((LANES, seq_len), BF16),
+        pltpu.VMEM((vocab // LANES * share, LANES), F32),
+        pltpu.VMEM((8, width), F32),
+        pltpu.VMEM((8, width), F32),
+        pltpu.VMEM((owners,) + small, F32),
+        pltpu.VMEM((slows,) + small, F32),
+        pltpu.VMEM((slows,) + small, F32),
+        pltpu.VMEM((slows,) + small, F32),
+        pltpu.VMEM((group,) + small, F32),
+        pltpu.VMEM((owners,) + small, F32),
+    ]
+    tail_scratch += [dma((owners,))] * 8 + [dma((12, max(slows, group)))]
+    back = backward_scratch(seq_len, width, hidden, heads_width, owners)
+    assert len(back) == BACK_SCRATCH and len(tail_scratch) == TAIL_SCRATCH
     return run(
-        functools.partial(tail_kernel, (len(gain_parts) - 1) // 2),
-        "tail",
-        [branch, ids_all, losses, *gain_parts, *squares],
+        functools.partial(end_kernel, points, scale, len(gain_parts)),
+        "first_and_tail",
+        [*operands, ids_all, losses, *gain_parts, *squares],
         [
             jax.ShapeDtypeStruct((share, vocab), F32),
             jax.ShapeDtypeStruct(small, F32),
             jax.ShapeDtypeStruct(small, F32),
         ],
-        [
-            pltpu.VMEM((owners, share, seq_len // 4), BF16),
-            pltpu.VMEM((owners, 4, share, seq_len // 4), BF16),
-            pltpu.VMEM((vocab // LANES * share, seq_len), BF16),
-            pltpu.VMEM((LANES, seq_len), BF16),
-            pltpu.VMEM((vocab // LANES * share, LANES), F32),
-            pltpu.VMEM((8, width), F32),
-            pltpu.VMEM((8, width), F32),
-            pltpu.VMEM((owners,) + small, F32),
-            pltpu.VMEM((slows,) + small, F32),
-            pltpu.VMEM((slows,) + small, F32),
-            pltpu.VMEM((slows,) + small, F32),
-            pltpu.VMEM((group,) + small, F32),
-            pltpu.VMEM((owners,) + small, F32),
-        ]
-        + [dma((owners,))] * 8
-        + [dma((12, max(slows, group)))],
+        made + back + tail_scratch,
         collective_id,
         loads,
+        away=AWAY,
+        lazy=LAZY,
     )
 
 
@@ -2080,7 +2108,8 @@
         and narrow == 4
         and wide % 2 == 0
         and rows == 1
-        and seq_len % (2 * CHUNKS * 128) == 0
+        and seq_len % (2 * CHUNKS * 16) == 0
+        and SPAN * seq_len == 2 * CHUNKS * QUERY_BLOCK
         and tables.shape[1] * wide % 256 == 0
         and attn_out.shape[1] % 16 == 0
         and attn_out.shape[1] <= LANES
@@ -2191,15 +2220,16 @@
     residual, normed, projected, mixed, middle, normed_two, log_sums, *four_w = kept[1]
     query_w, output_w, expand_w, reduce_w = four_w
     (grad, branch, d_out, d_query, gain_two, gain_one), carried = backward_block(
-        1, None, points, grad, branch, reduce_w, expand_w, output_w, normed_two, middle, gain_w, mixed,
-        projected, log_sums, key_seg, query_seg, query_w, residual, normed, wide, 2,
+        1, points,
+        [grad, branch, reduce_w, expand_w, output_w, normed_two, middle, gain_w, mixed]
+        + [projected, log_sums, key_seg, query_seg, query_w, residual, normed],
+        wide, 2,
         [ReduceLoad(by_owner(piece, 0), 0) for piece in d_last]
         + [PairLoad(made, 0, True), PairLoad(made, 0, True)],
     )
     for k in range(PIECES):
         carried = landed((TABLE, k), carried)
     red_sums, in_sums = carried
-    gain_grads = [None, None, gain_one, gain_two, gain_final]
 
     def start_first(carry, d_red, d_in):
         carry.loads[4].full, carry.loads[5].full = d_red, d_in
@@ -2219,22 +2249,17 @@
     )
     residual, normed, projected, mixed, middle, normed_two, log_sums, *four_w = kept[0]
     query_w, output_w, expand_w, reduce_w = four_w
-    (grad, branch, _, d_query, gain_two, gain_one), carried = backward_block(
-        0, math.sqrt(D), points, grad, branch, reduce_w, expand_w, output_w, normed_two, middle, gain_w, mixed,
-        projected, log_sums, key_seg, query_seg, query_w, residual, normed, wide, 3,
+    (own_first, total_small, scalars), carried = first_and_tail(
+        points, math.sqrt(D),
+        [grad, branch, reduce_w, expand_w, output_w, normed_two, middle, gain_w, mixed]
+        + [projected, log_sums, key_seg, query_seg, query_w, residual, normed],
+        ids_all, losses, (gain_one, gain_two, gain_final), squares, share, vocab, 4, 3,
         [LineLoad(red_sums, wide), LineLoad(in_sums, wide), ReduceLoad(d_out, 0), ReduceLoad(d_query, 1)]
-        + [ReduceLoad(made, 0, True), ReduceLoad(made, 0, True), PairLoad(made_out, 0, True), PairLoad(made_in, 1, True)],
-    )
-    for key in ((FFN_OUT, 1), (FFN_IN, 1), (ATTN_OUT, 1), (ATTN_IN, 1), (FFN_OUT, 0), (FFN_IN, 0)):
+        + [ReduceLoad(made, 0, True), ReduceLoad(made, 0, True), ReduceLoad(made_out, 0, True), ReduceLoad(made_in, 1, True)],
+    )
+    layer_keys = ((FFN_OUT, 1), (FFN_IN, 1), (ATTN_OUT, 1), (ATTN_IN, 1), (FFN_OUT, 0), (FFN_IN, 0), (ATTN_OUT, 0))
+    for key in layer_keys + ((ATTN_IN, 0),):
         carried = landed(key, carried)
-    out_sums, in_sums = carried
-    gain_grads[:2] = gain_one, gain_two
-
-    (own_first, total_small, scalars), carried = tail(
-        branch, ids_all, losses, gain_grads, squares, share, vocab, 4, 4,
-        [LineLoad(out_sums, wide), LineLoad(in_sums, wide)],
-    )
-    own[ATTN_OUT, 0], own[ATTN_IN, 0] = carried[0], carried[2]
     grad_attn_in, grad_attn_out, grad_ffn_in, grad_ffn_out = [
         jnp.stack([own[name, index] for index in range(layers)]) for name in (ATTN_IN, ATTN_OUT, FFN_IN, FFN_OUT)
     ]

time: 462 us -> 459 us (level)
    pallas_call x5 -> x4, Pallas kernels: 431 us -> 428 us  [run(): pl.pallas_call(kernel, out_shape=tuple(outs) + tuple((out for load in loa...]
where the time goes in v12:
time: 459 us; the launch traced here: 452 us
  Pallas kernels  428 us (93%)
  other arithmetic  12.5 us (3%)
  local copies, waits for them, and re-layouts  8.5 us (2%)
    pallas_call x4, Pallas kernels, run(): pl.pallas_call(kernel, out_shape=tuple(outs) + tuple((out for load in loa...  428 us
    convert_element_type x5, other arithmetic, adam(): return (weight_new, first_new, second_new, weight_new.astype(jnp.bfloat16))  10.5 us

profile of v12, /device:TPU:0, one launch (start us, length us, event | category | flops | bytes accessed | tf_op | source)
XLA Modules:
  0.0 452.5 jit_solution(15917121958735554044)
XLA Ops:
  0.7 0.6 multiply_exponential_fusion.refs_4_
  1.2 0.5 broadcast.79
  1.8 1.3 reduce.3
  3.1 0.6 reshape.110.refs_0_
  3.7 1.7 copy.50.refs_6_.refs_1_.refs_11_
  5.4 115.6 %front.1 = (f32[512,768]{1,0:T(8,128)}, bf16[1024,768]{1,0:T(8,128)(2,1)}, f32[8,768]{1,0:T(8,128)}, f32[8,128]{1,0:T(8,128)}, s32[8,4,256]{2,1,0:T(4,128)}, /*i...) custom-call(s32[4,256]{1,0:T(4,128)} %reshape.110.refs_0_, ...), custom_call_target="tpu_custom_call" | custom-call | tf_op jit(solution)/shard_map/front/pallas_call | solution.py:901
  121.1 1.2 slice.13
  122.3 115.4 %last_and_loss.1 = (bf16[3,1024,192]{2,1,0:T(8,128)(2,1)}, bf16[1024,192]{1,0:T(8,128)(2,1)}, f32[512,768]{1,0:T(8,128)}, bf16[1024,768]{1,0:T(8,128)(2,1)}, f32...) custom-call(bf16[1024,768]{1,0:T(8,128)(2,1)} %get-tuple-element.88., ...), custom_call_target="tpu_custom_call" | custom-call | tf_op jit(solution)/shard_map/last_and_loss/pallas_call | solution.py:901
  237.7 71.2 %backward_block.1 = (f32[512,768]{1,0:T(8,128)}, bf16[1024,768]{1,0:T(8,128)(2,1)}, bf16[8,96,192]{2,1,0:T(8,128)(2,1)}, bf16[3,8,96,192]{3,2,1,0:T(8,128)(2,1)}...) custom-call(f32[512,768]{1,0:T(8,128)} %get-tuple-element.96.refs_0_, ...), custom_call_target="tpu_custom_call" | custom-call | tf_op jit(solution)/shard_map/backward_block/pallas_call | solution.py:901
  308.9 0.0 copy-start.25
  309.0 0.0 copy-start.26
  309.0 0.0 copy-start.27
  309.0 0.0 copy-start.6
  309.0 0.0 copy-start.24
  309.0 126.0 %first_and_tail.1 = (f32[96,2048]{1,0:T(8,128)}, f32[8,128]{1,0:T(8,128)}, f32[8,128]{1,0:T(8,128)}, f32[96,768]{1,0:T(8,128)}, f32[8,128]{1,0:T(8,128)}, /*inde...) custom-call(f32[512,768]{1,0:T(8,128)} %get-tuple-element.108.refs_0, ...), custom_call_target="tpu_custom_call" | custom-call | tf_op jit(solution)/shard_map/first_and_tail/pallas_call | solution.py:901
  435.1 0.0 copy-start.1
  435.1 0.0 copy-start.8
  435.1 0.0 copy-start.9
  435.2 1.4 fusion.18
  437.3 1.3 fusion.6
  438.6 0.0 copy-done.6
  438.6 2.0 fusion.14
  440.6 0.0 copy-done.20
  440.6 0.0 copy-done.21
  440.6 0.0 copy-start.17
  440.6 0.1 maximum_bitcast_fusion
  440.7 0.0 copy-done.1
  440.7 0.0 copy-done.8
  440.7 0.0 copy-done.9
  440.7 0.0 copy-start.2
  440.7 0.0 copy-start.3
  440.8 0.0 copy-start.10
  440.8 0.0 copy-start.11
  440.8 0.0 copy-start.12
  440.8 0.0 copy-start.13
  440.8 1.6 fusion.16
  442.5 0.2 copy-done.10
  442.7 0.4 copy-done.11
  443.1 0.2 copy-done.12
  443.3 0.2 copy-done.13
  443.5 0.1 copy-done.14
  443.5 0.1 copy-done.15
  443.6 0.1 copy-done.16
  443.7 2.3 fusion.10
  446.1 1.0 copy-done.4
  447.1 0.5 copy-done.5
  447.6 0.2 copy-done.7
  447.8 3.3 fusion.8
  (25 shorter events, 0.1 us)
Async XLA Ops:
  308.9 128.3 %copy-start.25 = (f32[5,96]{1,0:T(8,128)S(1)}, f32[5,96]{1,0:T(8,128)}, u32[]{:S(2)}) copy-start(f32[5,96]{1,0:T(8,128)} %refs_2_.2) | copy-start | bytes 5764
  309.0 128.3 %copy-start.26 = (f32[5,96]{1,0:T(8,128)S(1)}, f32[5,96]{1,0:T(8,128)}, u32[]{:S(2)}) copy-start(f32[5,96]{1,0:T(8,128)} %param.39) | copy-start | bytes 5764
  309.0 128.3 %copy-start.27 = (f32[5,96]{1,0:T(8,128)S(1)}, f32[5,96]{1,0:T(8,128)}, u32[]{:S(2)}) copy-start(f32[5,96]{1,0:T(8,128)} %param.45) | copy-start | bytes 5764
  309.0 129.6 %copy-start.6 = (f32[2,96,192]{2,1,0:T(8,128)S(1)}, f32[2,96,192]{2,1,0:T(8,128)}, u32[]{:S(2)}) copy-start(f32[2,96,192]{2,1,0:T(8,128)} %refs_9_.2) | copy-start | bytes 442372
  309.0 129.6 %copy-start.24 = (f32[2,96,192]{2,1,0:T(8,128)S(1)}, f32[2,96,192]{2,1,0:T(8,128)}, u32[]{:S(2)}) copy-start(f32[2,96,192]{2,1,0:T(8,128)} %param.35) | copy-start | bytes 442372
  309.0 131.6 %copy-start.22 = (f32[96,512]{1,0:T(8,128)S(1)}, f32[96,512]{1,0:T(8,128)}, u32[]{:S(2)}) copy-start(f32[96,512]{1,0:T(8,128)} %get-tuple-element.146) | copy-start | bytes 589828
  309.0 131.6 %copy-start.23 = (f32[96,512]{1,0:T(8,128)S(1)}, f32[96,512]{1,0:T(8,128)}, u32[]{:S(2)}) copy-start(f32[96,512]{1,0:T(8,128)} %get-tuple-element.147) | copy-start | bytes 589828
  435.1 5.5 %copy-start.20 = (f32[96,512]{1,0:T(8,128)S(1)}, f32[96,512]{1,0:T(8,128)}, u32[]{:S(2)}) copy-start(f32[96,512]{1,0:T(8,128)} %get-tuple-element.144) | copy-start | bytes 589828
  435.1 5.5 %copy-start.21 = (f32[96,512]{1,0:T(8,128)S(1)}, f32[96,512]{1,0:T(8,128)}, u32[]{:S(2)}) copy-start(f32[96,512]{1,0:T(8,128)} %get-tuple-element.145) | copy-start | bytes 589828
  435.1 5.6 %copy-start.1 = (f32[2,3,96,192]{3,2,1,0:T(8,128)S(1)}, f32[2,3,96,192]{3,2,1,0:T(8,128)}, u32[]{:S(2)}) copy-start(f32[2,3,96,192]{3,2,1,0:T(8,128)} %refs_8_.2) | copy-start | bytes 1327108
  435.1 5.6 %copy-start.8 = (f32[2,3,96,192]{3,2,1,0:T(8,128)S(1)}, f32[2,3,96,192]{3,2,1,0:T(8,128)}, u32[]{:S(2)}) copy-start(f32[2,3,96,192]{3,2,1,0:T(8,128)} %param.34) | copy-start | bytes 1327108
  435.1 5.6 %copy-start.9 = (f32[2,3,96,192]{3,2,1,0:T(8,128)S(1)}, f32[2,3,96,192]{3,2,1,0:T(8,128)}, u32[]{:S(2)}) copy-start(f32[2,3,96,192]{3,2,1,0:T(8,128)} %param.40) | copy-start | bytes 1327108
  435.1 5.6 %copy-start.18 = (f32[3,96,192]{2,1,0:T(8,128)S(1)}, f32[3,96,192]{2,1,0:T(8,128)}, u32[]{:S(2)}) copy-start(f32[3,96,192]{2,1,0:T(8,128)} %get-tuple-element.136) | copy-start | bytes 663556
  435.1 5.6 %copy-start.19 = (f32[3,96,192]{2,1,0:T(8,128)S(1)}, f32[3,96,192]{2,1,0:T(8,128)}, u32[]{:S(2)}) copy-start(f32[3,96,192]{2,1,0:T(8,128)} %get-tuple-element.135) | copy-start | bytes 663556
  440.6 1.8 copy-start.17
  440.7 1.7 copy-start.2
  440.7 1.7 copy-start.3
  440.8 1.9 copy-start.10
  440.8 2.3 copy-start.11
  440.8 2.5 copy-start.12
  440.8 2.7 copy-start.13
  440.8 2.7 copy-start.14
  440.8 2.8 copy-start.15
  440.8 2.9 copy-start.16
  443.7 2.3 copy-start
  443.7 3.4 copy-start.4
  443.7 3.8 copy-start.5
  443.7 4.0 copy-start.7

commit v13 on v12

--- a/solution.py
+++ b/solution.py
@@ -1211,7 +1211,7 @@
         x = middle[rows, :] + second.take(j)
         result[rows, :] = x
         share_next.put(j, norm_of(x, gains[2 * layer + 2 : 2 * layer + 3, :]).astype(BF16))
-        if j == CHUNKS - 2:
+        if j == CHUNKS // 2 - 1:
             at_last()
     for j in range(CHUNKS):
         share_next.arrived(j)
@@ -1787,24 +1787,23 @@
     info[3:4, :] = mask / counts[COUNT_ROW : COUNT_ROW + 1, 0:1]
     info[4:5, :] = mask
     greet([{NARROW: lax.rem(me + k, 4)} for k in range(1, 4)] + carry.peers())
-    carry.begin(0, 1)
+    carry.begin(0, 1, 2)
 
     def at_half():
-        carry.begin(2)
+        carry.begin(3)
 
     def at_feed():
         carry.fetched()
         carry.end(0)
-        carry.hand_on(1)
-        carry.begin(3)
+        carry.hand_on(1, 2)
+        carry.begin(4)
 
     def at_sent():
         carry.leave(0, 1, 2, 3)
-        carry.hand_on(2)
-        carry.begin(4)
+        carry.hand_on(3)
 
     def at_last():
-        carry.hand_on(3)
+        carry.hand_on(4)
 
     forward_part(
         layer,
@@ -1813,7 +1812,6 @@
         normed, key_seg, query_seg, resid, gains,
         projected, mixed, middle, normed_two, log_sums, result, normed_next, *layer_refs,
     )
-    carry.hand_on(4)
     carry.end(1, 2, 3)
     loss_part(
         2 * layer + 2, normed_next, info, result, gains, carry.loads[1:], grad_out, branch, d_gain, losses, d_tables,

time: 459 us -> 460 us (level)
  no operation moved by 1% of the time
where the time goes in v13:
time: 460 us; the launch traced here: 453 us
  Pallas kernels  429 us (93%)
  other arithmetic  12.5 us (3%)
  local copies, waits for them, and re-layouts  8.5 us (2%)
    pallas_call x4, Pallas kernels, run(): pl.pallas_call(kernel, out_shape=tuple(outs) + tuple((out for load in loa...  429 us
    convert_element_type x5, other arithmetic, adam(): return (weight_new, first_new, second_new, weight_new.astype(jnp.bfloat16))  10.5 us

profile of v13, /device:TPU:0, one launch (start us, length us, event | category | flops | bytes accessed | tf_op | source)
XLA Modules:
  0.0 453.5 jit_solution(12736484350408310292)
XLA Ops:
  0.7 0.6 multiply_exponential_fusion.refs_4_
  1.2 0.5 broadcast.79
  1.8 1.3 reduce.3
  3.1 0.6 reshape.110.refs_0_
  3.7 1.7 copy.50.refs_6_.refs_1_.refs_11_
  5.4 115.6 %front.1 = (f32[512,768]{1,0:T(8,128)}, bf16[1024,768]{1,0:T(8,128)(2,1)}, f32[8,768]{1,0:T(8,128)}, f32[8,128]{1,0:T(8,128)}, s32[8,4,256]{2,1,0:T(4,128)}, /*i...) custom-call(s32[4,256]{1,0:T(4,128)} %reshape.110.refs_0_, ...), custom_call_target="tpu_custom_call" | custom-call | tf_op jit(solution)/shard_map/front/pallas_call | solution.py:901
  121.1 1.2 slice.13
  122.3 109.0 %last_and_loss.1 = (bf16[3,1024,192]{2,1,0:T(8,128)(2,1)}, bf16[1024,192]{1,0:T(8,128)(2,1)}, f32[512,768]{1,0:T(8,128)}, bf16[1024,768]{1,0:T(8,128)(2,1)}, f32...) custom-call(bf16[1024,768]{1,0:T(8,128)(2,1)} %get-tuple-element.88., ...), custom_call_target="tpu_custom_call" | custom-call | tf_op jit(solution)/shard_map/last_and_loss/pallas_call | solution.py:901
  231.3 78.2 %backward_block.1 = (f32[512,768]{1,0:T(8,128)}, bf16[1024,768]{1,0:T(8,128)(2,1)}, bf16[8,96,192]{2,1,0:T(8,128)(2,1)}, bf16[3,8,96,192]{3,2,1,0:T(8,128)(2,1)}...) custom-call(f32[512,768]{1,0:T(8,128)} %get-tuple-element.96.refs_0_, ...), custom_call_target="tpu_custom_call" | custom-call | tf_op jit(solution)/shard_map/backward_block/pallas_call | solution.py:901
  309.5 0.0 copy-start.25
  309.5 0.0 copy-start.26
  309.6 0.0 copy-start.27
  309.6 0.0 copy-start.6
  309.6 0.0 copy-start.24
  309.6 0.0 copy-start.22
  309.6 0.0 copy-start.23
  309.6 126.5 %first_and_tail.1 = (f32[96,2048]{1,0:T(8,128)}, f32[8,128]{1,0:T(8,128)}, f32[8,128]{1,0:T(8,128)}, f32[96,768]{1,0:T(8,128)}, f32[8,128]{1,0:T(8,128)}, /*inde...) custom-call(f32[512,768]{1,0:T(8,128)} %get-tuple-element.108.refs_0, ...), custom_call_target="tpu_custom_call" | custom-call | tf_op jit(solution)/shard_map/first_and_tail/pallas_call | solution.py:901
  436.1 0.0 copy-start.1
  436.1 0.0 copy-start.8
  436.1 0.0 copy-start.9
  436.2 1.4 fusion.18
  438.3 1.3 fusion.6
  439.6 0.0 copy-done.24
  439.6 2.0 fusion.14
  441.6 0.0 copy-done.22
  441.6 0.1 maximum_bitcast_fusion
  441.7 0.0 copy-start.2
  441.7 0.0 copy-start.3
  441.8 0.0 copy-start.10
  441.8 0.0 copy-start.11
  441.8 0.0 copy-start.12
  441.8 0.0 copy-start.13
  441.8 0.0 copy-start.14
  441.8 0.0 copy-start.15
  441.8 0.0 copy-start.16
  441.8 1.6 fusion.16
  443.5 0.2 copy-done.10
  443.7 0.4 copy-done.11
  444.1 0.2 copy-done.12
  444.3 0.2 copy-done.13
  444.5 0.1 copy-done.14
  444.5 0.1 copy-done.15
  444.6 0.1 copy-done.16
  444.7 2.3 fusion.10
  447.1 1.0 copy-done.4
  448.1 0.5 copy-done.5
  448.6 0.2 copy-done.7
  448.8 3.3 fusion.8
  (25 shorter events, 0.1 us)
Async XLA Ops:
  309.5 128.8 %copy-start.25 = (f32[5,96]{1,0:T(8,128)S(1)}, f32[5,96]{1,0:T(8,128)}, u32[]{:S(2)}) copy-start(f32[5,96]{1,0:T(8,128)} %refs_2_.2) | copy-start | bytes 5764
  309.5 128.8 %copy-start.26 = (f32[5,96]{1,0:T(8,128)S(1)}, f32[5,96]{1,0:T(8,128)}, u32[]{:S(2)}) copy-start(f32[5,96]{1,0:T(8,128)} %param.39) | copy-start | bytes 5764
  309.6 128.8 %copy-start.27 = (f32[5,96]{1,0:T(8,128)S(1)}, f32[5,96]{1,0:T(8,128)}, u32[]{:S(2)}) copy-start(f32[5,96]{1,0:T(8,128)} %param.45) | copy-start | bytes 5764
  309.6 130.1 %copy-start.6 = (f32[2,96,192]{2,1,0:T(8,128)S(1)}, f32[2,96,192]{2,1,0:T(8,128)}, u32[]{:S(2)}) copy-start(f32[2,96,192]{2,1,0:T(8,128)} %refs_9_.2) | copy-start | bytes 442372
  309.6 130.1 %copy-start.24 = (f32[2,96,192]{2,1,0:T(8,128)S(1)}, f32[2,96,192]{2,1,0:T(8,128)}, u32[]{:S(2)}) copy-start(f32[2,96,192]{2,1,0:T(8,128)} %param.35) | copy-start | bytes 442372
  309.6 132.0 %copy-start.22 = (f32[96,512]{1,0:T(8,128)S(1)}, f32[96,512]{1,0:T(8,128)}, u32[]{:S(2)}) copy-start(f32[96,512]{1,0:T(8,128)} %get-tuple-element.146) | copy-start | bytes 589828
  309.6 132.0 %copy-start.23 = (f32[96,512]{1,0:T(8,128)S(1)}, f32[96,512]{1,0:T(8,128)}, u32[]{:S(2)}) copy-start(f32[96,512]{1,0:T(8,128)} %get-tuple-element.147) | copy-start | bytes 589828
  436.1 5.5 %copy-start.20 = (f32[96,512]{1,0:T(8,128)S(1)}, f32[96,512]{1,0:T(8,128)}, u32[]{:S(2)}) copy-start(f32[96,512]{1,0:T(8,128)} %get-tuple-element.144) | copy-start | bytes 589828
  436.1 5.5 %copy-start.21 = (f32[96,512]{1,0:T(8,128)S(1)}, f32[96,512]{1,0:T(8,128)}, u32[]{:S(2)}) copy-start(f32[96,512]{1,0:T(8,128)} %get-tuple-element.145) | copy-start | bytes 589828
  436.1 5.6 %copy-start.1 = (f32[2,3,96,192]{3,2,1,0:T(8,128)S(1)}, f32[2,3,96,192]{3,2,1,0:T(8,128)}, u32[]{:S(2)}) copy-start(f32[2,3,96,192]{3,2,1,0:T(8,128)} %refs_8_.2) | copy-start | bytes 1327108
  436.1 5.6 %copy-start.8 = (f32[2,3,96,192]{3,2,1,0:T(8,128)S(1)}, f32[2,3,96,192]{3,2,1,0:T(8,128)}, u32[]{:S(2)}) copy-start(f32[2,3,96,192]{3,2,1,0:T(8,128)} %param.34) | copy-start | bytes 1327108
  436.1 5.6 %copy-start.9 = (f32[2,3,96,192]{3,2,1,0:T(8,128)S(1)}, f32[2,3,96,192]{3,2,1,0:T(8,128)}, u32[]{:S(2)}) copy-start(f32[2,3,96,192]{3,2,1,0:T(8,128)} %param.40) | copy-start | bytes 1327108
  436.1 5.6 %copy-start.18 = (f32[3,96,192]{2,1,0:T(8,128)S(1)}, f32[3,96,192]{2,1,0:T(8,128)}, u32[]{:S(2)}) copy-start(f32[3,96,192]{2,1,0:T(8,128)} %get-tuple-element.136) | copy-start | bytes 663556
  436.1 5.6 %copy-start.19 = (f32[3,96,192]{2,1,0:T(8,128)S(1)}, f32[3,96,192]{2,1,0:T(8,128)}, u32[]{:S(2)}) copy-start(f32[3,96,192]{2,1,0:T(8,128)} %get-tuple-element.135) | copy-start | bytes 663556
  441.6 1.8 copy-start.17
  441.7 1.7 copy-start.2
  441.7 1.7 copy-start.3
  441.8 1.9 copy-start.10
  441.8 2.3 copy-start.11
  441.8 2.5 copy-start.12
  441.8 2.7 copy-start.13
  441.8 2.7 copy-start.14
  441.8 2.8 copy-start.15
  441.8 2.9 copy-start.16
  444.7 2.3 copy-start
  444.7 3.4 copy-start.4
  444.7 3.8 copy-start.5
  444.7 4.0 copy-start.7
